TPU v7x, 32 devices: a whole 2x2x4 slice. The times are simulated.
32 devices in a mesh: batch: 4 (over y, x), seq: 8 (over z, core).
Axes of the slice: x: 2, y: 2, z: 4, core: 2. Of those that a mesh axis runs over, the one named last changes fastest.
Arguments:
- layer_input: bfloat16 [4, 1024, 1024], P('batch', 'seq'), may hold values from -6 to 6
- segment_ids: int32 [4, 1024], P('batch', 'seq'), may hold values from 0 to 7, never falling along the last dimension, each value on 1 to 512 neighbouring positions
- out_cotangent: bfloat16 [4, 1024, 1024], P('batch', 'seq'), may hold values from -6 to 6
- key_weight: bfloat16 [1024, 1024], P(('batch', 'seq')), may hold values from -0.1875 to 0.1875
- value_weight: bfloat16 [1024, 1024], P(('batch', 'seq')), may hold values from -0.1875 to 0.1875
- recept_weight: bfloat16 [1024, 1024], P(('batch', 'seq')), may hold values from -0.1875 to 0.1875
- output_weight: bfloat16 [1024, 1024], P(('batch', 'seq')), may hold values from -0.75 to 0.75
- channel_key: bfloat16 [1024, 4096], P(('batch', 'seq')), may hold values from -0.1875 to 0.1875
- channel_value: bfloat16 [4096, 1024], P(('batch', 'seq')), may hold values from -0.09375 to 0.09375
- channel_recept: bfloat16 [1024, 1024], P(('batch', 'seq')), may hold values from -0.1875 to 0.1875
- norm_gains: bfloat16 [2, 1024], P(None, ('batch', 'seq')), may hold values from 0.5 to 1.5
- norm_offsets: bfloat16 [2, 1024], P(None, ('batch', 'seq')), may hold values from -1.5 to 1.5
- mix_coeffs: bfloat16 [5, 1024], P(None, ('batch', 'seq')), may hold values from 0.049804688 to 0.94921875
- time_decay: bfloat16 [1024], P(('batch', 'seq')), may hold values from -7.59375 to -2.296875
- time_first: bfloat16 [1024], P(('batch', 'seq')), may hold values from -1 to 1
Outputs:
- block_output: bfloat16 [4, 1024, 1024], P('batch', 'seq')
- input_grad: float32 [4, 1024, 1024], P('batch', 'seq')
- key_grad: float32 [1024, 1024], P(('batch', 'seq'))
- value_grad: float32 [1024, 1024], P(('batch', 'seq'))
- recept_grad: float32 [1024, 1024], P(('batch', 'seq'))
- output_grad: float32 [1024, 1024], P(('batch', 'seq'))
- channel_key_grad: float32 [1024, 4096], P(('batch', 'seq'))
- channel_value_grad: float32 [4096, 1024], P(('batch', 'seq'))
- channel_recept_grad: float32 [1024, 1024], P(('batch', 'seq'))
- gains_grad: float32 [2, 1024], P(None, ('batch', 'seq'))
- offsets_grad: float32 [2, 1024], P(None, ('batch', 'seq'))
- mixes_grad: float32 [5, 1024], P(None, ('batch', 'seq'))
- decay_grad: float32 [1024], P(('batch', 'seq'))
- first_grad: float32 [1024], P(('batch', 'seq'))
Inputs may be any that keep to these rules, and one draw needn't show every extreme that they name: `segment_ids`: within a row the ids never fall and start at 0; each id marks one document of 1 to 512 positions, and one document has exactly 512.
All inputs are finite; a program needn't handle non-finite values.
Results may differ from a plain program's by a relative error of at most 0.008.
Values may be sent and summed in bfloat16 or wider, within the bound.
No kernel may reach another device: no remote copies, remote signals or barrier semaphores. Data moves between devices by JAX's collectives and lax.ppermute only.
A program may use at most 256 MiB of HBM per device.

v0:
```python
import jax
import jax.numpy as jnp
from jax import lax
from jax.sharding import PartitionSpec as P

EPS = 1e-05


def from_behind(block, axis, distance):
    devices = range(lax.axis_size(axis))
    route = [(i - distance, i) for i in devices if i - distance in devices]
    return lax.ppermute(block, axis, route)


def carried_in(x, axis, combine, identity, reverse):
    count, place = (lax.axis_size(axis), lax.axis_index(axis))
    everything = jax.tree.map(lambda part: lax.all_gather(part, axis), x)
    start = jax.tree.map(
        lambda part, zero: jnp.broadcast_to(jnp.asarray(zero, part.dtype), part.shape), x, identity
    )

    def hop(k, before):
        at = count - 1 - k if reverse else k
        reached = at > place if reverse else at < place
        new = combine(before, jax.tree.map(lambda part: part[at], everything))
        return jax.tree.map(lambda a, b: jnp.where(reached, a, b), new, before)

    return lax.fori_loop(0, count, hop, start)


def norm_forward(hidden, gain, offset):
    centred = hidden - jnp.mean(hidden, axis=-1, keepdims=True)
    scale = lax.rsqrt(jnp.mean(centred * centred, axis=-1, keepdims=True) + EPS)
    normed = centred * scale
    return (normed * gain + offset, normed, scale)


def norm_backward(grad, normed, scale, gain):
    gain_grad = jnp.sum(grad * normed, axis=(0, 1))
    offset_grad = jnp.sum(grad, axis=(0, 1))
    inner = grad * gain
    centred = inner - jnp.mean(inner, axis=-1, keepdims=True)
    input_part = scale * (centred - normed * jnp.mean(inner * normed, axis=-1, keepdims=True))
    return (input_part, gain_grad, offset_grad)


def linear_chain(earlier, later):
    return (
        later[0] + later[2] * earlier[0],
        later[1] + later[2] * earlier[1],
        earlier[2] * later[2],
    )


def shift_in(normed, before, continues):
    previous = jnp.concatenate([before[:, None, :], normed[:, :-1, :]], axis=1)
    return previous * continues[:, :, None]


def mixing(normed, prior, coeff):
    return (normed * coeff + prior * (1.0 - coeff)).astype(jnp.bfloat16)


def unmix(grad_mix, normed, prior, coeff):
    return (
        grad_mix * coeff,
        grad_mix * (1.0 - coeff),
        jnp.sum(grad_mix * (normed - prior), axis=(0, 1)),
    )


def project(active, weight):
    return jnp.einsum("rtd,de->rte", active, weight, preferred_element_type=jnp.float32)


def back_project(grad, weight):
    return jnp.einsum("rte,de->rtd", grad, weight, preferred_element_type=jnp.float32)


def weight_term(active, grad):
    return jnp.einsum("rtd,rte->de", active, grad, preferred_element_type=jnp.float32)


def local_sums(lookup_squashed, payload_squashed, fading_pace, restart_markers):
    row_count, token_count, feature_count = lookup_squashed.shape
    block_len = min(128, token_count)
    blocks = token_count // block_len
    shape_four = (row_count, blocks, block_len, feature_count)
    key_blocks = lookup_squashed.reshape(shape_four)
    value_blocks = payload_squashed.reshape(shape_four)
    reset_blocks = restart_markers.reshape(row_count, blocks, block_len)
    positions = jnp.arange(block_len, dtype=jnp.int32)
    places = positions.astype(jnp.float32)[:, None]
    inclusive = (positions[:, None] >= positions[None, :]).astype(jnp.float32)
    earlier = positions[:, None] > positions[None, :]
    counts = jnp.einsum("ts,rbs->rbt", inclusive, reset_blocks, precision=lax.Precision.HIGHEST)
    same_doc = jnp.abs(counts[..., :, None] - counts[..., None, :]) < 0.5
    inner_mask = jnp.logical_and(same_doc, earlier).astype(jnp.float32)
    growth = jnp.exp(key_blocks + fading_pace * places)
    weighted = growth * value_blocks
    shrink = jnp.exp(-fading_pace * (places - 1.0))
    inner_num = shrink * jnp.einsum(
        "rbts,rbsf->rbtf", inner_mask, weighted, precision=lax.Precision.HIGHEST
    )
    inner_den = shrink * jnp.einsum(
        "rbts,rbsf->rbtf", inner_mask, growth, precision=lax.Precision.HIGHEST
    )
    last_mask = (jnp.abs(counts - counts[..., -1:]) < 0.5).astype(jnp.float32)
    tail_factor = jnp.exp(-fading_pace * (block_len - 1.0))
    end_num = tail_factor * jnp.einsum(
        "rbs,rbsf->rbf", last_mask, weighted, precision=lax.Precision.HIGHEST
    )
    end_den = tail_factor * jnp.einsum(
        "rbs,rbsf->rbf", last_mask, growth, precision=lax.Precision.HIGHEST
    )
    opened = (counts < 0.5).astype(jnp.float32)
    block_factor = opened[:, :, -1:] * jnp.exp(-fading_pace * float(block_len))
    totals = lax.associative_scan(linear_chain, (end_num, end_den, block_factor), axis=1)
    carry_num = jnp.concatenate([jnp.zeros_like(end_num), totals[0][:, :-1]], axis=1)
    carry_den = jnp.concatenate([jnp.zeros_like(end_den), totals[1][:, :-1]], axis=1)
    reach_factor = opened[..., None] * jnp.exp(-fading_pace * places)
    segment_numerator = (inner_num + reach_factor * carry_num[:, :, None, :]).reshape(
        lookup_squashed.shape
    )
    portion_divisor = (inner_den + reach_factor * carry_den[:, :, None, :]).reshape(
        lookup_squashed.shape
    )
    return (
        segment_numerator,
        portion_divisor,
        totals[0][:, -1],
        totals[1][:, -1],
        totals[2][:, -1],
    )


def wkv_finish(
    segment_numerator,
    portion_divisor,
    lookup_squashed,
    payload_squashed,
    fading_pace,
    initial_reward,
    restart_markers,
    state_numerator,
    carried_divisor,
):
    places = jnp.arange(lookup_squashed.shape[1], dtype=jnp.float32)[:, None]
    still_open = (jnp.cumsum(restart_markers, axis=1) < 0.5).astype(jnp.float32)
    packet_beginning = still_open[..., None] * jnp.exp(-fading_pace * places)
    reward_table = jnp.exp(initial_reward + lookup_squashed)
    cumulative_dividend = (
        segment_numerator
        + packet_beginning * state_numerator[:, None, :]
        + reward_table * payload_squashed
    )
    cumulative_divisor = (
        portion_divisor + packet_beginning * carried_divisor[:, None, :] + reward_table
    )
    return (cumulative_dividend / cumulative_divisor, cumulative_divisor, packet_beginning)


def full_weighted_values(
    lookup_squashed,
    payload_squashed,
    fading_exponent,
    initial_reward,
    restart_markers,
    state_numerator,
    carried_divisor,
):
    fading_pace = jnp.exp(fading_exponent)
    segment_numerator, portion_divisor, sum_num, sum_den, factor = local_sums(
        lookup_squashed, payload_squashed, fading_pace, restart_markers
    )
    mixed_out = wkv_finish(
        segment_numerator,
        portion_divisor,
        lookup_squashed,
        payload_squashed,
        fading_pace,
        initial_reward,
        restart_markers,
        state_numerator,
        carried_divisor,
    )[0]
    return (mixed_out, sum_num + factor * state_numerator, sum_den + factor * carried_divisor)


def per_device(
    layer_input,
    segment_ids,
    out_cotangent,
    key_weight,
    value_weight,
    recept_weight,
    output_weight,
    channel_key,
    channel_value,
    channel_recept,
    norm_gains,
    norm_offsets,
    mix_coeffs,
    time_decay,
    time_first,
):
    piece_settings = (
        lax.all_gather(key_weight, ("batch", "seq"), axis=0, tiled=True),
        lax.all_gather(value_weight, ("batch", "seq"), axis=0, tiled=True),
        lax.all_gather(recept_weight, ("batch", "seq"), axis=0, tiled=True),
        lax.all_gather(output_weight, ("batch", "seq"), axis=0, tiled=True),
        lax.all_gather(norm_gains, ("batch", "seq"), axis=1, tiled=True),
        lax.all_gather(norm_offsets, ("batch", "seq"), axis=1, tiled=True),
        lax.all_gather(mix_coeffs, ("batch", "seq"), axis=1, tiled=True),
        lax.all_gather(time_decay, ("batch", "seq"), axis=0, tiled=True),
        lax.all_gather(time_first, ("batch", "seq"), axis=0, tiled=True),
    )
    amplitude_lines = piece_settings[4].astype(jnp.float32)
    shifting_lines = piece_settings[5].astype(jnp.float32)
    blend_coefficient_lines = piece_settings[6].astype(jnp.float32)
    fading_exponent = piece_settings[7].astype(jnp.float32)
    initial_reward = piece_settings[8].astype(jnp.float32)
    hidden = layer_input.astype(jnp.float32)
    normed_one, unit_one, scale_one = norm_forward(hidden, amplitude_lines[0], shifting_lines[0])
    before_one, before_id = from_behind(
        (normed_one[:, -1, :], segment_ids[:, -1].astype(jnp.float32)), "seq", 1
    )
    ids_float = segment_ids.astype(jnp.float32)
    previous_ids = jnp.concatenate([before_id[:, None], ids_float[:, :-1]], axis=1)
    continues = (ids_float == previous_ids).astype(jnp.float32)
    restart_markers = 1.0 - continues
    prior_one = shift_in(normed_one, before_one, continues)
    mix_key = mixing(normed_one, prior_one, blend_coefficient_lines[0])
    mix_value = mixing(normed_one, prior_one, blend_coefficient_lines[1])
    mix_recept = mixing(normed_one, prior_one, blend_coefficient_lines[2])
    lookup_squashed = project(mix_key, piece_settings[0])
    payload_squashed = project(mix_value, piece_settings[1])
    recept_act = jax.nn.sigmoid(project(mix_recept, piece_settings[2]))
    fading_pace = jnp.exp(fading_exponent)
    segment_numerator, portion_divisor, sum_num, sum_den, factor = local_sums(
        lookup_squashed, payload_squashed, fading_pace, restart_markers
    )
    identity = (jnp.zeros_like(sum_num), jnp.zeros_like(sum_den), jnp.ones_like(factor))
    state_numerator, carried_divisor, ignored_factor = carried_in(
        (sum_num, sum_den, factor), "seq", linear_chain, identity, False
    )
    scaled_lookup_payloads, cumulative_divisor, packet_beginning = wkv_finish(
        segment_numerator,
        portion_divisor,
        lookup_squashed,
        payload_squashed,
        fading_pace,
        initial_reward,
        restart_markers,
        state_numerator,
        carried_divisor,
    )
    gated = (recept_act * scaled_lookup_payloads).astype(jnp.bfloat16)
    middle = hidden + project(gated, piece_settings[3])
    channel_set = (
        lax.all_gather(channel_key, ("batch", "seq"), axis=0, tiled=True),
        lax.all_gather(channel_value, ("batch", "seq"), axis=0, tiled=True),
        lax.all_gather(channel_recept, ("batch", "seq"), axis=0, tiled=True),
    )
    normed_two, unit_two, scale_two = norm_forward(middle, amplitude_lines[1], shifting_lines[1])
    before_two = from_behind(normed_two[:, -1, :], "seq", 1)
    prior_two = shift_in(normed_two, before_two, continues)
    mix_hidden = mixing(normed_two, prior_two, blend_coefficient_lines[3])
    mix_gate = mixing(normed_two, prior_two, blend_coefficient_lines[4])
    hidden_pre = project(mix_hidden, channel_set[0])
    squared = jnp.square(jax.nn.relu(hidden_pre)).astype(jnp.bfloat16)
    channel_out = project(squared, channel_set[1])
    gate_act = jax.nn.sigmoid(project(mix_gate, channel_set[2]))
    block_output = (middle + gate_act * channel_out).astype(jnp.bfloat16)
    channel_back = (
        lax.all_gather(channel_key, ("batch", "seq"), axis=0, tiled=True),
        lax.all_gather(channel_value, ("batch", "seq"), axis=0, tiled=True),
        lax.all_gather(channel_recept, ("batch", "seq"), axis=0, tiled=True),
    )
    grad_out = out_cotangent.astype(jnp.float32)
    grad_values = (grad_out * gate_act).astype(jnp.bfloat16)
    grad_gate = (grad_out * channel_out * gate_act * (1.0 - gate_act)).astype(jnp.bfloat16)
    grad_squared = back_project(grad_values, channel_back[1])
    grad_hidden = (grad_squared * 2.0 * jax.nn.relu(hidden_pre)).astype(jnp.bfloat16)
    paired_sum = lax.psum_scatter(
        jnp.concatenate(
            [weight_term(mix_hidden, grad_hidden), weight_term(mix_gate, grad_gate)], axis=1
        ),
        ("batch", "seq"),
        scatter_dimension=0,
        tiled=True,
    )
    value_sum = lax.psum_scatter(
        weight_term(squared, grad_values), ("batch", "seq"), scatter_dimension=0, tiled=True
    )
    hidden_width = channel_key.shape[1]
    channel_key_grad = paired_sum[:, :hidden_width]
    channel_recept_grad = paired_sum[:, hidden_width:]
    grad_mix_hidden = back_project(grad_hidden, channel_back[0])
    grad_mix_gate = back_project(grad_gate, channel_back[2])
    own_hidden, passed_hidden, mix_grad_three = unmix(
        grad_mix_hidden, normed_two, prior_two, blend_coefficient_lines[3]
    )
    own_gate, passed_gate, mix_grad_four = unmix(
        grad_mix_gate, normed_two, prior_two, blend_coefficient_lines[4]
    )
    passed_two = (passed_hidden + passed_gate) * continues[..., None]
    after_two = from_behind(passed_two[:, 0, :], "seq", -1)
    grad_normed_two = (
        own_hidden
        + own_gate
        + jnp.concatenate([passed_two[:, 1:, :], after_two[:, None, :]], axis=1)
    )
    middle_part, gain_grad_two, offset_grad_two = norm_backward(
        grad_normed_two, unit_two, scale_two, amplitude_lines[1]
    )
    grad_middle = grad_out + middle_part
    token_back = (
        lax.all_gather(key_weight, ("batch", "seq"), axis=0, tiled=True),
        lax.all_gather(value_weight, ("batch", "seq"), axis=0, tiled=True),
        lax.all_gather(recept_weight, ("batch", "seq"), axis=0, tiled=True),
        lax.all_gather(output_weight, ("batch", "seq"), axis=0, tiled=True),
    )
    grad_attended = grad_middle.astype(jnp.bfloat16)
    output_term = weight_term(gated, grad_attended)
    grad_gated = back_project(grad_attended, token_back[3])
    grad_wkv = grad_gated * recept_act
    grad_recept = (grad_gated * scaled_lookup_payloads * recept_act * (1.0 - recept_act)).astype(
        jnp.bfloat16
    )
    share = grad_wkv * packet_beginning / cumulative_divisor
    direct_num = jnp.sum(share, axis=1)
    direct_den = -jnp.sum(share * scaled_lookup_payloads, axis=1)
    adjoint_num, adjoint_den, ignored_back = carried_in(
        (direct_num, direct_den, factor), "seq", linear_chain, identity, True
    )

    def entire_scaled_payloads(lookup_feed, payload_feed, fading_feed, reward_feed):
        return full_weighted_values(
            lookup_feed,
            payload_feed,
            fading_feed,
            reward_feed,
            restart_markers,
            state_numerator,
            carried_divisor,
        )

    discarded_output, backward_function = jax.vjp(
        entire_scaled_payloads, lookup_squashed, payload_squashed, fading_exponent, initial_reward
    )
    grad_key, grad_value, decay_term, first_term = backward_function(
        (grad_wkv, adjoint_num, adjoint_den)
    )
    grad_key_low = grad_key.astype(jnp.bfloat16)
    grad_value_low = grad_value.astype(jnp.bfloat16)
    key_term = weight_term(mix_key, grad_key_low)
    value_term = weight_term(mix_value, grad_value_low)
    recept_term = weight_term(mix_recept, grad_recept)
    grad_mix_key = back_project(grad_key_low, token_back[0])
    grad_mix_value = back_project(grad_value_low, token_back[1])
    grad_mix_recept = back_project(grad_recept, token_back[2])
    own_key, passed_key, mix_grad_zero = unmix(
        grad_mix_key, normed_one, prior_one, blend_coefficient_lines[0]
    )
    own_value, passed_value, mix_grad_one = unmix(
        grad_mix_value, normed_one, prior_one, blend_coefficient_lines[1]
    )
    own_recept, passed_recept, mix_grad_two = unmix(
        grad_mix_recept, normed_one, prior_one, blend_coefficient_lines[2]
    )
    passed_one = (passed_key + passed_value + passed_recept) * continues[..., None]
    after_one = from_behind(passed_one[:, 0, :], "seq", -1)
    grad_normed_one = (
        own_key
        + own_value
        + own_recept
        + jnp.concatenate([passed_one[:, 1:, :], after_one[:, None, :]], axis=1)
    )
    input_part, gain_grad_one, offset_grad_one = norm_backward(
        grad_normed_one, unit_one, scale_one, amplitude_lines[0]
    )
    input_grad = grad_middle + input_part
    gains_term = jnp.stack([gain_grad_one, gain_grad_two])
    offsets_term = jnp.stack([offset_grad_one, offset_grad_two])
    mixes_term = jnp.stack(
        [mix_grad_zero, mix_grad_one, mix_grad_two, mix_grad_three, mix_grad_four]
    )
    token_grads = (
        lax.psum_scatter(key_term, ("batch", "seq"), scatter_dimension=0, tiled=True),
        lax.psum_scatter(value_term, ("batch", "seq"), scatter_dimension=0, tiled=True),
        lax.psum_scatter(recept_term, ("batch", "seq"), scatter_dimension=0, tiled=True),
        lax.psum_scatter(output_term, ("batch", "seq"), scatter_dimension=0, tiled=True),
        lax.psum_scatter(gains_term, ("batch", "seq"), scatter_dimension=1, tiled=True),
        lax.psum_scatter(offsets_term, ("batch", "seq"), scatter_dimension=1, tiled=True),
        lax.psum_scatter(mixes_term, ("batch", "seq"), scatter_dimension=1, tiled=True),
        lax.psum_scatter(decay_term, ("batch", "seq"), scatter_dimension=0, tiled=True),
        lax.psum_scatter(first_term, ("batch", "seq"), scatter_dimension=0, tiled=True),
    )
    return (
        block_output,
        input_grad,
        token_grads[0],
        token_grads[1],
        token_grads[2],
        token_grads[3],
        channel_key_grad,
        value_sum,
        channel_recept_grad,
        token_grads[4],
        token_grads[5],
        token_grads[6],
        token_grads[7],
        token_grads[8],
    )


def solution(mesh):
    placed = (
        P("batch", "seq", None),
        P("batch", "seq"),
        P("batch", "seq", None),
        P(("batch", "seq"), None),
        P(("batch", "seq"), None),
        P(("batch", "seq"), None),
        P(("batch", "seq"), None),
        P(("batch", "seq"), None),
        P(("batch", "seq"), None),
        P(("batch", "seq"), None),
        P(None, ("batch", "seq")),
        P(None, ("batch", "seq")),
        P(None, ("batch", "seq")),
        P(("batch", "seq")),
        P(("batch", "seq")),
    )
    return jax.shard_map(
        per_device,
        mesh=mesh,
        in_specs=placed,
        out_specs=(
            P("batch", "seq", None),
            P("batch", "seq", None),
            P(("batch", "seq"), None),
            P(("batch", "seq"), None),
            P(("batch", "seq"), None),
            P(("batch", "seq"), None),
            P(("batch", "seq"), None),
            P(("batch", "seq"), None),
            P(("batch", "seq"), None),
            P(None, ("batch", "seq")),
            P(None, ("batch", "seq")),
            P(None, ("batch", "seq")),
            P(("batch", "seq")),
            P(("batch", "seq")),
        ),
        check_vma=False,
    )
```

profile of v0, /device:TPU:8, one launch (start us, length us, event | category | flops | bytes accessed | tf_op | source)
XLA Modules:
  0.0 1918.5 jit_solution(14674058062903814626)
XLA Ops:
  13.9 2.9 collective-permute-start.1
  16.7 37.0 %all-gather.5 = bf16[32,32,2]{1,2,0:T(2,128)(2,1)S(1)} all-gather(bf16[1,32,2]{1,2,0:T(2,128)(2,1)} %bitcast.418), channel_id=1, replica_groups=mesh['batch'=4,'seq'=8] {'batch','seq'}, dimensions={0}, use_global_device_ids=true | all-gather | bytes 4224 | tf_op jit(solution)/shard_map/all_gather | solution.py:212
  53.8 41.5 %all-gather.6 = bf16[32,32,2]{1,2,0:T(2,128)(2,1)S(1)} all-gather(bf16[1,32,2]{1,2,0:T(2,128)(2,1)} %bitcast.419), channel_id=1, replica_groups=mesh['batch'=4,'seq'=8] {'batch','seq'}, dimensions={0}, use_global_device_ids=true | all-gather | bytes 4224 | tf_op jit(solution)/shard_map/all_gather | solution.py:213
  98.9 2.2 collective-permute-start
  101.7 38.3 %all-reduce.5 = (bf16[1024]{0:T(1024)(128)(2,1)S(1)}, bf16[1024]{0:T(1024)(128)(2,1)S(1)}) all-reduce(bf16[1024]{0:T(1024)(128)(2,1)S(1)} %dynamic-update-slice, bf16[1024]{0:T(1024)(128)(2,1)S(1)} %dynamic-update-slice.1), channel_id=1, replica_groups=mesh['batch'=4,'seq'=8] {'batch','seq'}, use_global_device_ids=true, to_apply=%add | all-reduce | flops 2048 | bytes 8192
  140.0 38.4 %all-gather.7 = bf16[32,32,5]{1,2,0:T(8,128)(2,1)S(1)} all-gather(bf16[1,32,5]{1,2,0:T(8,128)(2,1)S(1)} %bitcast.417), channel_id=1, replica_groups=mesh['batch'=4,'seq'=8] {'batch','seq'}, dimensions={0}, use_global_device_ids=true | all-gather | bytes 10560 | tf_op jit(solution)/shard_map/all_gather | solution.py:214
  182.3 2.2 fusion.102
  185.7 2.2 fusion.98
  189.6 13.8 all-gather
  203.5 14.0 all-gather.1
  217.4 14.0 all-gather.2
  233.1 4.1 multiply_convert_fusion.2
  237.2 5.8 all-gather.22.cloned.1.call-done
  243.1 2.2 fusion.113
  245.7 2.3 collective-permute-start.2
  248.1 2.5 collective-permute-done.2
  251.7 49.5 %all-gather.24.cloned.1.call-done = bf16[1024,1024]{1,0:T(8,128)(2,1)} async-done(((bf16[32,1024]{1,0:T(8,128)(2,1)}), bf16[1024,1024]{1,0:T(8,128)(2,1)}) %all-gather.24.cloned.1.call-update) | async-done | bytes 2097168 | tf_op jit(solution)/shard_map/all_gather | solution.py:263
  301.3 2.9 fusion.9
  304.1 77.2 %all-gather.26.cloned.1.call-done = bf16[1024,4096]{1,0:T(8,128)(2,1)} async-done(((bf16[32,4096]{1,0:T(8,128)(2,1)}), bf16[1024,4096]{1,0:T(8,128)(2,1)}) %all-gather.26.cloned.1.call-update) | async-done | bytes 8388624 | tf_op jit(solution)/shard_map/all_gather | solution.py:261
  381.3 4.8 convolution_maximum_fusion
  386.1 74.1 %all-gather.28.cloned.1.call-done = bf16[4096,1024]{1,0:T(8,128)(2,1)} async-done(((bf16[128,1024]{1,0:T(8,128)(2,1)}), bf16[4096,1024]{1,0:T(8,128)(2,1)}) %all-gather.28.cloned.1.call-update) | async-done | bytes 8388624 | tf_op jit(solution)/shard_map/all_gather | solution.py:262
  460.2 6.6 fusion.3
  466.9 8.2 fusion.119
  475.2 2.1 fusion.56
  477.4 2.9 fusion.114
  481.3 2.5 collective-permute-start.3
  488.3 2.4 fusion.109
  490.8 13.5 all-gather.4
  504.3 14.0 all-gather.3
  521.3 2.0 fusion.15
  528.7 3.1 collective-permute-start.4
  536.8 2.7 fusion.120
  540.7 16.1 pad_maximum_fusion
  557.8 3.7 fusion.58
  561.5 3.9 fusion.104
  565.7 3.9 fusion.96
  569.8 3.8 fusion.100
  574.6 9.2 fusion.48
  584.6 39.3 %all-reduce.4 = (f32[1024]{0:T(1024)S(1)}, f32[1024]{0:T(1024)S(1)}) all-reduce(f32[1024]{0:T(1024)S(1)} %add_multiply_fusion.1, f32[1024]{0:T(1024)S(1)} %copy-done.75), channel_id=16, replica_groups=mesh['batch'=4,'seq'=8] {'batch','seq'}, use_global_device_ids=true, to_apply=%region_37.38.clone | all-reduce | flops 2048 | bytes 16384
  626.2 37.4 %reduce-scatter.28.cloned.1.call-done = f32[32,2]{1,0:T(8,128)} async-done(((f32[1024,2]{1,0:T(8,128)}), f32[32,2]{1,0:T(8,128)}) %reduce-scatter.28.cloned.1.call-update) | async-done | bytes 272
  665.0 131.4 %reduce-scatter.30.cloned.1.call-done = f32[32,2]{1,0:T(8,128)} async-done(((f32[1024,2]{1,0:T(8,128)}), f32[32,2]{1,0:T(8,128)}) %reduce-scatter.30.cloned.1.call-update) | async-done | bytes 272
  797.7 130.6 %reduce-scatter.32.cloned.1.call-done = f32[32,5]{1,0:T(8,128)} async-done(((f32[1024,5]{1,0:T(8,128)}), f32[32,5]{1,0:T(8,128)}) %reduce-scatter.32.cloned.1.call-update) | async-done | bytes 656
  929.7 226.4 %reduce-scatter.24.cloned.1.call-done = f32[32,5120]{1,0:T(8,128)} async-done(((f32[1024,5120]{1,0:T(8,128)}), f32[32,5120]{1,0:T(8,128)}) %reduce-scatter.24.cloned.1.call-update) | async-done | bytes 655376 | tf_op jit(solution)/shard_map/reduce_scatter | solution.py:285
  1159.6 139.0 %reduce-scatter.22.cloned.1.call-done = f32[32,1024]{1,0:T(8,128)} async-done(((f32[1024,1024]{1,0:T(8,128)}), f32[32,1024]{1,0:T(8,128)}) %reduce-scatter.22.cloned.1.call-update) | async-done | bytes 131088 | tf_op jit(solution)/shard_map/reduce_scatter | solution.py:393
  1298.6 142.9 %reduce-scatter.20.cloned.1.call-done = f32[32,1024]{1,0:T(8,128)} async-done(((f32[1024,1024]{1,0:T(8,128)}), f32[32,1024]{1,0:T(8,128)}) %reduce-scatter.20.cloned.1.call-update) | async-done | bytes 131088 | tf_op jit(solution)/shard_map/reduce_scatter | solution.py:392
  1441.6 141.9 %reduce-scatter.18.cloned.1.call-done = f32[32,1024]{1,0:T(8,128)} async-done(((f32[1024,1024]{1,0:T(8,128)}), f32[32,1024]{1,0:T(8,128)}) %reduce-scatter.18.cloned.1.call-update) | async-done | bytes 131088 | tf_op jit(solution)/shard_map/reduce_scatter | solution.py:391
  1583.5 142.4 %reduce-scatter.16.cloned.1.call-done = f32[32,1024]{1,0:T(8,128)} async-done(((f32[1024,1024]{1,0:T(8,128)}), f32[32,1024]{1,0:T(8,128)}) %reduce-scatter.16.cloned.1.call-update) | async-done | bytes 131088 | tf_op jit(solution)/shard_map/reduce_scatter | solution.py:390
  1725.9 185.6 %reduce-scatter.26.cloned.1.call-done = f32[128,1024]{1,0:T(8,128)} async-done(((f32[4096,1024]{1,0:T(8,128)}), f32[128,1024]{1,0:T(8,128)}) %reduce-scatter.26.cloned.1.call-update) | async-done | bytes 524304 | tf_op jit(solution)/shard_map/reduce_scatter | solution.py:293
  (331 shorter events, 52.6 us)
Async XLA Ops:
  7.2 94.0 %copy-start.83 = (s32[1,128]{1,0:T(1,128)S(1)}, s32[1,128]{1,0:T(1,128)}, u32[]{:S(2)}) copy-start(s32[1,128]{1,0:T(1,128)} %param.20) | copy-start | bytes 1540
  7.2 175.1 %copy-start = (bf16[1,128,1024]{2,1,0:T(8,128)(2,1)S(1)}, bf16[1,128,1024]{2,1,0:T(8,128)(2,1)}, u32[]{:S(2)}) copy-start(bf16[1,128,1024]{2,1,0:T(8,128)(2,1)} %param.19) | copy-start | bytes 786436
  7.2 94.0 %copy-start.84 = (bf16[32]{0:T(256)(128)(2,1)S(1)}, bf16[32]{0:T(256)(128)(2,1)}, u32[]{:S(2)}) copy-start(bf16[32]{0:T(256)(128)(2,1)} %param.32) | copy-start | bytes 196
  7.2 94.2 %copy-start.85 = (bf16[32]{0:T(256)(128)(2,1)S(1)}, bf16[32]{0:T(256)(128)(2,1)}, u32[]{:S(2)}) copy-start(bf16[32]{0:T(256)(128)(2,1)} %param.33) | copy-start | bytes 196
  7.2 132.8 %copy-start.82 = (bf16[5,32]{1,0:T(8,128)(2,1)S(1)}, bf16[5,32]{1,0:T(8,128)(2,1)}, u32[]{:S(2)}) copy-start(bf16[5,32]{1,0:T(8,128)(2,1)} %param.31) | copy-start | bytes 964
  7.2 175.1 %all-gather.18.cloned.1.call-start = ((), (), s32[]{:S(2)}) async-start(), calls=%async_computation.10 | async-start | bytes 2162688 | tf_op jit(solution)/shard_map/all_gather | solution.py:208
  8.0 177.7 %all-gather.20.cloned.1.call-start = ((), (), s32[]{:S(2)}) async-start(), calls=%async_computation.11 | async-start | bytes 2162688 | tf_op jit(solution)/shard_map/all_gather | solution.py:209
  8.7 224.3 %all-gather.16.cloned.1.call-start = ((), (), s32[]{:S(2)}) async-start(), calls=%async_computation.9 | async-start | bytes 2162688 | tf_op jit(solution)/shard_map/all_gather | solution.py:210
  9.4 233.6 %all-gather.22.cloned.1.call-start = ((), (), s32[]{:S(2)}) async-start(), calls=%async_computation.12 | async-start | bytes 2162688 | tf_op jit(solution)/shard_map/all_gather | solution.py:211
  10.0 291.2 %all-gather.24.cloned.1.call-start = ((), (), s32[]{:S(2)}) async-start(), calls=%async_computation.13 | async-start | bytes 2162688 | tf_op jit(solution)/shard_map/all_gather | solution.py:263
  10.6 370.7 %all-gather.26.cloned.1.call-start = ((), (), s32[]{:S(2)}) async-start(), calls=%async_computation.14 | async-start | bytes 8650752 | tf_op jit(solution)/shard_map/all_gather | solution.py:261
  11.2 449.0 %all-gather.28.cloned.1.call-start = ((), (), s32[]{:S(2)}) async-start(), calls=%async_computation.15 | async-start | bytes 8650752 | tf_op jit(solution)/shard_map/all_gather | solution.py:262
  11.9 651.7 %reduce-scatter.28.cloned.1.call-start = ((), (), s32[]{:S(2)}) async-start(), calls=%async_computation.22 | async-start | bytes 540672
  13.9 164.8 %collective-permute-start.1 = (f32[1]{0:T(128)}, f32[1]{0:T(128)}, u32[]{:S(2)}, u32[]{:S(2)}) collective-permute-start(f32[1]{0:T(128)} %bitcast.14), channel_id=1, source_target_pairs={{0,1},{1,2},{2,3},{3,4},{4,5},{5,6},{6,7},{8,9},{9,10},{10,11},{11... | collective-permute-start | bytes 20 | tf_op jit(solution)/shard_map/ppermute | solution.py:12
  96.5 136.6 %copy-start.63 = (f32[128]{0:T(128)}, f32[128]{0:T(128)S(1)}, u32[]{:S(2)}) copy-start(f32[128]{0:T(128)S(1)} %broadcast_multiply_fusion.5) | copy-start | bytes 1540
  97.7 135.4 %copy-start.69 = (f32[128]{0:T(128)}, f32[128]{0:T(128)S(1)}, u32[]{:S(2)}) copy-start(f32[128]{0:T(128)S(1)} %add_rsqrt_fusion.1) | copy-start | bytes 1540
  98.9 134.2 %copy-start.1 = (f32[1,128,1024]{2,1,0:T(8,128)}, f32[1,128,1024]{2,1,0:T(8,128)S(1)}, u32[]{:S(2)}) copy-start(f32[1,128,1024]{2,1,0:T(8,128)S(1)} %fusion.22) | copy-start | bytes 1572868
  98.9 83.4 %collective-permute-start = (f32[1,1024]{1,0:T(1,128)S(1)}, f32[1,1024]{1,0:T(1,128)S(1)}, u32[]{:S(2)}, u32[]{:S(2)}) collective-permute-start(f32[1,1024]{1,0:T(1,128)S(1)} %slice_bitcast_fusion.5), channel_id=1, source_target_pairs={{0,1},{1,2},{2,3},{3,4},{4,5},{5,6},{6,7},{8,9},{9,10},{10,11},{11... | collective-permute-start | bytes 12296 | tf_op jit(solution)/shard_map/ppermute | solution.py:12
  140.0 49.0 %copy-start.59 = (bf16[1024]{0:T(1024)(128)(2,1)}, bf16[1024]{0:T(1024)(128)(2,1)S(1)}, u32[]{:S(2)}) copy-start(bf16[1024]{0:T(1024)(128)(2,1)S(1)} %get-tuple-element.420) | copy-start | bytes 6148
  140.0 347.6 %copy-start.53 = (f32[1024]{0:T(1024)}, f32[1024]{0:T(1024)S(1)}, u32[]{:S(2)}) copy-start(f32[1024]{0:T(1024)S(1)} %convert_element_type.151) | copy-start | bytes 12292
  178.6 54.5 %copy-start.67 = (f32[128]{0:T(128)}, f32[128]{0:T(128)S(1)}, u32[]{:S(2)}) copy-start(f32[128]{0:T(128)S(1)} %iota_convert_fusion) | copy-start | bytes 1540
  178.6 54.5 %copy-start.78 = (f32[128]{0:T(128)}, f32[128]{0:T(128)S(1)}, u32[]{:S(2)}) copy-start(f32[128]{0:T(128)S(1)} %broadcast_add_fusion) | copy-start | bytes 1540
  178.6 54.5 %copy-start.51 = (f32[1024]{0:T(1024)}, f32[1024]{0:T(1024)S(1)}, u32[]{:S(2)}) copy-start(f32[1024]{0:T(1024)S(1)} %broadcast_subtract_fusion.4) | copy-start | bytes 12292
  179.3 301.7 %copy-start.61 = (f32[1,128]{1,0:T(1,128)}, f32[1,128]{1,0:T(1,128)S(1)}, u32[]{:S(2)}) copy-start(f32[1,128]{1,0:T(1,128)S(1)} %get-tuple-element.433) | copy-start | bytes 1540
  179.5 52.5 %copy-start.46 = (f32[1,128]{1,0:T(1,128)}, f32[1,128]{1,0:T(1,128)S(1)}, u32[]{:S(2)}) copy-start(f32[1,128]{1,0:T(1,128)S(1)} %fusion.73) | copy-start | bytes 1540
  181.7 306.0 %copy-start.80 = (f32[128]{0:T(128)}, f32[128]{0:T(128)S(1)}, u32[]{:S(2)}) copy-start(f32[128]{0:T(128)S(1)} %convert_reduce_fusion.1) | copy-start | bytes 1540
  182.3 50.8 %copy-start.44 = (f32[1,1024]{1,0:T(1,128)}, f32[1,1024]{1,0:T(1,128)S(1)}, u32[]{:S(2)}) copy-start(f32[1,1024]{1,0:T(1,128)S(1)} %collective-permute-done) | copy-start | bytes 12292
  187.8 45.3 %copy-start.8 = (f32[128,1024]{1,0:T(8,128)}, f32[128,1024]{1,0:T(8,128)S(1)}, u32[]{:S(2)}) copy-start(f32[128,1024]{1,0:T(8,128)S(1)} %fusion.98) | copy-start | bytes 1572868
  189.0 14.5 copy-start.49
  245.3 241.1 %copy-start.65 = (f32[128]{0:T(128)}, f32[128]{0:T(128)S(1)}, u32[]{:S(2)}) copy-start(f32[128]{0:T(128)S(1)} %broadcast_multiply_fusion.4) | copy-start | bytes 1540
  245.5 240.9 %copy-start.76 = (f32[128]{0:T(128)}, f32[128]{0:T(128)S(1)}, u32[]{:S(2)}) copy-start(f32[128]{0:T(128)S(1)} %add_rsqrt_fusion) | copy-start | bytes 1540
  245.7 58.4 %copy-start.12 = (f32[1,128,1024]{2,1,0:T(8,128)}, f32[1,128,1024]{2,1,0:T(8,128)S(1)}, u32[]{:S(2)}) copy-start(f32[1,128,1024]{2,1,0:T(8,128)S(1)} %multiply_add_fusion) | copy-start | bytes 1572868
  245.7 4.9 collective-permute-start.2
  250.6 53.5 %copy-start.73 = (f32[1,1024]{1,0:T(1,128)}, f32[1,1024]{1,0:T(1,128)S(1)}, u32[]{:S(2)}) copy-start(f32[1,1024]{1,0:T(1,128)S(1)} %collective-permute-done.2) | copy-start | bytes 12292
  251.7 129.6 %copy-start.37 = (bf16[128,1024]{1,0:T(8,128)(2,1)}, bf16[128,1024]{1,0:T(8,128)(2,1)S(1)}, u32[]{:S(2)}) copy-start(bf16[128,1024]{1,0:T(8,128)(2,1)S(1)} %get-tuple-element.440) | copy-start | bytes 786436
  460.2 15.0 slice-start
  466.9 10.4 slice-start.2
  481.3 3.6 collective-permute-start.3
  528.7 4.4 collective-permute-start.4
  535.6 260.7 %reduce-scatter.30.cloned.1.call-start = ((), (), s32[]{:S(2)}) async-start(), calls=%async_computation.23 | async-start | bytes 540672
  536.7 391.6 %reduce-scatter.32.cloned.1.call-start = ((), (), s32[]{:S(2)}) async-start(), calls=%async_computation.24 | async-start | bytes 540672
  540.6 615.5 %reduce-scatter.24.cloned.1.call-start = ((), (), s32[]{:S(2)}) async-start(), calls=%async_computation.20 | async-start | bytes 21626880 | tf_op jit(solution)/shard_map/reduce_scatter | solution.py:285
  556.8 741.9 %reduce-scatter.22.cloned.1.call-start = ((), (), s32[]{:S(2)}) async-start(), calls=%async_computation.19 | async-start | bytes 4325376 | tf_op jit(solution)/shard_map/reduce_scatter | solution.py:393
  561.5 880.1 %reduce-scatter.20.cloned.1.call-start = ((), (), s32[]{:S(2)}) async-start(), calls=%async_computation.18 | async-start | bytes 4325376 | tf_op jit(solution)/shard_map/reduce_scatter | solution.py:392
  565.4 1018.0 %reduce-scatter.18.cloned.1.call-start = ((), (), s32[]{:S(2)}) async-start(), calls=%async_computation.17 | async-start | bytes 4325376 | tf_op jit(solution)/shard_map/reduce_scatter | solution.py:391
  569.7 1156.2 %reduce-scatter.16.cloned.1.call-start = ((), (), s32[]{:S(2)}) async-start(), calls=%async_computation.16 | async-start | bytes 4325376 | tf_op jit(solution)/shard_map/reduce_scatter | solution.py:390
  573.6 1337.9 %reduce-scatter.26.cloned.1.call-start = ((), (), s32[]{:S(2)}) async-start(), calls=%async_computation.21 | async-start | bytes 17301504 | tf_op jit(solution)/shard_map/reduce_scatter | solution.py:293
  583.8 41.3 %copy-start.17 = (f32[128,1024]{1,0:T(8,128)S(1)}, f32[128,1024]{1,0:T(8,128)}, u32[]{:S(2)}) copy-start(f32[128,1024]{1,0:T(8,128)} %copy-done.16) | copy-start | bytes 1572868
  (63 other events, 219.1 us)
Sparse Core Ops, SparseCore 0:
  11.0 56.7 all-gather.17
  70.8 55.4 all-gather.19
  129.3 55.4 all-gather.15
  187.6 55.3 all-gather.21
  245.9 55.3 all-gather.23
  304.1 77.1 all-gather.25
  384.3 75.8 all-gather.27
  535.7 127.8 reduce-scatter.27
  665.9 130.3 reduce-scatter.29
  798.4 129.8 reduce-scatter.31
  930.7 225.3 reduce-scatter.23
  1158.9 139.6 reduce-scatter.21
  1301.6 139.9 reduce-scatter.19
  1444.4 139.0 reduce-scatter.17
  1586.3 139.5 reduce-scatter.15
  1728.7 182.7 reduce-scatter.25
where the time goes:
time: 1940 us; the launch traced here: 1920 us
  waiting for transfers between devices  1490 us (77%)
  blocking collectives  264 us (14%)
  matrix products  76.6 us (4%)
  other arithmetic  33.4 us (2%)
  local copies, waits for them, and re-layouts  19.9 us (1%)
    unnamed x19, waiting for transfers between devices  304 us
    reduce_scatter x1, waiting for transfers between devices, per_device(): lax.psum_scatter(jnp.concatenate([weight_term(mix_hidden, grad_hidden), w...  226 us
    reduce_scatter x1, waiting for transfers between devices, per_device(): lax.psum_scatter(weight_term(squared, grad_values), ('batch', 'seq'), sca...  186 us
    reduce_scatter x1, waiting for transfers between devices, per_device(): lax.psum_scatter(recept_term, ('batch', 'seq'), scatter_dimension=0, tile...  143 us
    reduce_scatter x1, waiting for transfers between devices, per_device(): lax.psum_scatter(key_term, ('batch', 'seq'), scatter_dimension=0, tiled=T...  142 us
    reduce_scatter x1, waiting for transfers between devices, per_device(): lax.psum_scatter(value_term, ('batch', 'seq'), scatter_dimension=0, tiled...  142 us
    reduce_scatter x1, waiting for transfers between devices, per_device(): lax.psum_scatter(output_term, ('batch', 'seq'), scatter_dimension=0, tile...  139 us
    unnamed x2, blocking collectives  77.6 us
  transfers between devices with their start and end apart: 21, of which 16 were waited for; matrix products, arithmetic and copies ran while one was open for 5% of the time, Pallas kernels for 0%

commit v1 on v0

v1 whole, which is shorter than its diff:
```python
import jax
import jax.numpy as jnp
from jax import lax
from jax.experimental import pallas as pl
from jax.experimental.pallas import tpu as pltpu
from jax.sharding import PartitionSpec as P

EPS = 1e-05
BOTH = ("batch", "seq")
LOW = jnp.bfloat16
FULL = jnp.float32
LANES = 128
SUBS = 8


def sizes():
    return lax.axis_size("batch"), lax.axis_size("seq")


def send(block, route):
    rows, cols = sizes()
    pairs = []
    for b in range(rows):
        for s in range(cols):
            target = route(b, s)
            if target is not None:
                pairs.append((b * cols + s, target[0] * cols + target[1]))
    return lax.ppermute(block, BOTH, pairs)


def send_next(block):
    cols = lax.axis_size("seq")
    return send(block, lambda b, s: (b, s + 1) if s + 1 < cols else None)


def send_back(block):
    return send(block, lambda b, s: (b, s - 1) if s > 0 else None)


def to_core(block):
    return send(block, lambda b, s: (b, s ^ 1))


def to_batch(block, k):
    return send(block, lambda b, s: (b ^ k, s))


def to_depth(block, k):
    return send(block, lambda b, s: (b, s ^ (2 * k)))


def share_rows(block):
    rows = lax.axis_size("batch")
    return jnp.concatenate([block] + [to_batch(block, k) for k in range(1, rows)], axis=0)


def return_rows(parts):
    rows = lax.axis_size("batch")
    count = parts.shape[0] // rows
    total = parts[:count]
    low = parts.astype(LOW)
    for k in range(1, rows):
        total = total + to_batch(low[k * count : (k + 1) * count], k).astype(FULL)
    return total


def scatter_sums(terms):
    rows, cols = sizes()
    b, s = lax.axis_index("batch"), lax.axis_index("seq")
    depth = cols // 2
    core, z = s % 2, s // 2
    count, height, width = terms.shape
    own = height // (rows * cols)

    def pick(x, at, axis):
        return lax.dynamic_index_in_dim(x, at, axis, keepdims=False)

    x = terms.astype(LOW).reshape(count, rows, depth, 2, own, width)
    got = to_core(pick(x, 1 - core, 3))
    y = (pick(x, core, 3).astype(FULL) + got.astype(FULL)).astype(LOW)
    total = pick(y, b, 1).astype(FULL)
    for k in range(1, rows):
        total = total + to_batch(pick(y, b ^ k, 1), k).astype(FULL)
    low = total.astype(LOW)
    result = pick(total, z, 1)
    for k in range(1, depth):
        result = result + to_depth(pick(low, z ^ k, 1), k).astype(FULL)
    return result


def sum_vectors(x):
    rows, cols = sizes()
    x = x + to_core(x)
    x = sum([to_batch(x, k) for k in range(1, rows)], x)
    return sum([to_depth(x, k) for k in range(1, cols // 2)], x)


def norm_forward(hidden, gain, offset):
    centred = hidden - jnp.mean(hidden, axis=-1, keepdims=True)
    scale = lax.rsqrt(jnp.mean(centred * centred, axis=-1, keepdims=True) + EPS)
    normed = centred * scale
    return normed * gain + offset, normed, scale


def norm_backward(grad, normed, scale, gain):
    gain_grad = jnp.sum(grad * normed, axis=0)
    offset_grad = jnp.sum(grad, axis=0)
    inner = grad * gain
    centred = inner - jnp.mean(inner, axis=-1, keepdims=True)
    input_part = scale * (centred - normed * jnp.mean(inner * normed, axis=-1, keepdims=True))
    return input_part, gain_grad, offset_grad


def mixing(normed, prior, coeff):
    return (normed * coeff + prior * (1.0 - coeff)).astype(LOW)


def project(active, weight):
    return jnp.einsum("td,de->te", active, weight, preferred_element_type=FULL)


def back_project(grad, weight):
    return jnp.einsum("te,de->td", grad, weight, preferred_element_type=FULL)


def weight_term(active, grad):
    return jnp.einsum("td,te->de", active, grad, preferred_element_type=FULL)


def to_tiles(x):
    count, width = x.shape
    blocks = width // LANES
    x = x.reshape(count // SUBS, SUBS, blocks, LANES).transpose(0, 2, 1, 3)
    return x.reshape(count * blocks, LANES)


def from_tiles(x, width):
    blocks = width // LANES
    count = x.shape[0] // blocks
    x = x.reshape(count // SUBS, blocks, SUBS, LANES).transpose(0, 2, 1, 3)
    return x.reshape(count, width)


def position(i, r, blocks):
    return pl.ds(i * (SUBS * blocks) + r, blocks, stride=SUBS)


def forward_scan(keep_ref, key_ref, value_ref, rates_ref, carry_ref, wkv_ref, inverse_ref, slope_ref):
    blocks = rates_ref.shape[1]
    fade, bonus = rates_ref[0], rates_ref[1]

    def eight(i, state):
        num, den, num_slope, den_slope = state
        for r in range(SUBS):
            at = position(i, r, blocks)
            key, value = key_ref[at, :], value_ref[at, :]
            keep = keep_ref[pl.ds(i * SUBS + r, 1), :]
            num, den, num_slope, den_slope = (
                num * keep,
                den * keep,
                num_slope * keep,
                den_slope * keep,
            )
            reward = jnp.exp(bonus + key)
            weight = jnp.exp(key)
            inverse = 1.0 / (den + reward)
            wkv = (num + reward * value) * inverse
            wkv_ref[at, :] = wkv
            inverse_ref[at, :] = inverse
            slope_ref[at, :] = (num_slope - wkv * den_slope) * inverse
            num_slope = fade * (num_slope + num)
            den_slope = fade * (den_slope + den)
            num = fade * num + weight * value
            den = fade * den + weight
        return num, den, num_slope, den_slope

    lax.fori_loop(
        0,
        keep_ref.shape[0] // SUBS,
        eight,
        (carry_ref[0], carry_ref[1], carry_ref[2], carry_ref[3]),
    )


def backward_scan(
    keep_ref, key_ref, value_ref, wkv_ref, share_ref, rates_ref, carry_ref, key_out, value_out, first_out
):
    blocks = rates_ref.shape[1]
    fade, bonus = rates_ref[0], rates_ref[1]
    groups = keep_ref.shape[0] // SUBS

    def eight(step, state):
        direct, scaled, first = state
        i = groups - 1 - step
        for r in reversed(range(SUBS)):
            at = position(i, r, blocks)
            key, value = key_ref[at, :], value_ref[at, :]
            wkv, share = wkv_ref[at, :], share_ref[at, :]
            keep = keep_ref[pl.ds(i * SUBS + r, 1), :]
            reward = share * jnp.exp(bonus + key)
            weight = jnp.exp(key)
            bonus_part = reward * (value - wkv)
            key_out[at, :] = weight * (direct * value - scaled) + bonus_part
            value_out[at, :] = weight * direct + reward
            first = first + bonus_part
            direct = (share + fade * direct) * keep
            scaled = (share * wkv + fade * scaled) * keep
        return direct, scaled, first

    first_out[...] = lax.fori_loop(
        0, groups, eight, (carry_ref[0], carry_ref[1], jnp.zeros_like(fade))
    )[2]


IN_VMEM = pl.BlockSpec(memory_space=pltpu.VMEM)
SMALL = pltpu.CompilerParams(vmem_limit_bytes=8 * 1024 * 1024)


def run_forward(keep, key, value, rates, carry):
    tiles = jax.ShapeDtypeStruct(key.shape, FULL)
    return pl.pallas_call(
        forward_scan,
        out_shape=(tiles, tiles, tiles),
        in_specs=[IN_VMEM] * 5,
        out_specs=(IN_VMEM,) * 3,
        compiler_params=SMALL,
        cost_estimate=pl.CostEstimate(
            flops=20 * key.size, bytes_accessed=20 * key.size, transcendentals=3 * key.size
        ),
    )(keep, key, value, rates, carry)


def run_backward(keep, key, value, wkv, share, rates, carry):
    tiles = jax.ShapeDtypeStruct(key.shape, FULL)
    return pl.pallas_call(
        backward_scan,
        out_shape=(tiles, tiles, jax.ShapeDtypeStruct(rates.shape[1:], FULL)),
        in_specs=[IN_VMEM] * 7,
        out_specs=(IN_VMEM,) * 3,
        compiler_params=SMALL,
        cost_estimate=pl.CostEstimate(
            flops=20 * key.size, bytes_accessed=24 * key.size, transcendentals=2 * key.size
        ),
    )(keep, key, value, wkv, share, rates, carry)


def per_device(
    layer_input,
    segment_ids,
    out_cotangent,
    key_weight,
    value_weight,
    recept_weight,
    output_weight,
    channel_key,
    channel_value,
    channel_recept,
    norm_gains,
    norm_offsets,
    mix_coeffs,
    time_decay,
    time_first,
):
    rows, cols = sizes()
    b, s = lax.axis_index("batch"), lax.axis_index("seq")
    device = b * cols + s
    length, width = layer_input.shape[1:]
    own = key_weight.shape[0]
    hidden_width = channel_key.shape[1]
    part_width = hidden_width // rows
    blocks = width // LANES

    raw = layer_input[0]
    ids = segment_ids[0].astype(FULL)
    edge = jnp.stack([raw[-1], jnp.full((width,), ids[-1]).astype(LOW)])
    edge = send_next(edge)
    before_id = jnp.where(s == 0, -1.0, edge[1, 0].astype(FULL))

    vectors = jnp.concatenate(
        [norm_gains, norm_offsets, mix_coeffs, time_decay[None], time_first[None]], axis=0
    )
    n_vectors = vectors.shape[0]
    vector_row = jnp.pad(vectors.reshape(1, -1), ((0, 15), (0, width - n_vectors * own)))
    packed = jnp.concatenate(
        [key_weight, value_weight, recept_weight, output_weight, channel_recept, vector_row], axis=0
    )
    gathered = lax.all_gather(packed, BOTH, axis=0)
    key_all, value_all, recept_all, output_all, gate_all = (
        gathered[:, i * own : (i + 1) * own].reshape(width, width) for i in range(5)
    )
    vectors = gathered[:, 5 * own, : n_vectors * own].reshape(rows * cols, n_vectors, own)
    vectors = vectors.transpose(1, 0, 2).reshape(n_vectors, width).astype(FULL)
    gains, offsets, coeffs = vectors[0:2], vectors[2:4], vectors[4:9]
    pace, bonus = jnp.exp(vectors[9]), vectors[10]

    crossed = channel_key.reshape(own, rows, part_width).transpose(1, 0, 2)
    crossed = lax.all_to_all(crossed, "batch", 0, 0)
    part_key = lax.all_gather(crossed, "seq", axis=1, tiled=True).reshape(width, part_width)
    part_value = lax.all_gather(channel_value, "seq", axis=0, tiled=True)

    hidden = raw.astype(FULL)
    normed_one, unit_one, scale_one = norm_forward(hidden, gains[0], offsets[0])
    edge_normed = norm_forward(edge[0:1].astype(FULL), gains[0], offsets[0])[0]
    previous_ids = jnp.concatenate([before_id[None], ids[:-1]])
    keep = (ids == previous_ids).astype(FULL)
    opened = (ids == before_id)[:, None]
    closing = (ids == ids[-1])[:, None]
    prior_one = jnp.concatenate([edge_normed, normed_one[:-1]], axis=0) * keep[:, None]
    mix_key = mixing(normed_one, prior_one, coeffs[0])
    mix_value = mixing(normed_one, prior_one, coeffs[1])
    mix_recept = mixing(normed_one, prior_one, coeffs[2])
    key_act = project(mix_key, key_all)
    value_act = project(mix_value, value_all)
    recept_act = jax.nn.sigmoid(project(mix_recept, recept_all))

    places = jnp.arange(length, dtype=FULL)[:, None]
    left = length - 1.0 - places
    sum_den = jnp.where(closing, jnp.exp(key_act - pace * left), 0.0)
    sum_num = sum_den * value_act
    local = jnp.stack(
        [
            jnp.sum(sum_num, axis=0),
            jnp.sum(sum_den, axis=0),
            jnp.sum(sum_num * left, axis=0),
            jnp.sum(sum_den * left, axis=0),
            jnp.full((width,), ids[-1]),
        ]
    )
    every = lax.all_gather(jnp.pad(local, ((0, 3), (0, 0))), "seq")
    order = jnp.arange(cols)
    span = (length * jnp.maximum(s - 1 - order, 0)).astype(FULL)[:, None]
    valid = ((order < s) & (every[:, 4, 0] == before_id))[:, None]
    reach = jnp.exp(-pace * span)
    carry = jnp.stack(
        [
            jnp.sum(jnp.where(valid, reach * every[:, 0], 0.0), axis=0),
            jnp.sum(jnp.where(valid, reach * every[:, 1], 0.0), axis=0),
            jnp.sum(jnp.where(valid, reach * (every[:, 2] + span * every[:, 0]), 0.0), axis=0),
            jnp.sum(jnp.where(valid, reach * (every[:, 3] + span * every[:, 1]), 0.0), axis=0),
        ]
    ).reshape(4, blocks, LANES)
    keep_lanes = jnp.broadcast_to(keep[:, None], (length, LANES))
    rates = jnp.stack([jnp.exp(-pace), bonus]).reshape(2, blocks, LANES)
    key_tiles, value_tiles = to_tiles(key_act), to_tiles(value_act)
    wkv_tiles, inverse_tiles, slope_tiles = run_forward(
        keep_lanes, key_tiles, value_tiles, rates, carry
    )
    wkv = from_tiles(wkv_tiles, width)
    inverse = from_tiles(inverse_tiles, width)
    slope = from_tiles(slope_tiles, width)
    gated = (recept_act * wkv).astype(LOW)
    middle = hidden + project(gated, output_all)

    normed_two, unit_two, scale_two = norm_forward(middle, gains[1], offsets[1])
    before_two = send_next(normed_two[-1:])
    prior_two = jnp.concatenate([before_two, normed_two[:-1]], axis=0) * keep[:, None]
    mix_hidden = mixing(normed_two, prior_two, coeffs[3])
    mix_gate = mixing(normed_two, prior_two, coeffs[4])
    shared = share_rows(mix_hidden)
    positive = jax.nn.relu(project(shared, part_key))
    squared = jnp.square(positive).astype(LOW)
    channel_out = return_rows(project(squared, part_value))
    gate = jax.nn.sigmoid(project(mix_gate, gate_all))
    block_output = (middle + gate * channel_out).astype(LOW)

    grad_out = out_cotangent[0].astype(FULL)
    grad_values = (grad_out * gate).astype(LOW)
    grad_gate = (grad_out * channel_out * gate * (1.0 - gate)).astype(LOW)
    shared_grad = share_rows(grad_values)
    grad_hidden = (back_project(shared_grad, part_value) * 2.0 * positive).astype(LOW)
    value_term = weight_term(squared, shared_grad).astype(LOW)
    hidden_term = weight_term(shared, grad_hidden).astype(LOW)
    grad_mix_hidden = return_rows(back_project(grad_hidden, part_key))
    grad_mix_gate = back_project(grad_gate, gate_all)
    channel_value_grad = lax.psum_scatter(value_term, "seq", scatter_dimension=0, tiled=True)
    hidden_term = hidden_term.reshape(rows, cols * own, part_width)
    hidden_sum = lax.psum_scatter(hidden_term, "seq", scatter_dimension=1, tiled=True)
    hidden_sum = lax.all_to_all(hidden_sum, "batch", 0, 0)
    channel_key_grad = hidden_sum.transpose(1, 0, 2).reshape(own, hidden_width).astype(FULL)

    own_two = grad_mix_hidden * coeffs[3] + grad_mix_gate * coeffs[4]
    passed_two = (
        grad_mix_hidden * (1.0 - coeffs[3]) + grad_mix_gate * (1.0 - coeffs[4])
    ) * keep[:, None]
    after_two = send_back(passed_two[:1])
    difference_two = normed_two - prior_two
    mix_three = jnp.sum(grad_mix_hidden * difference_two, axis=0)
    mix_four = jnp.sum(grad_mix_gate * difference_two, axis=0)
    grad_normed_two = own_two + jnp.concatenate([passed_two[1:], after_two], axis=0)
    middle_part, gain_two, offset_two = norm_backward(
        grad_normed_two, unit_two, scale_two, gains[1]
    )
    grad_middle = grad_out + middle_part

    grad_attended = grad_middle.astype(LOW)
    grad_gated = back_project(grad_attended, output_all)
    grad_wkv = grad_gated * recept_act
    grad_recept = (grad_gated * wkv * recept_act * (1.0 - recept_act)).astype(LOW)
    early = jnp.stack(
        [
            weight_term(gated, grad_attended).astype(LOW),
            weight_term(mix_gate, grad_gate).astype(LOW),
            weight_term(mix_recept, grad_recept).astype(LOW),
        ]
    )
    early_sums = scatter_sums(early)
    share = grad_wkv * inverse
    decay_term = -pace * jnp.sum(grad_wkv * slope, axis=0)
    head = jnp.where(opened, share * jnp.exp(-pace * places), 0.0)
    local_back = jnp.stack(
        [jnp.sum(head, axis=0), jnp.sum(head * wkv, axis=0), jnp.full((width,), before_id)]
    )
    every_back = lax.all_gather(jnp.pad(local_back, ((0, 5), (0, 0))), "seq")
    span_back = (length * jnp.maximum(order - 1 - s, 0)).astype(FULL)[:, None]
    valid_back = ((order > s) & (every_back[:, 2, 0] == ids[-1]))[:, None]
    reach_back = jnp.exp(-pace * span_back)
    carry_back = jnp.stack(
        [
            jnp.sum(jnp.where(valid_back, reach_back * every_back[:, 0], 0.0), axis=0),
            jnp.sum(jnp.where(valid_back, reach_back * every_back[:, 1], 0.0), axis=0),
        ]
    ).reshape(2, blocks, LANES)
    grad_key, grad_value, first_term = run_backward(
        keep_lanes, key_tiles, value_tiles, wkv_tiles, to_tiles(share), rates, carry_back
    )
    grad_key, grad_value = lax.optimization_barrier(
        (from_tiles(grad_key, width), from_tiles(grad_value, width))
    )
    grad_key, grad_value = grad_key.astype(LOW), grad_value.astype(LOW)
    late = jnp.stack(
        [weight_term(mix_key, grad_key).astype(LOW), weight_term(mix_value, grad_value).astype(LOW)]
    )
    late_sums = scatter_sums(late)
    grad_mix_key = back_project(grad_key, key_all)
    grad_mix_value = back_project(grad_value, value_all)
    grad_mix_recept = back_project(grad_recept, recept_all)
    own_one = (
        grad_mix_key * coeffs[0] + grad_mix_value * coeffs[1] + grad_mix_recept * coeffs[2]
    )
    passed_one = (
        grad_mix_key * (1.0 - coeffs[0])
        + grad_mix_value * (1.0 - coeffs[1])
        + grad_mix_recept * (1.0 - coeffs[2])
    ) * keep[:, None]
    after_one = send_back(passed_one[:1])
    difference_one = normed_one - prior_one
    grad_normed_one = own_one + jnp.concatenate([passed_one[1:], after_one], axis=0)
    input_part, gain_one, offset_one = norm_backward(
        grad_normed_one, unit_one, scale_one, gains[0]
    )
    input_grad = grad_middle + input_part

    sums = sum_vectors(
        jnp.stack(
            [
                gain_one,
                gain_two,
                offset_one,
                offset_two,
                jnp.sum(grad_mix_key * difference_one, axis=0),
                jnp.sum(grad_mix_value * difference_one, axis=0),
                jnp.sum(grad_mix_recept * difference_one, axis=0),
                mix_three,
                mix_four,
                decay_term,
                first_term.reshape(width),
            ]
        )
    )
    sums = lax.dynamic_slice(sums, (0, device * own), (n_vectors, own))
    return (
        block_output[None],
        input_grad[None],
        late_sums[0],
        late_sums[1],
        early_sums[2],
        early_sums[0],
        channel_key_grad,
        channel_value_grad.astype(FULL),
        early_sums[1],
        sums[0:2],
        sums[2:4],
        sums[4:9],
        sums[9],
        sums[10],
    )


def solution(mesh):
    tokens = P("batch", "seq", None)
    weight = P(BOTH, None)
    lines = P(None, BOTH)
    return jax.shard_map(
        per_device,
        mesh=mesh,
        in_specs=(tokens, P("batch", "seq"), tokens)
        + (weight,) * 7
        + (lines,) * 3
        + (P(BOTH),) * 2,
        out_specs=(tokens, tokens) + (weight,) * 7 + (lines,) * 3 + (P(BOTH),) * 2,
        check_vma=False,
    )
```

time: 1940 us -> 395 us (0.20)
  waiting for transfers between devices: 1490 us -> 164 us
  blocking collectives: 264 us -> 37.5 us
  starting transfers between devices: 13.9 us -> 51.5 us
  matrix products: 76.6 us -> 40.4 us
  local copies, waits for them, and re-layouts: 19.9 us -> 49.6 us
    reduce_scatter x6 -> x2, waiting for transfers between devices: 978 us -> 0.01 us  [the longest x1 0.01 us: per_device(): lax.psum_scatter(value_term, 'seq', scatter_dimension=0, tiled=True)]
    unnamed x19 -> x5, waiting for transfers between devices: 304 us -> 0.08 us
    all_gather x8 -> x2, blocking collectives: 186 us -> 28.3 us  [the longest x1 15.4 us: per_device(): every_back = lax.all_gather(jnp.pad(local_back, ((0, 5), (0, 0))), 'seq')]
    all_gather x7 -> x3, waiting for transfers between devices: 207 us -> 69.6 us  [the longest x1 69.6 us: per_device(): gathered = lax.all_gather(packed, BOTH, axis=0)]
    ppermute x5 -> x37, waiting for transfers between devices: 4.84 us -> 93.8 us  [send(): return lax.ppermute(block, BOTH, pairs)]
    unnamed x2 -> x0, blocking collectives: 77.6 us -> none
    dot_general x28 -> x21, matrix products: 76.6 us -> 40.4 us  [the longest x7 17.3 us: project(): return jnp.einsum('td,de->te', active, weight, preferred_element_type=FULL)]
    ppermute x5 -> x37, starting transfers between devices: 13 us -> 47.9 us  [send(): return lax.ppermute(block, BOTH, pairs)]
  transfers between devices with their start and end apart: 21 -> 43, of which waited for: 16 -> 26; matrix products, arithmetic and copies ran while one was open for 5% -> 25% of each run, Pallas kernels for 0% -> 0%
where the time goes in v1:
time: 395 us; the launch traced here: 393 us
  waiting for transfers between devices  164 us (42%)
  starting transfers between devices  51.5 us (13%)
  local copies, waits for them, and re-layouts  49.6 us (13%)
  matrix products  40.4 us (10%)
  blocking collectives  37.5 us (9%)
  other arithmetic  31.2 us (8%)
  between operations  17.7 us (4%)
    ppermute x37, waiting for transfers between devices, send(): return lax.ppermute(block, BOTH, pairs)  93.8 us
    all_gather x1, waiting for transfers between devices, per_device(): gathered = lax.all_gather(packed, BOTH, axis=0)  69.6 us
    ppermute x37, starting transfers between devices, send(): return lax.ppermute(block, BOTH, pairs)  47.9 us
    dot_general x7, matrix products, project(): return jnp.einsum('td,de->te', active, weight, preferred_element_type=FULL)  17.3 us
    all_gather x1, blocking collectives, per_device(): every_back = lax.all_gather(jnp.pad(local_back, ((0, 5), (0, 0))), 'seq')  15.4 us
    all_gather x1, blocking collectives, per_device(): every = lax.all_gather(jnp.pad(local, ((0, 3), (0, 0))), 'seq')  12.9 us
    unnamed x143, local copies, waits for them, and re-layouts  12.5 us
    dot_general x7, matrix products, weight_term(): return jnp.einsum('td,te->de', active, grad, preferred_element_type=FULL)  12 us
  transfers between devices with their start and end apart: 43, of which 26 were waited for; matrix products, arithmetic and copies ran while one was open for 25% of the time, Pallas kernels for 0%

profile of v1, /device:TPU:8, one launch (start us, length us, event | category | flops | bytes accessed | tf_op | source)
XLA Modules:
  0.0 392.8 jit_solution(966637656377270281)
XLA Ops:
  8.1 2.2 concatenate.59
  15.8 9.2 %all_to_all.10 = bf16[4,32,1024]{2,1,0:T(8,128)(2,1)S(1)} all-to-all(bf16[4,32,1024]{2,1,0:T(8,128)(2,1)S(1)} %copy.49), channel_id=1, replica_groups=mesh['batch'=4,'seq'=8] {'batch'}, dimensions={0} | all-to-all | bytes 524288 | tf_op jit(solution)/shard_map/all_to_all | solution.py:297
  27.3 1.9 collective-permute-start
  37.2 69.6 %all-gather.11.cloned.1.call-done = bf16[5632,1024]{1,0:T(8,128)(2,1)} async-done(((bf16[176,1024]{1,0:T(8,128)(2,1)}), bf16[5632,1024]{1,0:T(8,128)(2,1)}) %all-gather.11.cloned.1.call-update) | async-done | bytes 11534352 | tf_op jit(solution)/shard_map/all_gather | solution.py:287
  107.8 7.2 %fusion.139 = (bf16[32,32,1024]{2,1,0:T(8,128)(2,1)}, bf16[32,32,1024]{2,1,0:T(8,128)(2,1)}, bf16[32,32,1024]{2,1,0:T(8,128)(2,1)S(1)}, bf16[32,32,1024]{2,1,0:T(8,128)(2,1)}, bf16[32,32,1024]{2,1,0:T(8,128)(2,1)}) fusion(bf16[32,176,1024]{2,1,0:T(8,128)(2,1)} %bitcast.346), kind=kLoop, calls=%fused_computation.282 | loop fusion | bytes 20971520 | tf_op jit(solution)/shard_map/slice | solution.py:289
  124.7 2.2 fusion.63
  126.9 2.4 multiply_reduce_fusion.10
  131.5 12.9 %all-gather.1 = f32[64,1024]{1,0:T(8,128)S(1)} all-gather(f32[8,1024]{1,0:T(8,128)S(1)} %pad.14), channel_id=3, replica_groups=mesh['batch'=4,'seq'=8] {'seq'}, dimensions={0}, use_global_device_ids=true | all-gather | bytes 294912 | tf_op jit(solution)/shard_map/all_gather | solution.py:329
  146.4 3.2 multiply_convert_fusion.3
  152.0 2.4 collective-permute-start.1
  157.7 2.3 add_convert_fusion.4
  163.5 2.2 copy.51
  165.8 3.8 collective-permute-done.2
  169.5 5.8 %collective-permute-done.3 = bf16[128,1024]{1,0:T(8,128)(2,1)} collective-permute-done((bf16[128,1024]{1,0:T(8,128)(2,1)}, bf16[128,1024]{1,0:T(8,128)(2,1)}, u32[]{:S(2)}, u32[]{:S(2)}) %collective-permute-start.3) | collective-permute-done | bytes 262176 | tf_op jit(solution)/shard_map/ppermute | solution.py:28
  175.3 3.8 fusion.93
  179.1 3.6 fusion.147
  186.4 5.8 %collective-permute-done.5 = bf16[128,1024]{1,0:T(8,128)(2,1)S(1)} collective-permute-done((bf16[128,1024]{1,0:T(8,128)(2,1)S(1)}, bf16[128,1024]{1,0:T(8,128)(2,1)S(1)}, u32[]{:S(2)}, u32[]{:S(2)}) %collective-permute-start.5) | collective-permute-done | bytes 262176 | tf_op jit(solution)/shard_map/ppermute | solution.py:28
  192.1 4.0 %collective-permute-done.6 = bf16[128,1024]{1,0:T(8,128)(2,1)S(1)} collective-permute-done((bf16[128,1024]{1,0:T(8,128)(2,1)S(1)}, bf16[128,1024]{1,0:T(8,128)(2,1)S(1)}, u32[]{:S(2)}, u32[]{:S(2)}) %collective-permute-start.6) | collective-permute-done | bytes 262176 | tf_op jit(solution)/shard_map/ppermute | solution.py:28
  201.1 6.2 %collective-permute-done.10 = bf16[128,1024]{1,0:T(8,128)(2,1)S(1)} collective-permute-done((bf16[128,1024]{1,0:T(8,128)(2,1)S(1)}, bf16[128,1024]{1,0:T(8,128)(2,1)S(1)}, u32[]{:S(2)}, u32[]{:S(2)}) %collective-permute-start.10) | collective-permute-done | bytes 262176 | tf_op jit(solution)/shard_map/ppermute | solution.py:28
  207.3 2.8 collective-permute-done.8
  211.6 2.6 convolution_convert_fusion
  214.3 4.0 %multiply_convert_fusion = bf16[512,1024]{1,0:T(8,128)(2,1)S(1)} fusion(f32[512,1024]{1,0:T(8,128)} %fusion.93, bf16[1024,1024]{1,0:T(8,128)(2,1)} %all-gather.9.cloned.1.call-done, bf16[128,1024]{1,0:T(8,128)(2,1)} %copy-done.63, bf16[128,1024]{1,0:T(8,128)(2,1)} %copy-done.65, bf16[128,1024]{1,0:T(8,128)(2,1)} %copy-done.64, bf16[128,1024]{1,0:T(8,128)(2,1)} %copy-done.62), kind=kOutput, calls=%fused_computation.14 | convolution fusion | flops 1080033280 | bytes 6291456 | tf_op jit(solution)/shard_map/te,de->td/dot_general | solution.py:123
  223.3 2.1 convolution_convert_fusion.3
  225.4 3.4 collective-permute-done.11
  228.8 4.3 %collective-permute-done.12 = bf16[128,1024]{1,0:T(8,128)(2,1)S(1)} collective-permute-done((bf16[128,1024]{1,0:T(8,128)(2,1)S(1)}, bf16[128,1024]{1,0:T(8,128)(2,1)S(1)}, u32[]{:S(2)}, u32[]{:S(2)}) %collective-permute-start.12) | collective-permute-done | bytes 262176 | tf_op jit(solution)/shard_map/ppermute | solution.py:28
  233.1 2.2 multiply_reduce_fusion.1
  236.3 2.1 collective-permute-start.14
  238.4 3.8 convolution_convert_fusion.1
  246.8 15.4 %all-gather.2 = f32[64,1024]{1,0:T(8,128)S(1)} all-gather(f32[8,1024]{1,0:T(8,128)S(1)} %pad.15), channel_id=4, replica_groups=mesh['batch'=4,'seq'=8] {'seq'}, dimensions={0}, use_global_device_ids=true | all-gather | bytes 294912 | tf_op jit(solution)/shard_map/all_gather | solution.py:413
  271.4 2.0 dynamic-slice_bitcast_fusion
  279.3 3.9 collective-permute-start.15
  292.4 1.9 collective-permute-done.33
  294.3 2.0 collective-permute-start.34
  296.6 3.4 fusion.1
  306.1 1.9 collective-permute-done.36
  308.1 7.0 %collective-permute-done.17 = bf16[2,4,32,1024]{3,2,1,0:T(8,128)(2,1)S(1)} collective-permute-done((bf16[2,4,32,1024]{3,2,1,0:T(8,128)(2,1)S(1)}, bf16[2,4,32,1024]{3,2,1,0:T(8,128)(2,1)S(1)}, u32[]{:S(2)}, u32[]{:S(2)}) %collective-permute-start.17) | collective-permute-done | bytes 524320 | tf_op jit(solution)/shard_map/ppermute | solution.py:28
  315.1 8.8 %collective-permute-done.18 = bf16[2,4,32,1024]{3,2,1,0:T(8,128)(2,1)S(1)} collective-permute-done((bf16[2,4,32,1024]{3,2,1,0:T(8,128)(2,1)S(1)}, bf16[2,4,32,1024]{3,2,1,0:T(8,128)(2,1)S(1)}, u32[]{:S(2)}, u32[]{:S(2)}) %collective-permute-start.18) | collective-permute-done | bytes 524320 | tf_op jit(solution)/shard_map/ppermute | solution.py:28
  324.8 3.4 fusion
  334.4 2.4 collective-permute-start.21
  338.0 4.8 %collective-permute-done.21 = bf16[2,32,1024]{2,1,0:T(8,128)(2,1)S(1)} collective-permute-done((bf16[2,32,1024]{2,1,0:T(8,128)(2,1)S(1)}, bf16[2,32,1024]{2,1,0:T(8,128)(2,1)S(1)}, u32[]{:S(2)}, u32[]{:S(2)}) %collective-permute-start.21) | collective-permute-done | bytes 131104 | tf_op jit(solution)/shard_map/ppermute | solution.py:28
  342.8 2.2 collective-permute-done.22
  347.6 3.4 all-to-all-start.1
  351.0 13.6 %collective-permute-done.25 = bf16[3,4,32,1024]{3,2,1,0:T(8,128)(2,1)} collective-permute-done((bf16[3,4,32,1024]{3,2,1,0:T(8,128)(2,1)}, bf16[3,4,32,1024]{3,2,1,0:T(8,128)(2,1)}, u32[]{:S(2)}, u32[]{:S(2)}) %collective-permute-start.25) | collective-permute-done | bytes 786464 | tf_op jit(solution)/shard_map/ppermute | solution.py:28
  365.3 3.4 fusion.133
  370.4 2.6 collective-permute-start.28
  373.9 2.8 collective-permute-done.27
  376.7 5.4 %collective-permute-done.28 = bf16[3,32,1024]{2,1,0:T(8,128)(2,1)S(1)} collective-permute-done((bf16[3,32,1024]{2,1,0:T(8,128)(2,1)S(1)}, bf16[3,32,1024]{2,1,0:T(8,128)(2,1)S(1)}, u32[]{:S(2)}, u32[]{:S(2)}) %collective-permute-start.28) | collective-permute-done | bytes 196640 | tf_op jit(solution)/shard_map/ppermute | solution.py:28
  382.1 2.3 collective-permute-done.29
  (329 shorter events, 104.4 us)
Async XLA Ops:
  7.2 20.1 %copy-start.1 = (bf16[1,128,1024]{2,1,0:T(8,128)(2,1)S(1)}, bf16[1,128,1024]{2,1,0:T(8,128)(2,1)}, u32[]{:S(2)}) copy-start(bf16[1,128,1024]{2,1,0:T(8,128)(2,1)} %param.15) | copy-start | bytes 786436
  7.2 99.6 %all-gather.11.cloned.1.call-start = ((), (), s32[]{:S(2)}) async-start(), calls=%async_computation.8 | async-start | bytes 11894784 | tf_op jit(solution)/shard_map/all_gather | solution.py:287
  14.5 149.0 %all-gather.7.cloned.1.call-start = ((), (), s32[]{:S(2)}) async-start(), calls=%async_computation.4 | async-start | bytes 2359296 | tf_op jit(solution)/shard_map/all_gather | solution.py:298
  26.0 153.1 %all-gather.9.cloned.1.call-start = ((), (), s32[]{:S(2)}) async-start(), calls=%async_computation.5 | async-start | bytes 2359296 | tf_op jit(solution)/shard_map/all_gather | solution.py:299
  27.3 5.0 %collective-permute-start = (bf16[2,1024]{1,0:T(2,128)(2,1)S(1)}, bf16[2,1024]{1,0:T(2,128)(2,1)S(1)}, u32[]{:S(2)}, u32[]{:S(2)}) collective-permute-start(bf16[2,1024]{1,0:T(2,128)(2,1)S(1)} %stack.112), channel_id=1, source_target_pairs={{0,1},{1,2},{2,3},{3,4},{4,5},{5,6},{6,7},{8,9},{9,10},{10,11},{11... | collective-permute-start | bytes 12296 | tf_op jit(solution)/shard_map/ppermute | solution.py:28
  29.3 316.5 %reduce-scatter.5.cloned.1.call-start = ((), (), s32[]{:S(2)}) async-start(), calls=%async_computation.7 | async-start | bytes 2359296 | tf_op jit(solution)/shard_map/reduce_scatter | solution.py:375
  29.5 88.2 %copy-start.48 = (f32[128]{0:T(128)}, f32[128]{0:T(128)S(1)}, u32[]{:S(2)}) copy-start(f32[128]{0:T(128)S(1)} %broadcast_multiply_fusion.5) | copy-start | bytes 1540
  30.3 87.4 %copy-start.50 = (f32[128]{0:T(128)}, f32[128]{0:T(128)S(1)}, u32[]{:S(2)}) copy-start(f32[128]{0:T(128)S(1)} %get-tuple-element.173) | copy-start | bytes 1540
  152.0 5.7 %collective-permute-start.1 = (f32[1,1024]{1,0:T(1,128)}, f32[1,1024]{1,0:T(1,128)}, u32[]{:S(2)}, u32[]{:S(2)}) collective-permute-start(f32[1,1024]{1,0:T(1,128)} %slice.300), channel_id=1, source_target_pairs={{0,1},{1,2},{2,3},{3,4},{4,5},{5,6},{6,7},{8,9},{9,10},{10,11},{11... | collective-permute-start | bytes 12296 | tf_op jit(solution)/shard_map/ppermute | solution.py:28
  160.0 9.5 %collective-permute-start.2 = (bf16[128,1024]{1,0:T(8,128)(2,1)}, bf16[128,1024]{1,0:T(8,128)(2,1)}, u32[]{:S(2)}, u32[]{:S(2)}) collective-permute-start(bf16[128,1024]{1,0:T(8,128)(2,1)} %get-tuple-element.102), channel_id=1, source_target_pairs={{0,8},{1,9},{2,10},{3,11},{4,12},{5,13},{6,14},{7,15},{8,0},{9,1},... | collective-permute-start | bytes 786440 | tf_op jit(solution)/shard_map/ppermute | solution.py:28
  161.4 13.9 %collective-permute-start.3 = (bf16[128,1024]{1,0:T(8,128)(2,1)}, bf16[128,1024]{1,0:T(8,128)(2,1)}, u32[]{:S(2)}, u32[]{:S(2)}) collective-permute-start(bf16[128,1024]{1,0:T(8,128)(2,1)} %get-tuple-element.102), channel_id=1, source_target_pairs={{0,16},{1,17},{2,18},{3,19},{4,20},{5,21},{6,22},{7,23},{8,24},{9,... | collective-permute-start | bytes 786440 | tf_op jit(solution)/shard_map/ppermute | solution.py:28
  161.9 13.4 %collective-permute-start.4 = (bf16[128,1024]{1,0:T(8,128)(2,1)}, bf16[128,1024]{1,0:T(8,128)(2,1)}, u32[]{:S(2)}, u32[]{:S(2)}) collective-permute-start(bf16[128,1024]{1,0:T(8,128)(2,1)} %get-tuple-element.102), channel_id=1, source_target_pairs={{0,24},{1,25},{2,26},{3,27},{4,28},{5,29},{6,30},{7,31},{8,16},{9,... | collective-permute-start | bytes 786440 | tf_op jit(solution)/shard_map/ppermute | solution.py:28
  182.8 9.3 %collective-permute-start.5 = (bf16[128,1024]{1,0:T(8,128)(2,1)S(1)}, bf16[128,1024]{1,0:T(8,128)(2,1)S(1)}, u32[]{:S(2)}, u32[]{:S(2)}) collective-permute-start(bf16[128,1024]{1,0:T(8,128)(2,1)S(1)} %get-tuple-element.108), channel_id=1, source_target_pairs={{0,8},{1,9},{2,10},{3,11},{4,12},{5,13},{6,14},{7,15},{8,0},{9,1},... | collective-permute-start | bytes 786440 | tf_op jit(solution)/shard_map/ppermute | solution.py:28
  183.5 12.6 %collective-permute-start.6 = (bf16[128,1024]{1,0:T(8,128)(2,1)S(1)}, bf16[128,1024]{1,0:T(8,128)(2,1)S(1)}, u32[]{:S(2)}, u32[]{:S(2)}) collective-permute-start(bf16[128,1024]{1,0:T(8,128)(2,1)S(1)} %get-tuple-element.110), channel_id=1, source_target_pairs={{0,16},{1,17},{2,18},{3,19},{4,20},{5,21},{6,22},{7,23},{8,24},{9,... | collective-permute-start | bytes 786440 | tf_op jit(solution)/shard_map/ppermute | solution.py:28
  184.9 11.2 %collective-permute-start.7 = (bf16[128,1024]{1,0:T(8,128)(2,1)S(1)}, bf16[128,1024]{1,0:T(8,128)(2,1)S(1)}, u32[]{:S(2)}, u32[]{:S(2)}) collective-permute-start(bf16[128,1024]{1,0:T(8,128)(2,1)S(1)} %get-tuple-element.109), channel_id=1, source_target_pairs={{0,24},{1,25},{2,26},{3,27},{4,28},{5,29},{6,30},{7,31},{8,16},{9,... | collective-permute-start | bytes 786440 | tf_op jit(solution)/shard_map/ppermute | solution.py:28
  197.6 9.7 %collective-permute-start.10 = (bf16[128,1024]{1,0:T(8,128)(2,1)S(1)}, bf16[128,1024]{1,0:T(8,128)(2,1)S(1)}, u32[]{:S(2)}, u32[]{:S(2)}) collective-permute-start(bf16[128,1024]{1,0:T(8,128)(2,1)S(1)} %get-tuple-element.114), channel_id=1, source_target_pairs={{0,24},{1,25},{2,26},{3,27},{4,28},{5,29},{6,30},{7,31},{8,16},{9,... | collective-permute-start | bytes 786440 | tf_op jit(solution)/shard_map/ppermute | solution.py:28
  199.0 11.1 %collective-permute-start.8 = (bf16[128,1024]{1,0:T(8,128)(2,1)S(1)}, bf16[128,1024]{1,0:T(8,128)(2,1)S(1)}, u32[]{:S(2)}, u32[]{:S(2)}) collective-permute-start(bf16[128,1024]{1,0:T(8,128)(2,1)S(1)} %get-tuple-element.114), channel_id=1, source_target_pairs={{0,8},{1,9},{2,10},{3,11},{4,12},{5,13},{6,14},{7,15},{8,0},{9,1},... | collective-permute-start | bytes 786440 | tf_op jit(solution)/shard_map/ppermute | solution.py:28
  200.4 9.7 %collective-permute-start.9 = (bf16[128,1024]{1,0:T(8,128)(2,1)S(1)}, bf16[128,1024]{1,0:T(8,128)(2,1)S(1)}, u32[]{:S(2)}, u32[]{:S(2)}) collective-permute-start(bf16[128,1024]{1,0:T(8,128)(2,1)S(1)} %get-tuple-element.114), channel_id=1, source_target_pairs={{0,16},{1,17},{2,18},{3,19},{4,20},{5,21},{6,22},{7,23},{8,24},{9,... | collective-permute-start | bytes 786440 | tf_op jit(solution)/shard_map/ppermute | solution.py:28
  214.2 133.4 %reduce-scatter.3.cloned.1.call-start = ((), (), s32[]{:S(2)}) async-start(), calls=%async_computation.6 | async-start | bytes 2359296 | tf_op jit(solution)/shard_map/reduce_scatter | solution.py:377
  219.7 9.0 %collective-permute-start.11 = (bf16[128,1024]{1,0:T(8,128)(2,1)S(1)}, bf16[128,1024]{1,0:T(8,128)(2,1)S(1)}, u32[]{:S(2)}, u32[]{:S(2)}) collective-permute-start(bf16[128,1024]{1,0:T(8,128)(2,1)S(1)} %get-tuple-element.105), channel_id=1, source_target_pairs={{0,8},{1,9},{2,10},{3,11},{4,12},{5,13},{6,14},{7,15},{8,0},{9,1},... | collective-permute-start | bytes 786440 | tf_op jit(solution)/shard_map/ppermute | solution.py:28
  220.5 12.6 %collective-permute-start.12 = (bf16[128,1024]{1,0:T(8,128)(2,1)S(1)}, bf16[128,1024]{1,0:T(8,128)(2,1)S(1)}, u32[]{:S(2)}, u32[]{:S(2)}) collective-permute-start(bf16[128,1024]{1,0:T(8,128)(2,1)S(1)} %get-tuple-element.107), channel_id=1, source_target_pairs={{0,16},{1,17},{2,18},{3,19},{4,20},{5,21},{6,22},{7,23},{8,24},{9,... | collective-permute-start | bytes 786440 | tf_op jit(solution)/shard_map/ppermute | solution.py:28
  221.7 11.3 %collective-permute-start.13 = (bf16[128,1024]{1,0:T(8,128)(2,1)S(1)}, bf16[128,1024]{1,0:T(8,128)(2,1)S(1)}, u32[]{:S(2)}, u32[]{:S(2)}) collective-permute-start(bf16[128,1024]{1,0:T(8,128)(2,1)S(1)} %get-tuple-element.106), channel_id=1, source_target_pairs={{0,24},{1,25},{2,26},{3,27},{4,28},{5,29},{6,30},{7,31},{8,16},{9,... | collective-permute-start | bytes 786440 | tf_op jit(solution)/shard_map/ppermute | solution.py:28
  236.3 7.2 %collective-permute-start.14 = (f32[1,1024]{1,0:T(1,128)S(1)}, f32[1,1024]{1,0:T(1,128)S(1)}, u32[]{:S(2)}, u32[]{:S(2)}) collective-permute-start(f32[1,1024]{1,0:T(1,128)S(1)} %slice.313), channel_id=1, source_target_pairs={{1,0},{2,1},{3,2},{4,3},{5,4},{6,5},{7,6},{9,8},{10,9},{11,10},{12... | collective-permute-start | bytes 12296 | tf_op jit(solution)/shard_map/ppermute | solution.py:28
  269.7 26.9 %collective-permute-start.16 = (bf16[2,4,4,32,1024]{4,3,2,1,0:T(8,128)(2,1)}, bf16[2,4,4,32,1024]{4,3,2,1,0:T(8,128)(2,1)}, u32[]{:S(2)}, u32[]{:S(2)}) collective-permute-start(bf16[2,4,4,32,1024]{4,3,2,1,0:T(8,128)(2,1)} %fusion.3), channel_id=1, source_target_pairs={{0,1},{1,0},{2,3},{3,2},{4,5},{5,4},{6,7},{7,6},{8,9},{9,8},{10,11... | collective-permute-start | bytes 6291464 | tf_op jit(solution)/shard_map/ppermute | solution.py:28
  275.2 49.6 %collective-permute-start.23 = (bf16[3,4,4,32,1024]{4,3,2,1,0:T(8,128)(2,1)}, bf16[3,4,4,32,1024]{4,3,2,1,0:T(8,128)(2,1)}, u32[]{:S(2)}, u32[]{:S(2)}) collective-permute-start(bf16[3,4,4,32,1024]{4,3,2,1,0:T(8,128)(2,1)} %dynamic-slice_bitcast_fusion), channel_id=1, source_target_pairs={{0,1},{1,0},{2,3},{3,2},{4,5},{5,4},{6,7},{7,6},{8,9},{9,8},{10,11... | collective-permute-start | bytes 9437192 | tf_op jit(solution)/shard_map/ppermute | solution.py:28
  279.3 4.9 %collective-permute-start.15 = (f32[1,1024]{1,0:T(1,128)S(1)}, f32[1,1024]{1,0:T(1,128)S(1)}, u32[]{:S(2)}, u32[]{:S(2)}) collective-permute-start(f32[1,1024]{1,0:T(1,128)S(1)} %slice.318), channel_id=1, source_target_pairs={{1,0},{2,1},{3,2},{4,3},{5,4},{6,5},{7,6},{9,8},{10,9},{11,10},{12... | collective-permute-start | bytes 12296 | tf_op jit(solution)/shard_map/ppermute | solution.py:28
  285.1 1.8 collective-permute-start.30
  286.9 4.5 %collective-permute-start.31 = (f32[11,1024]{1,0:T(8,128)S(1)}, f32[11,1024]{1,0:T(8,128)S(1)}, u32[]{:S(2)}, u32[]{:S(2)}) collective-permute-start(f32[11,1024]{1,0:T(8,128)S(1)} %add.349), channel_id=1, source_target_pairs={{0,8},{1,9},{2,10},{3,11},{4,12},{5,13},{6,14},{7,15},{8,0},{9,1},... | collective-permute-start | bytes 135176 | tf_op jit(solution)/shard_map/ppermute | solution.py:28
  287.3 5.1 %collective-permute-start.32 = (f32[11,1024]{1,0:T(8,128)S(1)}, f32[11,1024]{1,0:T(8,128)S(1)}, u32[]{:S(2)}, u32[]{:S(2)}) collective-permute-start(f32[11,1024]{1,0:T(8,128)S(1)} %add.349), channel_id=1, source_target_pairs={{0,16},{1,17},{2,18},{3,19},{4,20},{5,21},{6,22},{7,23},{8,24},{9,... | collective-permute-start | bytes 135176 | tf_op jit(solution)/shard_map/ppermute | solution.py:28
  289.2 5.2 %collective-permute-start.33 = (f32[11,1024]{1,0:T(8,128)S(1)}, f32[11,1024]{1,0:T(8,128)S(1)}, u32[]{:S(2)}, u32[]{:S(2)}) collective-permute-start(f32[11,1024]{1,0:T(8,128)S(1)} %add.349), channel_id=1, source_target_pairs={{0,24},{1,25},{2,26},{3,27},{4,28},{5,29},{6,30},{7,31},{8,16},{9,... | collective-permute-start | bytes 135176 | tf_op jit(solution)/shard_map/ppermute | solution.py:28
  294.3 7.6 %collective-permute-start.34 = (f32[11,1024]{1,0:T(8,128)S(1)}, f32[11,1024]{1,0:T(8,128)S(1)}, u32[]{:S(2)}, u32[]{:S(2)}) collective-permute-start(f32[11,1024]{1,0:T(8,128)S(1)} %add_add_fusion), channel_id=1, source_target_pairs={{0,2},{1,3},{2,0},{3,1},{4,6},{5,7},{6,4},{7,5},{8,10},{9,11},{10,... | collective-permute-start | bytes 135176 | tf_op jit(solution)/shard_map/ppermute | solution.py:28
  296.3 7.4 %collective-permute-start.35 = (f32[11,1024]{1,0:T(8,128)S(1)}, f32[11,1024]{1,0:T(8,128)S(1)}, u32[]{:S(2)}, u32[]{:S(2)}) collective-permute-start(f32[11,1024]{1,0:T(8,128)S(1)} %add_add_fusion), channel_id=1, source_target_pairs={{0,4},{1,5},{2,6},{3,7},{4,0},{5,1},{6,2},{7,3},{8,12},{9,13},{10,... | collective-permute-start | bytes 135176 | tf_op jit(solution)/shard_map/ppermute | solution.py:28
  296.6 28.2 %slice-start = ((s8[6291456]{0:T(1024)(128)(4,1)}), s8[4194304]{0:T(1024)(128)(4,1)S(1)}, s32[]{:S(2)}) async-start(s8[6291456]{0:T(1024)(128)(4,1)} %bitcast.337), calls=%async_computation.9 | async-start | bytes 8388608
  300.0 24.8 %slice-start.1 = ((s8[6291456]{0:T(1024)(128)(4,1)}), s8[2097152]{0:T(1024)(128)(4,1)S(1)}, s32[]{:S(2)}) async-start(s8[6291456]{0:T(1024)(128)(4,1)} %bitcast.337), calls=%async_computation.10 | async-start | bytes 4194304
  300.2 14.9 %collective-permute-start.17 = (bf16[2,4,32,1024]{3,2,1,0:T(8,128)(2,1)S(1)}, bf16[2,4,32,1024]{3,2,1,0:T(8,128)(2,1)S(1)}, u32[]{:S(2)}, u32[]{:S(2)}) collective-permute-start(bf16[2,4,32,1024]{3,2,1,0:T(8,128)(2,1)S(1)} %get-tuple-element.98), channel_id=1, source_target_pairs={{0,8},{1,9},{2,10},{3,11},{4,12},{5,13},{6,14},{7,15},{8,0},{9,1},... | collective-permute-start | bytes 1572872 | tf_op jit(solution)/shard_map/ppermute | solution.py:28
  301.1 22.9 %collective-permute-start.18 = (bf16[2,4,32,1024]{3,2,1,0:T(8,128)(2,1)S(1)}, bf16[2,4,32,1024]{3,2,1,0:T(8,128)(2,1)S(1)}, u32[]{:S(2)}, u32[]{:S(2)}) collective-permute-start(bf16[2,4,32,1024]{3,2,1,0:T(8,128)(2,1)S(1)} %get-tuple-element.100), channel_id=1, source_target_pairs={{0,16},{1,17},{2,18},{3,19},{4,20},{5,21},{6,22},{7,23},{8,24},{9,... | collective-permute-start | bytes 1572872 | tf_op jit(solution)/shard_map/ppermute | solution.py:28
  302.0 21.9 %collective-permute-start.19 = (bf16[2,4,32,1024]{3,2,1,0:T(8,128)(2,1)S(1)}, bf16[2,4,32,1024]{3,2,1,0:T(8,128)(2,1)S(1)}, u32[]{:S(2)}, u32[]{:S(2)}) collective-permute-start(bf16[2,4,32,1024]{3,2,1,0:T(8,128)(2,1)S(1)} %get-tuple-element.99), channel_id=1, source_target_pairs={{0,24},{1,25},{2,26},{3,27},{4,28},{5,29},{6,30},{7,31},{8,16},{9,... | collective-permute-start | bytes 1572872 | tf_op jit(solution)/shard_map/ppermute | solution.py:28
  303.8 4.3 %collective-permute-start.36 = (f32[11,1024]{1,0:T(8,128)S(1)}, f32[11,1024]{1,0:T(8,128)S(1)}, u32[]{:S(2)}, u32[]{:S(2)}) collective-permute-start(f32[11,1024]{1,0:T(8,128)S(1)} %add_add_fusion), channel_id=1, source_target_pairs={{0,6},{1,7},{2,4},{3,5},{4,2},{5,3},{6,0},{7,1},{8,14},{9,15},{10,... | collective-permute-start | bytes 135176 | tf_op jit(solution)/shard_map/ppermute | solution.py:28
  324.4 12.5 %collective-permute-start.20 = (bf16[2,32,1024]{2,1,0:T(8,128)(2,1)S(1)}, bf16[2,32,1024]{2,1,0:T(8,128)(2,1)S(1)}, u32[]{:S(2)}, u32[]{:S(2)}) collective-permute-start(bf16[2,32,1024]{2,1,0:T(8,128)(2,1)S(1)} %get-tuple-element.115), channel_id=1, source_target_pairs={{0,2},{1,3},{2,0},{3,1},{4,6},{5,7},{6,4},{7,5},{8,10},{9,11},{10,... | collective-permute-start | bytes 393224 | tf_op jit(solution)/shard_map/ppermute | solution.py:28
  329.7 21.3 %collective-permute-start.24 = (bf16[3,4,32,1024]{3,2,1,0:T(8,128)(2,1)}, bf16[3,4,32,1024]{3,2,1,0:T(8,128)(2,1)}, u32[]{:S(2)}, u32[]{:S(2)}) collective-permute-start(bf16[3,4,32,1024]{3,2,1,0:T(8,128)(2,1)} %get-tuple-element.95), channel_id=1, source_target_pairs={{0,8},{1,9},{2,10},{3,11},{4,12},{5,13},{6,14},{7,15},{8,0},{9,1},... | collective-permute-start | bytes 2359304 | tf_op jit(solution)/shard_map/ppermute | solution.py:28
  331.0 33.6 %collective-permute-start.25 = (bf16[3,4,32,1024]{3,2,1,0:T(8,128)(2,1)}, bf16[3,4,32,1024]{3,2,1,0:T(8,128)(2,1)}, u32[]{:S(2)}, u32[]{:S(2)}) collective-permute-start(bf16[3,4,32,1024]{3,2,1,0:T(8,128)(2,1)} %get-tuple-element.97), channel_id=1, source_target_pairs={{0,16},{1,17},{2,18},{3,19},{4,20},{5,21},{6,22},{7,23},{8,24},{9,... | collective-permute-start | bytes 2359304 | tf_op jit(solution)/shard_map/ppermute | solution.py:28
  331.6 33.7 %collective-permute-start.26 = (bf16[3,4,32,1024]{3,2,1,0:T(8,128)(2,1)}, bf16[3,4,32,1024]{3,2,1,0:T(8,128)(2,1)}, u32[]{:S(2)}, u32[]{:S(2)}) collective-permute-start(bf16[3,4,32,1024]{3,2,1,0:T(8,128)(2,1)} %get-tuple-element.96), channel_id=1, source_target_pairs={{0,24},{1,25},{2,26},{3,27},{4,28},{5,29},{6,30},{7,31},{8,16},{9,... | collective-permute-start | bytes 2359304 | tf_op jit(solution)/shard_map/ppermute | solution.py:28
  334.4 8.4 %collective-permute-start.21 = (bf16[2,32,1024]{2,1,0:T(8,128)(2,1)S(1)}, bf16[2,32,1024]{2,1,0:T(8,128)(2,1)S(1)}, u32[]{:S(2)}, u32[]{:S(2)}) collective-permute-start(bf16[2,32,1024]{2,1,0:T(8,128)(2,1)S(1)} %get-tuple-element.117), channel_id=1, source_target_pairs={{0,4},{1,5},{2,6},{3,7},{4,0},{5,1},{6,2},{7,3},{8,12},{9,13},{10,... | collective-permute-start | bytes 393224 | tf_op jit(solution)/shard_map/ppermute | solution.py:28
  336.8 8.2 %collective-permute-start.22 = (bf16[2,32,1024]{2,1,0:T(8,128)(2,1)S(1)}, bf16[2,32,1024]{2,1,0:T(8,128)(2,1)S(1)}, u32[]{:S(2)}, u32[]{:S(2)}) collective-permute-start(bf16[2,32,1024]{2,1,0:T(8,128)(2,1)S(1)} %get-tuple-element.116), channel_id=1, source_target_pairs={{0,6},{1,7},{2,4},{3,5},{4,2},{5,3},{6,0},{7,1},{8,14},{9,15},{10,... | collective-permute-start | bytes 393224 | tf_op jit(solution)/shard_map/ppermute | solution.py:28
  347.6 25.4 %all-to-all-start.1 = ((bf16[4,32,1024]{2,1,0:T(8,128)(2,1)}), bf16[4,32,1024]{2,1,0:T(8,128)(2,1)S(1)}, u32[]{:S(2)}, u32[]{:S(2)}) async-start(bf16[4,32,1024]{2,1,0:T(8,128)(2,1)} %reduce-scatter.3.cloned.1.call-done), calls=%async_computation.2 | async-start | bytes 524288 | tf_op jit(solution)/shard_map/all_to_all | solution.py:378
  368.8 7.9 %collective-permute-start.27 = (bf16[3,32,1024]{2,1,0:T(8,128)(2,1)S(1)}, bf16[3,32,1024]{2,1,0:T(8,128)(2,1)S(1)}, u32[]{:S(2)}, u32[]{:S(2)}) collective-permute-start(bf16[3,32,1024]{2,1,0:T(8,128)(2,1)S(1)} %get-tuple-element.111), channel_id=1, source_target_pairs={{0,2},{1,3},{2,0},{3,1},{4,6},{5,7},{6,4},{7,5},{8,10},{9,11},{10,... | collective-permute-start | bytes 589832 | tf_op jit(solution)/shard_map/ppermute | solution.py:28
  370.4 11.7 %collective-permute-start.28 = (bf16[3,32,1024]{2,1,0:T(8,128)(2,1)S(1)}, bf16[3,32,1024]{2,1,0:T(8,128)(2,1)S(1)}, u32[]{:S(2)}, u32[]{:S(2)}) collective-permute-start(bf16[3,32,1024]{2,1,0:T(8,128)(2,1)S(1)} %get-tuple-element.113), channel_id=1, source_target_pairs={{0,4},{1,5},{2,6},{3,7},{4,0},{5,1},{6,2},{7,3},{8,12},{9,13},{10,... | collective-permute-start | bytes 589832 | tf_op jit(solution)/shard_map/ppermute | solution.py:28
  373.0 11.4 %collective-permute-start.29 = (bf16[3,32,1024]{2,1,0:T(8,128)(2,1)S(1)}, bf16[3,32,1024]{2,1,0:T(8,128)(2,1)S(1)}, u32[]{:S(2)}, u32[]{:S(2)}) collective-permute-start(bf16[3,32,1024]{2,1,0:T(8,128)(2,1)S(1)} %get-tuple-element.112), channel_id=1, source_target_pairs={{0,6},{1,7},{2,4},{3,5},{4,2},{5,3},{6,0},{7,1},{8,14},{9,15},{10,... | collective-permute-start | bytes 589832 | tf_op jit(solution)/shard_map/ppermute | solution.py:28
  (64 other events, 361.1 us)
Sparse Core Ops, SparseCore 0:
  14.7 92.1 all-gather.10
  109.0 27.8 all-gather.6
  138.4 28.9 all-gather.8
  214.3 32.4 reduce-scatter.4
  248.9 37.6 reduce-scatter.2

commit v2 on v1

v2 whole, which is shorter than its diff:
```python
import jax
import jax.numpy as jnp
from jax import lax
from jax.experimental import pallas as pl
from jax.experimental.pallas import tpu as pltpu
from jax.sharding import PartitionSpec as P

EPS = 1e-05
BOTH = ("batch", "seq")
LOW = jnp.bfloat16
FULL = jnp.float32
LANES = 128
SUBS = 8
MIB = 1024 * 1024
COST = 1024
IN_VMEM = pl.BlockSpec(memory_space=pltpu.VMEM)
ANYWHERE = pl.BlockSpec(memory_space=pl.ANY)
IN_HBM = pl.BlockSpec(memory_space=pltpu.HBM)


def sizes():
    return lax.axis_size("batch"), lax.axis_size("seq")


def places():
    s = lax.axis_index("seq")
    return lax.axis_index("batch"), s >> 1, s & 1


def send(block, route):
    rows, cols = sizes()
    pairs = []
    for b in range(rows):
        for s in range(cols):
            target = route(b, s)
            if target is not None:
                pairs.append((b * cols + s, target[0] * cols + target[1]))
    return lax.ppermute(block, BOTH, pairs)


def send_next(block):
    cols = lax.axis_size("seq")
    return send(block, lambda b, s: (b, s + 1) if s + 1 < cols else None)


def send_back(block):
    return send(block, lambda b, s: (b, s - 1) if s > 0 else None)


def to_core(block):
    return send(block, lambda b, s: (b, s ^ 1))


def to_batch(block, k):
    return send(block, lambda b, s: (b ^ k, s))


def to_depth(block, k):
    return send(block, lambda b, s: (b, s ^ (2 * k)))


def fuse(body, outs, *args, after=(), limit=16, flops=0, plain=False, fetch=False):
    if plain:
        return tuple(body(*args))
    count, held = len(args), len(args) + len(after)

    def kernel(*refs):
        taken = refs[:count]
        if fetch:
            taken, arrived = refs[held + len(outs) : -1], refs[-1]
            copies = [
                pltpu.make_async_copy(refs[i], taken[i], arrived.at[i]) for i in range(count)
            ]
            for copy in copies:
                copy.start()
            for copy in copies:
                copy.wait()
        results = body(*[ref[...] for ref in taken])
        for ref, value in zip(refs[held : held + len(outs)], results, strict=True):
            ref[...] = value

    return pl.pallas_call(
        kernel,
        out_shape=tuple(jax.ShapeDtypeStruct(shape, dtype) for shape, dtype in outs),
        in_specs=[IN_HBM if fetch else IN_VMEM] * count + [ANYWHERE] * len(after),
        out_specs=(IN_VMEM,) * len(outs),
        scratch_shapes=[pltpu.VMEM(x.shape, x.dtype) for x in args]
        + [pltpu.SemaphoreType.DMA((count,))]
        if fetch
        else [],
        compiler_params=pltpu.CompilerParams(vmem_limit_bytes=limit * MIB),
        cost_estimate=pl.CostEstimate(flops=COST, bytes_accessed=COST, transcendentals=0),
    )(*args, *after)


def dot(x, w):
    return lax.dot_general(x, w, (((1,), (0,)), ((), ())), preferred_element_type=FULL)


def dot_back(x, w):
    return lax.dot_general(x, w, (((1,), (1,)), ((), ())), preferred_element_type=FULL)


def dot_rows(x, y):
    return lax.dot_general(x, y, (((0,), (0,)), ((), ())), preferred_element_type=FULL)


def restore(x, order):
    high = x.astype(LOW)
    rest = (x - high.astype(FULL)).astype(LOW)
    return dot_back(high, order) + dot_back(rest, order)


def restore_in(x, order):
    high = x.astype(LOW)
    rest = (x - high.astype(FULL)).astype(LOW)
    return dot(high, order) + dot(rest, order)


def row_index(shape):
    return lax.broadcasted_iota(jnp.int32, shape, 0)


def stack_rows(rows, count=SUBS):
    width = rows[0].shape[1]
    index = row_index((count, width))
    out = jnp.zeros((count, width), FULL)
    for i, row in enumerate(rows):
        out = jnp.where(index == i, row, out)
    return out


def down(x, first, plain):
    rolled = jnp.roll(x, 1, 0) if plain else pltpu.roll(x, 1, 0)
    return jnp.where(row_index(x.shape) == 0, first, rolled)


def up(x, last, plain):
    count = x.shape[0]
    rolled = jnp.roll(x, -1, 0) if plain else pltpu.roll(x, count - 1, 0)
    return jnp.where(row_index(x.shape) == count - 1, last, rolled)


def column_sum(x):
    return jnp.sum(x, axis=0, keepdims=True)


def lane_mean(x):
    return jnp.mean(x, axis=-1, keepdims=True)


def unit_norm(hidden):
    centred = hidden - lane_mean(hidden)
    scale = lax.rsqrt(lane_mean(centred * centred) + EPS)
    return centred * scale, scale


def norm_backward(grad, unit, scale, gain):
    inner = grad * gain
    centred = inner - lane_mean(inner)
    return scale * (centred - unit * lane_mean(inner * unit))


def mixing(normed, prior, coeff):
    return (normed * coeff + prior * (1.0 - coeff)).astype(LOW)


def pick(values, index):
    out = values[0]
    for i in range(1, len(values)):
        out = jnp.where(index == i, values[i], out)
    return out


def log2(n):
    return n.bit_length() - 1


def untile(x, blocks):
    count = x.shape[0] // blocks
    x = x.reshape(count // SUBS, blocks, SUBS, LANES)
    return jnp.concatenate([x[:, i].reshape(count, LANES) for i in range(blocks)], axis=1)


def to_lanes(row):
    return jnp.concatenate(
        [row[:, i * LANES : (i + 1) * LANES] for i in range(row.shape[1] // LANES)], axis=0
    )


def from_lanes(x):
    return jnp.concatenate([x[i : i + 1] for i in range(x.shape[0])], axis=1)


def to_tiles(x):
    count, width = x.shape
    blocks = width // LANES
    x = x.reshape(count // SUBS, SUBS, blocks, LANES).transpose(0, 2, 1, 3)
    return x.reshape(count * blocks, LANES)


def from_tiles(x, width):
    blocks = width // LANES
    count = x.shape[0] // blocks
    x = x.reshape(count // SUBS, blocks, SUBS, LANES).transpose(0, 2, 1, 3)
    return x.reshape(count, width)


def position(i, r, blocks):
    return pl.ds(i * (SUBS * blocks) + r, blocks, stride=SUBS)


def forward_scan(keep_ref, key_ref, value_ref, rates_ref, carry_ref, out_ref):
    blocks = rates_ref.shape[1]
    fade, bonus = rates_ref[0], rates_ref[1]

    def eight(i, state):
        num, den, num_slope, den_slope = state
        for r in range(SUBS):
            at = position(i, r, blocks)
            key, value = key_ref[at, :], value_ref[at, :]
            keep = keep_ref[pl.ds(i * SUBS + r, 1), :]
            num, den, num_slope, den_slope = (
                num * keep,
                den * keep,
                num_slope * keep,
                den_slope * keep,
            )
            reward = jnp.exp(bonus + key)
            weight = jnp.exp(key)
            inverse = 1.0 / (den + reward)
            wkv = (num + reward * value) * inverse
            out_ref[0, at, :] = wkv
            out_ref[1, at, :] = inverse
            out_ref[2, at, :] = (num_slope - wkv * den_slope) * inverse
            num_slope = fade * (num_slope + num)
            den_slope = fade * (den_slope + den)
            num = fade * num + weight * value
            den = fade * den + weight
        return num, den, num_slope, den_slope

    lax.fori_loop(
        0,
        keep_ref.shape[0] // SUBS,
        eight,
        (carry_ref[0], carry_ref[1], carry_ref[2], carry_ref[3]),
    )


def backward_scan(
    keep_ref, key_ref, value_ref, scanned_ref, share_ref, rates_ref, carry_ref, key_out, value_out, first_out
):
    blocks = rates_ref.shape[1]
    fade, bonus = rates_ref[0], rates_ref[1]
    groups = keep_ref.shape[0] // SUBS

    def eight(step, state):
        direct, scaled, first = state
        i = groups - 1 - step
        for r in reversed(range(SUBS)):
            at = position(i, r, blocks)
            key, value = key_ref[at, :], value_ref[at, :]
            wkv, share = scanned_ref[0, at, :], share_ref[at, :]
            keep = keep_ref[pl.ds(i * SUBS + r, 1), :]
            reward = share * jnp.exp(bonus + key)
            weight = jnp.exp(key)
            bonus_part = reward * (value - wkv)
            key_out[at, :] = weight * (direct * value - scaled) + bonus_part
            value_out[at, :] = weight * direct + reward
            first = first + bonus_part
            direct = (share + fade * direct) * keep
            scaled = (share * wkv + fade * scaled) * keep
        return direct, scaled, first

    first_out[...] = lax.fori_loop(
        0, groups, eight, (carry_ref[0], carry_ref[1], jnp.zeros_like(fade))
    )[2]


def run_forward(keep, key, value, rates, carry):
    return pl.pallas_call(
        forward_scan,
        out_shape=jax.ShapeDtypeStruct((3,) + key.shape, FULL),
        in_specs=[IN_VMEM] * 5,
        out_specs=IN_VMEM,
        compiler_params=pltpu.CompilerParams(vmem_limit_bytes=8 * MIB),
        cost_estimate=pl.CostEstimate(
            flops=20 * key.size, bytes_accessed=20 * key.size, transcendentals=3 * key.size
        ),
    )(keep, key, value, rates, carry)


def run_backward(keep, key, value, wkv, share, rates, carry):
    tiles = jax.ShapeDtypeStruct(key.shape, FULL)
    return pl.pallas_call(
        backward_scan,
        out_shape=(tiles, tiles, jax.ShapeDtypeStruct(rates.shape[1:], FULL)),
        in_specs=[IN_VMEM] * 7,
        out_specs=(IN_VMEM,) * 3,
        compiler_params=pltpu.CompilerParams(vmem_limit_bytes=8 * MIB),
        cost_estimate=pl.CostEstimate(
            flops=20 * key.size, bytes_accessed=24 * key.size, transcendentals=2 * key.size
        ),
    )(keep, key, value, wkv, share, rates, carry)


def moved(sums, span, pace):
    fade = jnp.exp(-pace * span)
    if len(sums) == 4:
        num, den, num_slope, den_slope = sums
        return [
            fade * num,
            fade * den,
            fade * (num_slope + span * num),
            fade * (den_slope + span * den),
        ]
    return [fade * x for x in sums]


def split_message(message, count):
    return [message[i : i + 1] for i in range(count)], message[count : count + 1], message[count + 1 : count + 2]


def by_place(message, other):
    core = places()[2]
    return jnp.where(core == 0, message, other), jnp.where(core == 0, other, message)


def chip_sums(count, length, forward):
    def body(message, other, vectors):
        pace = jnp.exp(vectors[9:10])
        first, second = by_place(message, other)
        one, one_last, one_before = split_message(first, count)
        two, two_last, _ = split_message(second, count)
        near, far = (two, one) if forward else (one, two)
        through = (two_last == one_last) if forward else (one_last == one_before)
        far = moved(far, float(length), pace)
        sums = [n + jnp.where(through, f, 0.0) for n, f in zip(near, far, strict=True)]
        return (stack_rows(sums + [two_last, one_before]),)

    return body


def carried(count, length, forward):
    def body(message, other, vectors, *got):
        depth = len(got) + 1
        _, z, core = places()
        pace = jnp.exp(vectors[9:10])
        first, second = by_place(message, other)
        one, one_last, one_before = split_message(first, count)
        two, two_last, _ = split_message(second, count)
        total = [jnp.zeros_like(x) for x in one]
        for k in range(1, depth):
            sums, last, before = split_message(got[k - 1], count)
            if forward:
                valid = (last == one_before) & (z >= k)
            else:
                valid = (before == two_last) & (z < depth - k)
            sums = moved(sums, 2.0 * length * (k - 1), pace)
            total = [t + jnp.where(valid, x, 0.0) for t, x in zip(total, sums, strict=True)]
        inner, through = (one, one_last == one_before) if forward else (two, two_last == one_last)
        passed = moved(total, float(length), pace)
        passed = [x + jnp.where(through, y, 0.0) for x, y in zip(inner, passed, strict=True)]
        chosen = core == (1 if forward else 0)
        return (
            jnp.stack(
                [to_lanes(jnp.where(chosen, p, t)) for p, t in zip(passed, total, strict=True)]
            ),
        )

    return body


def carry_exchange(values, vectors, length, forward, plain, after=()):
    cols = lax.axis_size("seq")
    count = 4 if forward else 2
    width = values.shape[1]
    other = to_core(values)
    (chip,) = fuse(
        chip_sums(count, length, forward), [((SUBS, width), FULL)], values, other, vectors, plain=plain
    )
    step = 1 if forward else -1

    def route(k):
        def go(b, s):
            target = s + 2 * k * step
            return (b, target) if 0 <= target < cols else None

        return go

    got = [send(chip, route(k)) for k in range(1, cols // 2)]
    return fuse(
        carried(count, length, forward),
        [((count, width // LANES, LANES), FULL)],
        values,
        other,
        vectors,
        *got,
        after=after,
        plain=plain,
    )[0]


def add_batch(own, got, plain, after=()):
    count, height, width = own.shape
    depth = lax.axis_size("seq") // 2
    part = height // depth

    def body(own, *got):
        total = sum((x.astype(FULL) for x in got), own.astype(FULL))
        return [total[:, :part]] + [
            total[:, k * part : (k + 1) * part].astype(LOW) for k in range(1, depth)
        ]

    return fuse(
        body,
        [((count, part, width), FULL)] + [((count, part, width), LOW)] * (depth - 1),
        own,
        *got,
        after=after,
        plain=plain,
    )


def add_depth(pieces, plain, after=()):
    count, part, width = pieces[0].shape
    got = [to_depth(pieces[k], k) for k in range(1, len(pieces))]

    def body(own, *got):
        total = sum((x.astype(FULL) for x in got), own)
        return [total[i] for i in range(count)]

    return fuse(body, [((part, width), FULL)] * count, pieces[0], *got, after=after, plain=plain)


def per_device(
    layer_input,
    segment_ids,
    out_cotangent,
    key_weight,
    value_weight,
    recept_weight,
    output_weight,
    channel_key,
    channel_value,
    channel_recept,
    norm_gains,
    norm_offsets,
    mix_coeffs,
    time_decay,
    time_first,
):
    rows, cols = sizes()
    depth = cols // 2
    length, width = layer_input.shape[1:]
    own = key_weight.shape[0]
    hidden_width = channel_key.shape[1]
    part_width = hidden_width // rows
    half = width // 2
    plain = own % 16 != 0
    low_act, full_act = ((length, width), LOW), ((length, width), FULL)
    narrow = ((length, LANES), FULL)
    square = ((width, width), LOW)
    edge_row = ((SUBS, width), FULL)
    raw, cotangent = layer_input[0], out_cotangent[0]
    mac = 2 * length * width * width

    small = [norm_gains, norm_offsets, mix_coeffs, time_decay[None], time_first[None]]
    n_vectors = sum(x.shape[0] for x in small)

    def prepare(key, value, recept, output, gate, cross, raw, ids, *small):
        b, z, core = places()
        device = b * cols + z * 2 + core
        lane = lax.broadcasted_iota(jnp.int32, (own, width), 1)
        home = (lane == device * own + row_index((own, width))).astype(FULL).astype(LOW)
        placed = jnp.zeros((16, width), FULL)
        at = 0
        for x in small:
            x = dot(x, home)
            for i in range(x.shape[0]):
                placed = jnp.where(row_index(placed.shape) == at, x[i : i + 1], placed)
                at += 1
        blocks = [cross[:, j * part_width : (j + 1) * part_width] for j in range(rows)]
        ids = ids.astype(FULL)
        last = raw[length - 16 :].astype(FULL)[15:16]
        edge = stack_rows([last, jnp.broadcast_to(ids[:, length - 1 :], (1, width))], 16)
        return (
            [
                jnp.concatenate([key, value, placed.astype(LOW)], axis=0),
                jnp.concatenate([recept, output, gate], axis=0),
                edge,
                jnp.broadcast_to(ids, (LANES, length)).T,
            ]
            + [pick(blocks, b ^ k) for k in range(rows)]
        )

    first_pack, second_pack, edge, ids_lanes, *crossing = fuse(
        prepare,
        [((2 * own + 16, width), LOW), ((3 * own, width), LOW), ((16, width), FULL), narrow]
        + [((own, part_width), LOW)] * rows,
        key_weight,
        value_weight,
        recept_weight,
        output_weight,
        channel_recept,
        channel_key,
        raw,
        segment_ids,
        *small,
        plain=plain,
        fetch=True,
    )
    deep_got = [to_depth(first_pack, k) for k in range(1, depth)]
    cross_got = [to_batch(crossing[k], k) for k in range(1, rows)]
    edge = send_next(edge)

    def begin(raw, edge, ids):
        b, z, core = places()
        place = lax.broadcasted_iota(jnp.int32, (1, width), 1)
        block, row = place >> log2(own), place & (own - 1)
        k_core = block >> log2(rows * depth)
        k_batch = (block >> log2(depth)) & (rows - 1)
        k_depth = block & (depth - 1)
        target = ((k_batch ^ b) << log2(cols)) + ((k_depth ^ z) << 1) + (k_core ^ core)
        feature = (target << log2(own)) + row
        order = jnp.concatenate(
            [
                (row_index((LANES, width)) + i * LANES == feature).astype(FULL).astype(LOW)
                for i in range(width // LANES)
            ],
            axis=0,
        )
        unit, scale = unit_norm(dot(raw, order))
        edge_unit = unit_norm(dot(edge.astype(LOW), order))[0]
        before = jnp.where((z == 0) & (core == 0), -1.0, edge[1:2])
        before_lanes = before[:, :LANES]
        last = ids[length - 1 : length]
        keep = (ids == down(ids, before_lanes, plain)).astype(FULL)
        opened = (ids == before_lanes).astype(FULL)
        closing = (ids == last).astype(FULL)
        last = jnp.broadcast_to(last[:, :1], (1, width))
        scale = jnp.broadcast_to(scale, (length, LANES))
        return (
            order,
            unit,
            keep,
            jnp.concatenate([keep, opened, closing, scale], axis=1),
            stack_rows([edge_unit[0:1], last, before]),
        )

    order, unit_one, keep, statics, edges = fuse(
        begin,
        [square, full_act, narrow, ((length, 4 * LANES), FULL), edge_row],
        raw,
        edge,
        ids_lanes,
        plain=plain,
        flops=mac,
    )

    first_deep, second_pack = fuse(
        lambda second, *x: (jnp.stack(x), second),
        [((depth,) + first_pack.shape, LOW), (second_pack.shape, LOW)],
        second_pack,
        first_pack,
        *deep_got,
        after=(order, *cross_got),
        plain=plain,
    )
    first_wide = [to_batch(first_deep, k) for k in range(1, rows)]
    first_pieces = [first_deep] + first_wide
    first_pieces = first_pieces + [to_core(piece) for piece in first_pieces]
    second_got = [to_depth(second_pack, k) for k in range(1, depth)]

    cross_rows = rows * own * part_width // width
    packed_rows = cross_rows + channel_value.shape[0]

    def deepen(value, *x):
        b = places()[0]
        cross, x = x[:rows], x[rows:]
        cross = jnp.concatenate([pick(cross, j ^ b) for j in range(rows)], axis=0)
        return (
            jnp.stack([y[: 2 * own] for y in x]),
            jnp.stack([y[2 * own :] for y in x]),
            jnp.concatenate([cross.reshape(cross_rows, width), value], axis=0),
        )

    second_deep, third_deep, channel_pack = fuse(
        deepen,
        [
            ((depth, 2 * own, width), LOW),
            ((depth, own, width), LOW),
            ((packed_rows, width), LOW),
        ],
        channel_value,
        crossing[0],
        *cross_got,
        second_pack,
        *second_got,
        after=first_wide,
        plain=plain,
    )
    channel_pack = lax.all_gather(channel_pack, "seq", axis=0, tiled=True)

    def unpack_channel(x):
        x = x.reshape(cols, packed_rows, width)
        key = x[:, :cross_rows].reshape(cols, rows, own, part_width)
        key = jnp.concatenate(
            [key[j, i] for i in range(rows) for j in range(cols)], axis=0
        )
        return key, x[:, cross_rows:].reshape(part_width, width)

    part_key, part_value = fuse(
        unpack_channel,
        [((width, part_width), LOW), ((part_width, width), LOW)],
        channel_pack,
        plain=plain,
    )

    second_wide = [to_batch(second_deep, k) for k in range(1, rows)]
    (third_deep,) = fuse(
        lambda x: (x,), [(third_deep.shape, LOW)], third_deep, after=second_wide, plain=plain
    )
    third_wide = [to_batch(third_deep, k) for k in range(1, rows)]

    def joined(deep, wide, after):
        (mine,) = fuse(
            lambda *x: (jnp.concatenate(x, axis=0),),
            [((rows * depth,) + deep.shape[1:], LOW)],
            deep,
            *wide,
            after=after,
            plain=plain,
        )
        return mine, to_core(mine)


    def gathered(pieces, start):
        return jnp.concatenate(
            [piece[:, start : start + own].reshape(-1, width) for piece in pieces], axis=0
        )

    def front(unit, statics, edges, order, *pieces):
        vectors = sum(
            piece[k, 2 * own :].astype(FULL) for piece in pieces for k in range(depth)
        )
        lines = dot(vectors.astype(LOW), order)
        normed = unit * lines[0:1] + lines[2:3]
        edge_normed = edges[0:1] * lines[0:1] + lines[2:3]
        prior = down(normed, edge_normed, plain) * statics[:, :1]
        mix_key = mixing(normed, prior, lines[4:5])
        mix_value = mixing(normed, prior, lines[5:6])
        mix_recept = mixing(normed, prior, lines[6:7])
        key_all, value_all = gathered(pieces, 0), gathered(pieces, own)
        key, value = dot(mix_key, key_all), dot(mix_value, value_all)
        pace = jnp.exp(vectors[9:10])
        left = length - 1.0 - row_index((length, width)).astype(FULL)
        den = jnp.where(statics[:, 2 * LANES : 2 * LANES + 1] > 0.5, jnp.exp(key - pace * left), 0.0)
        num = den * value
        message = stack_rows(
            [column_sum(num), column_sum(den), column_sum(num * left), column_sum(den * left)]
            + [edges[1:2], edges[2:3]]
        )
        return (
            jnp.concatenate([vectors, lines], axis=0),
            normed - prior,
            jnp.stack([mix_key, mix_value, mix_recept]),
            jnp.stack([key_all, value_all]),
            key,
            value,
            message,
            jnp.stack([to_lanes(jnp.exp(-pace)), to_lanes(vectors[10:11])]),
        )

    (
        vectors,
        difference_one,
        mixes,
        first_all,
        key_act,
        value_act,
        message,
        rates,
    ) = fuse(
        front,
        [
            ((32, width), FULL),
            full_act,
            ((3, length, width), LOW),
            ((2, width, width), LOW),
            full_act,
            full_act,
            edge_row,
            ((2, width // LANES, LANES), FULL),
        ],
        unit_one,
        statics,
        edges,
        order,
        *first_pieces,
        plain=plain,
        limit=32,
        flops=2 * mac,
    )
    carry = carry_exchange(message, vectors, length, True, plain)
    mixes_got = to_core(mixes)

    def receptance(mixes, *pieces):
        recept_all, output_all = gathered(pieces, 0), gathered(pieces, own)
        return jax.nn.sigmoid(dot(mixes[2], recept_all)), jnp.stack([recept_all, output_all])

    recept_act, second_all = fuse(
        receptance,
        [full_act, ((2, width, width), LOW)],
        mixes,
        *joined(second_deep, second_wide, (message,)),
        plain=plain,
        limit=32,
        flops=mac,
    )
    key_tiles, value_tiles = to_tiles(key_act), to_tiles(value_act)
    scanned = run_forward(keep, key_tiles, value_tiles, rates, carry)

    def attend(scanned, recept, order, second_all, raw, vectors):
        gated = dot((recept * untile(scanned[0], width // LANES)).astype(LOW), order).astype(LOW)
        middle = raw.astype(FULL) + dot(gated, second_all[1])
        unit, scale = unit_norm(middle)
        normed = unit * vectors[1:2] + vectors[3:4]
        return (
            gated,
            middle,
            jnp.concatenate([unit, jnp.broadcast_to(scale, (length, LANES))], axis=1),
            stack_rows([normed[length - 1 :]]),
        )

    gated, middle, unit_two, edge_two = fuse(
        attend,
        [low_act, full_act, ((length, width + LANES), FULL), edge_row],
        scanned,
        recept_act,
        order,
        second_all,
        raw,
        vectors,
        plain=plain,
        flops=2 * mac,
    )
    edge_two = send_next(edge_two)

    def mix_two(unit, edge, statics, vectors):
        normed = unit[:, :width] * vectors[1:2] + vectors[3:4]
        prior = down(normed, edge[0:1], plain) * statics[:, :1]
        return (
            mixing(normed, prior, vectors[7:8]),
            mixing(normed, prior, vectors[8:9]),
            normed - prior,
        )

    mix_hidden, mix_gate, difference_two = fuse(
        mix_two, [low_act, low_act, full_act], unit_two, edge_two, statics, vectors, plain=plain
    )
    shared = [mix_hidden] + [to_batch(mix_hidden, k) for k in range(1, rows)]

    def channel(x, key, value):
        positive = jnp.maximum(dot(x, key), 0.0)
        squared = (positive * positive).astype(LOW)
        return squared, dot(squared, value)

    def channel_low(x, key, value):
        squared, out = channel(x, key, value)
        return squared, out.astype(LOW)

    hidden_act = ((length, part_width), LOW)
    squares, returned = [], []
    for k in range(rows):
        squared, out = fuse(
            channel_low if k else channel,
            [hidden_act, low_act if k else full_act],
            shared[k],
            part_key,
            part_value,
            plain=plain,
            flops=2 * mac,
        )
        squares.append(squared)
        returned.append(to_batch(out, k) if k else out)

    def gating(mix, order, *pieces):
        gate_all = gathered(pieces, 0)
        mix = dot(mix, order).astype(LOW)
        return jax.nn.sigmoid(dot(mix, gate_all)), mix, gate_all

    gate, mix_gate, gate_all = fuse(
        gating,
        [full_act, low_act, square],
        mix_gate,
        order,
        *joined(third_deep, third_wide, (gated,)),
        plain=plain,
        flops=2 * mac,
    )

    def finish(own_part, gate, middle, grad_out, *got):
        out = sum((x.astype(FULL) for x in got), own_part)
        grad_out = grad_out.astype(FULL)
        return (
            (middle + gate * out).astype(LOW),
            (grad_out * gate).astype(LOW),
            (grad_out * out * gate * (1.0 - gate)).astype(LOW),
        )

    block_output, grad_values, grad_gate = fuse(
        finish,
        [low_act, low_act, low_act],
        returned[0],
        gate,
        middle,
        cotangent,
        *returned[1:],
        plain=plain,
    )

    shared_grad = [grad_values] + [to_batch(grad_values, k) for k in range(1, rows)]

    def channel_back(grad, squared, key, value):
        positive = jnp.sqrt(squared.astype(FULL))
        hidden = (dot_back(grad, value) * 2.0 * positive).astype(LOW)
        return hidden, dot_back(hidden, key)

    def channel_back_low(grad, squared, key, value):
        hidden, out = channel_back(grad, squared, key, value)
        return hidden, out.astype(LOW)

    hiddens, returned = [], []
    for k in range(rows):
        hidden, out = fuse(
            channel_back_low if k else channel_back,
            [hidden_act, low_act if k else full_act],
            shared_grad[k],
            squares[k],
            part_key,
            part_value,
            plain=plain,
            flops=2 * mac,
        )
        hiddens.append(hidden)
        returned.append(to_batch(out, k) if k else out)

    def channel_terms(*x):
        shared, hiddens, squares, grads = (
            jnp.concatenate(x[i * rows : (i + 1) * rows], axis=0) for i in range(4)
        )
        key = dot_rows(shared, hiddens).astype(LOW)
        value = dot_rows(squares, grads).astype(LOW)
        key = key.reshape(rows, cols, own, part_width)
        value_rows = part_width // cols
        parts = []
        for j in range(cols):
            block = jnp.concatenate([key[i, j] for i in range(rows)], axis=0)
            parts += [
                block.reshape(cross_rows, width),
                value[j * value_rows : (j + 1) * value_rows],
            ]
        return (jnp.concatenate(parts, axis=0),)

    (channel_term,) = fuse(
        channel_terms,
        [((cols * packed_rows, width), LOW)],
        *shared,
        *hiddens,
        *squares,
        *shared_grad,
        after=returned[1:],
        plain=plain,
        limit=32,
        flops=2 * rows * mac,
    )
    channel_sum = lax.psum_scatter(channel_term, "seq", scatter_dimension=0, tiled=True)

    def gating_back(grad, gate_all, order):
        return (restore(dot_back(grad, gate_all), order),)

    (grad_mix_gate,) = fuse(
        gating_back, [full_act], grad_gate, gate_all, order, plain=plain, flops=3 * mac
    )

    def paired(active, active_got, grad, grad_got):
        return dot_rows(
            jnp.concatenate([active[:, :half], active_got[:, half:]], axis=0),
            jnp.concatenate([grad, grad_got], axis=0),
        ).astype(LOW)

    def cut(terms):
        part = half // rows
        return [
            jnp.stack([term[k * part : (k + 1) * part] for term in terms]) for k in range(rows)
        ]

    def gate_terms(mix_gate, mix_gate_got, grad_gate, grad_gate_got):
        return cut([paired(mix_gate, mix_gate_got, grad_gate, grad_gate_got)])

    def early_terms(gated, gated_got, mixes, mixes_got, grads, grads_got):
        return cut(
            [
                paired(gated, gated_got, grads[0], grads_got[0]),
                paired(mixes[2], mixes_got[2], grads[1], grads_got[1]),
            ]
        )

    mix_gate_got, grad_gate_got = to_core(mix_gate), to_core(grad_gate)
    gated_got = to_core(gated)
    gate_term = fuse(
        gate_terms,
        [((1, half // rows, width), LOW)] * rows,
        mix_gate,
        mix_gate_got,
        grad_gate,
        grad_gate_got,
        after=returned[1:],
        plain=plain,
        flops=mac,
    )
    gate_got = [to_batch(gate_term[k], k) for k in range(1, rows)]
    gate_pieces = add_batch(gate_term[0], gate_got, plain)

    def unmix_two(own_part, grad_gate, difference, statics, vectors, *got):
        grad_hidden = sum((x.astype(FULL) for x in got), own_part)
        mix_h, mix_g = vectors[7:8], vectors[8:9]
        passed = (grad_hidden * (1.0 - mix_h) + grad_gate * (1.0 - mix_g)) * statics[:, :1]
        return (
            grad_hidden * mix_h + grad_gate * mix_g,
            passed,
            stack_rows([passed[0:1]]),
            stack_rows([column_sum(grad_hidden * difference), column_sum(grad_gate * difference)]),
        )

    own_two, passed_two, after_two, mix_sums_two = fuse(
        unmix_two,
        [full_act, full_act, edge_row, edge_row],
        returned[0],
        grad_mix_gate,
        difference_two,
        statics,
        vectors,
        *returned[1:],
        plain=plain,
    )
    after_two = send_back(after_two)

    def middle_back(
        own_part, passed, after, unit, grad_out, vectors, mix_sums, recept, scanned,
        second_all, order, statics, edges,
    ):
        wkv, inverse, slope = (untile(scanned[i], width // LANES) for i in range(3))
        unit, scale = unit[:, :width], unit[:, width : width + 1]
        grad_normed = own_part + up(passed, after[0:1], plain)
        part = norm_backward(grad_normed, unit, scale, vectors[1:2])
        grad_middle = grad_out.astype(FULL) + part
        grad_low = grad_middle.astype(LOW)
        grad_gated = restore(dot_back(grad_low, second_all[1]), order)
        grad_wkv = grad_gated * recept
        grad_recept = (grad_wkv * wkv * (1.0 - recept)).astype(LOW)
        share = grad_wkv * inverse
        pace = jnp.exp(vectors[9:10])
        step = row_index((length, width)).astype(FULL)
        head = jnp.where(statics[:, LANES : LANES + 1] > 0.5, share * jnp.exp(-pace * step), 0.0)
        return (
            grad_middle,
            jnp.stack([grad_low, grad_recept]),
            share,
            stack_rows([column_sum(head), column_sum(head * wkv), edges[1:2], edges[2:3]]),
            stack_rows(
                [
                    column_sum(grad_normed * unit),
                    column_sum(grad_normed),
                    mix_sums[0:1],
                    mix_sums[1:2],
                    -pace * column_sum(grad_wkv * slope),
                ]
            ),
        )

    grad_middle, grad_pair, share, message, sums_two = fuse(
        middle_back,
        [full_act, ((2, length, width), LOW), full_act, edge_row, edge_row],
        own_two,
        passed_two,
        after_two,
        unit_two,
        cotangent,
        vectors,
        mix_sums_two,
        recept_act,
        scanned,
        second_all,
        order,
        statics,
        edges,
        after=(channel_term, gate_term[0]),
        plain=plain,
        limit=24,
        flops=3 * mac,
    )

    early = fuse(
        early_terms,
        [((2, half // rows, width), LOW)] * rows,
        gated,
        gated_got,
        mixes,
        mixes_got,
        grad_pair,
        to_core(grad_pair),
        plain=plain,
        limit=24,
        flops=2 * mac,
    )
    early_got = [to_batch(early[k], k) for k in range(1, rows)]

    carry_back = carry_exchange(message, vectors, length, False, plain, after=early)
    grad_key, grad_value, first_term = run_backward(
        keep, key_tiles, value_tiles, scanned, to_tiles(share), rates, carry_back
    )

    def lower(key, value):
        return (jnp.stack([key.astype(LOW), value.astype(LOW)]),)

    (grad_late,) = fuse(
        lower,
        [((2, length, width), LOW)],
        *lax.optimization_barrier((from_tiles(grad_key, width), from_tiles(grad_value, width))),
        plain=plain,
    )

    def late_terms(mixes, mixes_got, grads, grads_got):
        return cut([paired(mixes[i], mixes_got[i], grads[i], grads_got[i]) for i in range(2)])

    late = fuse(
        late_terms,
        [((2, half // rows, width), LOW)] * rows,
        mixes,
        mixes_got,
        grad_late,
        to_core(grad_late),
        after=gate_pieces,
        plain=plain,
        flops=2 * mac,
    )
    late_got = [to_batch(late[k], k) for k in range(1, rows)]
    early_pieces = add_batch(early[0], early_got, plain)
    output_grad, recept_grad = add_depth(early_pieces, plain)
    (gate_grad,) = add_depth(gate_pieces, plain)
    late_pieces = add_batch(late[0], late_got, plain, (output_grad, gate_grad))
    key_grad, value_grad = add_depth(late_pieces, plain)

    def unmix_one(grads, grad_pair, first_all, second_all, vectors, statics, difference, order):
        lines = vectors[16:]
        grad_key = dot_back(grads[0], first_all[0])
        grad_value = dot_back(grads[1], first_all[1])
        grad_recept = dot_back(grad_pair[1], second_all[0])
        m_key, m_value, m_recept = lines[4:5], lines[5:6], lines[6:7]
        passed = (
            grad_key * (1.0 - m_key) + grad_value * (1.0 - m_value) + grad_recept * (1.0 - m_recept)
        ) * statics[:, :1]
        return (
            grad_key * m_key + grad_value * m_value + grad_recept * m_recept,
            passed,
            restore(passed[:16], order)[:SUBS],
            stack_rows([column_sum(x * difference) for x in (grad_key, grad_value, grad_recept)]),
        )

    own_one, passed_one, after_one, mix_sums_one = fuse(
        unmix_one,
        [full_act, full_act, edge_row, edge_row],
        grad_late,
        grad_pair,
        first_all,
        second_all,
        vectors,
        statics,
        difference_one,
        order,
        plain=plain,
        limit=24,
        flops=3 * mac,
    )
    after_one = send_back(after_one)

    def input_back(
        own_part, passed, after, unit, statics, vectors, order, grad_middle, mix_sums, sums_two, first
    ):
        lines, scale = vectors[16:], statics[:, 3 * LANES : 3 * LANES + 1]
        after = jnp.where(row_index((16, width)) == 0, after[0:1], 0.0)
        grad_normed = own_part + up(passed, restore_in(after, order)[0:1], plain)
        part = norm_backward(grad_normed, unit, scale, lines[0:1])
        ordered = stack_rows(
            [
                column_sum(grad_normed * unit),
                column_sum(grad_normed),
                mix_sums[0:1],
                mix_sums[1:2],
                mix_sums[2:3],
            ],
            16,
        )
        ordered = restore(ordered, order)
        total = [ordered[0:1], sums_two[0:1], ordered[1:2], sums_two[1:2]]
        total += [ordered[2:3], ordered[3:4], ordered[4:5], sums_two[2:3], sums_two[3:4]]
        total += [sums_two[4:5], from_lanes(first)]
        return grad_middle + restore(part, order), stack_rows(total, 16)

    input_grad, sums = fuse(
        input_back,
        [full_act, ((16, width), FULL)],
        own_one,
        passed_one,
        after_one,
        unit_one,
        statics,
        vectors,
        order,
        grad_middle,
        mix_sums_one,
        sums_two,
        first_term,
        plain=plain,
        limit=24,
        flops=2 * mac,
    )
    sums = sums + to_core(sums)
    (sums,) = fuse(
        lambda *x: (sum(x[1:], x[0]),),
        [((16, width), FULL)],
        sums,
        *[to_batch(sums, k) for k in range(1, rows)],
        after=late_pieces,
        plain=plain,
    )

    def own_columns(*got):
        b, z, core = places()
        total = sum(got[1:], got[0])
        device = b * cols + z * 2 + core
        if plain:
            total = lax.dynamic_slice(total, (0, device * own), (16, own))
        else:
            total = pltpu.roll(total, (width - device * own) & (width - 1), 1)[:, :own]
        return total[0:2], total[2:4], total[4:9], total[9:10], total[10:11]

    gains_grad, offsets_grad, mixes_grad, decay_grad, first_grad = fuse(
        own_columns,
        [((2, own), FULL), ((2, own), FULL), ((5, own), FULL), ((1, own), FULL), ((1, own), FULL)],
        sums,
        *[to_depth(sums, k) for k in range(1, depth)],
        after=(key_grad,),
        plain=plain,
    )

    def uncross(x):
        b = places()[0]
        blocks = x[:cross_rows].reshape(rows, own, part_width)
        return [pick([blocks[j] for j in range(rows)], b ^ k) for k in range(rows)]

    leaving = fuse(uncross, [((own, part_width), LOW)] * rows, channel_sum, plain=plain)

    def assemble(x, *blocks):
        b = places()[0]
        blocks = [block.astype(FULL) for block in blocks]
        return (
            jnp.concatenate([pick(blocks, j ^ b) for j in range(rows)], axis=1),
            x[cross_rows:].astype(FULL),
        )

    channel_key_grad, channel_value_grad = fuse(
        assemble,
        [((own, hidden_width), FULL), (channel_value.shape, FULL)],
        channel_sum,
        leaving[0],
        *[to_batch(leaving[k], k) for k in range(1, rows)],
        plain=plain,
    )
    return (
        block_output[None],
        input_grad[None],
        key_grad,
        value_grad,
        recept_grad,
        output_grad,
        channel_key_grad,
        channel_value_grad,
        gate_grad,
        gains_grad,
        offsets_grad,
        mixes_grad,
        decay_grad[0],
        first_grad[0],
    )


def solution(mesh):
    tokens = P("batch", "seq", None)
    weight = P(BOTH, None)
    lines = P(None, BOTH)
    return jax.shard_map(
        per_device,
        mesh=mesh,
        in_specs=(tokens, P("batch", "seq"), tokens)
        + (weight,) * 7
        + (lines,) * 3
        + (P(BOTH),) * 2,
        out_specs=(tokens, tokens) + (weight,) * 7 + (lines,) * 3 + (P(BOTH),) * 2,
        check_vma=False,
    )
```

time: 395 us -> 350 us (0.89)
  starting transfers between devices: 51.5 us -> 122 us
  waiting for transfers between devices: 164 us -> 115 us
  Pallas kernels: 1.34 us -> 49.2 us
  matrix products: 40.4 us -> 0 us
  blocking collectives: 37.5 us -> 0 us
  other arithmetic: 31.2 us -> 0.01 us
    ppermute x37 -> x82, starting transfers between devices: 47.9 us -> 122 us  [send(): return lax.ppermute(block, BOTH, pairs)]
    all_gather x3 -> x1, waiting for transfers between devices: 69.6 us -> 0.01 us  [per_device(): channel_pack = lax.all_gather(channel_pack, 'seq', axis=0, tiled=True)]
    pallas_call x1 -> x47, Pallas kernels: 0.72 us -> 48.6 us  [the longest x46 47.9 us: fuse(): pl.pallas_call(kernel, out_shape=tuple((jax.ShapeDtypeStruct(shape, dtype...]
    dot_general x21 -> x0, matrix products: 40.4 us -> none  [the longest x7 17.3 us: project(): return jnp.einsum('td,de->te', active, weight, preferred_element_type=FULL)]
    unnamed x143 -> x166, local copies, waits for them, and re-layouts: 12.5 us -> 46.6 us
    all_gather x2 -> x0, blocking collectives: 28.3 us -> none  [the longest x1 15.4 us: per_device(): every_back = lax.all_gather(jnp.pad(local_back, ((0, 5), (0, 0))), 'seq')]
    ppermute x37 -> x82, waiting for transfers between devices: 93.8 us -> 115 us  [send(): return lax.ppermute(block, BOTH, pairs)]
    convert_element_type x9 -> x0, other arithmetic: 15.2 us -> none  [the longest x2 6.8 us: scatter_sums(): y = (pick(x, core, 3).astype(FULL) + got.astype(FULL)).astype(LOW)]
  transfers between devices with their start and end apart: 43 -> 84, of which waited for: 26 -> 34; matrix products, arithmetic and copies ran while one was open for 25% -> 0% of each run, Pallas kernels for 0% -> 12%
where the time goes in v2:
time: 350 us; the launch traced here: 347 us
  starting transfers between devices  122 us (35%)
  waiting for transfers between devices  115 us (33%)
  Pallas kernels  49.2 us (14%)
  local copies, waits for them, and re-layouts  46.6 us (13%)
  between operations  15 us (4%)
    ppermute x82, starting transfers between devices, send(): return lax.ppermute(block, BOTH, pairs)  122 us
    ppermute x82, waiting for transfers between devices, send(): return lax.ppermute(block, BOTH, pairs)  115 us
    pallas_call x46, Pallas kernels, fuse(): pl.pallas_call(kernel, out_shape=tuple((jax.ShapeDtypeStruct(shape, dtype...  47.9 us
    unnamed x166, local copies, waits for them, and re-layouts  46.6 us
  transfers between devices with their start and end apart: 84, of which 34 were waited for; matrix products, arithmetic and copies ran while one was open for 0% of the time, Pallas kernels for 12%

profile of v2, /device:TPU:8, one launch (start us, length us, event | category | flops | bytes accessed | tf_op | source)
XLA Modules:
  0.0 347.4 jit_solution(5508357058031544320)
XLA Ops:
  18.3 3.0 collective-permute-start.2
  25.2 6.3 %collective-permute-done.refs_1_ = f32[16,1024]{1,0:T(8,128)S(1)} collective-permute-done((f32[16,1024]{1,0:T(8,128)S(1)}, f32[16,1024]{1,0:T(8,128)S(1)}, u32[]{:S(2)}, u32[]{:S(2)}) %collective-permute-start) | collective-permute-done | bytes 65568 | tf_op jit(solution)/shard_map/ppermute | solution.py:38
  41.9 8.4 %collective-permute-start.19 = (bf16[96,1024]{1,0:T(8,128)(2,1)S(1)}, bf16[96,1024]{1,0:T(8,128)(2,1)S(1)}, u32[]{:S(2)}, u32[]{:S(2)}) collective-permute-start(bf16[96,1024]{1,0:T(8,128)(2,1)S(1)} %get-tuple-element.152.refs_5_), channel_id=1, source_target_pairs={{0,4},{1,5},{2,6},{3,7},{4,0},{5,1},{6,2},{7,3},{8,12},{9,13},{10,... | collective-permute-start | bytes 589832 | tf_op jit(solution)/shard_map/ppermute | solution.py:38
  50.3 5.4 %collective-permute-start.20 = (bf16[96,1024]{1,0:T(8,128)(2,1)S(1)}, bf16[96,1024]{1,0:T(8,128)(2,1)S(1)}, u32[]{:S(2)}, u32[]{:S(2)}) collective-permute-start(bf16[96,1024]{1,0:T(8,128)(2,1)S(1)} %get-tuple-element.152.refs_5_), channel_id=1, source_target_pairs={{0,6},{1,7},{2,4},{3,5},{4,2},{5,3},{6,0},{7,1},{8,14},{9,15},{10,... | collective-permute-start | bytes 589832 | tf_op jit(solution)/shard_map/ppermute | solution.py:38
  55.7 5.5 %collective-permute-done.19.refs_7_ = bf16[96,1024]{1,0:T(8,128)(2,1)S(1)} collective-permute-done((bf16[96,1024]{1,0:T(8,128)(2,1)S(1)}, bf16[96,1024]{1,0:T(8,128)(2,1)S(1)}, u32[]{:S(2)}, u32[]{:S(2)}) %collective-permute-start.19) | collective-permute-done | bytes 196640 | tf_op jit(solution)/shard_map/ppermute | solution.py:38
  61.3 3.3 collective-permute-done.20.refs_8_
  64.6 4.0 %collective-permute-done.9.refs_7_.refs_11_ = bf16[4,80,1024]{2,1,0:T(8,128)(2,1)S(1)} collective-permute-done((bf16[4,80,1024]{2,1,0:T(8,128)(2,1)S(1)}, bf16[4,80,1024]{2,1,0:T(8,128)(2,1)S(1)}, u32[]{:S(2)}, u32[]{:S(2)}) %collective-permute-start.9) | collective-permute-done | bytes 655392 | tf_op jit(solution)/shard_map/ppermute | solution.py:38
  70.7 2.8 collective-permute-start.10
  87.1 2.0 collective-permute-done.21.refs_1_
  89.1 12.2 %collective-permute-done.22.refs_2_ = bf16[4,64,1024]{2,1,0:T(8,128)(2,1)S(1)} collective-permute-done((bf16[4,64,1024]{2,1,0:T(8,128)(2,1)}, bf16[4,64,1024]{2,1,0:T(8,128)(2,1)S(1)}, u32[]{:S(2)}, u32[]{:S(2)}) %collective-permute-start.22) | collective-permute-done | bytes 524320 | tf_op jit(solution)/shard_map/ppermute | solution.py:38
  109.4 4.6 %collective-permute-done.15.refs_3_ = f32[8,1024]{1,0:T(8,128)S(1)} collective-permute-done((f32[8,1024]{1,0:T(8,128)S(1)}, f32[8,1024]{1,0:T(8,128)S(1)}, u32[]{:S(2)}, u32[]{:S(2)}) %collective-permute-start.15) | collective-permute-done | bytes 32800 | tf_op jit(solution)/shard_map/ppermute | solution.py:38
  122.5 2.6 collective-permute-start.25
  125.1 8.5 %collective-permute-done.25.refs_1_ = f32[8,1024]{1,0:T(8,128)S(1)} collective-permute-done((f32[8,1024]{1,0:T(8,128)S(1)}, f32[8,1024]{1,0:T(8,128)S(1)}, u32[]{:S(2)}, u32[]{:S(2)}) %collective-permute-start.25) | collective-permute-done | bytes 32800 | tf_op jit(solution)/shard_map/ppermute | solution.py:38
  139.1 2.2 copy-done.9
  141.6 3.4 collective-permute-done.30.refs_0_.refs_1_
  151.4 2.5 collective-permute-start.35
  153.9 2.4 shard_map.270
  161.1 2.5 collective-permute-start.36
  165.0 5.2 %collective-permute-done.36.refs_0_.refs_13_ = bf16[128,1024]{1,0:T(8,128)(2,1)S(1)} collective-permute-done((bf16[128,1024]{1,0:T(8,128)(2,1)S(1)}, bf16[128,1024]{1,0:T(8,128)(2,1)S(1)}, u32[]{:S(2)}, u32[]{:S(2)}) %collective-permute-start.36) | collective-permute-done | bytes 262176 | tf_op jit(solution)/shard_map/ppermute | solution.py:38
  171.7 2.5 collective-permute-start.37
  177.4 2.5 collective-permute-start.41
  182.2 2.8 collective-permute-done.39.refs_6_.refs_17_.refs_5_
  185.0 3.5 %shard_map.281.refs_13_ = bf16[2048,1024]{1,0:T(8,128)(2,1)S(1)} custom-call(bf16[128,1024]{1,0:T(8,128)(2,1)S(1)} %copy-done.41, bf16[128,1024]{1,0:T(8,128)(2,1)} %collective-permute-done.30.refs_0_.refs_1_, bf16[128,1024]{1,0:T(8,128)(2,1)} %collective-permute-done.32.refs_0_.refs_2_, bf16[128,1024]{1,0:T(8,128)(2,1)} %collective-permute-done.34.refs_0_.refs_3_, ...), custom_call_target="tpu_custom_call" | custom-call | flops 1024 | bytes 1024 | tf_op jit(solution)/shard_map/pallas_call | solution.py:82
  188.5 2.0 copy-done.2
  195.2 2.4 shard_map.276.refs_1_
  200.3 11.2 %collective-permute-start.42 = (f32[8,1024]{1,0:T(8,128)S(1)}, f32[8,1024]{1,0:T(8,128)S(1)}, u32[]{:S(2)}, u32[]{:S(2)}) collective-permute-start(f32[8,1024]{1,0:T(8,128)S(1)} %get-tuple-element.186), channel_id=1, source_target_pairs={{1,0},{2,1},{3,2},{4,3},{5,4},{6,5},{7,6},{9,8},{10,9},{11,10},{12... | collective-permute-start | bytes 98312 | tf_op jit(solution)/shard_map/ppermute | solution.py:38
  218.1 2.5 shard_map.283
  224.7 3.2 collective-permute-start.46
  232.1 3.6 %collective-permute-done.47.refs_4_ = f32[8,1024]{1,0:T(8,128)S(1)} collective-permute-done((f32[8,1024]{1,0:T(8,128)S(1)}, f32[8,1024]{1,0:T(8,128)S(1)}, u32[]{:S(2)}, u32[]{:S(2)}) %collective-permute-start.47) | collective-permute-done | bytes 32800 | tf_op jit(solution)/shard_map/ppermute | solution.py:38
  236.6 2.4 collective-permute-start.54
  239.9 2.6 collective-permute-start.56
  242.5 3.7 %collective-permute-done.54.refs_1_ = bf16[1,128,1024]{2,1,0:T(8,128)(2,1)S(1)} collective-permute-done((bf16[1,128,1024]{2,1,0:T(8,128)(2,1)S(1)}, bf16[1,128,1024]{2,1,0:T(8,128)(2,1)S(1)}, u32[]{:S(2)}, u32[]{:S(2)}) %collective-permute-start.54) | collective-permute-done | bytes 262176 | tf_op jit(solution)/shard_map/ppermute | solution.py:38
  247.4 2.2 collective-permute-start.62
  249.6 13.8 %collective-permute-done.56.refs_3_ = bf16[1,128,1024]{2,1,0:T(8,128)(2,1)S(1)} collective-permute-done((bf16[1,128,1024]{2,1,0:T(8,128)(2,1)S(1)}, bf16[1,128,1024]{2,1,0:T(8,128)(2,1)S(1)}, u32[]{:S(2)}, u32[]{:S(2)}) %collective-permute-start.56) | collective-permute-done | bytes 262176 | tf_op jit(solution)/shard_map/ppermute | solution.py:38
  263.5 2.7 collective-permute-start.66
  274.4 3.5 %collective-permute-done.61.refs_2_ = bf16[2,128,1024]{2,1,0:T(8,128)(2,1)S(1)} collective-permute-done((bf16[2,128,1024]{2,1,0:T(8,128)(2,1)S(1)}, bf16[2,128,1024]{2,1,0:T(8,128)(2,1)S(1)}, u32[]{:S(2)}, u32[]{:S(2)}) %collective-permute-start.61) | collective-permute-done | bytes 524320 | tf_op jit(solution)/shard_map/ppermute | solution.py:38
  277.9 3.3 shard_map.289
  281.3 2.3 collective-permute-start.52
  284.9 2.2 collective-permute-start.63
  287.1 3.9 %shard_map.290 = (f32[128,1024]{1,0:T(8,128)}, f32[16,1024]{1,0:T(8,128)S(1)}) custom-call(f32[128,1024]{1,0:T(8,128)S(1)} %get-tuple-element.207.refs_0_, f32[128,1024]{1,0:T(8,128)S(1)} %get-tuple-element.208.refs_1_, f32[8,1024]{1,0:T(8,128)S(1)} %collective-permute-done.52.refs_2_, f32[128,1024]{1,0:T(8,128)S(1)} %copy-done.35, ...), custom_call_target="tpu_custom_call" | custom-call | flops 1024 | bytes 1024 | tf_op jit(solution)/shard_map/pallas_call | solution.py:82
  292.3 4.6 %collective-permute-start.64 = (bf16[2,32,1024]{2,1,0:T(8,128)(2,1)S(1)}, bf16[2,32,1024]{2,1,0:T(8,128)(2,1)S(1)}, u32[]{:S(2)}, u32[]{:S(2)}) collective-permute-start(bf16[2,32,1024]{2,1,0:T(8,128)(2,1)S(1)} %get-tuple-element.228), channel_id=1, source_target_pairs={{0,4},{1,5},{2,6},{3,7},{4,0},{5,1},{6,2},{7,3},{8,12},{9,13},{10,... | collective-permute-start | bytes 393224 | tf_op jit(solution)/shard_map/ppermute | solution.py:38
  296.9 8.7 %collective-permute-done.64.refs_2_ = bf16[2,32,1024]{2,1,0:T(8,128)(2,1)S(1)} collective-permute-done((bf16[2,32,1024]{2,1,0:T(8,128)(2,1)S(1)}, bf16[2,32,1024]{2,1,0:T(8,128)(2,1)S(1)}, u32[]{:S(2)}, u32[]{:S(2)}) %collective-permute-start.64) | collective-permute-done | bytes 131104 | tf_op jit(solution)/shard_map/ppermute | solution.py:38
  309.4 3.0 collective-permute-start.78
  314.6 3.9 %collective-permute-start.70 = (bf16[2,32,1024]{2,1,0:T(8,128)(2,1)S(1)}, bf16[2,32,1024]{2,1,0:T(8,128)(2,1)S(1)}, u32[]{:S(2)}, u32[]{:S(2)}) collective-permute-start(bf16[2,32,1024]{2,1,0:T(8,128)(2,1)S(1)} %get-tuple-element.233.refs_6_), channel_id=1, source_target_pairs={{0,4},{1,5},{2,6},{3,7},{4,0},{5,1},{6,2},{7,3},{8,12},{9,13},{10,... | collective-permute-start | bytes 393224 | tf_op jit(solution)/shard_map/ppermute | solution.py:38
  320.1 2.0 collective-permute-start.80
  323.2 4.1 %collective-permute-done.79.refs_1_ = f32[16,1024]{1,0:T(8,128)S(1)} collective-permute-done((f32[16,1024]{1,0:T(8,128)S(1)}, f32[16,1024]{1,0:T(8,128)S(1)}, u32[]{:S(2)}, u32[]{:S(2)}) %collective-permute-start.79) | collective-permute-done | bytes 65568 | tf_op jit(solution)/shard_map/ppermute | solution.py:38
  327.4 3.0 collective-permute-start.81
  331.1 2.2 collective-permute-done.71.refs_3_
  (337 shorter events, 135.2 us)
Async XLA Ops:
  7.2 132.0 %all-gather.2.cloned.1.call-start = ((), (), s32[]{:S(2)}) async-start(), calls=%async_computation.1 | async-start | bytes 4718592 | tf_op jit(solution)/shard_map/all_gather | solution.py:603
  18.2 20.0 %collective-permute-start.1 = (bf16[80,1024]{1,0:T(8,128)(2,1)S(1)}, bf16[80,1024]{1,0:T(8,128)(2,1)S(1)}, u32[]{:S(2)}, u32[]{:S(2)}) collective-permute-start(bf16[80,1024]{1,0:T(8,128)(2,1)S(1)} %get-tuple-element.140.refs_1_), channel_id=1, source_target_pairs={{0,2},{1,3},{2,0},{3,1},{4,6},{5,7},{6,4},{7,5},{8,10},{9,11},{10,... | collective-permute-start | bytes 491528 | tf_op jit(solution)/shard_map/ppermute | solution.py:38
  18.3 20.0 %collective-permute-start.2 = (bf16[80,1024]{1,0:T(8,128)(2,1)S(1)}, bf16[80,1024]{1,0:T(8,128)(2,1)S(1)}, u32[]{:S(2)}, u32[]{:S(2)}) collective-permute-start(bf16[80,1024]{1,0:T(8,128)(2,1)S(1)} %get-tuple-element.140.refs_1_), channel_id=1, source_target_pairs={{0,4},{1,5},{2,6},{3,7},{4,0},{5,1},{6,2},{7,3},{8,12},{9,13},{10,... | collective-permute-start | bytes 491528 | tf_op jit(solution)/shard_map/ppermute | solution.py:38
  21.3 16.9 %collective-permute-start.3 = (bf16[80,1024]{1,0:T(8,128)(2,1)S(1)}, bf16[80,1024]{1,0:T(8,128)(2,1)S(1)}, u32[]{:S(2)}, u32[]{:S(2)}) collective-permute-start(bf16[80,1024]{1,0:T(8,128)(2,1)S(1)} %get-tuple-element.140.refs_1_), channel_id=1, source_target_pairs={{0,6},{1,7},{2,4},{3,5},{4,2},{5,3},{6,0},{7,1},{8,14},{9,15},{10,... | collective-permute-start | bytes 491528 | tf_op jit(solution)/shard_map/ppermute | solution.py:38
  38.3 26.2 %collective-permute-start.7 = (bf16[4,80,1024]{2,1,0:T(8,128)(2,1)S(1)}, bf16[4,80,1024]{2,1,0:T(8,128)(2,1)S(1)}, u32[]{:S(2)}, u32[]{:S(2)}) collective-permute-start(bf16[4,80,1024]{2,1,0:T(8,128)(2,1)S(1)} %get-tuple-element.144.refs_4_), channel_id=1, source_target_pairs={{0,8},{1,9},{2,10},{3,11},{4,12},{5,13},{6,14},{7,15},{8,0},{9,1},... | collective-permute-start | bytes 1966088 | tf_op jit(solution)/shard_map/ppermute | solution.py:38
  39.9 24.7 %collective-permute-start.8 = (bf16[4,80,1024]{2,1,0:T(8,128)(2,1)S(1)}, bf16[4,80,1024]{2,1,0:T(8,128)(2,1)S(1)}, u32[]{:S(2)}, u32[]{:S(2)}) collective-permute-start(bf16[4,80,1024]{2,1,0:T(8,128)(2,1)S(1)} %get-tuple-element.144.refs_4_), channel_id=1, source_target_pairs={{0,16},{1,17},{2,18},{3,19},{4,20},{5,21},{6,22},{7,23},{8,24},{9,... | collective-permute-start | bytes 1966088 | tf_op jit(solution)/shard_map/ppermute | solution.py:38
  40.4 28.2 %collective-permute-start.9 = (bf16[4,80,1024]{2,1,0:T(8,128)(2,1)S(1)}, bf16[4,80,1024]{2,1,0:T(8,128)(2,1)S(1)}, u32[]{:S(2)}, u32[]{:S(2)}) collective-permute-start(bf16[4,80,1024]{2,1,0:T(8,128)(2,1)S(1)} %get-tuple-element.144.refs_4_), channel_id=1, source_target_pairs={{0,24},{1,25},{2,26},{3,27},{4,28},{5,29},{6,30},{7,31},{8,16},{9,... | collective-permute-start | bytes 1966088 | tf_op jit(solution)/shard_map/ppermute | solution.py:38
  41.9 19.4 %collective-permute-start.19 = (bf16[96,1024]{1,0:T(8,128)(2,1)S(1)}, bf16[96,1024]{1,0:T(8,128)(2,1)S(1)}, u32[]{:S(2)}, u32[]{:S(2)}) collective-permute-start(bf16[96,1024]{1,0:T(8,128)(2,1)S(1)} %get-tuple-element.152.refs_5_), channel_id=1, source_target_pairs={{0,4},{1,5},{2,6},{3,7},{4,0},{5,1},{6,2},{7,3},{8,12},{9,13},{10,... | collective-permute-start | bytes 589832 | tf_op jit(solution)/shard_map/ppermute | solution.py:38
  50.3 14.2 %collective-permute-start.20 = (bf16[96,1024]{1,0:T(8,128)(2,1)S(1)}, bf16[96,1024]{1,0:T(8,128)(2,1)S(1)}, u32[]{:S(2)}, u32[]{:S(2)}) collective-permute-start(bf16[96,1024]{1,0:T(8,128)(2,1)S(1)} %get-tuple-element.152.refs_5_), channel_id=1, source_target_pairs={{0,6},{1,7},{2,4},{3,5},{4,2},{5,3},{6,0},{7,1},{8,14},{9,15},{10,... | collective-permute-start | bytes 589832 | tf_op jit(solution)/shard_map/ppermute | solution.py:38
  70.7 251.5 %reduce-scatter.2.cloned.1.call-start = ((), (), s32[]{:S(2)}) async-start(), calls=%async_computation.2 | async-start | bytes 4718592 | tf_op jit(solution)/shard_map/reduce_scatter | solution.py:878
  74.2 14.9 %collective-permute-start.21 = (bf16[4,64,1024]{2,1,0:T(8,128)(2,1)}, bf16[4,64,1024]{2,1,0:T(8,128)(2,1)S(1)}, u32[]{:S(2)}, u32[]{:S(2)}) collective-permute-start(bf16[4,64,1024]{2,1,0:T(8,128)(2,1)} %get-tuple-element.153.refs_0_), channel_id=1, source_target_pairs={{0,8},{1,9},{2,10},{3,11},{4,12},{5,13},{6,14},{7,15},{8,0},{9,1},... | collective-permute-start | bytes 1572872 | tf_op jit(solution)/shard_map/ppermute | solution.py:38
  75.7 25.6 %collective-permute-start.22 = (bf16[4,64,1024]{2,1,0:T(8,128)(2,1)}, bf16[4,64,1024]{2,1,0:T(8,128)(2,1)S(1)}, u32[]{:S(2)}, u32[]{:S(2)}) collective-permute-start(bf16[4,64,1024]{2,1,0:T(8,128)(2,1)} %get-tuple-element.153.refs_0_), channel_id=1, source_target_pairs={{0,16},{1,17},{2,18},{3,19},{4,20},{5,21},{6,22},{7,23},{8,24},{9,... | collective-permute-start | bytes 1572872 | tf_op jit(solution)/shard_map/ppermute | solution.py:38
  77.0 24.3 %collective-permute-start.23 = (bf16[4,64,1024]{2,1,0:T(8,128)(2,1)}, bf16[4,64,1024]{2,1,0:T(8,128)(2,1)S(1)}, u32[]{:S(2)}, u32[]{:S(2)}) collective-permute-start(bf16[4,64,1024]{2,1,0:T(8,128)(2,1)} %get-tuple-element.153.refs_0_), channel_id=1, source_target_pairs={{0,24},{1,25},{2,26},{3,27},{4,28},{5,29},{6,30},{7,31},{8,16},{9,... | collective-permute-start | bytes 1572872 | tf_op jit(solution)/shard_map/ppermute | solution.py:38
  102.5 16.0 %collective-permute-start.24 = (bf16[16,64,1024]{2,1,0:T(8,128)(2,1)S(1)}, bf16[16,64,1024]{2,1,0:T(8,128)(2,1)S(1)}, u32[]{:S(2)}, u32[]{:S(2)}) collective-permute-start(bf16[16,64,1024]{2,1,0:T(8,128)(2,1)S(1)} %shard_map.262.refs_1_), channel_id=1, source_target_pairs={{0,1},{1,0},{2,3},{3,2},{4,5},{5,4},{6,7},{7,6},{8,9},{9,8},{10,11... | collective-permute-start | bytes 6291464 | tf_op jit(solution)/shard_map/ppermute | solution.py:38
  102.6 18.8 %collective-permute-start.26 = (bf16[4,32,1024]{2,1,0:T(8,128)(2,1)S(1)}, bf16[4,32,1024]{2,1,0:T(8,128)(2,1)S(1)}, u32[]{:S(2)}, u32[]{:S(2)}) collective-permute-start(bf16[4,32,1024]{2,1,0:T(8,128)(2,1)S(1)} %shard_map.268.refs_0_), channel_id=1, source_target_pairs={{0,8},{1,9},{2,10},{3,11},{4,12},{5,13},{6,14},{7,15},{8,0},{9,1},... | collective-permute-start | bytes 786440 | tf_op jit(solution)/shard_map/ppermute | solution.py:38
  103.2 18.2 %collective-permute-start.27 = (bf16[4,32,1024]{2,1,0:T(8,128)(2,1)S(1)}, bf16[4,32,1024]{2,1,0:T(8,128)(2,1)S(1)}, u32[]{:S(2)}, u32[]{:S(2)}) collective-permute-start(bf16[4,32,1024]{2,1,0:T(8,128)(2,1)S(1)} %shard_map.268.refs_0_), channel_id=1, source_target_pairs={{0,16},{1,17},{2,18},{3,19},{4,20},{5,21},{6,22},{7,23},{8,24},{9,... | collective-permute-start | bytes 786440 | tf_op jit(solution)/shard_map/ppermute | solution.py:38
  104.6 16.8 %collective-permute-start.28 = (bf16[4,32,1024]{2,1,0:T(8,128)(2,1)S(1)}, bf16[4,32,1024]{2,1,0:T(8,128)(2,1)S(1)}, u32[]{:S(2)}, u32[]{:S(2)}) collective-permute-start(bf16[4,32,1024]{2,1,0:T(8,128)(2,1)S(1)} %shard_map.268.refs_0_), channel_id=1, source_target_pairs={{0,24},{1,25},{2,26},{3,27},{4,28},{5,29},{6,30},{7,31},{8,16},{9,... | collective-permute-start | bytes 786440 | tf_op jit(solution)/shard_map/ppermute | solution.py:38
  122.5 31.3 %collective-permute-start.29 = (bf16[16,32,1024]{2,1,0:T(8,128)(2,1)}, bf16[16,32,1024]{2,1,0:T(8,128)(2,1)}, u32[]{:S(2)}, u32[]{:S(2)}) collective-permute-start(bf16[16,32,1024]{2,1,0:T(8,128)(2,1)} %shard_map.269.refs_2_), channel_id=1, source_target_pairs={{0,1},{1,0},{2,3},{3,2},{4,5},{5,4},{6,7},{7,6},{8,9},{9,8},{10,11... | collective-permute-start | bytes 3145736 | tf_op jit(solution)/shard_map/ppermute | solution.py:38
  122.5 11.1 %collective-permute-start.25 = (f32[8,1024]{1,0:T(8,128)S(1)}, f32[8,1024]{1,0:T(8,128)S(1)}, u32[]{:S(2)}, u32[]{:S(2)}) collective-permute-start(f32[8,1024]{1,0:T(8,128)S(1)} %get-tuple-element.157), channel_id=1, source_target_pairs={{0,1},{1,2},{2,3},{3,4},{4,5},{5,6},{6,7},{8,9},{9,10},{10,11},{11... | collective-permute-start | bytes 98312 | tf_op jit(solution)/shard_map/ppermute | solution.py:38
  136.4 11.0 %collective-permute-start.32 = (bf16[128,1024]{1,0:T(8,128)(2,1)S(1)}, bf16[128,1024]{1,0:T(8,128)(2,1)}, u32[]{:S(2)}, u32[]{:S(2)}) collective-permute-start(bf16[128,1024]{1,0:T(8,128)(2,1)S(1)} %get-tuple-element.158.refs_0_), channel_id=1, source_target_pairs={{0,16},{1,17},{2,18},{3,19},{4,20},{5,21},{6,22},{7,23},{8,24},{9,... | collective-permute-start | bytes 786440 | tf_op jit(solution)/shard_map/ppermute | solution.py:38
  137.8 11.9 %collective-permute-start.34 = (bf16[128,1024]{1,0:T(8,128)(2,1)S(1)}, bf16[128,1024]{1,0:T(8,128)(2,1)}, u32[]{:S(2)}, u32[]{:S(2)}) collective-permute-start(bf16[128,1024]{1,0:T(8,128)(2,1)S(1)} %get-tuple-element.158.refs_0_), channel_id=1, source_target_pairs={{0,24},{1,25},{2,26},{3,27},{4,28},{5,29},{6,30},{7,31},{8,16},{9,... | collective-permute-start | bytes 786440 | tf_op jit(solution)/shard_map/ppermute | solution.py:38
  146.7 11.6 %collective-permute-start.31 = (bf16[128,1024]{1,0:T(8,128)(2,1)S(1)}, bf16[128,1024]{1,0:T(8,128)(2,1)S(1)}, u32[]{:S(2)}, u32[]{:S(2)}) collective-permute-start(bf16[128,1024]{1,0:T(8,128)(2,1)S(1)} %get-tuple-element.168), channel_id=1, source_target_pairs={{0,8},{1,9},{2,10},{3,11},{4,12},{5,13},{6,14},{7,15},{8,0},{9,1},... | collective-permute-start | bytes 786440 | tf_op jit(solution)/shard_map/ppermute | solution.py:38
  149.2 10.9 %collective-permute-start.33 = (bf16[128,1024]{1,0:T(8,128)(2,1)S(1)}, bf16[128,1024]{1,0:T(8,128)(2,1)S(1)}, u32[]{:S(2)}, u32[]{:S(2)}) collective-permute-start(bf16[128,1024]{1,0:T(8,128)(2,1)S(1)} %get-tuple-element.169), channel_id=1, source_target_pairs={{0,16},{1,17},{2,18},{3,19},{4,20},{5,21},{6,22},{7,23},{8,24},{9,... | collective-permute-start | bytes 786440 | tf_op jit(solution)/shard_map/ppermute | solution.py:38
  163.5 10.7 %collective-permute-start.38 = (bf16[128,1024]{1,0:T(8,128)(2,1)S(1)}, bf16[128,1024]{1,0:T(8,128)(2,1)S(1)}, u32[]{:S(2)}, u32[]{:S(2)}) collective-permute-start(bf16[128,1024]{1,0:T(8,128)(2,1)S(1)} %get-tuple-element.172.refs_0_.refs_12_), channel_id=1, source_target_pairs={{0,16},{1,17},{2,18},{3,19},{4,20},{5,21},{6,22},{7,23},{8,24},{9,... | collective-permute-start | bytes 786440 | tf_op jit(solution)/shard_map/ppermute | solution.py:38
  163.5 12.3 %collective-permute-start.40 = (bf16[128,1024]{1,0:T(8,128)(2,1)S(1)}, bf16[128,1024]{1,0:T(8,128)(2,1)S(1)}, u32[]{:S(2)}, u32[]{:S(2)}) collective-permute-start(bf16[128,1024]{1,0:T(8,128)(2,1)S(1)} %get-tuple-element.172.refs_0_.refs_12_), channel_id=1, source_target_pairs={{0,24},{1,25},{2,26},{3,27},{4,28},{5,29},{6,30},{7,31},{8,16},{9,... | collective-permute-start | bytes 786440 | tf_op jit(solution)/shard_map/ppermute | solution.py:38
  171.7 10.5 %collective-permute-start.37 = (bf16[128,1024]{1,0:T(8,128)(2,1)S(1)}, bf16[128,1024]{1,0:T(8,128)(2,1)S(1)}, u32[]{:S(2)}, u32[]{:S(2)}) collective-permute-start(bf16[128,1024]{1,0:T(8,128)(2,1)S(1)} %get-tuple-element.179), channel_id=1, source_target_pairs={{0,8},{1,9},{2,10},{3,11},{4,12},{5,13},{6,14},{7,15},{8,0},{9,1},... | collective-permute-start | bytes 786440 | tf_op jit(solution)/shard_map/ppermute | solution.py:38
  192.0 37.2 %collective-permute-start.50 = (bf16[3,128,1024]{2,1,0:T(8,128)(2,1)S(1)}, bf16[3,128,1024]{2,1,0:T(8,128)(2,1)S(1)}, u32[]{:S(2)}, u32[]{:S(2)}) collective-permute-start(bf16[3,128,1024]{2,1,0:T(8,128)(2,1)S(1)} %get-tuple-element.150.refs_0_.refs_2_), channel_id=1, source_target_pairs={{0,1},{1,0},{2,3},{3,2},{4,5},{5,4},{6,7},{7,6},{8,9},{9,8},{10,11... | collective-permute-start | bytes 2359304 | tf_op jit(solution)/shard_map/ppermute | solution.py:38
  192.1 19.4 %collective-permute-start.43 = (bf16[128,1024]{1,0:T(8,128)(2,1)}, bf16[128,1024]{1,0:T(8,128)(2,1)S(1)}, u32[]{:S(2)}, u32[]{:S(2)}) collective-permute-start(bf16[128,1024]{1,0:T(8,128)(2,1)} %copy-done.60), channel_id=1, source_target_pairs={{0,1},{1,0},{2,3},{3,2},{4,5},{5,4},{6,7},{7,6},{8,9},{9,8},{10,11... | collective-permute-start | bytes 786440 | tf_op jit(solution)/shard_map/ppermute | solution.py:38
  192.6 18.9 %collective-permute-start.44 = (bf16[128,1024]{1,0:T(8,128)(2,1)}, bf16[128,1024]{1,0:T(8,128)(2,1)S(1)}, u32[]{:S(2)}, u32[]{:S(2)}) collective-permute-start(bf16[128,1024]{1,0:T(8,128)(2,1)} %copy-done.42), channel_id=1, source_target_pairs={{0,1},{1,0},{2,3},{3,2},{4,5},{5,4},{6,7},{7,6},{8,9},{9,8},{10,11... | collective-permute-start | bytes 786440 | tf_op jit(solution)/shard_map/ppermute | solution.py:38
  200.3 13.6 %collective-permute-start.42 = (f32[8,1024]{1,0:T(8,128)S(1)}, f32[8,1024]{1,0:T(8,128)S(1)}, u32[]{:S(2)}, u32[]{:S(2)}) collective-permute-start(f32[8,1024]{1,0:T(8,128)S(1)} %get-tuple-element.186), channel_id=1, source_target_pairs={{1,0},{2,1},{3,2},{4,3},{5,4},{6,5},{7,6},{9,8},{10,9},{11,10},{12... | collective-permute-start | bytes 98312 | tf_op jit(solution)/shard_map/ppermute | solution.py:38
  236.5 29.7 %collective-permute-start.53 = (bf16[2,128,1024]{2,1,0:T(8,128)(2,1)S(1)}, bf16[2,128,1024]{2,1,0:T(8,128)(2,1)S(1)}, u32[]{:S(2)}, u32[]{:S(2)}) collective-permute-start(bf16[2,128,1024]{2,1,0:T(8,128)(2,1)S(1)} %shard_map.288.refs_0_.refs_2_), channel_id=1, source_target_pairs={{0,1},{1,0},{2,3},{3,2},{4,5},{5,4},{6,7},{7,6},{8,9},{9,8},{10,11... | collective-permute-start | bytes 1572872 | tf_op jit(solution)/shard_map/ppermute | solution.py:38
  239.4 33.2 %collective-permute-start.60 = (bf16[2,128,1024]{2,1,0:T(8,128)(2,1)S(1)}, bf16[2,128,1024]{2,1,0:T(8,128)(2,1)S(1)}, u32[]{:S(2)}, u32[]{:S(2)}) collective-permute-start(bf16[2,128,1024]{2,1,0:T(8,128)(2,1)S(1)} %get-tuple-element.198.refs_7_), channel_id=1, source_target_pairs={{0,8},{1,9},{2,10},{3,11},{4,12},{5,13},{6,14},{7,15},{8,0},{9,1},... | collective-permute-start | bytes 1572872 | tf_op jit(solution)/shard_map/ppermute | solution.py:38
  239.9 23.5 %collective-permute-start.56 = (bf16[1,128,1024]{2,1,0:T(8,128)(2,1)S(1)}, bf16[1,128,1024]{2,1,0:T(8,128)(2,1)S(1)}, u32[]{:S(2)}, u32[]{:S(2)}) collective-permute-start(bf16[1,128,1024]{2,1,0:T(8,128)(2,1)S(1)} %get-tuple-element.217), channel_id=1, source_target_pairs={{0,24},{1,25},{2,26},{3,27},{4,28},{5,29},{6,30},{7,31},{8,16},{9,... | collective-permute-start | bytes 786440 | tf_op jit(solution)/shard_map/ppermute | solution.py:38
  246.2 31.7 %collective-permute-start.61 = (bf16[2,128,1024]{2,1,0:T(8,128)(2,1)S(1)}, bf16[2,128,1024]{2,1,0:T(8,128)(2,1)S(1)}, u32[]{:S(2)}, u32[]{:S(2)}) collective-permute-start(bf16[2,128,1024]{2,1,0:T(8,128)(2,1)S(1)} %get-tuple-element.199.refs_8_), channel_id=1, source_target_pairs={{0,16},{1,17},{2,18},{3,19},{4,20},{5,21},{6,22},{7,23},{8,24},{9,... | collective-permute-start | bytes 1572872 | tf_op jit(solution)/shard_map/ppermute | solution.py:38
  247.4 33.8 %collective-permute-start.62 = (bf16[2,128,1024]{2,1,0:T(8,128)(2,1)S(1)}, bf16[2,128,1024]{2,1,0:T(8,128)(2,1)S(1)}, u32[]{:S(2)}, u32[]{:S(2)}) collective-permute-start(bf16[2,128,1024]{2,1,0:T(8,128)(2,1)S(1)} %get-tuple-element.200.refs_9_), channel_id=1, source_target_pairs={{0,24},{1,25},{2,26},{3,27},{4,28},{5,29},{6,30},{7,31},{8,16},{9,... | collective-permute-start | bytes 1572872 | tf_op jit(solution)/shard_map/ppermute | solution.py:38
  268.4 41.0 %collective-permute-start.57 = (bf16[2,128,1024]{2,1,0:T(8,128)(2,1)S(1)}, bf16[2,128,1024]{2,1,0:T(8,128)(2,1)S(1)}, u32[]{:S(2)}, u32[]{:S(2)}) collective-permute-start(bf16[2,128,1024]{2,1,0:T(8,128)(2,1)S(1)} %get-tuple-element.223), channel_id=1, source_target_pairs={{0,8},{1,9},{2,10},{3,11},{4,12},{5,13},{6,14},{7,15},{8,0},{9,1},... | collective-permute-start | bytes 1572872 | tf_op jit(solution)/shard_map/ppermute | solution.py:38
  271.4 41.1 %collective-permute-start.58 = (bf16[2,128,1024]{2,1,0:T(8,128)(2,1)S(1)}, bf16[2,128,1024]{2,1,0:T(8,128)(2,1)S(1)}, u32[]{:S(2)}, u32[]{:S(2)}) collective-permute-start(bf16[2,128,1024]{2,1,0:T(8,128)(2,1)S(1)} %get-tuple-element.224), channel_id=1, source_target_pairs={{0,16},{1,17},{2,18},{3,19},{4,20},{5,21},{6,22},{7,23},{8,24},{9,... | collective-permute-start | bytes 1572872 | tf_op jit(solution)/shard_map/ppermute | solution.py:38
  272.6 39.9 %collective-permute-start.59 = (bf16[2,128,1024]{2,1,0:T(8,128)(2,1)S(1)}, bf16[2,128,1024]{2,1,0:T(8,128)(2,1)S(1)}, u32[]{:S(2)}, u32[]{:S(2)}) collective-permute-start(bf16[2,128,1024]{2,1,0:T(8,128)(2,1)S(1)} %get-tuple-element.225), channel_id=1, source_target_pairs={{0,24},{1,25},{2,26},{3,27},{4,28},{5,29},{6,30},{7,31},{8,16},{9,... | collective-permute-start | bytes 1572872 | tf_op jit(solution)/shard_map/ppermute | solution.py:38
  277.9 13.1 %collective-permute-start.68 = (bf16[1,32,1024]{2,1,0:T(8,128)(2,1)S(1)}, bf16[1,32,1024]{2,1,0:T(8,128)(2,1)S(1)}, u32[]{:S(2)}, u32[]{:S(2)}) collective-permute-start(bf16[1,32,1024]{2,1,0:T(8,128)(2,1)S(1)} %get-tuple-element.221.refs_7_), channel_id=1, source_target_pairs={{0,6},{1,7},{2,4},{3,5},{4,2},{5,3},{6,0},{7,1},{8,14},{9,15},{10,... | collective-permute-start | bytes 196616 | tf_op jit(solution)/shard_map/ppermute | solution.py:38
  284.9 12.0 %collective-permute-start.63 = (bf16[2,32,1024]{2,1,0:T(8,128)(2,1)S(1)}, bf16[2,32,1024]{2,1,0:T(8,128)(2,1)S(1)}, u32[]{:S(2)}, u32[]{:S(2)}) collective-permute-start(bf16[2,32,1024]{2,1,0:T(8,128)(2,1)S(1)} %get-tuple-element.227), channel_id=1, source_target_pairs={{0,2},{1,3},{2,0},{3,1},{4,6},{5,7},{6,4},{7,5},{8,10},{9,11},{10,... | collective-permute-start | bytes 393224 | tf_op jit(solution)/shard_map/ppermute | solution.py:38
  292.3 13.2 %collective-permute-start.64 = (bf16[2,32,1024]{2,1,0:T(8,128)(2,1)S(1)}, bf16[2,32,1024]{2,1,0:T(8,128)(2,1)S(1)}, u32[]{:S(2)}, u32[]{:S(2)}) collective-permute-start(bf16[2,32,1024]{2,1,0:T(8,128)(2,1)S(1)} %get-tuple-element.228), channel_id=1, source_target_pairs={{0,4},{1,5},{2,6},{3,7},{4,0},{5,1},{6,2},{7,3},{8,12},{9,13},{10,... | collective-permute-start | bytes 393224 | tf_op jit(solution)/shard_map/ppermute | solution.py:38
  296.9 11.4 %collective-permute-start.65 = (bf16[2,32,1024]{2,1,0:T(8,128)(2,1)S(1)}, bf16[2,32,1024]{2,1,0:T(8,128)(2,1)S(1)}, u32[]{:S(2)}, u32[]{:S(2)}) collective-permute-start(bf16[2,32,1024]{2,1,0:T(8,128)(2,1)S(1)} %get-tuple-element.229), channel_id=1, source_target_pairs={{0,6},{1,7},{2,4},{3,5},{4,2},{5,3},{6,0},{7,1},{8,14},{9,15},{10,... | collective-permute-start | bytes 393224 | tf_op jit(solution)/shard_map/ppermute | solution.py:38
  305.5 13.0 %collective-permute-start.76 = (f32[16,1024]{1,0:T(8,128)S(1)}, f32[16,1024]{1,0:T(8,128)S(1)}, u32[]{:S(2)}, u32[]{:S(2)}) collective-permute-start(f32[16,1024]{1,0:T(8,128)S(1)} %add.5.refs_0_), channel_id=1, source_target_pairs={{0,8},{1,9},{2,10},{3,11},{4,12},{5,13},{6,14},{7,15},{8,0},{9,1},... | collective-permute-start | bytes 196616 | tf_op jit(solution)/shard_map/ppermute | solution.py:38
  308.3 10.2 %collective-permute-start.77 = (f32[16,1024]{1,0:T(8,128)S(1)}, f32[16,1024]{1,0:T(8,128)S(1)}, u32[]{:S(2)}, u32[]{:S(2)}) collective-permute-start(f32[16,1024]{1,0:T(8,128)S(1)} %add.5.refs_0_), channel_id=1, source_target_pairs={{0,16},{1,17},{2,18},{3,19},{4,20},{5,21},{6,22},{7,23},{8,24},{9,... | collective-permute-start | bytes 196616 | tf_op jit(solution)/shard_map/ppermute | solution.py:38
  314.6 15.9 %collective-permute-start.69 = (bf16[2,32,1024]{2,1,0:T(8,128)(2,1)S(1)}, bf16[2,32,1024]{2,1,0:T(8,128)(2,1)S(1)}, u32[]{:S(2)}, u32[]{:S(2)}) collective-permute-start(bf16[2,32,1024]{2,1,0:T(8,128)(2,1)S(1)} %get-tuple-element.232.refs_5_), channel_id=1, source_target_pairs={{0,2},{1,3},{2,0},{3,1},{4,6},{5,7},{6,4},{7,5},{8,10},{9,11},{10,... | collective-permute-start | bytes 393224 | tf_op jit(solution)/shard_map/ppermute | solution.py:38
  314.6 15.8 %collective-permute-start.70 = (bf16[2,32,1024]{2,1,0:T(8,128)(2,1)S(1)}, bf16[2,32,1024]{2,1,0:T(8,128)(2,1)S(1)}, u32[]{:S(2)}, u32[]{:S(2)}) collective-permute-start(bf16[2,32,1024]{2,1,0:T(8,128)(2,1)S(1)} %get-tuple-element.233.refs_6_), channel_id=1, source_target_pairs={{0,4},{1,5},{2,6},{3,7},{4,0},{5,1},{6,2},{7,3},{8,12},{9,13},{10,... | collective-permute-start | bytes 393224 | tf_op jit(solution)/shard_map/ppermute | solution.py:38
  318.5 14.8 %collective-permute-start.71 = (bf16[2,32,1024]{2,1,0:T(8,128)(2,1)S(1)}, bf16[2,32,1024]{2,1,0:T(8,128)(2,1)S(1)}, u32[]{:S(2)}, u32[]{:S(2)}) collective-permute-start(bf16[2,32,1024]{2,1,0:T(8,128)(2,1)S(1)} %get-tuple-element.234.refs_7_), channel_id=1, source_target_pairs={{0,6},{1,7},{2,4},{3,5},{4,2},{5,3},{6,0},{7,1},{8,14},{9,15},{10,... | collective-permute-start | bytes 393224 | tf_op jit(solution)/shard_map/ppermute | solution.py:38
  320.1 14.5 %collective-permute-start.80 = (f32[16,1024]{1,0:T(8,128)S(1)}, f32[16,1024]{1,0:T(8,128)S(1)}, u32[]{:S(2)}, u32[]{:S(2)}) collective-permute-start(f32[16,1024]{1,0:T(8,128)S(1)} %shard_map.300.refs_0_), channel_id=1, source_target_pairs={{0,4},{1,5},{2,6},{3,7},{4,0},{5,1},{6,2},{7,3},{8,12},{9,13},{10,... | collective-permute-start | bytes 196616 | tf_op jit(solution)/shard_map/ppermute | solution.py:38
  (119 other events, 751.7 us)
Sparse Core Ops, SparseCore 0:
  70.8 46.1 all-gather.1
  192.1 55.0 reduce-scatter.1

commit v3 on v2

--- a/solution.py
+++ b/solution.py
@@ -14,7 +14,6 @@
 MIB = 1024 * 1024
 COST = 1024
 IN_VMEM = pl.BlockSpec(memory_space=pltpu.VMEM)
-ANYWHERE = pl.BlockSpec(memory_space=pl.ANY)
 IN_HBM = pl.BlockSpec(memory_space=pltpu.HBM)
 
 
@@ -59,10 +58,12 @@
     return send(block, lambda b, s: (b, s ^ (2 * k)))
 
 
-def fuse(body, outs, *args, after=(), limit=16, flops=0, plain=False, fetch=False):
+def fuse(body, outs, *args, after=(), limit=16, plain=False, fetch=False, token=False):
     if plain:
-        return tuple(body(*args))
+        return tuple(body(*args)) + (None,) * token
+    after = [x for x in after if x is not None]
     count, held = len(args), len(args) + len(after)
+    outs = [*outs, ((SUBS, LANES), FULL)] if token else outs
 
     def kernel(*refs):
         taken = refs[:count]
@@ -76,13 +77,16 @@
             for copy in copies:
                 copy.wait()
         results = body(*[ref[...] for ref in taken])
+        if token:
+            results = [*results, jnp.zeros((SUBS, LANES), FULL)]
         for ref, value in zip(refs[held : held + len(outs)], results, strict=True):
             ref[...] = value
+
 
     return pl.pallas_call(
         kernel,
         out_shape=tuple(jax.ShapeDtypeStruct(shape, dtype) for shape, dtype in outs),
-        in_specs=[IN_HBM if fetch else IN_VMEM] * count + [ANYWHERE] * len(after),
+        in_specs=[IN_HBM if fetch else IN_VMEM] * count + [IN_VMEM] * len(after),
         out_specs=(IN_VMEM,) * len(outs),
         scratch_shapes=[pltpu.VMEM(x.shape, x.dtype) for x in args]
         + [pltpu.SemaphoreType.DMA((count,))]
@@ -371,13 +375,17 @@
     return body
 
 
-def carry_exchange(values, vectors, length, forward, plain, after=()):
+def carry_start(values, vectors, length, forward, plain):
     cols = lax.axis_size("seq")
     count = 4 if forward else 2
-    width = values.shape[1]
     other = to_core(values)
     (chip,) = fuse(
-        chip_sums(count, length, forward), [((SUBS, width), FULL)], values, other, vectors, plain=plain
+        chip_sums(count, length, forward),
+        [((SUBS, values.shape[1]), FULL)],
+        values,
+        other,
+        vectors,
+        plain=plain,
     )
     step = 1 if forward else -1
 
@@ -388,49 +396,103 @@
 
         return go
 
-    got = [send(chip, route(k)) for k in range(1, cols // 2)]
+    return chip, [values, other, vectors] + [send(chip, route(k)) for k in range(1, cols // 2)]
+
+
+def carry_end(parts, length, forward, plain, after=()):
+    count = 4 if forward else 2
     return fuse(
         carried(count, length, forward),
-        [((count, width // LANES, LANES), FULL)],
-        values,
-        other,
-        vectors,
-        *got,
+        [((count, parts[0].shape[1] // LANES, LANES), FULL)],
+        *parts,
         after=after,
         plain=plain,
     )[0]
 
 
-def add_batch(own, got, plain, after=()):
-    count, height, width = own.shape
+def split_parts(x):
+    high = x.astype(LOW)
+    return [high, (x - high.astype(FULL)).astype(LOW)]
+
+
+def add_batch(own, got, count, plain, after=(), vectors=None):
     depth = lax.axis_size("seq") // 2
-    part = height // depth
+    height, width = own.shape
+    extra = 32 if vectors is not None else 0
+    height -= extra
+    part = height // (count * depth)
+    inputs = [own, *got] + ([vectors] if extra else [])
 
     def body(own, *got):
-        total = sum((x.astype(FULL) for x in got), own.astype(FULL))
-        return [total[:, :part]] + [
-            total[:, k * part : (k + 1) * part].astype(LOW) for k in range(1, depth)
+        got, sums = (got[:-1], got[-1]) if extra else (got, None)
+        got = [x.astype(FULL) for x in got]
+        total = sum((x[:height] for x in got), own[:height].astype(FULL))
+        blocks = [
+            [total[(i * depth + k) * part : (i * depth + k + 1) * part] for i in range(count)]
+            for k in range(depth)
         ]
+        first, rest = blocks[0], [[x.astype(LOW) for x in block] for block in blocks[1:]]
+        if extra:
+            sums = sum((x[height : height + 16] + x[height + 16 :] for x in got), sums)
+            first, rest = first + [sums], [block + split_parts(sums) for block in rest]
+        return [jnp.concatenate(x, axis=0) for x in [first, *rest]]
 
     return fuse(
         body,
-        [((count, part, width), FULL)] + [((count, part, width), LOW)] * (depth - 1),
-        own,
-        *got,
+        [((count * part + extra // 2, width), FULL)]
+        + [((count * part + extra, width), LOW)] * (depth - 1),
+        *inputs,
         after=after,
         plain=plain,
-    )
-
-
-def add_depth(pieces, plain, after=()):
-    count, part, width = pieces[0].shape
+        token=True,
+    )
+
+
+def add_depth(pieces, count, part, outs, last, plain, after=()):
+    width = pieces[0].shape[1]
+    height = count * part
     got = [to_depth(pieces[k], k) for k in range(1, len(pieces))]
 
     def body(own, *got):
-        total = sum((x.astype(FULL) for x in got), own)
-        return [total[i] for i in range(count)]
-
-    return fuse(body, [((part, width), FULL)] * count, pieces[0], *got, after=after, plain=plain)
+        got = [x.astype(FULL) for x in got]
+        total = sum((x[:height] for x in got), own[:height])
+        results = [total[i * part : (i + 1) * part] for i in range(count)]
+        if last is not None:
+            sums = sum((x[height : height + 16] + x[height + 16 :] for x in got), own[height:])
+            results += last(sums)
+        return results
+
+    return fuse(
+        body, [((part, width), FULL)] * count + outs, pieces[0], *got, after=after, plain=plain
+    )
+
+
+def halve_depth(pieces, plain):
+    half = len(pieces) // 2
+    height, width = pieces[0].shape
+    joined = fuse(
+        lambda *x: (jnp.concatenate(x, axis=0),),
+        [((half * height, width), LOW)],
+        *pieces[half:],
+        plain=plain,
+    )[0]
+    got = to_depth(joined, half)
+
+    def body(own, *rest):
+        rest, got = rest[:-1], rest[-1].astype(FULL)
+        blocks = [got[i * height : (i + 1) * height] for i in range(half)]
+        return [own + blocks[0]] + [
+            (x.astype(FULL) + y).astype(LOW) for x, y in zip(rest, blocks[1:], strict=True)
+        ]
+
+    return fuse(
+        body,
+        [((height, width), FULL)] + [((height, width), LOW)] * (half - 1),
+        *pieces[:half],
+        got,
+        plain=plain,
+        token=True,
+    )
 
 
 def per_device(
@@ -509,6 +571,7 @@
         *small,
         plain=plain,
         fetch=True,
+        limit=58,
     )
     deep_got = [to_depth(first_pack, k) for k in range(1, depth)]
     cross_got = [to_batch(crossing[k], k) for k in range(1, rows)]
@@ -555,7 +618,6 @@
         edge,
         ids_lanes,
         plain=plain,
-        flops=mac,
     )
 
     first_deep, second_pack = fuse(
@@ -700,30 +762,27 @@
         *first_pieces,
         plain=plain,
         limit=32,
-        flops=2 * mac,
-    )
-    carry = carry_exchange(message, vectors, length, True, plain)
-    mixes_got = to_core(mixes)
+    )
+    carry = carry_end(carry_start(message, vectors, length, True, plain)[1], length, True, plain)
 
     def receptance(mixes, *pieces):
-        recept_all, output_all = gathered(pieces, 0), gathered(pieces, own)
-        return jax.nn.sigmoid(dot(mixes[2], recept_all)), jnp.stack([recept_all, output_all])
-
-    recept_act, second_all = fuse(
+        recept_all = gathered(pieces, 0)
+        return jax.nn.sigmoid(dot(mixes[2], recept_all)), recept_all, gathered(pieces, own)
+
+    recept_act, recept_all, output_all = fuse(
         receptance,
-        [full_act, ((2, width, width), LOW)],
+        [full_act, square, square],
         mixes,
-        *joined(second_deep, second_wide, (message,)),
+        *joined(second_deep, second_wide, (carry,)),
         plain=plain,
         limit=32,
-        flops=mac,
     )
     key_tiles, value_tiles = to_tiles(key_act), to_tiles(value_act)
     scanned = run_forward(keep, key_tiles, value_tiles, rates, carry)
 
-    def attend(scanned, recept, order, second_all, raw, vectors):
+    def attend(scanned, recept, order, output_all, raw, vectors):
         gated = dot((recept * untile(scanned[0], width // LANES)).astype(LOW), order).astype(LOW)
-        middle = raw.astype(FULL) + dot(gated, second_all[1])
+        middle = raw.astype(FULL) + dot(gated, output_all)
         unit, scale = unit_norm(middle)
         normed = unit * vectors[1:2] + vectors[3:4]
         return (
@@ -739,11 +798,10 @@
         scanned,
         recept_act,
         order,
-        second_all,
+        output_all,
         raw,
         vectors,
         plain=plain,
-        flops=2 * mac,
     )
     edge_two = send_next(edge_two)
 
@@ -780,24 +838,25 @@
             part_key,
             part_value,
             plain=plain,
-            flops=2 * mac,
         )
         squares.append(squared)
         returned.append(to_batch(out, k) if k else out)
 
-    def gating(mix, order, *pieces):
+    def gating(mix, order, gated, mixes, *pieces):
         gate_all = gathered(pieces, 0)
         mix = dot(mix, order).astype(LOW)
-        return jax.nn.sigmoid(dot(mix, gate_all)), mix, gate_all
-
-    gate, mix_gate, gate_all = fuse(
+        sides = jnp.stack([mixes[0], mixes[1], mixes[2], gated, mix])
+        return jax.nn.sigmoid(dot(mix, gate_all)), sides, gate_all
+
+    gate, sides, gate_all = fuse(
         gating,
-        [full_act, low_act, square],
+        [full_act, ((5, length, width), LOW), square],
         mix_gate,
         order,
-        *joined(third_deep, third_wide, (gated,)),
-        plain=plain,
-        flops=2 * mac,
+        gated,
+        mixes,
+        *joined(third_deep, third_wide, (edge_two,)),
+        plain=plain,
     )
 
     def finish(own_part, gate, middle, grad_out, *got):
@@ -831,21 +890,150 @@
         hidden, out = channel_back(grad, squared, key, value)
         return hidden, out.astype(LOW)
 
-    hiddens, returned = [], []
-    for k in range(rows):
+    def channel_back_own(grad, squared, key, value, grad_gate, gate_all, order):
+        hidden, out = channel_back(grad, squared, key, value)
+        return hidden, out, restore(dot_back(grad_gate, gate_all), order)
+
+    hidden, out, grad_mix_gate = fuse(
+        channel_back_own,
+        [hidden_act, full_act, full_act],
+        shared_grad[0],
+        squares[0],
+        part_key,
+        part_value,
+        grad_gate,
+        gate_all,
+        order,
+        plain=plain,
+    )
+    hiddens, returned = [hidden], [out]
+    for k in range(1, rows):
         hidden, out = fuse(
-            channel_back_low if k else channel_back,
-            [hidden_act, low_act if k else full_act],
+            channel_back_low,
+            [hidden_act, low_act],
             shared_grad[k],
             squares[k],
             part_key,
             part_value,
             plain=plain,
-            flops=2 * mac,
         )
         hiddens.append(hidden)
-        returned.append(to_batch(out, k) if k else out)
-
+        returned.append(to_batch(out, k))
+
+    def paired(active, active_got, grad, grad_got):
+        return dot_rows(
+            jnp.concatenate([active[:, :half], active_got[:, half:]], axis=0),
+            jnp.concatenate([grad, grad_got], axis=0),
+        ).astype(LOW)
+
+    def cut(terms, *more):
+        part = half // rows
+        return [
+            jnp.concatenate([term[k * part : (k + 1) * part] for term in terms] + list(more), axis=0)
+            for k in range(rows)
+        ]
+
+    def early_terms(sides, sides_got, grads, grads_got):
+        return cut(
+            [
+                paired(sides[side], sides_got[side], grads[i], grads_got[i])
+                for i, side in enumerate((3, 2, 4))
+            ]
+        )
+
+    sides_got = to_core(sides)
+
+    def unmix_two(own_part, grad_gate, difference, statics, vectors, *got):
+        grad_hidden = sum((x.astype(FULL) for x in got), own_part)
+        mix_h, mix_g = vectors[7:8], vectors[8:9]
+        passed = (grad_hidden * (1.0 - mix_h) + grad_gate * (1.0 - mix_g)) * statics[:, :1]
+        return (
+            grad_hidden * mix_h + grad_gate * mix_g,
+            passed,
+            stack_rows([passed[0:1]]),
+            stack_rows([column_sum(grad_hidden * difference), column_sum(grad_gate * difference)]),
+        )
+
+    own_two, passed_two, after_two, mix_sums_two = fuse(
+        unmix_two,
+        [full_act, full_act, edge_row, edge_row],
+        returned[0],
+        grad_mix_gate,
+        difference_two,
+        statics,
+        vectors,
+        *returned[1:],
+        plain=plain,
+    )
+    after_two = send_back(after_two)
+
+    def middle_back(
+        own_part, passed, after, unit, grad_out, vectors, mix_sums, recept, scanned,
+        output_all, order, statics, edges, grad_gate,
+    ):
+        wkv, inverse, slope = (untile(scanned[i], width // LANES) for i in range(3))
+        unit, scale = unit[:, :width], unit[:, width : width + 1]
+        grad_normed = own_part + up(passed, after[0:1], plain)
+        part = norm_backward(grad_normed, unit, scale, vectors[1:2])
+        grad_middle = grad_out.astype(FULL) + part
+        grad_low = grad_middle.astype(LOW)
+        grad_gated = restore(dot_back(grad_low, output_all), order)
+        grad_wkv = grad_gated * recept
+        grad_recept = (grad_wkv * wkv * (1.0 - recept)).astype(LOW)
+        share = grad_wkv * inverse
+        pace = jnp.exp(vectors[9:10])
+        step = row_index((length, width)).astype(FULL)
+        head = jnp.where(statics[:, LANES : LANES + 1] > 0.5, share * jnp.exp(-pace * step), 0.0)
+        return (
+            grad_middle,
+            jnp.stack([grad_low, grad_recept, grad_gate]),
+            share,
+            stack_rows([column_sum(head), column_sum(head * wkv), edges[1:2], edges[2:3]]),
+            stack_rows(
+                [
+                    column_sum(grad_normed * unit),
+                    column_sum(grad_normed),
+                    mix_sums[0:1],
+                    mix_sums[1:2],
+                    -pace * column_sum(grad_wkv * slope),
+                ]
+            ),
+        )
+
+    grad_middle, grad_three, share, message, sums_two = fuse(
+        middle_back,
+        [full_act, ((3, length, width), LOW), full_act, edge_row, edge_row],
+        own_two,
+        passed_two,
+        after_two,
+        unit_two,
+        cotangent,
+        vectors,
+        mix_sums_two,
+        recept_act,
+        scanned,
+        output_all,
+        order,
+        statics,
+        edges,
+        grad_gate,
+        plain=plain,
+        limit=24,
+    )
+
+    chip_back, carry_parts = carry_start(message, vectors, length, False, plain)
+
+    *early, early_token = fuse(
+        early_terms,
+        [((3 * half // rows, width), LOW)] * rows,
+        sides,
+        sides_got,
+        grad_three,
+        to_core(grad_three),
+        after=(chip_back,),
+        plain=plain,
+        token=True,
+    )
     def channel_terms(*x):
         shared, hiddens, squares, grads = (
             jnp.concatenate(x[i * rows : (i + 1) * rows], axis=0) for i in range(4)
@@ -863,161 +1051,20 @@
             ]
         return (jnp.concatenate(parts, axis=0),)
 
-    (channel_term,) = fuse(
+    channel_term, channel_token = fuse(
         channel_terms,
         [((cols * packed_rows, width), LOW)],
         *shared,
         *hiddens,
         *squares,
         *shared_grad,
-        after=returned[1:],
-        plain=plain,
+        after=(early_token,),
+        plain=plain,
+        token=True,
         limit=32,
-        flops=2 * rows * mac,
     )
     channel_sum = lax.psum_scatter(channel_term, "seq", scatter_dimension=0, tiled=True)
-
-    def gating_back(grad, gate_all, order):
-        return (restore(dot_back(grad, gate_all), order),)
-
-    (grad_mix_gate,) = fuse(
-        gating_back, [full_act], grad_gate, gate_all, order, plain=plain, flops=3 * mac
-    )
-
-    def paired(active, active_got, grad, grad_got):
-        return dot_rows(
-            jnp.concatenate([active[:, :half], active_got[:, half:]], axis=0),
-            jnp.concatenate([grad, grad_got], axis=0),
-        ).astype(LOW)
-
-    def cut(terms):
-        part = half // rows
-        return [
-            jnp.stack([term[k * part : (k + 1) * part] for term in terms]) for k in range(rows)
-        ]
-
-    def gate_terms(mix_gate, mix_gate_got, grad_gate, grad_gate_got):
-        return cut([paired(mix_gate, mix_gate_got, grad_gate, grad_gate_got)])
-
-    def early_terms(gated, gated_got, mixes, mixes_got, grads, grads_got):
-        return cut(
-            [
-                paired(gated, gated_got, grads[0], grads_got[0]),
-                paired(mixes[2], mixes_got[2], grads[1], grads_got[1]),
-            ]
-        )
-
-    mix_gate_got, grad_gate_got = to_core(mix_gate), to_core(grad_gate)
-    gated_got = to_core(gated)
-    gate_term = fuse(
-        gate_terms,
-        [((1, half // rows, width), LOW)] * rows,
-        mix_gate,
-        mix_gate_got,
-        grad_gate,
-        grad_gate_got,
-        after=returned[1:],
-        plain=plain,
-        flops=mac,
-    )
-    gate_got = [to_batch(gate_term[k], k) for k in range(1, rows)]
-    gate_pieces = add_batch(gate_term[0], gate_got, plain)
-
-    def unmix_two(own_part, grad_gate, difference, statics, vectors, *got):
-        grad_hidden = sum((x.astype(FULL) for x in got), own_part)
-        mix_h, mix_g = vectors[7:8], vectors[8:9]
-        passed = (grad_hidden * (1.0 - mix_h) + grad_gate * (1.0 - mix_g)) * statics[:, :1]
-        return (
-            grad_hidden * mix_h + grad_gate * mix_g,
-            passed,
-            stack_rows([passed[0:1]]),
-            stack_rows([column_sum(grad_hidden * difference), column_sum(grad_gate * difference)]),
-        )
-
-    own_two, passed_two, after_two, mix_sums_two = fuse(
-        unmix_two,
-        [full_act, full_act, edge_row, edge_row],
-        returned[0],
-        grad_mix_gate,
-        difference_two,
-        statics,
-        vectors,
-        *returned[1:],
-        plain=plain,
-    )
-    after_two = send_back(after_two)
-
-    def middle_back(
-        own_part, passed, after, unit, grad_out, vectors, mix_sums, recept, scanned,
-        second_all, order, statics, edges,
-    ):
-        wkv, inverse, slope = (untile(scanned[i], width // LANES) for i in range(3))
-        unit, scale = unit[:, :width], unit[:, width : width + 1]
-        grad_normed = own_part + up(passed, after[0:1], plain)
-        part = norm_backward(grad_normed, unit, scale, vectors[1:2])
-        grad_middle = grad_out.astype(FULL) + part
-        grad_low = grad_middle.astype(LOW)
-        grad_gated = restore(dot_back(grad_low, second_all[1]), order)
-        grad_wkv = grad_gated * recept
-        grad_recept = (grad_wkv * wkv * (1.0 - recept)).astype(LOW)
-        share = grad_wkv * inverse
-        pace = jnp.exp(vectors[9:10])
-        step = row_index((length, width)).astype(FULL)
-        head = jnp.where(statics[:, LANES : LANES + 1] > 0.5, share * jnp.exp(-pace * step), 0.0)
-        return (
-            grad_middle,
-            jnp.stack([grad_low, grad_recept]),
-            share,
-            stack_rows([column_sum(head), column_sum(head * wkv), edges[1:2], edges[2:3]]),
-            stack_rows(
-                [
-                    column_sum(grad_normed * unit),
-                    column_sum(grad_normed),
-                    mix_sums[0:1],
-                    mix_sums[1:2],
-                    -pace * column_sum(grad_wkv * slope),
-                ]
-            ),
-        )
-
-    grad_middle, grad_pair, share, message, sums_two = fuse(
-        middle_back,
-        [full_act, ((2, length, width), LOW), full_act, edge_row, edge_row],
-        own_two,
-        passed_two,
-        after_two,
-        unit_two,
-        cotangent,
-        vectors,
-        mix_sums_two,
-        recept_act,
-        scanned,
-        second_all,
-        order,
-        statics,
-        edges,
-        after=(channel_term, gate_term[0]),
-        plain=plain,
-        limit=24,
-        flops=3 * mac,
-    )
-
-    early = fuse(
-        early_terms,
-        [((2, half // rows, width), LOW)] * rows,
-        gated,
-        gated_got,
-        mixes,
-        mixes_got,
-        grad_pair,
-        to_core(grad_pair),
-        plain=plain,
-        limit=24,
-        flops=2 * mac,
-    )
-    early_got = [to_batch(early[k], k) for k in range(1, rows)]
-
-    carry_back = carry_exchange(message, vectors, length, False, plain, after=early)
+    carry_back = carry_end(carry_parts, length, False, plain, (channel_token, early_token))
     grad_key, grad_value, first_term = run_backward(
         keep, key_tiles, value_tiles, scanned, to_tiles(share), rates, carry_back
     )
@@ -1032,32 +1079,11 @@
         plain=plain,
     )
 
-    def late_terms(mixes, mixes_got, grads, grads_got):
-        return cut([paired(mixes[i], mixes_got[i], grads[i], grads_got[i]) for i in range(2)])
-
-    late = fuse(
-        late_terms,
-        [((2, half // rows, width), LOW)] * rows,
-        mixes,
-        mixes_got,
-        grad_late,
-        to_core(grad_late),
-        after=gate_pieces,
-        plain=plain,
-        flops=2 * mac,
-    )
-    late_got = [to_batch(late[k], k) for k in range(1, rows)]
-    early_pieces = add_batch(early[0], early_got, plain)
-    output_grad, recept_grad = add_depth(early_pieces, plain)
-    (gate_grad,) = add_depth(gate_pieces, plain)
-    late_pieces = add_batch(late[0], late_got, plain, (output_grad, gate_grad))
-    key_grad, value_grad = add_depth(late_pieces, plain)
-
-    def unmix_one(grads, grad_pair, first_all, second_all, vectors, statics, difference, order):
+    def unmix_one(grads, grad_three, first_all, recept_all, vectors, statics, difference, order):
         lines = vectors[16:]
         grad_key = dot_back(grads[0], first_all[0])
         grad_value = dot_back(grads[1], first_all[1])
-        grad_recept = dot_back(grad_pair[1], second_all[0])
+        grad_recept = dot_back(grad_three[1], recept_all)
         m_key, m_value, m_recept = lines[4:5], lines[5:6], lines[6:7]
         passed = (
             grad_key * (1.0 - m_key) + grad_value * (1.0 - m_value) + grad_recept * (1.0 - m_recept)
@@ -1073,16 +1099,15 @@
         unmix_one,
         [full_act, full_act, edge_row, edge_row],
         grad_late,
-        grad_pair,
+        grad_three,
         first_all,
-        second_all,
+        recept_all,
         vectors,
         statics,
         difference_one,
         order,
         plain=plain,
         limit=24,
-        flops=3 * mac,
     )
     after_one = send_back(after_one)
 
@@ -1125,49 +1150,56 @@
         first_term,
         plain=plain,
         limit=24,
-        flops=2 * mac,
     )
     sums = sums + to_core(sums)
-    (sums,) = fuse(
-        lambda *x: (sum(x[1:], x[0]),),
-        [((16, width), FULL)],
+    early_got = [to_batch(early[k], k) for k in range(1, rows)]
+    *early_pieces, early_wide_token = add_batch(early[0], early_got, 3, plain, (sums,))
+    early_half = None
+    if depth == 4:
+        *early_pieces, early_half = halve_depth(early_pieces, plain)
+
+    def late_terms(sides, sides_got, grads, grads_got, sums):
+        terms = [paired(sides[i], sides_got[i], grads[i], grads_got[i]) for i in range(2)]
+        return cut(terms, *split_parts(sums))
+
+    late = fuse(
+        late_terms,
+        [((2 * half // rows + 32, width), LOW)] * rows,
+        sides,
+        sides_got,
+        grad_late,
+        to_core(grad_late),
         sums,
-        *[to_batch(sums, k) for k in range(1, rows)],
-        after=late_pieces,
-        plain=plain,
-    )
-
-    def own_columns(*got):
+        after=(early_wide_token,),
+        plain=plain,
+    )
+    late_got = [to_batch(late[k], k) for k in range(1, rows)]
+    def own_columns(total):
         b, z, core = places()
-        total = sum(got[1:], got[0])
         device = b * cols + z * 2 + core
         if plain:
             total = lax.dynamic_slice(total, (0, device * own), (16, own))
         else:
             total = pltpu.roll(total, (width - device * own) & (width - 1), 1)[:, :own]
-        return total[0:2], total[2:4], total[4:9], total[9:10], total[10:11]
-
-    gains_grad, offsets_grad, mixes_grad, decay_grad, first_grad = fuse(
+        return [total[0:2], total[2:4], total[4:9], total[9:10], total[10:11]]
+
+    *late_pieces, _ = add_batch(late[0], late_got, 2, plain, (early_half,), vectors=sums)
+    output_grad, recept_grad, gate_grad = add_depth(early_pieces, 3, own, [], None, plain)
+    key_grad, value_grad, gains_grad, offsets_grad, mixes_grad, decay_grad, first_grad = add_depth(
+        late_pieces,
+        2,
+        own,
+        [((2, own), FULL), ((2, own), FULL), ((5, own), FULL), ((1, own), FULL), ((1, own), FULL)],
         own_columns,
-        [((2, own), FULL), ((2, own), FULL), ((5, own), FULL), ((1, own), FULL), ((1, own), FULL)],
-        sums,
-        *[to_depth(sums, k) for k in range(1, depth)],
-        after=(key_grad,),
-        plain=plain,
-    )
-
-    def uncross(x):
-        b = places()[0]
-        blocks = x[:cross_rows].reshape(rows, own, part_width)
-        return [pick([blocks[j] for j in range(rows)], b ^ k) for k in range(rows)]
-
-    leaving = fuse(uncross, [((own, part_width), LOW)] * rows, channel_sum, plain=plain)
-
-    def assemble(x, *blocks):
-        b = places()[0]
-        blocks = [block.astype(FULL) for block in blocks]
+        plain,
+    )
+
+    crossed = channel_sum[:cross_rows].reshape(rows, own, part_width)
+    crossed = lax.all_to_all(crossed, "batch", 0, 0)
+
+    def assemble(x, crossed):
         return (
-            jnp.concatenate([pick(blocks, j ^ b) for j in range(rows)], axis=1),
+            jnp.concatenate([crossed[j].astype(FULL) for j in range(rows)], axis=1),
             x[cross_rows:].astype(FULL),
         )
 
@@ -1175,8 +1207,7 @@
         assemble,
         [((own, hidden_width), FULL), (channel_value.shape, FULL)],
         channel_sum,
-        leaving[0],
-        *[to_batch(leaving[k], k) for k in range(1, rows)],
+        crossed,
         plain=plain,
     )
     return (

time: 350 us -> 293 us (0.84)
  starting transfers between devices: 122 us -> 93.3 us
  waiting for transfers between devices: 115 us -> 101 us
  local copies, waits for them, and re-layouts: 46.6 us -> 34.3 us
    ppermute x82 -> x63, starting transfers between devices: 122 us -> 89.9 us  [send(): return lax.ppermute(block, BOTH, pairs)]
    unnamed x166 -> x138, local copies, waits for them, and re-layouts: 46.6 us -> 32.6 us
    ppermute x82 -> x63, waiting for transfers between devices: 115 us -> 101 us  [send(): return lax.ppermute(block, BOTH, pairs)]
    pallas_call x46 -> x41, Pallas kernels: 47.9 us -> 46.4 us  [fuse(): pl.pallas_call(kernel, out_shape=tuple((jax.ShapeDtypeStruct(shape, dtype...]
  transfers between devices with their start and end apart: 84 -> 66, of which waited for: 34 -> 26; matrix products, arithmetic and copies ran while one was open for 0% -> 1% of each run, Pallas kernels for 12% -> 13%
where the time goes in v3:
time: 293 us; the launch traced here: 292 us
  waiting for transfers between devices  101 us (34%)
  starting transfers between devices  93.3 us (32%)
  Pallas kernels  47.7 us (16%)
  local copies, waits for them, and re-layouts  34.3 us (12%)
  between operations  15 us (5%)
    ppermute x63, waiting for transfers between devices, send(): return lax.ppermute(block, BOTH, pairs)  101 us
    ppermute x63, starting transfers between devices, send(): return lax.ppermute(block, BOTH, pairs)  89.9 us
    pallas_call x41, Pallas kernels, fuse(): pl.pallas_call(kernel, out_shape=tuple((jax.ShapeDtypeStruct(shape, dtype...  46.4 us
    unnamed x138, local copies, waits for them, and re-layouts  32.6 us
  transfers between devices with their start and end apart: 66, of which 26 were waited for; matrix products, arithmetic and copies ran while one was open for 1% of the time, Pallas kernels for 13%

profile of v3, /device:TPU:8, one launch (start us, length us, event | category | flops | bytes accessed | tf_op | source)
XLA Modules:
  0.0 291.6 jit_solution(3955869958033546349)
XLA Ops:
  7.2 2.3 shard_map.254
  9.7 3.0 %collective-permute-start.2 = (bf16[80,1024]{1,0:T(8,128)(2,1)}, bf16[80,1024]{1,0:T(8,128)(2,1)S(1)}, u32[]{:S(2)}, u32[]{:S(2)}) collective-permute-start(bf16[80,1024]{1,0:T(8,128)(2,1)} %get-tuple-element.138.refs_1_), channel_id=1, source_target_pairs={{0,4},{1,5},{2,6},{3,7},{4,0},{5,1},{6,2},{7,3},{8,12},{9,13},{10,... | collective-permute-start | bytes 491528 | tf_op jit(solution)/shard_map/ppermute | solution.py:37
  13.2 1.9 collective-permute-start
  16.6 6.5 %collective-permute-done.refs_1_ = f32[16,1024]{1,0:T(8,128)S(1)} collective-permute-done((f32[16,1024]{1,0:T(8,128)}, f32[16,1024]{1,0:T(8,128)S(1)}, u32[]{:S(2)}, u32[]{:S(2)}) %collective-permute-start) | collective-permute-done | bytes 65568 | tf_op jit(solution)/shard_map/ppermute | solution.py:37
  35.5 8.4 %collective-permute-start.19 = (bf16[96,1024]{1,0:T(8,128)(2,1)S(1)}, bf16[96,1024]{1,0:T(8,128)(2,1)S(1)}, u32[]{:S(2)}, u32[]{:S(2)}) collective-permute-start(bf16[96,1024]{1,0:T(8,128)(2,1)S(1)} %get-tuple-element.150.refs_5_), channel_id=1, source_target_pairs={{0,4},{1,5},{2,6},{3,7},{4,0},{5,1},{6,2},{7,3},{8,12},{9,13},{10,... | collective-permute-start | bytes 589832 | tf_op jit(solution)/shard_map/ppermute | solution.py:37
  44.0 5.5 %collective-permute-start.20 = (bf16[96,1024]{1,0:T(8,128)(2,1)S(1)}, bf16[96,1024]{1,0:T(8,128)(2,1)S(1)}, u32[]{:S(2)}, u32[]{:S(2)}) collective-permute-start(bf16[96,1024]{1,0:T(8,128)(2,1)S(1)} %get-tuple-element.150.refs_5_), channel_id=1, source_target_pairs={{0,6},{1,7},{2,4},{3,5},{4,2},{5,3},{6,0},{7,1},{8,14},{9,15},{10,... | collective-permute-start | bytes 589832 | tf_op jit(solution)/shard_map/ppermute | solution.py:37
  49.4 5.5 %collective-permute-done.19.refs_7_ = bf16[96,1024]{1,0:T(8,128)(2,1)S(1)} collective-permute-done((bf16[96,1024]{1,0:T(8,128)(2,1)S(1)}, bf16[96,1024]{1,0:T(8,128)(2,1)S(1)}, u32[]{:S(2)}, u32[]{:S(2)}) %collective-permute-start.19) | collective-permute-done | bytes 196640 | tf_op jit(solution)/shard_map/ppermute | solution.py:37
  54.9 3.4 %collective-permute-done.20.refs_8_ = bf16[96,1024]{1,0:T(8,128)(2,1)S(1)} collective-permute-done((bf16[96,1024]{1,0:T(8,128)(2,1)S(1)}, bf16[96,1024]{1,0:T(8,128)(2,1)S(1)}, u32[]{:S(2)}, u32[]{:S(2)}) %collective-permute-start.20) | collective-permute-done | bytes 196640 | tf_op jit(solution)/shard_map/ppermute | solution.py:37
  58.3 3.8 %collective-permute-done.9.refs_7_.refs_11_ = bf16[4,80,1024]{2,1,0:T(8,128)(2,1)S(1)} collective-permute-done((bf16[4,80,1024]{2,1,0:T(8,128)(2,1)S(1)}, bf16[4,80,1024]{2,1,0:T(8,128)(2,1)S(1)}, u32[]{:S(2)}, u32[]{:S(2)}) %collective-permute-start.9) | collective-permute-done | bytes 655392 | tf_op jit(solution)/shard_map/ppermute | solution.py:37
  65.5 2.9 %collective-permute-start.10 = (bf16[4,80,1024]{2,1,0:T(8,128)(2,1)}, bf16[4,80,1024]{2,1,0:T(8,128)(2,1)S(1)}, u32[]{:S(2)}, u32[]{:S(2)}) collective-permute-start(bf16[4,80,1024]{2,1,0:T(8,128)(2,1)} %copy-done.38), channel_id=1, source_target_pairs={{0,1},{1,0},{2,3},{3,2},{4,5},{5,4},{6,7},{7,6},{8,9},{9,8},{10,11... | collective-permute-start | bytes 1966088 | tf_op jit(solution)/shard_map/ppermute | solution.py:37
  79.3 2.0 copy-done.11
  82.7 1.9 collective-permute-start.15
  85.9 3.5 %collective-permute-done.15.refs_3_ = f32[8,1024]{1,0:T(8,128)S(1)} collective-permute-done((f32[8,1024]{1,0:T(8,128)S(1)}, f32[8,1024]{1,0:T(8,128)S(1)}, u32[]{:S(2)}, u32[]{:S(2)}) %collective-permute-start.15) | collective-permute-done | bytes 32800 | tf_op jit(solution)/shard_map/ppermute | solution.py:37
  90.3 5.8 %collective-permute-done.22.refs_2_ = bf16[4,64,1024]{2,1,0:T(8,128)(2,1)S(1)} collective-permute-done((bf16[4,64,1024]{2,1,0:T(8,128)(2,1)}, bf16[4,64,1024]{2,1,0:T(8,128)(2,1)S(1)}, u32[]{:S(2)}, u32[]{:S(2)}) %collective-permute-start.22) | collective-permute-done | bytes 524320 | tf_op jit(solution)/shard_map/ppermute | solution.py:37
  103.6 2.1 collective-permute-start.25
  105.7 5.3 %collective-permute-done.27.refs_2_ = bf16[4,32,1024]{2,1,0:T(8,128)(2,1)S(1)} collective-permute-done((bf16[4,32,1024]{2,1,0:T(8,128)(2,1)S(1)}, bf16[4,32,1024]{2,1,0:T(8,128)(2,1)S(1)}, u32[]{:S(2)}, u32[]{:S(2)}) %collective-permute-start.27) | collective-permute-done | bytes 262176 | tf_op jit(solution)/shard_map/ppermute | solution.py:37
  117.2 2.2 copy-done.10
  119.7 3.5 %collective-permute-done.30.refs_0_.refs_1_ = bf16[128,1024]{1,0:T(8,128)(2,1)} collective-permute-done((bf16[128,1024]{1,0:T(8,128)(2,1)}, bf16[128,1024]{1,0:T(8,128)(2,1)}, u32[]{:S(2)}, u32[]{:S(2)}) %collective-permute-start.30) | collective-permute-done | bytes 262176 | tf_op jit(solution)/shard_map/ppermute | solution.py:37
  126.4 3.0 %collective-permute-done.32.refs_0_.refs_2_ = bf16[128,1024]{1,0:T(8,128)(2,1)} collective-permute-done((bf16[128,1024]{1,0:T(8,128)(2,1)}, bf16[128,1024]{1,0:T(8,128)(2,1)}, u32[]{:S(2)}, u32[]{:S(2)}) %collective-permute-start.32) | collective-permute-done | bytes 262176 | tf_op jit(solution)/shard_map/ppermute | solution.py:37
  135.1 2.1 shard_map.270
  137.2 2.0 shard_map.267
  139.2 8.3 %collective-permute-done.33.refs_5_ = bf16[128,1024]{1,0:T(8,128)(2,1)S(1)} collective-permute-done((bf16[128,1024]{1,0:T(8,128)(2,1)S(1)}, bf16[128,1024]{1,0:T(8,128)(2,1)S(1)}, u32[]{:S(2)}, u32[]{:S(2)}) %collective-permute-start.33) | collective-permute-done | bytes 262176 | tf_op jit(solution)/shard_map/ppermute | solution.py:37
  148.4 1.8 collective-permute-start.38
  151.9 2.9 collective-permute-done.36.refs_0_.refs_13_
  158.0 2.4 collective-permute-start.39
  161.9 2.1 collective-permute-start.41
  164.1 3.5 %shard_map.275 = (bf16[128,1024]{1,0:T(8,128)(2,1)S(1)}, f32[128,1024]{1,0:T(8,128)S(1)}, f32[128,1024]{1,0:T(8,128)S(1)}) custom-call(bf16[128,1024]{1,0:T(8,128)(2,1)S(1)} %get-tuple-element.170.refs_0_.refs_12_, bf16[128,1024]{1,0:T(8,128)(2,1)S(1)} %get-tuple-element.171.refs_1_.refs_8_, bf16[1024,1024]{1,0:T(8,128)(2,1)S(1)} %get-tuple-element.158.refs_1_.refs_2_, ...), custom_call_target="tpu_custom_call" | custom-call | flops 1024 | bytes 1024 | tf_op jit(solution)/shard_map/pallas_call | solution.py:86
  167.7 2.7 collective-permute-done.39.refs_6_
  171.0 2.1 collective-permute-start.42
  174.5 2.6 shard_map.280
  177.7 1.8 collective-permute-done.43.refs_1_
  184.2 3.6 %shard_map.283 = (bf16[2048,1024]{1,0:T(8,128)(2,1)S(1)}, f32[8,128]{1,0:T(8,128)S(1)}) custom-call(bf16[128,1024]{1,0:T(8,128)(2,1)} %get-tuple-element.156.refs_0_, bf16[128,1024]{1,0:T(8,128)(2,1)} %collective-permute-done.30.refs_0_.refs_1_, bf16[128,1024]{1,0:T(8,128)(2,1)} %collective-permute-done.32.refs_0_.refs_2_, ...), custom_call_target="tpu_custom_call" | custom-call | flops 1024 | bytes 1024 | tf_op jit(solution)/shard_map/pallas_call | solution.py:86
  187.8 2.1 copy-done.9
  193.4 3.7 %collective-permute-start.44 = (f32[8,1024]{1,0:T(8,128)S(1)}, f32[8,1024]{1,0:T(8,128)S(1)}, u32[]{:S(2)}, u32[]{:S(2)}) collective-permute-start(f32[8,1024]{1,0:T(8,128)S(1)} %shard_map.281.refs_4_), channel_id=1, source_target_pairs={{2,0},{3,1},{4,2},{5,3},{6,4},{7,5},{10,8},{11,9},{12,10},{13,11},... | collective-permute-start | bytes 98312 | tf_op jit(solution)/shard_map/ppermute | solution.py:37
  198.4 2.0 collective-permute-done.44.refs_3_
  201.0 3.5 %collective-permute-done.45.refs_4_ = f32[8,1024]{1,0:T(8,128)S(1)} collective-permute-done((f32[8,1024]{1,0:T(8,128)S(1)}, f32[8,1024]{1,0:T(8,128)S(1)}, u32[]{:S(2)}, u32[]{:S(2)}) %collective-permute-start.45) | collective-permute-done | bytes 32800 | tf_op jit(solution)/shard_map/ppermute | solution.py:37
  213.1 3.3 %shard_map.287 = (f32[128,1024]{1,0:T(8,128)S(1)}, f32[128,1024]{1,0:T(8,128)S(1)}, f32[8,1024]{1,0:T(8,128)S(1)}, f32[8,1024]{1,0:T(8,128)S(1)}) custom-call(bf16[2,128,1024]{2,1,0:T(8,128)(2,1)S(1)} %shard_map.286.refs_0_.refs_2_, bf16[3,128,1024]{2,1,0:T(8,128)(2,1)S(1)} %get-tuple-element.194.refs_2_.refs_1_, bf16[2,1024,1024]{2,1,0:T(8,128)(2,1)S(1)} %copy-done.12, ...), custom_call_target="tpu_custom_call" | custom-call | flops 1024 | bytes 1024 | tf_op jit(solution)/shard_map/pallas_call | solution.py:86
  216.5 6.9 %collective-permute-start.49 = (f32[8,1024]{1,0:T(8,128)S(1)}, f32[8,1024]{1,0:T(8,128)S(1)}, u32[]{:S(2)}, u32[]{:S(2)}) collective-permute-start(f32[8,1024]{1,0:T(8,128)S(1)} %get-tuple-element.206), channel_id=1, source_target_pairs={{1,0},{2,1},{3,2},{4,3},{5,4},{6,5},{7,6},{9,8},{10,9},{11,10},{12... | collective-permute-start | bytes 98312 | tf_op jit(solution)/shard_map/ppermute | solution.py:37
  223.4 2.1 collective-permute-done.49.refs_2_
  225.5 3.9 %shard_map.288 = (f32[128,1024]{1,0:T(8,128)}, f32[16,1024]{1,0:T(8,128)S(1)}) custom-call(f32[128,1024]{1,0:T(8,128)S(1)} %get-tuple-element.204.refs_0_, f32[128,1024]{1,0:T(8,128)S(1)} %get-tuple-element.205.refs_1_, f32[8,1024]{1,0:T(8,128)S(1)} %collective-permute-done.49.refs_2_, f32[128,1024]{1,0:T(8,128)S(1)} %copy-done.33, ...), custom_call_target="tpu_custom_call" | custom-call | flops 1024 | bytes 1024 | tf_op jit(solution)/shard_map/pallas_call | solution.py:86
  231.9 1.7 collective-permute-start.55
  235.6 18.2 %collective-permute-done.58.refs_2_ = bf16[192,1024]{1,0:T(8,128)(2,1)S(1)} collective-permute-done((bf16[192,1024]{1,0:T(8,128)(2,1)S(1)}, bf16[192,1024]{1,0:T(8,128)(2,1)S(1)}, u32[]{:S(2)}, u32[]{:S(2)}) %collective-permute-start.58) | collective-permute-done | bytes 393248 | tf_op jit(solution)/shard_map/ppermute | solution.py:37
  253.8 4.3 %collective-permute-start.62 = (bf16[96,1024]{1,0:T(8,128)(2,1)S(1)}, bf16[96,1024]{1,0:T(8,128)(2,1)S(1)}, u32[]{:S(2)}, u32[]{:S(2)}) collective-permute-start(bf16[96,1024]{1,0:T(8,128)(2,1)S(1)} %get-tuple-element.234), channel_id=1, source_target_pairs={{0,2},{1,3},{2,0},{3,1},{4,6},{5,7},{6,4},{7,5},{8,10},{9,11},{10,... | collective-permute-start | bytes 589832 | tf_op jit(solution)/shard_map/ppermute | solution.py:37
  258.1 3.3 %collective-permute-done.56.refs_2_ = bf16[288,1024]{1,0:T(8,128)(2,1)S(1)} collective-permute-done((bf16[288,1024]{1,0:T(8,128)(2,1)S(1)}, bf16[288,1024]{1,0:T(8,128)(2,1)S(1)}, u32[]{:S(2)}, u32[]{:S(2)}) %collective-permute-start.56) | collective-permute-done | bytes 589856 | tf_op jit(solution)/shard_map/ppermute | solution.py:37
  262.0 3.0 %collective-permute-start.59 = (bf16[96,1024]{1,0:T(8,128)(2,1)S(1)}, bf16[96,1024]{1,0:T(8,128)(2,1)S(1)}, u32[]{:S(2)}, u32[]{:S(2)}) collective-permute-start(bf16[96,1024]{1,0:T(8,128)(2,1)S(1)} %get-tuple-element.228), channel_id=1, source_target_pairs={{0,2},{1,3},{2,0},{3,1},{4,6},{5,7},{6,4},{7,5},{8,10},{9,11},{10,... | collective-permute-start | bytes 589832 | tf_op jit(solution)/shard_map/ppermute | solution.py:37
  268.3 3.4 %all-to-all-start = ((bf16[4,32,1024]{2,1,0:T(8,128)(2,1)}), bf16[4,32,1024]{2,1,0:T(8,128)(2,1)S(1)}, u32[]{:S(2)}, u32[]{:S(2)}) async-start(bf16[4,32,1024]{2,1,0:T(8,128)(2,1)} %bitcast.25), calls=%async_computation.1 | async-start | bytes 524288 | tf_op jit(solution)/shard_map/all_to_all | solution.py:1198
  272.5 6.4 %collective-permute-done.60.refs_2_ = bf16[96,1024]{1,0:T(8,128)(2,1)S(1)} collective-permute-done((bf16[96,1024]{1,0:T(8,128)(2,1)S(1)}, bf16[96,1024]{1,0:T(8,128)(2,1)S(1)}, u32[]{:S(2)}, u32[]{:S(2)}) %collective-permute-start.60) | collective-permute-done | bytes 196640 | tf_op jit(solution)/shard_map/ppermute | solution.py:37
  278.9 4.1 %collective-permute-done.61.refs_3_ = bf16[96,1024]{1,0:T(8,128)(2,1)S(1)} collective-permute-done((bf16[96,1024]{1,0:T(8,128)(2,1)S(1)}, bf16[96,1024]{1,0:T(8,128)(2,1)S(1)}, u32[]{:S(2)}, u32[]{:S(2)}) %collective-permute-start.61) | collective-permute-done | bytes 196640 | tf_op jit(solution)/shard_map/ppermute | solution.py:37
  (269 shorter events, 94.1 us)
Async XLA Ops:
  7.2 110.0 %all-gather.2.cloned.1.call-start = ((), (), s32[]{:S(2)}) async-start(), calls=%async_computation.2 | async-start | bytes 4718592 | tf_op jit(solution)/shard_map/all_gather | solution.py:665
  9.6 20.4 %collective-permute-start.1 = (bf16[80,1024]{1,0:T(8,128)(2,1)}, bf16[80,1024]{1,0:T(8,128)(2,1)S(1)}, u32[]{:S(2)}, u32[]{:S(2)}) collective-permute-start(bf16[80,1024]{1,0:T(8,128)(2,1)} %get-tuple-element.138.refs_1_), channel_id=1, source_target_pairs={{0,2},{1,3},{2,0},{3,1},{4,6},{5,7},{6,4},{7,5},{8,10},{9,11},{10,... | collective-permute-start | bytes 491528 | tf_op jit(solution)/shard_map/ppermute | solution.py:37
  9.7 20.4 %collective-permute-start.2 = (bf16[80,1024]{1,0:T(8,128)(2,1)}, bf16[80,1024]{1,0:T(8,128)(2,1)S(1)}, u32[]{:S(2)}, u32[]{:S(2)}) collective-permute-start(bf16[80,1024]{1,0:T(8,128)(2,1)} %get-tuple-element.138.refs_1_), channel_id=1, source_target_pairs={{0,4},{1,5},{2,6},{3,7},{4,0},{5,1},{6,2},{7,3},{8,12},{9,13},{10,... | collective-permute-start | bytes 491528 | tf_op jit(solution)/shard_map/ppermute | solution.py:37
  12.7 17.3 %collective-permute-start.3 = (bf16[80,1024]{1,0:T(8,128)(2,1)}, bf16[80,1024]{1,0:T(8,128)(2,1)S(1)}, u32[]{:S(2)}, u32[]{:S(2)}) collective-permute-start(bf16[80,1024]{1,0:T(8,128)(2,1)} %get-tuple-element.138.refs_1_), channel_id=1, source_target_pairs={{0,6},{1,7},{2,4},{3,5},{4,2},{5,3},{6,0},{7,1},{8,14},{9,15},{10,... | collective-permute-start | bytes 491528 | tf_op jit(solution)/shard_map/ppermute | solution.py:37
  13.2 10.0 %collective-permute-start = (f32[16,1024]{1,0:T(8,128)}, f32[16,1024]{1,0:T(8,128)S(1)}, u32[]{:S(2)}, u32[]{:S(2)}) collective-permute-start(f32[16,1024]{1,0:T(8,128)} %get-tuple-element.130), channel_id=1, source_target_pairs={{0,1},{1,2},{2,3},{3,4},{4,5},{5,6},{6,7},{8,9},{9,10},{10,11},{11... | collective-permute-start | bytes 196616 | tf_op jit(solution)/shard_map/ppermute | solution.py:37
  15.1 9.6 %collective-permute-start.4 = (bf16[32,1024]{1,0:T(8,128)(2,1)}, bf16[32,1024]{1,0:T(8,128)(2,1)S(1)}, u32[]{:S(2)}, u32[]{:S(2)}) collective-permute-start(bf16[32,1024]{1,0:T(8,128)(2,1)} %get-tuple-element.139), channel_id=1, source_target_pairs={{0,8},{1,9},{2,10},{3,11},{4,12},{5,13},{6,14},{7,15},{8,0},{9,1},... | collective-permute-start | bytes 196616 | tf_op jit(solution)/shard_map/ppermute | solution.py:37
  32.0 26.3 %collective-permute-start.7 = (bf16[4,80,1024]{2,1,0:T(8,128)(2,1)S(1)}, bf16[4,80,1024]{2,1,0:T(8,128)(2,1)S(1)}, u32[]{:S(2)}, u32[]{:S(2)}) collective-permute-start(bf16[4,80,1024]{2,1,0:T(8,128)(2,1)S(1)} %get-tuple-element.142.refs_4_), channel_id=1, source_target_pairs={{0,8},{1,9},{2,10},{3,11},{4,12},{5,13},{6,14},{7,15},{8,0},{9,1},... | collective-permute-start | bytes 1966088 | tf_op jit(solution)/shard_map/ppermute | solution.py:37
  33.5 24.8 %collective-permute-start.8 = (bf16[4,80,1024]{2,1,0:T(8,128)(2,1)S(1)}, bf16[4,80,1024]{2,1,0:T(8,128)(2,1)S(1)}, u32[]{:S(2)}, u32[]{:S(2)}) collective-permute-start(bf16[4,80,1024]{2,1,0:T(8,128)(2,1)S(1)} %get-tuple-element.142.refs_4_), channel_id=1, source_target_pairs={{0,16},{1,17},{2,18},{3,19},{4,20},{5,21},{6,22},{7,23},{8,24},{9,... | collective-permute-start | bytes 1966088 | tf_op jit(solution)/shard_map/ppermute | solution.py:37
  34.0 28.1 %collective-permute-start.9 = (bf16[4,80,1024]{2,1,0:T(8,128)(2,1)S(1)}, bf16[4,80,1024]{2,1,0:T(8,128)(2,1)S(1)}, u32[]{:S(2)}, u32[]{:S(2)}) collective-permute-start(bf16[4,80,1024]{2,1,0:T(8,128)(2,1)S(1)} %get-tuple-element.142.refs_4_), channel_id=1, source_target_pairs={{0,24},{1,25},{2,26},{3,27},{4,28},{5,29},{6,30},{7,31},{8,16},{9,... | collective-permute-start | bytes 1966088 | tf_op jit(solution)/shard_map/ppermute | solution.py:37
  35.5 8.4 %collective-permute-start.18 = (bf16[96,1024]{1,0:T(8,128)(2,1)S(1)}, bf16[96,1024]{1,0:T(8,128)(2,1)S(1)}, u32[]{:S(2)}, u32[]{:S(2)}) collective-permute-start(bf16[96,1024]{1,0:T(8,128)(2,1)S(1)} %get-tuple-element.150.refs_5_), channel_id=1, source_target_pairs={{0,2},{1,3},{2,0},{3,1},{4,6},{5,7},{6,4},{7,5},{8,10},{9,11},{10,... | collective-permute-start | bytes 589832 | tf_op jit(solution)/shard_map/ppermute | solution.py:37
  35.5 19.4 %collective-permute-start.19 = (bf16[96,1024]{1,0:T(8,128)(2,1)S(1)}, bf16[96,1024]{1,0:T(8,128)(2,1)S(1)}, u32[]{:S(2)}, u32[]{:S(2)}) collective-permute-start(bf16[96,1024]{1,0:T(8,128)(2,1)S(1)} %get-tuple-element.150.refs_5_), channel_id=1, source_target_pairs={{0,4},{1,5},{2,6},{3,7},{4,0},{5,1},{6,2},{7,3},{8,12},{9,13},{10,... | collective-permute-start | bytes 589832 | tf_op jit(solution)/shard_map/ppermute | solution.py:37
  44.0 14.3 %collective-permute-start.20 = (bf16[96,1024]{1,0:T(8,128)(2,1)S(1)}, bf16[96,1024]{1,0:T(8,128)(2,1)S(1)}, u32[]{:S(2)}, u32[]{:S(2)}) collective-permute-start(bf16[96,1024]{1,0:T(8,128)(2,1)S(1)} %get-tuple-element.150.refs_5_), channel_id=1, source_target_pairs={{0,6},{1,7},{2,4},{3,5},{4,2},{5,3},{6,0},{7,1},{8,14},{9,15},{10,... | collective-permute-start | bytes 589832 | tf_op jit(solution)/shard_map/ppermute | solution.py:37
  65.4 201.1 %reduce-scatter.2.cloned.1.call-start = ((), (), s32[]{:S(2)}) async-start(), calls=%async_computation.3 | async-start | bytes 4718592 | tf_op jit(solution)/shard_map/reduce_scatter | solution.py:1066
  69.0 21.3 %collective-permute-start.21 = (bf16[4,64,1024]{2,1,0:T(8,128)(2,1)}, bf16[4,64,1024]{2,1,0:T(8,128)(2,1)S(1)}, u32[]{:S(2)}, u32[]{:S(2)}) collective-permute-start(bf16[4,64,1024]{2,1,0:T(8,128)(2,1)} %copy-done.49), channel_id=1, source_target_pairs={{0,8},{1,9},{2,10},{3,11},{4,12},{5,13},{6,14},{7,15},{8,0},{9,1},... | collective-permute-start | bytes 1572872 | tf_op jit(solution)/shard_map/ppermute | solution.py:37
  70.5 25.6 %collective-permute-start.22 = (bf16[4,64,1024]{2,1,0:T(8,128)(2,1)}, bf16[4,64,1024]{2,1,0:T(8,128)(2,1)S(1)}, u32[]{:S(2)}, u32[]{:S(2)}) collective-permute-start(bf16[4,64,1024]{2,1,0:T(8,128)(2,1)} %copy-done.49), channel_id=1, source_target_pairs={{0,16},{1,17},{2,18},{3,19},{4,20},{5,21},{6,22},{7,23},{8,24},{9,... | collective-permute-start | bytes 1572872 | tf_op jit(solution)/shard_map/ppermute | solution.py:37
  71.9 24.3 %collective-permute-start.23 = (bf16[4,64,1024]{2,1,0:T(8,128)(2,1)}, bf16[4,64,1024]{2,1,0:T(8,128)(2,1)S(1)}, u32[]{:S(2)}, u32[]{:S(2)}) collective-permute-start(bf16[4,64,1024]{2,1,0:T(8,128)(2,1)} %copy-done.49), channel_id=1, source_target_pairs={{0,24},{1,25},{2,26},{3,27},{4,28},{5,29},{6,30},{7,31},{8,16},{9,... | collective-permute-start | bytes 1572872 | tf_op jit(solution)/shard_map/ppermute | solution.py:37
  96.4 9.3 %collective-permute-start.26 = (bf16[4,32,1024]{2,1,0:T(8,128)(2,1)S(1)}, bf16[4,32,1024]{2,1,0:T(8,128)(2,1)S(1)}, u32[]{:S(2)}, u32[]{:S(2)}) collective-permute-start(bf16[4,32,1024]{2,1,0:T(8,128)(2,1)S(1)} %shard_map.268.refs_0_), channel_id=1, source_target_pairs={{0,8},{1,9},{2,10},{3,11},{4,12},{5,13},{6,14},{7,15},{8,0},{9,1},... | collective-permute-start | bytes 786440 | tf_op jit(solution)/shard_map/ppermute | solution.py:37
  97.0 14.0 %collective-permute-start.27 = (bf16[4,32,1024]{2,1,0:T(8,128)(2,1)S(1)}, bf16[4,32,1024]{2,1,0:T(8,128)(2,1)S(1)}, u32[]{:S(2)}, u32[]{:S(2)}) collective-permute-start(bf16[4,32,1024]{2,1,0:T(8,128)(2,1)S(1)} %shard_map.268.refs_0_), channel_id=1, source_target_pairs={{0,16},{1,17},{2,18},{3,19},{4,20},{5,21},{6,22},{7,23},{8,24},{9,... | collective-permute-start | bytes 786440 | tf_op jit(solution)/shard_map/ppermute | solution.py:37
  98.4 12.6 %collective-permute-start.28 = (bf16[4,32,1024]{2,1,0:T(8,128)(2,1)S(1)}, bf16[4,32,1024]{2,1,0:T(8,128)(2,1)S(1)}, u32[]{:S(2)}, u32[]{:S(2)}) collective-permute-start(bf16[4,32,1024]{2,1,0:T(8,128)(2,1)S(1)} %shard_map.268.refs_0_), channel_id=1, source_target_pairs={{0,24},{1,25},{2,26},{3,27},{4,28},{5,29},{6,30},{7,31},{8,16},{9,... | collective-permute-start | bytes 786440 | tf_op jit(solution)/shard_map/ppermute | solution.py:37
  103.6 7.4 %collective-permute-start.25 = (f32[8,1024]{1,0:T(8,128)S(1)}, f32[8,1024]{1,0:T(8,128)S(1)}, u32[]{:S(2)}, u32[]{:S(2)}) collective-permute-start(f32[8,1024]{1,0:T(8,128)S(1)} %get-tuple-element.155), channel_id=1, source_target_pairs={{0,1},{1,2},{2,3},{3,4},{4,5},{5,6},{6,7},{8,9},{9,10},{10,11},{11... | collective-permute-start | bytes 98312 | tf_op jit(solution)/shard_map/ppermute | solution.py:37
  111.1 23.9 %collective-permute-start.29 = (bf16[16,32,1024]{2,1,0:T(8,128)(2,1)S(1)}, bf16[16,32,1024]{2,1,0:T(8,128)(2,1)}, u32[]{:S(2)}, u32[]{:S(2)}) collective-permute-start(bf16[16,32,1024]{2,1,0:T(8,128)(2,1)S(1)} %shard_map.269.refs_4_), channel_id=1, source_target_pairs={{0,1},{1,0},{2,3},{3,2},{4,5},{5,4},{6,7},{7,6},{8,9},{9,8},{10,11... | collective-permute-start | bytes 3145736 | tf_op jit(solution)/shard_map/ppermute | solution.py:37
  113.7 9.4 %collective-permute-start.30 = (bf16[128,1024]{1,0:T(8,128)(2,1)}, bf16[128,1024]{1,0:T(8,128)(2,1)}, u32[]{:S(2)}, u32[]{:S(2)}) collective-permute-start(bf16[128,1024]{1,0:T(8,128)(2,1)} %get-tuple-element.156.refs_0_), channel_id=1, source_target_pairs={{0,8},{1,9},{2,10},{3,11},{4,12},{5,13},{6,14},{7,15},{8,0},{9,1},... | collective-permute-start | bytes 786440 | tf_op jit(solution)/shard_map/ppermute | solution.py:37
  115.2 14.3 %collective-permute-start.32 = (bf16[128,1024]{1,0:T(8,128)(2,1)}, bf16[128,1024]{1,0:T(8,128)(2,1)}, u32[]{:S(2)}, u32[]{:S(2)}) collective-permute-start(bf16[128,1024]{1,0:T(8,128)(2,1)} %get-tuple-element.156.refs_0_), channel_id=1, source_target_pairs={{0,16},{1,17},{2,18},{3,19},{4,20},{5,21},{6,22},{7,23},{8,24},{9,... | collective-permute-start | bytes 786440 | tf_op jit(solution)/shard_map/ppermute | solution.py:37
  115.7 16.0 %collective-permute-start.34 = (bf16[128,1024]{1,0:T(8,128)(2,1)}, bf16[128,1024]{1,0:T(8,128)(2,1)}, u32[]{:S(2)}, u32[]{:S(2)}) collective-permute-start(bf16[128,1024]{1,0:T(8,128)(2,1)} %get-tuple-element.156.refs_0_), channel_id=1, source_target_pairs={{0,24},{1,25},{2,26},{3,27},{4,28},{5,29},{6,30},{7,31},{8,16},{9,... | collective-permute-start | bytes 786440 | tf_op jit(solution)/shard_map/ppermute | solution.py:37
  124.9 14.3 %collective-permute-start.31 = (bf16[128,1024]{1,0:T(8,128)(2,1)S(1)}, bf16[128,1024]{1,0:T(8,128)(2,1)S(1)}, u32[]{:S(2)}, u32[]{:S(2)}) collective-permute-start(bf16[128,1024]{1,0:T(8,128)(2,1)S(1)} %get-tuple-element.166), channel_id=1, source_target_pairs={{0,8},{1,9},{2,10},{3,11},{4,12},{5,13},{6,14},{7,15},{8,0},{9,1},... | collective-permute-start | bytes 786440 | tf_op jit(solution)/shard_map/ppermute | solution.py:37
  131.2 16.3 %collective-permute-start.33 = (bf16[128,1024]{1,0:T(8,128)(2,1)S(1)}, bf16[128,1024]{1,0:T(8,128)(2,1)S(1)}, u32[]{:S(2)}, u32[]{:S(2)}) collective-permute-start(bf16[128,1024]{1,0:T(8,128)(2,1)S(1)} %get-tuple-element.167), channel_id=1, source_target_pairs={{0,16},{1,17},{2,18},{3,19},{4,20},{5,21},{6,22},{7,23},{8,24},{9,... | collective-permute-start | bytes 786440 | tf_op jit(solution)/shard_map/ppermute | solution.py:37
  133.4 14.1 %collective-permute-start.35 = (bf16[128,1024]{1,0:T(8,128)(2,1)S(1)}, bf16[128,1024]{1,0:T(8,128)(2,1)S(1)}, u32[]{:S(2)}, u32[]{:S(2)}) collective-permute-start(bf16[128,1024]{1,0:T(8,128)(2,1)S(1)} %get-tuple-element.168), channel_id=1, source_target_pairs={{0,24},{1,25},{2,26},{3,27},{4,28},{5,29},{6,30},{7,31},{8,16},{9,... | collective-permute-start | bytes 786440 | tf_op jit(solution)/shard_map/ppermute | solution.py:37
  148.4 8.0 %collective-permute-start.38 = (bf16[128,1024]{1,0:T(8,128)(2,1)S(1)}, bf16[128,1024]{1,0:T(8,128)(2,1)S(1)}, u32[]{:S(2)}, u32[]{:S(2)}) collective-permute-start(bf16[128,1024]{1,0:T(8,128)(2,1)S(1)} %get-tuple-element.170.refs_0_.refs_12_), channel_id=1, source_target_pairs={{0,16},{1,17},{2,18},{3,19},{4,20},{5,21},{6,22},{7,23},{8,24},{9,... | collective-permute-start | bytes 786440 | tf_op jit(solution)/shard_map/ppermute | solution.py:37
  150.3 10.1 %collective-permute-start.40 = (bf16[128,1024]{1,0:T(8,128)(2,1)S(1)}, bf16[128,1024]{1,0:T(8,128)(2,1)S(1)}, u32[]{:S(2)}, u32[]{:S(2)}) collective-permute-start(bf16[128,1024]{1,0:T(8,128)(2,1)S(1)} %get-tuple-element.170.refs_0_.refs_12_), channel_id=1, source_target_pairs={{0,24},{1,25},{2,26},{3,27},{4,28},{5,29},{6,30},{7,31},{8,16},{9,... | collective-permute-start | bytes 786440 | tf_op jit(solution)/shard_map/ppermute | solution.py:37
  151.9 27.6 %collective-permute-start.47 = (bf16[5,128,1024]{2,1,0:T(8,128)(2,1)S(1)}, bf16[5,128,1024]{2,1,0:T(8,128)(2,1)S(1)}, u32[]{:S(2)}, u32[]{:S(2)}) collective-permute-start(bf16[5,128,1024]{2,1,0:T(8,128)(2,1)S(1)} %get-tuple-element.193.refs_0_), channel_id=1, source_target_pairs={{0,1},{1,0},{2,3},{3,2},{4,5},{5,4},{6,7},{7,6},{8,9},{9,8},{10,11... | collective-permute-start | bytes 3932168 | tf_op jit(solution)/shard_map/ppermute | solution.py:37
  156.3 11.3 %collective-permute-start.37 = (bf16[128,1024]{1,0:T(8,128)(2,1)S(1)}, bf16[128,1024]{1,0:T(8,128)(2,1)S(1)}, u32[]{:S(2)}, u32[]{:S(2)}) collective-permute-start(bf16[128,1024]{1,0:T(8,128)(2,1)S(1)} %get-tuple-element.178), channel_id=1, source_target_pairs={{0,8},{1,9},{2,10},{3,11},{4,12},{5,13},{6,14},{7,15},{8,0},{9,1},... | collective-permute-start | bytes 786440 | tf_op jit(solution)/shard_map/ppermute | solution.py:37
  158.0 12.4 %collective-permute-start.39 = (bf16[128,1024]{1,0:T(8,128)(2,1)S(1)}, bf16[128,1024]{1,0:T(8,128)(2,1)S(1)}, u32[]{:S(2)}, u32[]{:S(2)}) collective-permute-start(bf16[128,1024]{1,0:T(8,128)(2,1)S(1)} %get-tuple-element.180), channel_id=1, source_target_pairs={{0,16},{1,17},{2,18},{3,19},{4,20},{5,21},{6,22},{7,23},{8,24},{9,... | collective-permute-start | bytes 786440 | tf_op jit(solution)/shard_map/ppermute | solution.py:37
  161.9 8.4 %collective-permute-start.41 = (bf16[128,1024]{1,0:T(8,128)(2,1)S(1)}, bf16[128,1024]{1,0:T(8,128)(2,1)S(1)}, u32[]{:S(2)}, u32[]{:S(2)}) collective-permute-start(bf16[128,1024]{1,0:T(8,128)(2,1)S(1)} %get-tuple-element.182), channel_id=1, source_target_pairs={{0,24},{1,25},{2,26},{3,27},{4,28},{5,29},{6,30},{7,31},{8,16},{9,... | collective-permute-start | bytes 786440 | tf_op jit(solution)/shard_map/ppermute | solution.py:37
  189.9 40.8 %collective-permute-start.52 = (bf16[384,1024]{1,0:T(8,128)(2,1)}, bf16[384,1024]{1,0:T(8,128)(2,1)S(1)}, u32[]{:S(2)}, u32[]{:S(2)}) collective-permute-start(bf16[384,1024]{1,0:T(8,128)(2,1)} %copy-done.68), channel_id=1, source_target_pairs={{0,8},{1,9},{2,10},{3,11},{4,12},{5,13},{6,14},{7,15},{8,0},{9,1},... | collective-permute-start | bytes 2359304 | tf_op jit(solution)/shard_map/ppermute | solution.py:37
  191.5 39.1 %collective-permute-start.53 = (bf16[384,1024]{1,0:T(8,128)(2,1)}, bf16[384,1024]{1,0:T(8,128)(2,1)S(1)}, u32[]{:S(2)}, u32[]{:S(2)}) collective-permute-start(bf16[384,1024]{1,0:T(8,128)(2,1)} %copy-done.67), channel_id=1, source_target_pairs={{0,16},{1,17},{2,18},{3,19},{4,20},{5,21},{6,22},{7,23},{8,24},{9,... | collective-permute-start | bytes 2359304 | tf_op jit(solution)/shard_map/ppermute | solution.py:37
  192.4 38.3 %collective-permute-start.54 = (bf16[384,1024]{1,0:T(8,128)(2,1)}, bf16[384,1024]{1,0:T(8,128)(2,1)S(1)}, u32[]{:S(2)}, u32[]{:S(2)}) collective-permute-start(bf16[384,1024]{1,0:T(8,128)(2,1)} %copy-done.66), channel_id=1, source_target_pairs={{0,24},{1,25},{2,26},{3,27},{4,28},{5,29},{6,30},{7,31},{8,16},{9,... | collective-permute-start | bytes 2359304 | tf_op jit(solution)/shard_map/ppermute | solution.py:37
  197.1 7.4 %collective-permute-start.45 = (f32[8,1024]{1,0:T(8,128)S(1)}, f32[8,1024]{1,0:T(8,128)S(1)}, u32[]{:S(2)}, u32[]{:S(2)}) collective-permute-start(f32[8,1024]{1,0:T(8,128)S(1)} %shard_map.281.refs_4_), channel_id=1, source_target_pairs={{4,0},{5,1},{6,2},{7,3},{12,8},{13,9},{14,10},{15,11},{20,16},{21,... | collective-permute-start | bytes 98312 | tf_op jit(solution)/shard_map/ppermute | solution.py:37
  209.9 21.3 %collective-permute-start.50 = (bf16[2,128,1024]{2,1,0:T(8,128)(2,1)S(1)}, bf16[2,128,1024]{2,1,0:T(8,128)(2,1)S(1)}, u32[]{:S(2)}, u32[]{:S(2)}) collective-permute-start(bf16[2,128,1024]{2,1,0:T(8,128)(2,1)S(1)} %shard_map.286.refs_0_.refs_2_), channel_id=1, source_target_pairs={{0,1},{1,0},{2,3},{3,2},{4,5},{5,4},{6,7},{7,6},{8,9},{9,8},{10,11... | collective-permute-start | bytes 1572872 | tf_op jit(solution)/shard_map/ppermute | solution.py:37
  216.5 9.0 %collective-permute-start.49 = (f32[8,1024]{1,0:T(8,128)S(1)}, f32[8,1024]{1,0:T(8,128)S(1)}, u32[]{:S(2)}, u32[]{:S(2)}) collective-permute-start(f32[8,1024]{1,0:T(8,128)S(1)} %get-tuple-element.206), channel_id=1, source_target_pairs={{1,0},{2,1},{3,2},{4,3},{5,4},{6,5},{7,6},{9,8},{10,9},{11,10},{12... | collective-permute-start | bytes 98312 | tf_op jit(solution)/shard_map/ppermute | solution.py:37
  231.9 26.2 %collective-permute-start.55 = (bf16[288,1024]{1,0:T(8,128)(2,1)S(1)}, bf16[288,1024]{1,0:T(8,128)(2,1)S(1)}, u32[]{:S(2)}, u32[]{:S(2)}) collective-permute-start(bf16[288,1024]{1,0:T(8,128)(2,1)S(1)} %get-tuple-element.219), channel_id=1, source_target_pairs={{0,8},{1,9},{2,10},{3,11},{4,12},{5,13},{6,14},{7,15},{8,0},{9,1},... | collective-permute-start | bytes 1769480 | tf_op jit(solution)/shard_map/ppermute | solution.py:37
  233.6 27.7 %collective-permute-start.56 = (bf16[288,1024]{1,0:T(8,128)(2,1)S(1)}, bf16[288,1024]{1,0:T(8,128)(2,1)S(1)}, u32[]{:S(2)}, u32[]{:S(2)}) collective-permute-start(bf16[288,1024]{1,0:T(8,128)(2,1)S(1)} %get-tuple-element.220), channel_id=1, source_target_pairs={{0,16},{1,17},{2,18},{3,19},{4,20},{5,21},{6,22},{7,23},{8,24},{9,... | collective-permute-start | bytes 1769480 | tf_op jit(solution)/shard_map/ppermute | solution.py:37
  234.7 26.6 %collective-permute-start.57 = (bf16[288,1024]{1,0:T(8,128)(2,1)S(1)}, bf16[288,1024]{1,0:T(8,128)(2,1)S(1)}, u32[]{:S(2)}, u32[]{:S(2)}) collective-permute-start(bf16[288,1024]{1,0:T(8,128)(2,1)S(1)} %get-tuple-element.221), channel_id=1, source_target_pairs={{0,24},{1,25},{2,26},{3,27},{4,28},{5,29},{6,30},{7,31},{8,16},{9,... | collective-permute-start | bytes 1769480 | tf_op jit(solution)/shard_map/ppermute | solution.py:37
  235.5 18.3 %collective-permute-start.58 = (bf16[192,1024]{1,0:T(8,128)(2,1)S(1)}, bf16[192,1024]{1,0:T(8,128)(2,1)S(1)}, u32[]{:S(2)}, u32[]{:S(2)}) collective-permute-start(bf16[192,1024]{1,0:T(8,128)(2,1)S(1)} %shard_map.291), channel_id=1, source_target_pairs={{0,4},{1,5},{2,6},{3,7},{4,0},{5,1},{6,2},{7,3},{8,12},{9,13},{10,... | collective-permute-start | bytes 1179656 | tf_op jit(solution)/shard_map/ppermute | solution.py:37
  253.8 17.9 %collective-permute-start.62 = (bf16[96,1024]{1,0:T(8,128)(2,1)S(1)}, bf16[96,1024]{1,0:T(8,128)(2,1)S(1)}, u32[]{:S(2)}, u32[]{:S(2)}) collective-permute-start(bf16[96,1024]{1,0:T(8,128)(2,1)S(1)} %get-tuple-element.234), channel_id=1, source_target_pairs={{0,2},{1,3},{2,0},{3,1},{4,6},{5,7},{6,4},{7,5},{8,10},{9,11},{10,... | collective-permute-start | bytes 589832 | tf_op jit(solution)/shard_map/ppermute | solution.py:37
  262.0 10.5 %collective-permute-start.59 = (bf16[96,1024]{1,0:T(8,128)(2,1)S(1)}, bf16[96,1024]{1,0:T(8,128)(2,1)S(1)}, u32[]{:S(2)}, u32[]{:S(2)}) collective-permute-start(bf16[96,1024]{1,0:T(8,128)(2,1)S(1)} %get-tuple-element.228), channel_id=1, source_target_pairs={{0,2},{1,3},{2,0},{3,1},{4,6},{5,7},{6,4},{7,5},{8,10},{9,11},{10,... | collective-permute-start | bytes 589832 | tf_op jit(solution)/shard_map/ppermute | solution.py:37
  265.1 13.8 %collective-permute-start.60 = (bf16[96,1024]{1,0:T(8,128)(2,1)S(1)}, bf16[96,1024]{1,0:T(8,128)(2,1)S(1)}, u32[]{:S(2)}, u32[]{:S(2)}) collective-permute-start(bf16[96,1024]{1,0:T(8,128)(2,1)S(1)} %get-tuple-element.229), channel_id=1, source_target_pairs={{0,4},{1,5},{2,6},{3,7},{4,0},{5,1},{6,2},{7,3},{8,12},{9,13},{10,... | collective-permute-start | bytes 589832 | tf_op jit(solution)/shard_map/ppermute | solution.py:37
  265.1 17.9 %collective-permute-start.61 = (bf16[96,1024]{1,0:T(8,128)(2,1)S(1)}, bf16[96,1024]{1,0:T(8,128)(2,1)S(1)}, u32[]{:S(2)}, u32[]{:S(2)}) collective-permute-start(bf16[96,1024]{1,0:T(8,128)(2,1)S(1)} %get-tuple-element.230), channel_id=1, source_target_pairs={{0,6},{1,7},{2,4},{3,5},{4,2},{5,3},{6,0},{7,1},{8,14},{9,15},{10,... | collective-permute-start | bytes 589832 | tf_op jit(solution)/shard_map/ppermute | solution.py:37
  268.3 15.5 %all-to-all-start = ((bf16[4,32,1024]{2,1,0:T(8,128)(2,1)}), bf16[4,32,1024]{2,1,0:T(8,128)(2,1)S(1)}, u32[]{:S(2)}, u32[]{:S(2)}) async-start(bf16[4,32,1024]{2,1,0:T(8,128)(2,1)} %bitcast.25), calls=%async_computation.1 | async-start | bytes 524288 | tf_op jit(solution)/shard_map/all_to_all | solution.py:1198
  (87 other events, 658.4 us)
Sparse Core Ops, SparseCore 0:
  65.6 48.4 all-gather.1
  190.0 47.6 reduce-scatter.1

commit v4 on v3

--- a/solution.py
+++ b/solution.py
@@ -345,23 +345,33 @@
     return body
 
 
+def joined_sums(count, length, chips):
+    def body(near, far, vectors):
+        pace = jnp.exp(vectors[9:10])
+        sums, last, before = split_message(near, count)
+        more, far_last, far_before = split_message(far, count)
+        more = moved(more, 2.0 * length * chips, pace)
+        sums = [x + jnp.where(last == before, y, 0.0) for x, y in zip(sums, more, strict=True)]
+        ids = [last, far_before] if count == 4 else [far_last, before]
+        return (stack_rows(sums + ids),)
+
+    return body
+
+
 def carried(count, length, forward):
     def body(message, other, vectors, *got):
-        depth = len(got) + 1
-        _, z, core = places()
+        core = places()[2]
         pace = jnp.exp(vectors[9:10])
         first, second = by_place(message, other)
         one, one_last, one_before = split_message(first, count)
         two, two_last, _ = split_message(second, count)
-        total = [jnp.zeros_like(x) for x in one]
-        for k in range(1, depth):
-            sums, last, before = split_message(got[k - 1], count)
-            if forward:
-                valid = (last == one_before) & (z >= k)
-            else:
-                valid = (before == two_last) & (z < depth - k)
-            sums = moved(sums, 2.0 * length * (k - 1), pace)
-            total = [t + jnp.where(valid, x, 0.0) for t, x in zip(total, sums, strict=True)]
+        total, last, before = split_message(got[0], count)
+        through, chips = last == before, 1
+        for i, message in enumerate(got[1:]):
+            sums, last, before = split_message(message, count)
+            sums = moved(sums, 2.0 * length * chips, pace)
+            total = [t + jnp.where(through, x, 0.0) for t, x in zip(total, sums, strict=True)]
+            through, chips = through & (last == before), chips + 2 ** (i + 1)
         inner, through = (one, one_last == one_before) if forward else (two, two_last == one_last)
         passed = moved(total, float(length), pace)
         passed = [x + jnp.where(through, y, 0.0) for x, y in zip(inner, passed, strict=True)]
@@ -375,28 +385,43 @@
     return body
 
 
-def carry_start(values, vectors, length, forward, plain):
+def carry_chip(values, vectors, length, forward, plain):
+    count = 4 if forward else 2
+    width = values.shape[1]
+    other = to_core(values)
+    (chip,) = fuse(
+        chip_sums(count, length, forward), [((SUBS, width), FULL)], values, other, vectors, plain=plain
+    )
+    return other, chip
+
+
+def carry_steps(chip, vectors, length, forward, plain, after=()):
     cols = lax.axis_size("seq")
     count = 4 if forward else 2
-    other = to_core(values)
-    (chip,) = fuse(
-        chip_sums(count, length, forward),
-        [((SUBS, values.shape[1]), FULL)],
-        values,
-        other,
-        vectors,
-        plain=plain,
-    )
-    step = 1 if forward else -1
-
-    def route(k):
+    width = chip.shape[1]
+
+    def route(step):
         def go(b, s):
-            target = s + 2 * k * step
+            target = s + 2 * step * (1 if forward else -1)
             return (b, target) if 0 <= target < cols else None
 
         return go
 
-    return chip, [values, other, vectors] + [send(chip, route(k)) for k in range(1, cols // 2)]
+    got, sums, step = [], chip, 1
+    while step < cols // 2:
+        got.append(send(sums, route(step)))
+        if 2 * step < cols // 2:
+            (sums,) = fuse(
+                joined_sums(count, length, step),
+                [((SUBS, width), FULL)],
+                sums,
+                got[-1],
+                vectors,
+                after=after,
+                plain=plain,
+            )
+        step *= 2
+    return got
 
 
 def carry_end(parts, length, forward, plain, after=()):
@@ -620,9 +645,14 @@
         plain=plain,
     )
 
+    def deepen_first(second, *x):
+        vectors = sum(y[2 * own :].astype(FULL) for y in x).astype(LOW)
+        parts = [y[i * own : (i + 1) * own] for i in range(2) for y in x]
+        return jnp.concatenate(parts + [vectors], axis=0), second
+
     first_deep, second_pack = fuse(
-        lambda second, *x: (jnp.stack(x), second),
-        [((depth,) + first_pack.shape, LOW), (second_pack.shape, LOW)],
+        deepen_first,
+        [((2 * depth * own + 16, width), LOW), (second_pack.shape, LOW)],
         second_pack,
         first_pack,
         *deep_got,
@@ -703,9 +733,8 @@
         )
 
     def front(unit, statics, edges, order, *pieces):
-        vectors = sum(
-            piece[k, 2 * own :].astype(FULL) for piece in pieces for k in range(depth)
-        )
+        height = depth * own
+        vectors = sum(piece[2 * height :].astype(FULL) for piece in pieces)
         lines = dot(vectors.astype(LOW), order)
         normed = unit * lines[0:1] + lines[2:3]
         edge_normed = edges[0:1] * lines[0:1] + lines[2:3]
@@ -713,7 +742,8 @@
         mix_key = mixing(normed, prior, lines[4:5])
         mix_value = mixing(normed, prior, lines[5:6])
         mix_recept = mixing(normed, prior, lines[6:7])
-        key_all, value_all = gathered(pieces, 0), gathered(pieces, own)
+        key_all = jnp.concatenate([piece[:height] for piece in pieces], axis=0)
+        value_all = jnp.concatenate([piece[height : 2 * height] for piece in pieces], axis=0)
         key, value = dot(mix_key, key_all), dot(mix_value, value_all)
         pace = jnp.exp(vectors[9:10])
         left = length - 1.0 - row_index((length, width)).astype(FULL)
@@ -763,7 +793,9 @@
         plain=plain,
         limit=32,
     )
-    carry = carry_end(carry_start(message, vectors, length, True, plain)[1], length, True, plain)
+    other, chip = carry_chip(message, vectors, length, True, plain)
+    got = carry_steps(chip, vectors, length, True, plain)
+    carry = carry_end([message, other, vectors] + got, length, True, plain)
 
     def receptance(mixes, *pieces):
         recept_all = gathered(pieces, 0)
@@ -814,8 +846,8 @@
             normed - prior,
         )
 
-    mix_hidden, mix_gate, difference_two = fuse(
-        mix_two, [low_act, low_act, full_act], unit_two, edge_two, statics, vectors, plain=plain
+    mix_hidden, mix_gate, difference_two, mixed_token = fuse(
+        mix_two, [low_act, low_act, full_act], unit_two, edge_two, statics, vectors, plain=plain, token=True
     )
     shared = [mix_hidden] + [to_batch(mix_hidden, k) for k in range(1, rows)]
 
@@ -855,7 +887,7 @@
         order,
         gated,
         mixes,
-        *joined(third_deep, third_wide, (edge_two,)),
+        *joined(third_deep, third_wide, (mixed_token,)),
         plain=plain,
     )
 
@@ -1021,7 +1053,7 @@
         limit=24,
     )
 
-    chip_back, carry_parts = carry_start(message, vectors, length, False, plain)
+    other, chip_back = carry_chip(message, vectors, length, False, plain)
 
     *early, early_token = fuse(
         early_terms,
@@ -1034,6 +1066,10 @@
         plain=plain,
         token=True,
     )
+    carry_parts = [message, other, vectors] + carry_steps(
+        chip_back, vectors, length, False, plain, (early_token,)
+    )
+    early_got = [to_batch(early[k], k) for k in range(1, rows)]
     def channel_terms(*x):
         shared, hiddens, squares, grads = (
             jnp.concatenate(x[i * rows : (i + 1) * rows], axis=0) for i in range(4)
@@ -1061,7 +1097,7 @@
         after=(early_token,),
         plain=plain,
         token=True,
-        limit=32,
+        limit=12,
     )
     channel_sum = lax.psum_scatter(channel_term, "seq", scatter_dimension=0, tiled=True)
     carry_back = carry_end(carry_parts, length, False, plain, (channel_token, early_token))
@@ -1152,7 +1188,6 @@
         limit=24,
     )
     sums = sums + to_core(sums)
-    early_got = [to_batch(early[k], k) for k in range(1, rows)]
     *early_pieces, early_wide_token = add_batch(early[0], early_got, 3, plain, (sums,))
     early_half = None
     if depth == 4:

time: 293 us -> 282 us (0.962)
  starting transfers between devices: 93.3 us -> 88.4 us
  waiting for transfers between devices: 101 us -> 96.4 us
    ppermute x63 -> x61, starting transfers between devices: 89.9 us -> 84.9 us  [send(): return lax.ppermute(block, BOTH, pairs)]
    ppermute x63 -> x61, waiting for transfers between devices: 101 us -> 96.3 us  [send(): return lax.ppermute(block, BOTH, pairs)]
    pallas_call x41 -> x43, Pallas kernels: 46.4 us -> 46.6 us  [fuse(): pl.pallas_call(kernel, out_shape=tuple((jax.ShapeDtypeStruct(shape, dtype...]
  transfers between devices with their start and end apart: 66 -> 64, of which waited for: 26 -> 28; matrix products, arithmetic and copies ran while one was open for 1% -> 1% of each run, Pallas kernels for 13% -> 14%
where the time goes in v4:
time: 282 us; the launch traced here: 281 us
  waiting for transfers between devices  96.4 us (34%)
  starting transfers between devices  88.4 us (31%)
  Pallas kernels  47.9 us (17%)
  local copies, waits for them, and re-layouts  33.4 us (12%)
  between operations  15 us (5%)
    ppermute x61, waiting for transfers between devices, send(): return lax.ppermute(block, BOTH, pairs)  96.3 us
    ppermute x61, starting transfers between devices, send(): return lax.ppermute(block, BOTH, pairs)  84.9 us
    pallas_call x43, Pallas kernels, fuse(): pl.pallas_call(kernel, out_shape=tuple((jax.ShapeDtypeStruct(shape, dtype...  46.6 us
    unnamed x138, local copies, waits for them, and re-layouts  31.6 us
  transfers between devices with their start and end apart: 64, of which 28 were waited for; matrix products, arithmetic and copies ran while one was open for 1% of the time, Pallas kernels for 14%

profile of v4, /device:TPU:8, one launch (start us, length us, event | category | flops | bytes accessed | tf_op | source)
XLA Modules:
  0.0 281.0 jit_solution(3738281051896892479)
XLA Ops:
  7.2 2.3 shard_map.254
  9.7 3.0 %collective-permute-start.2 = (bf16[80,1024]{1,0:T(8,128)(2,1)}, bf16[80,1024]{1,0:T(8,128)(2,1)S(1)}, u32[]{:S(2)}, u32[]{:S(2)}) collective-permute-start(bf16[80,1024]{1,0:T(8,128)(2,1)} %get-tuple-element.139.refs_1_), channel_id=1, source_target_pairs={{0,4},{1,5},{2,6},{3,7},{4,0},{5,1},{6,2},{7,3},{8,12},{9,13},{10,... | collective-permute-start | bytes 491528 | tf_op jit(solution)/shard_map/ppermute | solution.py:37
  13.2 1.9 collective-permute-start
  16.6 6.5 %collective-permute-done.refs_1_ = f32[16,1024]{1,0:T(8,128)S(1)} collective-permute-done((f32[16,1024]{1,0:T(8,128)}, f32[16,1024]{1,0:T(8,128)S(1)}, u32[]{:S(2)}, u32[]{:S(2)}) %collective-permute-start) | collective-permute-done | bytes 65568 | tf_op jit(solution)/shard_map/ppermute | solution.py:37
  35.5 8.4 %collective-permute-start.18 = (bf16[96,1024]{1,0:T(8,128)(2,1)S(1)}, bf16[96,1024]{1,0:T(8,128)(2,1)S(1)}, u32[]{:S(2)}, u32[]{:S(2)}) collective-permute-start(bf16[96,1024]{1,0:T(8,128)(2,1)S(1)} %get-tuple-element.151.refs_5_), channel_id=1, source_target_pairs={{0,4},{1,5},{2,6},{3,7},{4,0},{5,1},{6,2},{7,3},{8,12},{9,13},{10,... | collective-permute-start | bytes 589832 | tf_op jit(solution)/shard_map/ppermute | solution.py:37
  44.0 5.5 %collective-permute-start.19 = (bf16[96,1024]{1,0:T(8,128)(2,1)S(1)}, bf16[96,1024]{1,0:T(8,128)(2,1)S(1)}, u32[]{:S(2)}, u32[]{:S(2)}) collective-permute-start(bf16[96,1024]{1,0:T(8,128)(2,1)S(1)} %get-tuple-element.151.refs_5_), channel_id=1, source_target_pairs={{0,6},{1,7},{2,4},{3,5},{4,2},{5,3},{6,0},{7,1},{8,14},{9,15},{10,... | collective-permute-start | bytes 589832 | tf_op jit(solution)/shard_map/ppermute | solution.py:37
  49.4 5.5 %collective-permute-done.18.refs_7_ = bf16[96,1024]{1,0:T(8,128)(2,1)S(1)} collective-permute-done((bf16[96,1024]{1,0:T(8,128)(2,1)S(1)}, bf16[96,1024]{1,0:T(8,128)(2,1)S(1)}, u32[]{:S(2)}, u32[]{:S(2)}) %collective-permute-start.18) | collective-permute-done | bytes 196640 | tf_op jit(solution)/shard_map/ppermute | solution.py:37
  54.9 3.4 %collective-permute-done.19.refs_8_ = bf16[96,1024]{1,0:T(8,128)(2,1)S(1)} collective-permute-done((bf16[96,1024]{1,0:T(8,128)(2,1)S(1)}, bf16[96,1024]{1,0:T(8,128)(2,1)S(1)}, u32[]{:S(2)}, u32[]{:S(2)}) %collective-permute-start.19) | collective-permute-done | bytes 196640 | tf_op jit(solution)/shard_map/ppermute | solution.py:37
  61.6 2.5 collective-permute-start.10
  74.4 2.0 copy-done.11
  77.7 1.9 collective-permute-start.15
  79.7 4.6 %collective-permute-done.15.refs_1_.refs_3_ = f32[8,1024]{1,0:T(8,128)S(1)} collective-permute-done((f32[8,1024]{1,0:T(8,128)S(1)}, f32[8,1024]{1,0:T(8,128)S(1)}, u32[]{:S(2)}, u32[]{:S(2)}) %collective-permute-start.15) | collective-permute-done | bytes 32800 | tf_op jit(solution)/shard_map/ppermute | solution.py:37
  85.6 2.5 collective-permute-done.16.refs_4_
  88.2 3.4 %collective-permute-done.21.refs_2_ = bf16[4,64,1024]{2,1,0:T(8,128)(2,1)S(1)} collective-permute-done((bf16[4,64,1024]{2,1,0:T(8,128)(2,1)}, bf16[4,64,1024]{2,1,0:T(8,128)(2,1)S(1)}, u32[]{:S(2)}, u32[]{:S(2)}) %collective-permute-start.21) | collective-permute-done | bytes 524320 | tf_op jit(solution)/shard_map/ppermute | solution.py:37
  99.7 2.1 collective-permute-start.24
  101.8 3.8 %collective-permute-done.24.refs_1_ = f32[8,1024]{1,0:T(8,128)S(1)} collective-permute-done((f32[8,1024]{1,0:T(8,128)S(1)}, f32[8,1024]{1,0:T(8,128)S(1)}, u32[]{:S(2)}, u32[]{:S(2)}) %collective-permute-start.24) | collective-permute-done | bytes 32800 | tf_op jit(solution)/shard_map/ppermute | solution.py:37
  111.6 2.2 copy-done.10
  114.1 3.5 %collective-permute-done.29.refs_0_.refs_1_ = bf16[128,1024]{1,0:T(8,128)(2,1)} collective-permute-done((bf16[128,1024]{1,0:T(8,128)(2,1)}, bf16[128,1024]{1,0:T(8,128)(2,1)}, u32[]{:S(2)}, u32[]{:S(2)}) %collective-permute-start.29) | collective-permute-done | bytes 262176 | tf_op jit(solution)/shard_map/ppermute | solution.py:37
  120.0 1.9 collective-permute-done.31.refs_0_.refs_2_
  125.0 1.7 shard_map.274
  128.4 2.1 shard_map.271
  130.5 2.0 shard_map.268
  132.5 3.0 %collective-permute-done.32.refs_5_ = bf16[128,1024]{1,0:T(8,128)(2,1)S(1)} collective-permute-done((bf16[128,1024]{1,0:T(8,128)(2,1)S(1)}, bf16[128,1024]{1,0:T(8,128)(2,1)S(1)}, u32[]{:S(2)}, u32[]{:S(2)}) %collective-permute-start.32) | collective-permute-done | bytes 262176 | tf_op jit(solution)/shard_map/ppermute | solution.py:37
  136.4 2.3 collective-permute-start.35
  140.2 2.9 %collective-permute-done.35.refs_0_.refs_13_ = bf16[128,1024]{1,0:T(8,128)(2,1)S(1)} collective-permute-done((bf16[128,1024]{1,0:T(8,128)(2,1)S(1)}, bf16[128,1024]{1,0:T(8,128)(2,1)S(1)}, u32[]{:S(2)}, u32[]{:S(2)}) %collective-permute-start.35) | collective-permute-done | bytes 262176 | tf_op jit(solution)/shard_map/ppermute | solution.py:37
  144.6 2.1 collective-permute-start.36
  152.0 3.5 %shard_map.276 = (bf16[128,1024]{1,0:T(8,128)(2,1)S(1)}, f32[128,1024]{1,0:T(8,128)S(1)}, f32[128,1024]{1,0:T(8,128)S(1)}) custom-call(bf16[128,1024]{1,0:T(8,128)(2,1)S(1)} %get-tuple-element.172.refs_0_.refs_12_, bf16[128,1024]{1,0:T(8,128)(2,1)S(1)} %get-tuple-element.173.refs_1_.refs_8_, bf16[1024,1024]{1,0:T(8,128)(2,1)S(1)} %get-tuple-element.159.refs_1_.refs_2_, ...), custom_call_target="tpu_custom_call" | custom-call | flops 1024 | bytes 1024 | tf_op jit(solution)/shard_map/pallas_call | solution.py:86
  155.6 4.6 %collective-permute-done.38.refs_6_ = bf16[128,1024]{1,0:T(8,128)(2,1)S(1)} collective-permute-done((bf16[128,1024]{1,0:T(8,128)(2,1)S(1)}, bf16[128,1024]{1,0:T(8,128)(2,1)S(1)}, u32[]{:S(2)}, u32[]{:S(2)}) %collective-permute-start.38) | collective-permute-done | bytes 262176 | tf_op jit(solution)/shard_map/ppermute | solution.py:37
  160.8 2.1 collective-permute-start.41
  164.3 2.6 shard_map.281
  166.9 1.8 collective-permute-start.45
  168.8 1.9 collective-permute-done.42.refs_1_
  174.5 3.8 %shard_map.285 = (bf16[2048,1024]{1,0:T(8,128)(2,1)S(1)}, f32[8,128]{1,0:T(8,128)S(1)}) custom-call(bf16[128,1024]{1,0:T(8,128)(2,1)} %get-tuple-element.157.refs_0_, bf16[128,1024]{1,0:T(8,128)(2,1)} %collective-permute-done.29.refs_0_.refs_1_, bf16[128,1024]{1,0:T(8,128)(2,1)} %collective-permute-done.31.refs_0_.refs_2_, ...), custom_call_target="tpu_custom_call" | custom-call | flops 1024 | bytes 1024 | tf_op jit(solution)/shard_map/pallas_call | solution.py:86
  178.3 1.9 copy-done.9
  183.9 3.9 %collective-permute-start.43 = (f32[8,1024]{1,0:T(8,128)S(1)}, f32[8,1024]{1,0:T(8,128)S(1)}, u32[]{:S(2)}, u32[]{:S(2)}) collective-permute-start(f32[8,1024]{1,0:T(8,128)S(1)} %shard_map.282.refs_4_.refs_0_), channel_id=1, source_target_pairs={{2,0},{3,1},{4,2},{5,3},{6,4},{7,5},{10,8},{11,9},{12,10},{13,11},... | collective-permute-start | bytes 98312 | tf_op jit(solution)/shard_map/ppermute | solution.py:37
  187.8 2.5 collective-permute-done.43.refs_1_.refs_3_
  191.6 6.3 %collective-permute-done.46.refs_4_ = f32[8,1024]{1,0:T(8,128)S(1)} collective-permute-done((f32[8,1024]{1,0:T(8,128)S(1)}, f32[8,1024]{1,0:T(8,128)S(1)}, u32[]{:S(2)}, u32[]{:S(2)}) %collective-permute-start.46) | collective-permute-done | bytes 32800 | tf_op jit(solution)/shard_map/ppermute | solution.py:37
  206.5 3.3 %shard_map.289 = (f32[128,1024]{1,0:T(8,128)S(1)}, f32[128,1024]{1,0:T(8,128)S(1)}, f32[8,1024]{1,0:T(8,128)S(1)}, f32[8,1024]{1,0:T(8,128)S(1)}) custom-call(bf16[2,128,1024]{2,1,0:T(8,128)(2,1)S(1)} %shard_map.288.refs_0_.refs_2_, bf16[3,128,1024]{2,1,0:T(8,128)(2,1)S(1)} %get-tuple-element.192.refs_2_.refs_1_, bf16[2,1024,1024]{2,1,0:T(8,128)(2,1)S(1)} %copy-done.12, ...), custom_call_target="tpu_custom_call" | custom-call | flops 1024 | bytes 1024 | tf_op jit(solution)/shard_map/pallas_call | solution.py:86
  209.8 3.1 %collective-permute-start.47 = (f32[8,1024]{1,0:T(8,128)S(1)}, f32[8,1024]{1,0:T(8,128)S(1)}, u32[]{:S(2)}, u32[]{:S(2)}) collective-permute-start(f32[8,1024]{1,0:T(8,128)S(1)} %get-tuple-element.208), channel_id=1, source_target_pairs={{1,0},{2,1},{3,2},{4,3},{5,4},{6,5},{7,6},{9,8},{10,9},{11,10},{12... | collective-permute-start | bytes 98312 | tf_op jit(solution)/shard_map/ppermute | solution.py:37
  212.9 2.2 collective-permute-done.47.refs_2_
  215.1 3.9 %shard_map.290 = (f32[128,1024]{1,0:T(8,128)}, f32[16,1024]{1,0:T(8,128)S(1)}) custom-call(f32[128,1024]{1,0:T(8,128)S(1)} %get-tuple-element.206.refs_0_, f32[128,1024]{1,0:T(8,128)S(1)} %get-tuple-element.207.refs_1_, f32[8,1024]{1,0:T(8,128)S(1)} %collective-permute-done.47.refs_2_, f32[128,1024]{1,0:T(8,128)S(1)} %copy-done.25, ...), custom_call_target="tpu_custom_call" | custom-call | flops 1024 | bytes 1024 | tf_op jit(solution)/shard_map/pallas_call | solution.py:86
  225.2 18.8 %collective-permute-done.56.refs_2_ = bf16[192,1024]{1,0:T(8,128)(2,1)S(1)} collective-permute-done((bf16[192,1024]{1,0:T(8,128)(2,1)S(1)}, bf16[192,1024]{1,0:T(8,128)(2,1)S(1)}, u32[]{:S(2)}, u32[]{:S(2)}) %collective-permute-start.56) | collective-permute-done | bytes 393248 | tf_op jit(solution)/shard_map/ppermute | solution.py:37
  244.1 4.3 %collective-permute-start.60 = (bf16[96,1024]{1,0:T(8,128)(2,1)S(1)}, bf16[96,1024]{1,0:T(8,128)(2,1)S(1)}, u32[]{:S(2)}, u32[]{:S(2)}) collective-permute-start(bf16[96,1024]{1,0:T(8,128)(2,1)S(1)} %get-tuple-element.236), channel_id=1, source_target_pairs={{0,2},{1,3},{2,0},{3,1},{4,6},{5,7},{6,4},{7,5},{8,10},{9,11},{10,... | collective-permute-start | bytes 589832 | tf_op jit(solution)/shard_map/ppermute | solution.py:37
  251.2 2.6 collective-permute-start.57
  255.4 1.7 slice.4
  257.1 3.4 %all-to-all-start = ((bf16[4,32,1024]{2,1,0:T(8,128)(2,1)}), bf16[4,32,1024]{2,1,0:T(8,128)(2,1)S(1)}, u32[]{:S(2)}, u32[]{:S(2)}) async-start(bf16[4,32,1024]{2,1,0:T(8,128)(2,1)} %bitcast.25), calls=%async_computation.1 | async-start | bytes 524288 | tf_op jit(solution)/shard_map/all_to_all | solution.py:1233
  261.3 6.4 %collective-permute-done.58.refs_2_ = bf16[96,1024]{1,0:T(8,128)(2,1)S(1)} collective-permute-done((bf16[96,1024]{1,0:T(8,128)(2,1)S(1)}, bf16[96,1024]{1,0:T(8,128)(2,1)S(1)}, u32[]{:S(2)}, u32[]{:S(2)}) %collective-permute-start.58) | collective-permute-done | bytes 196640 | tf_op jit(solution)/shard_map/ppermute | solution.py:37
  267.7 4.7 %collective-permute-done.59.refs_3_ = bf16[96,1024]{1,0:T(8,128)(2,1)S(1)} collective-permute-done((bf16[96,1024]{1,0:T(8,128)(2,1)S(1)}, bf16[96,1024]{1,0:T(8,128)(2,1)S(1)}, u32[]{:S(2)}, u32[]{:S(2)}) %collective-permute-start.59) | collective-permute-done | bytes 196640 | tf_op jit(solution)/shard_map/ppermute | solution.py:37
  (267 shorter events, 93.5 us)
Async XLA Ops:
  7.2 104.4 %all-gather.2.cloned.1.call-start = ((), (), s32[]{:S(2)}) async-start(), calls=%async_computation.2 | async-start | bytes 4718592 | tf_op jit(solution)/shard_map/all_gather | solution.py:695
  9.6 20.4 %collective-permute-start.1 = (bf16[80,1024]{1,0:T(8,128)(2,1)}, bf16[80,1024]{1,0:T(8,128)(2,1)S(1)}, u32[]{:S(2)}, u32[]{:S(2)}) collective-permute-start(bf16[80,1024]{1,0:T(8,128)(2,1)} %get-tuple-element.139.refs_1_), channel_id=1, source_target_pairs={{0,2},{1,3},{2,0},{3,1},{4,6},{5,7},{6,4},{7,5},{8,10},{9,11},{10,... | collective-permute-start | bytes 491528 | tf_op jit(solution)/shard_map/ppermute | solution.py:37
  9.7 20.4 %collective-permute-start.2 = (bf16[80,1024]{1,0:T(8,128)(2,1)}, bf16[80,1024]{1,0:T(8,128)(2,1)S(1)}, u32[]{:S(2)}, u32[]{:S(2)}) collective-permute-start(bf16[80,1024]{1,0:T(8,128)(2,1)} %get-tuple-element.139.refs_1_), channel_id=1, source_target_pairs={{0,4},{1,5},{2,6},{3,7},{4,0},{5,1},{6,2},{7,3},{8,12},{9,13},{10,... | collective-permute-start | bytes 491528 | tf_op jit(solution)/shard_map/ppermute | solution.py:37
  12.7 17.3 %collective-permute-start.3 = (bf16[80,1024]{1,0:T(8,128)(2,1)}, bf16[80,1024]{1,0:T(8,128)(2,1)S(1)}, u32[]{:S(2)}, u32[]{:S(2)}) collective-permute-start(bf16[80,1024]{1,0:T(8,128)(2,1)} %get-tuple-element.139.refs_1_), channel_id=1, source_target_pairs={{0,6},{1,7},{2,4},{3,5},{4,2},{5,3},{6,0},{7,1},{8,14},{9,15},{10,... | collective-permute-start | bytes 491528 | tf_op jit(solution)/shard_map/ppermute | solution.py:37
  13.2 10.0 %collective-permute-start = (f32[16,1024]{1,0:T(8,128)}, f32[16,1024]{1,0:T(8,128)S(1)}, u32[]{:S(2)}, u32[]{:S(2)}) collective-permute-start(f32[16,1024]{1,0:T(8,128)} %get-tuple-element.131), channel_id=1, source_target_pairs={{0,1},{1,2},{2,3},{3,4},{4,5},{5,6},{6,7},{8,9},{9,10},{10,11},{11... | collective-permute-start | bytes 196616 | tf_op jit(solution)/shard_map/ppermute | solution.py:37
  15.1 9.6 %collective-permute-start.4 = (bf16[32,1024]{1,0:T(8,128)(2,1)}, bf16[32,1024]{1,0:T(8,128)(2,1)S(1)}, u32[]{:S(2)}, u32[]{:S(2)}) collective-permute-start(bf16[32,1024]{1,0:T(8,128)(2,1)} %get-tuple-element.140), channel_id=1, source_target_pairs={{0,8},{1,9},{2,10},{3,11},{4,12},{5,13},{6,14},{7,15},{8,0},{9,1},... | collective-permute-start | bytes 196616 | tf_op jit(solution)/shard_map/ppermute | solution.py:37
  23.1 6.8 %collective-permute-start.5 = (bf16[32,1024]{1,0:T(8,128)(2,1)}, bf16[32,1024]{1,0:T(8,128)(2,1)S(1)}, u32[]{:S(2)}, u32[]{:S(2)}) collective-permute-start(bf16[32,1024]{1,0:T(8,128)(2,1)} %get-tuple-element.141), channel_id=1, source_target_pairs={{0,16},{1,17},{2,18},{3,19},{4,20},{5,21},{6,22},{7,23},{8,24},{9,... | collective-permute-start | bytes 196616 | tf_op jit(solution)/shard_map/ppermute | solution.py:37
  32.0 26.3 %collective-permute-start.7 = (bf16[272,1024]{1,0:T(8,128)(2,1)S(1)}, bf16[272,1024]{1,0:T(8,128)(2,1)S(1)}, u32[]{:S(2)}, u32[]{:S(2)}) collective-permute-start(bf16[272,1024]{1,0:T(8,128)(2,1)S(1)} %get-tuple-element.143.refs_4_), channel_id=1, source_target_pairs={{0,8},{1,9},{2,10},{3,11},{4,12},{5,13},{6,14},{7,15},{8,0},{9,1},... | collective-permute-start | bytes 1671176 | tf_op jit(solution)/shard_map/ppermute | solution.py:37
  33.5 24.8 %collective-permute-start.8 = (bf16[272,1024]{1,0:T(8,128)(2,1)S(1)}, bf16[272,1024]{1,0:T(8,128)(2,1)S(1)}, u32[]{:S(2)}, u32[]{:S(2)}) collective-permute-start(bf16[272,1024]{1,0:T(8,128)(2,1)S(1)} %get-tuple-element.143.refs_4_), channel_id=1, source_target_pairs={{0,16},{1,17},{2,18},{3,19},{4,20},{5,21},{6,22},{7,23},{8,24},{9,... | collective-permute-start | bytes 1671176 | tf_op jit(solution)/shard_map/ppermute | solution.py:37
  34.0 24.3 %collective-permute-start.9 = (bf16[272,1024]{1,0:T(8,128)(2,1)S(1)}, bf16[272,1024]{1,0:T(8,128)(2,1)S(1)}, u32[]{:S(2)}, u32[]{:S(2)}) collective-permute-start(bf16[272,1024]{1,0:T(8,128)(2,1)S(1)} %get-tuple-element.143.refs_4_), channel_id=1, source_target_pairs={{0,24},{1,25},{2,26},{3,27},{4,28},{5,29},{6,30},{7,31},{8,16},{9,... | collective-permute-start | bytes 1671176 | tf_op jit(solution)/shard_map/ppermute | solution.py:37
  35.5 8.4 %collective-permute-start.17 = (bf16[96,1024]{1,0:T(8,128)(2,1)S(1)}, bf16[96,1024]{1,0:T(8,128)(2,1)S(1)}, u32[]{:S(2)}, u32[]{:S(2)}) collective-permute-start(bf16[96,1024]{1,0:T(8,128)(2,1)S(1)} %get-tuple-element.151.refs_5_), channel_id=1, source_target_pairs={{0,2},{1,3},{2,0},{3,1},{4,6},{5,7},{6,4},{7,5},{8,10},{9,11},{10,... | collective-permute-start | bytes 589832 | tf_op jit(solution)/shard_map/ppermute | solution.py:37
  35.5 19.4 %collective-permute-start.18 = (bf16[96,1024]{1,0:T(8,128)(2,1)S(1)}, bf16[96,1024]{1,0:T(8,128)(2,1)S(1)}, u32[]{:S(2)}, u32[]{:S(2)}) collective-permute-start(bf16[96,1024]{1,0:T(8,128)(2,1)S(1)} %get-tuple-element.151.refs_5_), channel_id=1, source_target_pairs={{0,4},{1,5},{2,6},{3,7},{4,0},{5,1},{6,2},{7,3},{8,12},{9,13},{10,... | collective-permute-start | bytes 589832 | tf_op jit(solution)/shard_map/ppermute | solution.py:37
  44.0 14.3 %collective-permute-start.19 = (bf16[96,1024]{1,0:T(8,128)(2,1)S(1)}, bf16[96,1024]{1,0:T(8,128)(2,1)S(1)}, u32[]{:S(2)}, u32[]{:S(2)}) collective-permute-start(bf16[96,1024]{1,0:T(8,128)(2,1)S(1)} %get-tuple-element.151.refs_5_), channel_id=1, source_target_pairs={{0,6},{1,7},{2,4},{3,5},{4,2},{5,3},{6,0},{7,1},{8,14},{9,15},{10,... | collective-permute-start | bytes 589832 | tf_op jit(solution)/shard_map/ppermute | solution.py:37
  61.6 193.8 %reduce-scatter.2.cloned.1.call-start = ((), (), s32[]{:S(2)}) async-start(), calls=%async_computation.3 | async-start | bytes 4718592 | tf_op jit(solution)/shard_map/reduce_scatter | solution.py:1102
  64.7 23.5 %collective-permute-start.20 = (bf16[4,64,1024]{2,1,0:T(8,128)(2,1)}, bf16[4,64,1024]{2,1,0:T(8,128)(2,1)S(1)}, u32[]{:S(2)}, u32[]{:S(2)}) collective-permute-start(bf16[4,64,1024]{2,1,0:T(8,128)(2,1)} %copy-done.49), channel_id=1, source_target_pairs={{0,8},{1,9},{2,10},{3,11},{4,12},{5,13},{6,14},{7,15},{8,0},{9,1},... | collective-permute-start | bytes 1572872 | tf_op jit(solution)/shard_map/ppermute | solution.py:37
  65.9 25.6 %collective-permute-start.21 = (bf16[4,64,1024]{2,1,0:T(8,128)(2,1)}, bf16[4,64,1024]{2,1,0:T(8,128)(2,1)S(1)}, u32[]{:S(2)}, u32[]{:S(2)}) collective-permute-start(bf16[4,64,1024]{2,1,0:T(8,128)(2,1)} %copy-done.49), channel_id=1, source_target_pairs={{0,16},{1,17},{2,18},{3,19},{4,20},{5,21},{6,22},{7,23},{8,24},{9,... | collective-permute-start | bytes 1572872 | tf_op jit(solution)/shard_map/ppermute | solution.py:37
  67.3 24.3 %collective-permute-start.22 = (bf16[4,64,1024]{2,1,0:T(8,128)(2,1)}, bf16[4,64,1024]{2,1,0:T(8,128)(2,1)S(1)}, u32[]{:S(2)}, u32[]{:S(2)}) collective-permute-start(bf16[4,64,1024]{2,1,0:T(8,128)(2,1)} %copy-done.49), channel_id=1, source_target_pairs={{0,24},{1,25},{2,26},{3,27},{4,28},{5,29},{6,30},{7,31},{8,16},{9,... | collective-permute-start | bytes 1572872 | tf_op jit(solution)/shard_map/ppermute | solution.py:37
  91.9 15.5 %collective-permute-start.25 = (bf16[4,32,1024]{2,1,0:T(8,128)(2,1)S(1)}, bf16[4,32,1024]{2,1,0:T(8,128)(2,1)S(1)}, u32[]{:S(2)}, u32[]{:S(2)}) collective-permute-start(bf16[4,32,1024]{2,1,0:T(8,128)(2,1)S(1)} %shard_map.269.refs_0_), channel_id=1, source_target_pairs={{0,8},{1,9},{2,10},{3,11},{4,12},{5,13},{6,14},{7,15},{8,0},{9,1},... | collective-permute-start | bytes 786440 | tf_op jit(solution)/shard_map/ppermute | solution.py:37
  92.5 14.9 %collective-permute-start.26 = (bf16[4,32,1024]{2,1,0:T(8,128)(2,1)S(1)}, bf16[4,32,1024]{2,1,0:T(8,128)(2,1)S(1)}, u32[]{:S(2)}, u32[]{:S(2)}) collective-permute-start(bf16[4,32,1024]{2,1,0:T(8,128)(2,1)S(1)} %shard_map.269.refs_0_), channel_id=1, source_target_pairs={{0,16},{1,17},{2,18},{3,19},{4,20},{5,21},{6,22},{7,23},{8,24},{9,... | collective-permute-start | bytes 786440 | tf_op jit(solution)/shard_map/ppermute | solution.py:37
  93.9 13.5 %collective-permute-start.27 = (bf16[4,32,1024]{2,1,0:T(8,128)(2,1)S(1)}, bf16[4,32,1024]{2,1,0:T(8,128)(2,1)S(1)}, u32[]{:S(2)}, u32[]{:S(2)}) collective-permute-start(bf16[4,32,1024]{2,1,0:T(8,128)(2,1)S(1)} %shard_map.269.refs_0_), channel_id=1, source_target_pairs={{0,24},{1,25},{2,26},{3,27},{4,28},{5,29},{6,30},{7,31},{8,16},{9,... | collective-permute-start | bytes 786440 | tf_op jit(solution)/shard_map/ppermute | solution.py:37
  107.5 20.9 %collective-permute-start.28 = (bf16[16,32,1024]{2,1,0:T(8,128)(2,1)S(1)}, bf16[16,32,1024]{2,1,0:T(8,128)(2,1)}, u32[]{:S(2)}, u32[]{:S(2)}) collective-permute-start(bf16[16,32,1024]{2,1,0:T(8,128)(2,1)S(1)} %shard_map.270.refs_4_), channel_id=1, source_target_pairs={{0,1},{1,0},{2,3},{3,2},{4,5},{5,4},{6,7},{7,6},{8,9},{9,8},{10,11... | collective-permute-start | bytes 3145736 | tf_op jit(solution)/shard_map/ppermute | solution.py:37
  108.1 9.5 %collective-permute-start.29 = (bf16[128,1024]{1,0:T(8,128)(2,1)}, bf16[128,1024]{1,0:T(8,128)(2,1)}, u32[]{:S(2)}, u32[]{:S(2)}) collective-permute-start(bf16[128,1024]{1,0:T(8,128)(2,1)} %get-tuple-element.157.refs_0_), channel_id=1, source_target_pairs={{0,8},{1,9},{2,10},{3,11},{4,12},{5,13},{6,14},{7,15},{8,0},{9,1},... | collective-permute-start | bytes 786440 | tf_op jit(solution)/shard_map/ppermute | solution.py:37
  108.7 13.2 %collective-permute-start.31 = (bf16[128,1024]{1,0:T(8,128)(2,1)}, bf16[128,1024]{1,0:T(8,128)(2,1)}, u32[]{:S(2)}, u32[]{:S(2)}) collective-permute-start(bf16[128,1024]{1,0:T(8,128)(2,1)} %get-tuple-element.157.refs_0_), channel_id=1, source_target_pairs={{0,16},{1,17},{2,18},{3,19},{4,20},{5,21},{6,22},{7,23},{8,24},{9,... | collective-permute-start | bytes 786440 | tf_op jit(solution)/shard_map/ppermute | solution.py:37
  110.1 14.9 %collective-permute-start.33 = (bf16[128,1024]{1,0:T(8,128)(2,1)}, bf16[128,1024]{1,0:T(8,128)(2,1)}, u32[]{:S(2)}, u32[]{:S(2)}) collective-permute-start(bf16[128,1024]{1,0:T(8,128)(2,1)} %get-tuple-element.157.refs_0_), channel_id=1, source_target_pairs={{0,24},{1,25},{2,26},{3,27},{4,28},{5,29},{6,30},{7,31},{8,16},{9,... | collective-permute-start | bytes 786440 | tf_op jit(solution)/shard_map/ppermute | solution.py:37
  119.3 13.2 %collective-permute-start.30 = (bf16[128,1024]{1,0:T(8,128)(2,1)S(1)}, bf16[128,1024]{1,0:T(8,128)(2,1)S(1)}, u32[]{:S(2)}, u32[]{:S(2)}) collective-permute-start(bf16[128,1024]{1,0:T(8,128)(2,1)S(1)} %get-tuple-element.168), channel_id=1, source_target_pairs={{0,8},{1,9},{2,10},{3,11},{4,12},{5,13},{6,14},{7,15},{8,0},{9,1},... | collective-permute-start | bytes 786440 | tf_op jit(solution)/shard_map/ppermute | solution.py:37
  123.7 11.8 %collective-permute-start.32 = (bf16[128,1024]{1,0:T(8,128)(2,1)S(1)}, bf16[128,1024]{1,0:T(8,128)(2,1)S(1)}, u32[]{:S(2)}, u32[]{:S(2)}) collective-permute-start(bf16[128,1024]{1,0:T(8,128)(2,1)S(1)} %get-tuple-element.169), channel_id=1, source_target_pairs={{0,16},{1,17},{2,18},{3,19},{4,20},{5,21},{6,22},{7,23},{8,24},{9,... | collective-permute-start | bytes 786440 | tf_op jit(solution)/shard_map/ppermute | solution.py:37
  126.7 8.8 %collective-permute-start.34 = (bf16[128,1024]{1,0:T(8,128)(2,1)S(1)}, bf16[128,1024]{1,0:T(8,128)(2,1)S(1)}, u32[]{:S(2)}, u32[]{:S(2)}) collective-permute-start(bf16[128,1024]{1,0:T(8,128)(2,1)S(1)} %get-tuple-element.170), channel_id=1, source_target_pairs={{0,24},{1,25},{2,26},{3,27},{4,28},{5,29},{6,30},{7,31},{8,16},{9,... | collective-permute-start | bytes 786440 | tf_op jit(solution)/shard_map/ppermute | solution.py:37
  136.4 6.7 %collective-permute-start.35 = (bf16[128,1024]{1,0:T(8,128)(2,1)S(1)}, bf16[128,1024]{1,0:T(8,128)(2,1)S(1)}, u32[]{:S(2)}, u32[]{:S(2)}) collective-permute-start(bf16[128,1024]{1,0:T(8,128)(2,1)S(1)} %get-tuple-element.172.refs_0_.refs_12_), channel_id=1, source_target_pairs={{0,8},{1,9},{2,10},{3,11},{4,12},{5,13},{6,14},{7,15},{8,0},{9,1},... | collective-permute-start | bytes 786440 | tf_op jit(solution)/shard_map/ppermute | solution.py:37
  138.8 8.8 %collective-permute-start.37 = (bf16[128,1024]{1,0:T(8,128)(2,1)S(1)}, bf16[128,1024]{1,0:T(8,128)(2,1)S(1)}, u32[]{:S(2)}, u32[]{:S(2)}) collective-permute-start(bf16[128,1024]{1,0:T(8,128)(2,1)S(1)} %get-tuple-element.172.refs_0_.refs_12_), channel_id=1, source_target_pairs={{0,16},{1,17},{2,18},{3,19},{4,20},{5,21},{6,22},{7,23},{8,24},{9,... | collective-permute-start | bytes 786440 | tf_op jit(solution)/shard_map/ppermute | solution.py:37
  138.8 10.4 %collective-permute-start.39 = (bf16[128,1024]{1,0:T(8,128)(2,1)S(1)}, bf16[128,1024]{1,0:T(8,128)(2,1)S(1)}, u32[]{:S(2)}, u32[]{:S(2)}) collective-permute-start(bf16[128,1024]{1,0:T(8,128)(2,1)S(1)} %get-tuple-element.172.refs_0_.refs_12_), channel_id=1, source_target_pairs={{0,24},{1,25},{2,26},{3,27},{4,28},{5,29},{6,30},{7,31},{8,16},{9,... | collective-permute-start | bytes 786440 | tf_op jit(solution)/shard_map/ppermute | solution.py:37
  140.2 30.5 %collective-permute-start.44 = (bf16[5,128,1024]{2,1,0:T(8,128)(2,1)S(1)}, bf16[5,128,1024]{2,1,0:T(8,128)(2,1)S(1)}, u32[]{:S(2)}, u32[]{:S(2)}) collective-permute-start(bf16[5,128,1024]{2,1,0:T(8,128)(2,1)S(1)} %get-tuple-element.191.refs_0_), channel_id=1, source_target_pairs={{0,1},{1,0},{2,3},{3,2},{4,5},{5,4},{6,7},{7,6},{8,9},{9,8},{10,11... | collective-permute-start | bytes 3932168 | tf_op jit(solution)/shard_map/ppermute | solution.py:37
  144.6 10.9 %collective-permute-start.36 = (bf16[128,1024]{1,0:T(8,128)(2,1)S(1)}, bf16[128,1024]{1,0:T(8,128)(2,1)S(1)}, u32[]{:S(2)}, u32[]{:S(2)}) collective-permute-start(bf16[128,1024]{1,0:T(8,128)(2,1)S(1)} %get-tuple-element.180), channel_id=1, source_target_pairs={{0,8},{1,9},{2,10},{3,11},{4,12},{5,13},{6,14},{7,15},{8,0},{9,1},... | collective-permute-start | bytes 786440 | tf_op jit(solution)/shard_map/ppermute | solution.py:37
  149.1 11.1 %collective-permute-start.38 = (bf16[128,1024]{1,0:T(8,128)(2,1)S(1)}, bf16[128,1024]{1,0:T(8,128)(2,1)S(1)}, u32[]{:S(2)}, u32[]{:S(2)}) collective-permute-start(bf16[128,1024]{1,0:T(8,128)(2,1)S(1)} %get-tuple-element.182), channel_id=1, source_target_pairs={{0,16},{1,17},{2,18},{3,19},{4,20},{5,21},{6,22},{7,23},{8,24},{9,... | collective-permute-start | bytes 786440 | tf_op jit(solution)/shard_map/ppermute | solution.py:37
  150.7 9.5 %collective-permute-start.40 = (bf16[128,1024]{1,0:T(8,128)(2,1)S(1)}, bf16[128,1024]{1,0:T(8,128)(2,1)S(1)}, u32[]{:S(2)}, u32[]{:S(2)}) collective-permute-start(bf16[128,1024]{1,0:T(8,128)(2,1)S(1)} %get-tuple-element.184), channel_id=1, source_target_pairs={{0,24},{1,25},{2,26},{3,27},{4,28},{5,29},{6,30},{7,31},{8,16},{9,... | collective-permute-start | bytes 786440 | tf_op jit(solution)/shard_map/ppermute | solution.py:37
  180.3 40.0 %collective-permute-start.50 = (bf16[384,1024]{1,0:T(8,128)(2,1)}, bf16[384,1024]{1,0:T(8,128)(2,1)S(1)}, u32[]{:S(2)}, u32[]{:S(2)}) collective-permute-start(bf16[384,1024]{1,0:T(8,128)(2,1)} %copy-done.68), channel_id=1, source_target_pairs={{0,8},{1,9},{2,10},{3,11},{4,12},{5,13},{6,14},{7,15},{8,0},{9,1},... | collective-permute-start | bytes 2359304 | tf_op jit(solution)/shard_map/ppermute | solution.py:37
  181.4 38.9 %collective-permute-start.51 = (bf16[384,1024]{1,0:T(8,128)(2,1)}, bf16[384,1024]{1,0:T(8,128)(2,1)S(1)}, u32[]{:S(2)}, u32[]{:S(2)}) collective-permute-start(bf16[384,1024]{1,0:T(8,128)(2,1)} %copy-done.67), channel_id=1, source_target_pairs={{0,16},{1,17},{2,18},{3,19},{4,20},{5,21},{6,22},{7,23},{8,24},{9,... | collective-permute-start | bytes 2359304 | tf_op jit(solution)/shard_map/ppermute | solution.py:37
  182.7 37.6 %collective-permute-start.52 = (bf16[384,1024]{1,0:T(8,128)(2,1)}, bf16[384,1024]{1,0:T(8,128)(2,1)S(1)}, u32[]{:S(2)}, u32[]{:S(2)}) collective-permute-start(bf16[384,1024]{1,0:T(8,128)(2,1)} %copy-done.66), channel_id=1, source_target_pairs={{0,24},{1,25},{2,26},{3,27},{4,28},{5,29},{6,30},{7,31},{8,16},{9,... | collective-permute-start | bytes 2359304 | tf_op jit(solution)/shard_map/ppermute | solution.py:37
  190.3 7.6 %collective-permute-start.46 = (f32[8,1024]{1,0:T(8,128)S(1)}, f32[8,1024]{1,0:T(8,128)S(1)}, u32[]{:S(2)}, u32[]{:S(2)}) collective-permute-start(f32[8,1024]{1,0:T(8,128)S(1)} %shard_map.284), channel_id=1, source_target_pairs={{4,0},{5,1},{6,2},{7,3},{12,8},{13,9},{14,10},{15,11},{20,16},{21,... | collective-permute-start | bytes 98312 | tf_op jit(solution)/shard_map/ppermute | solution.py:37
  203.2 17.5 %collective-permute-start.48 = (bf16[2,128,1024]{2,1,0:T(8,128)(2,1)S(1)}, bf16[2,128,1024]{2,1,0:T(8,128)(2,1)S(1)}, u32[]{:S(2)}, u32[]{:S(2)}) collective-permute-start(bf16[2,128,1024]{2,1,0:T(8,128)(2,1)S(1)} %shard_map.288.refs_0_.refs_2_), channel_id=1, source_target_pairs={{0,1},{1,0},{2,3},{3,2},{4,5},{5,4},{6,7},{7,6},{8,9},{9,8},{10,11... | collective-permute-start | bytes 1572872 | tf_op jit(solution)/shard_map/ppermute | solution.py:37
  221.5 26.9 %collective-permute-start.53 = (bf16[288,1024]{1,0:T(8,128)(2,1)S(1)}, bf16[288,1024]{1,0:T(8,128)(2,1)S(1)}, u32[]{:S(2)}, u32[]{:S(2)}) collective-permute-start(bf16[288,1024]{1,0:T(8,128)(2,1)S(1)} %get-tuple-element.221), channel_id=1, source_target_pairs={{0,8},{1,9},{2,10},{3,11},{4,12},{5,13},{6,14},{7,15},{8,0},{9,1},... | collective-permute-start | bytes 1769480 | tf_op jit(solution)/shard_map/ppermute | solution.py:37
  222.5 26.7 %collective-permute-start.54 = (bf16[288,1024]{1,0:T(8,128)(2,1)S(1)}, bf16[288,1024]{1,0:T(8,128)(2,1)S(1)}, u32[]{:S(2)}, u32[]{:S(2)}) collective-permute-start(bf16[288,1024]{1,0:T(8,128)(2,1)S(1)} %get-tuple-element.222), channel_id=1, source_target_pairs={{0,16},{1,17},{2,18},{3,19},{4,20},{5,21},{6,22},{7,23},{8,24},{9,... | collective-permute-start | bytes 1769480 | tf_op jit(solution)/shard_map/ppermute | solution.py:37
  223.8 26.8 %collective-permute-start.55 = (bf16[288,1024]{1,0:T(8,128)(2,1)S(1)}, bf16[288,1024]{1,0:T(8,128)(2,1)S(1)}, u32[]{:S(2)}, u32[]{:S(2)}) collective-permute-start(bf16[288,1024]{1,0:T(8,128)(2,1)S(1)} %get-tuple-element.223), channel_id=1, source_target_pairs={{0,24},{1,25},{2,26},{3,27},{4,28},{5,29},{6,30},{7,31},{8,16},{9,... | collective-permute-start | bytes 1769480 | tf_op jit(solution)/shard_map/ppermute | solution.py:37
  225.1 18.9 %collective-permute-start.56 = (bf16[192,1024]{1,0:T(8,128)(2,1)S(1)}, bf16[192,1024]{1,0:T(8,128)(2,1)S(1)}, u32[]{:S(2)}, u32[]{:S(2)}) collective-permute-start(bf16[192,1024]{1,0:T(8,128)(2,1)S(1)} %shard_map.293), channel_id=1, source_target_pairs={{0,4},{1,5},{2,6},{3,7},{4,0},{5,1},{6,2},{7,3},{8,12},{9,13},{10,... | collective-permute-start | bytes 1179656 | tf_op jit(solution)/shard_map/ppermute | solution.py:37
  244.1 16.4 %collective-permute-start.60 = (bf16[96,1024]{1,0:T(8,128)(2,1)S(1)}, bf16[96,1024]{1,0:T(8,128)(2,1)S(1)}, u32[]{:S(2)}, u32[]{:S(2)}) collective-permute-start(bf16[96,1024]{1,0:T(8,128)(2,1)S(1)} %get-tuple-element.236), channel_id=1, source_target_pairs={{0,2},{1,3},{2,0},{3,1},{4,6},{5,7},{6,4},{7,5},{8,10},{9,11},{10,... | collective-permute-start | bytes 589832 | tf_op jit(solution)/shard_map/ppermute | solution.py:37
  251.2 10.1 %collective-permute-start.57 = (bf16[96,1024]{1,0:T(8,128)(2,1)S(1)}, bf16[96,1024]{1,0:T(8,128)(2,1)S(1)}, u32[]{:S(2)}, u32[]{:S(2)}) collective-permute-start(bf16[96,1024]{1,0:T(8,128)(2,1)S(1)} %get-tuple-element.230), channel_id=1, source_target_pairs={{0,2},{1,3},{2,0},{3,1},{4,6},{5,7},{6,4},{7,5},{8,10},{9,11},{10,... | collective-permute-start | bytes 589832 | tf_op jit(solution)/shard_map/ppermute | solution.py:37
  253.9 13.8 %collective-permute-start.58 = (bf16[96,1024]{1,0:T(8,128)(2,1)S(1)}, bf16[96,1024]{1,0:T(8,128)(2,1)S(1)}, u32[]{:S(2)}, u32[]{:S(2)}) collective-permute-start(bf16[96,1024]{1,0:T(8,128)(2,1)S(1)} %get-tuple-element.231), channel_id=1, source_target_pairs={{0,4},{1,5},{2,6},{3,7},{4,0},{5,1},{6,2},{7,3},{8,12},{9,13},{10,... | collective-permute-start | bytes 589832 | tf_op jit(solution)/shard_map/ppermute | solution.py:37
  253.9 18.5 %collective-permute-start.59 = (bf16[96,1024]{1,0:T(8,128)(2,1)S(1)}, bf16[96,1024]{1,0:T(8,128)(2,1)S(1)}, u32[]{:S(2)}, u32[]{:S(2)}) collective-permute-start(bf16[96,1024]{1,0:T(8,128)(2,1)S(1)} %get-tuple-element.232), channel_id=1, source_target_pairs={{0,6},{1,7},{2,4},{3,5},{4,2},{5,3},{6,0},{7,1},{8,14},{9,15},{10,... | collective-permute-start | bytes 589832 | tf_op jit(solution)/shard_map/ppermute | solution.py:37
  257.1 16.0 %all-to-all-start = ((bf16[4,32,1024]{2,1,0:T(8,128)(2,1)}), bf16[4,32,1024]{2,1,0:T(8,128)(2,1)S(1)}, u32[]{:S(2)}, u32[]{:S(2)}) async-start(bf16[4,32,1024]{2,1,0:T(8,128)(2,1)} %bitcast.25), calls=%async_computation.1 | async-start | bytes 524288 | tf_op jit(solution)/shard_map/all_to_all | solution.py:1233
  (85 other events, 622.4 us)
Sparse Core Ops, SparseCore 0:
  61.7 46.7 all-gather.1
  180.4 47.0 reduce-scatter.1

commit v5 on v4

--- a/solution.py
+++ b/solution.py
@@ -12,7 +12,7 @@
 LANES = 128
 SUBS = 8
 MIB = 1024 * 1024
-COST = 1024
+COST = 2000000
 IN_VMEM = pl.BlockSpec(memory_space=pltpu.VMEM)
 IN_HBM = pl.BlockSpec(memory_space=pltpu.HBM)
 
@@ -1218,7 +1218,7 @@
             total = pltpu.roll(total, (width - device * own) & (width - 1), 1)[:, :own]
         return [total[0:2], total[2:4], total[4:9], total[9:10], total[10:11]]
 
-    *late_pieces, _ = add_batch(late[0], late_got, 2, plain, (early_half,), vectors=sums)
+    *late_pieces, late_token = add_batch(late[0], late_got, 2, plain, (early_half,), vectors=sums)
     output_grad, recept_grad, gate_grad = add_depth(early_pieces, 3, own, [], None, plain)
     key_grad, value_grad, gains_grad, offsets_grad, mixes_grad, decay_grad, first_grad = add_depth(
         late_pieces,
@@ -1229,7 +1229,13 @@
         plain,
     )
 
-    crossed = channel_sum[:cross_rows].reshape(rows, own, part_width)
+    (crossed,) = fuse(
+        lambda x: (x[:cross_rows].reshape(rows, own, part_width),),
+        [((rows, own, part_width), LOW)],
+        channel_sum,
+        after=(late_token,),
+        plain=plain,
+    )
     crossed = lax.all_to_all(crossed, "batch", 0, 0)
 
     def assemble(x, crossed):

time: 282 us -> 281 us (level)
    pallas_call x43 -> x44, Pallas kernels: 46.6 us -> 48.7 us  [fuse(): pl.pallas_call(kernel, out_shape=tuple((jax.ShapeDtypeStruct(shape, dtype...]
    unnamed x138 -> x140, local copies, waits for them, and re-layouts: 31.6 us -> 30.9 us
  transfers between devices with their start and end apart: 64 -> 64, of which waited for: 28 -> 28; matrix products, arithmetic and copies ran while one was open for 1% -> 0% of each run, Pallas kernels for 14% -> 14%
where the time goes in v5:
time: 281 us; the launch traced here: 280 us
  waiting for transfers between devices  96 us (34%)
  starting transfers between devices  88.3 us (31%)
  Pallas kernels  50 us (18%)
  local copies, waits for them, and re-layouts  30.9 us (11%)
  between operations  15 us (5%)
    ppermute x61, waiting for transfers between devices, send(): return lax.ppermute(block, BOTH, pairs)  95.9 us
    ppermute x61, starting transfers between devices, send(): return lax.ppermute(block, BOTH, pairs)  84.8 us
    pallas_call x44, Pallas kernels, fuse(): pl.pallas_call(kernel, out_shape=tuple((jax.ShapeDtypeStruct(shape, dtype...  48.7 us
    unnamed x140, local copies, waits for them, and re-layouts  30.9 us
  transfers between devices with their start and end apart: 64, of which 28 were waited for; matrix products, arithmetic and copies ran while one was open for 0% of the time, Pallas kernels for 14%

profile of v5, /device:TPU:8, one launch (start us, length us, event | category | flops | bytes accessed | tf_op | source)
XLA Modules:
  0.0 280.2 jit_solution(10630319522130192194)
XLA Ops:
  7.2 2.3 shard_map.254
  9.7 3.0 %collective-permute-start.2 = (bf16[80,1024]{1,0:T(8,128)(2,1)}, bf16[80,1024]{1,0:T(8,128)(2,1)S(1)}, u32[]{:S(2)}, u32[]{:S(2)}) collective-permute-start(bf16[80,1024]{1,0:T(8,128)(2,1)} %get-tuple-element.140.refs_1_), channel_id=1, source_target_pairs={{0,4},{1,5},{2,6},{3,7},{4,0},{5,1},{6,2},{7,3},{8,12},{9,13},{10,... | collective-permute-start | bytes 491528 | tf_op jit(solution)/shard_map/ppermute | solution.py:37
  13.2 1.9 collective-permute-start
  16.6 6.5 %collective-permute-done.refs_1_ = f32[16,1024]{1,0:T(8,128)S(1)} collective-permute-done((f32[16,1024]{1,0:T(8,128)}, f32[16,1024]{1,0:T(8,128)S(1)}, u32[]{:S(2)}, u32[]{:S(2)}) %collective-permute-start) | collective-permute-done | bytes 65568 | tf_op jit(solution)/shard_map/ppermute | solution.py:37
  35.5 8.4 %collective-permute-start.18 = (bf16[96,1024]{1,0:T(8,128)(2,1)S(1)}, bf16[96,1024]{1,0:T(8,128)(2,1)S(1)}, u32[]{:S(2)}, u32[]{:S(2)}) collective-permute-start(bf16[96,1024]{1,0:T(8,128)(2,1)S(1)} %get-tuple-element.152.refs_5_), channel_id=1, source_target_pairs={{0,4},{1,5},{2,6},{3,7},{4,0},{5,1},{6,2},{7,3},{8,12},{9,13},{10,... | collective-permute-start | bytes 589832 | tf_op jit(solution)/shard_map/ppermute | solution.py:37
  44.0 5.5 %collective-permute-start.19 = (bf16[96,1024]{1,0:T(8,128)(2,1)S(1)}, bf16[96,1024]{1,0:T(8,128)(2,1)S(1)}, u32[]{:S(2)}, u32[]{:S(2)}) collective-permute-start(bf16[96,1024]{1,0:T(8,128)(2,1)S(1)} %get-tuple-element.152.refs_5_), channel_id=1, source_target_pairs={{0,6},{1,7},{2,4},{3,5},{4,2},{5,3},{6,0},{7,1},{8,14},{9,15},{10,... | collective-permute-start | bytes 589832 | tf_op jit(solution)/shard_map/ppermute | solution.py:37
  49.4 5.5 %collective-permute-done.18.refs_7_ = bf16[96,1024]{1,0:T(8,128)(2,1)S(1)} collective-permute-done((bf16[96,1024]{1,0:T(8,128)(2,1)S(1)}, bf16[96,1024]{1,0:T(8,128)(2,1)S(1)}, u32[]{:S(2)}, u32[]{:S(2)}) %collective-permute-start.18) | collective-permute-done | bytes 196640 | tf_op jit(solution)/shard_map/ppermute | solution.py:37
  54.9 3.4 %collective-permute-done.19.refs_8_ = bf16[96,1024]{1,0:T(8,128)(2,1)S(1)} collective-permute-done((bf16[96,1024]{1,0:T(8,128)(2,1)S(1)}, bf16[96,1024]{1,0:T(8,128)(2,1)S(1)}, u32[]{:S(2)}, u32[]{:S(2)}) %collective-permute-start.19) | collective-permute-done | bytes 196640 | tf_op jit(solution)/shard_map/ppermute | solution.py:37
  61.6 2.5 collective-permute-start.10
  74.4 2.0 copy-done.11
  77.7 1.9 collective-permute-start.15
  79.7 4.6 %collective-permute-done.15.refs_1_.refs_3_ = f32[8,1024]{1,0:T(8,128)S(1)} collective-permute-done((f32[8,1024]{1,0:T(8,128)S(1)}, f32[8,1024]{1,0:T(8,128)S(1)}, u32[]{:S(2)}, u32[]{:S(2)}) %collective-permute-start.15) | collective-permute-done | bytes 32800 | tf_op jit(solution)/shard_map/ppermute | solution.py:37
  85.6 2.5 collective-permute-done.16.refs_4_
  88.2 3.4 %collective-permute-done.21.refs_2_ = bf16[4,64,1024]{2,1,0:T(8,128)(2,1)S(1)} collective-permute-done((bf16[4,64,1024]{2,1,0:T(8,128)(2,1)}, bf16[4,64,1024]{2,1,0:T(8,128)(2,1)S(1)}, u32[]{:S(2)}, u32[]{:S(2)}) %collective-permute-start.21) | collective-permute-done | bytes 524320 | tf_op jit(solution)/shard_map/ppermute | solution.py:37
  99.7 2.1 collective-permute-start.24
  101.8 3.8 %collective-permute-done.24.refs_1_ = f32[8,1024]{1,0:T(8,128)S(1)} collective-permute-done((f32[8,1024]{1,0:T(8,128)S(1)}, f32[8,1024]{1,0:T(8,128)S(1)}, u32[]{:S(2)}, u32[]{:S(2)}) %collective-permute-start.24) | collective-permute-done | bytes 32800 | tf_op jit(solution)/shard_map/ppermute | solution.py:37
  111.6 2.2 copy-done.10
  114.0 3.5 %collective-permute-done.29.refs_0_.refs_1_ = bf16[128,1024]{1,0:T(8,128)(2,1)} collective-permute-done((bf16[128,1024]{1,0:T(8,128)(2,1)}, bf16[128,1024]{1,0:T(8,128)(2,1)}, u32[]{:S(2)}, u32[]{:S(2)}) %collective-permute-start.29) | collective-permute-done | bytes 262176 | tf_op jit(solution)/shard_map/ppermute | solution.py:37
  120.0 1.9 collective-permute-done.31.refs_0_.refs_2_
  121.9 1.7 shard_map.273
  125.0 1.7 shard_map.274
  128.4 2.1 shard_map.271
  130.5 2.0 shard_map.268
  132.6 2.9 %collective-permute-done.32.refs_5_ = bf16[128,1024]{1,0:T(8,128)(2,1)S(1)} collective-permute-done((bf16[128,1024]{1,0:T(8,128)(2,1)S(1)}, bf16[128,1024]{1,0:T(8,128)(2,1)S(1)}, u32[]{:S(2)}, u32[]{:S(2)}) %collective-permute-start.32) | collective-permute-done | bytes 262176 | tf_op jit(solution)/shard_map/ppermute | solution.py:37
  136.4 2.4 collective-permute-start.35
  140.2 2.9 %collective-permute-done.35.refs_0_.refs_13_ = bf16[128,1024]{1,0:T(8,128)(2,1)S(1)} collective-permute-done((bf16[128,1024]{1,0:T(8,128)(2,1)S(1)}, bf16[128,1024]{1,0:T(8,128)(2,1)S(1)}, u32[]{:S(2)}, u32[]{:S(2)}) %collective-permute-start.35) | collective-permute-done | bytes 262176 | tf_op jit(solution)/shard_map/ppermute | solution.py:37
  144.6 2.1 collective-permute-start.36
  152.0 3.5 %shard_map.276 = (bf16[128,1024]{1,0:T(8,128)(2,1)S(1)}, f32[128,1024]{1,0:T(8,128)S(1)}, f32[128,1024]{1,0:T(8,128)S(1)}) custom-call(bf16[128,1024]{1,0:T(8,128)(2,1)S(1)} %get-tuple-element.173.refs_0_.refs_12_, bf16[128,1024]{1,0:T(8,128)(2,1)S(1)} %get-tuple-element.174.refs_1_.refs_8_, bf16[1024,1024]{1,0:T(8,128)(2,1)S(1)} %get-tuple-element.160.refs_1_.refs_2_, ...), custom_call_target="tpu_custom_call" | custom-call | flops 2000000 | bytes 2000000 | tf_op jit(solution)/shard_map/pallas_call | solution.py:86
  155.6 4.7 %collective-permute-done.38.refs_6_ = bf16[128,1024]{1,0:T(8,128)(2,1)S(1)} collective-permute-done((bf16[128,1024]{1,0:T(8,128)(2,1)S(1)}, bf16[128,1024]{1,0:T(8,128)(2,1)S(1)}, u32[]{:S(2)}, u32[]{:S(2)}) %collective-permute-start.38) | collective-permute-done | bytes 262176 | tf_op jit(solution)/shard_map/ppermute | solution.py:37
  160.8 2.1 collective-permute-start.41
  164.3 2.6 shard_map.281
  166.9 1.8 collective-permute-start.45
  168.8 1.9 collective-permute-done.42.refs_1_
  172.7 4.3 %shard_map.285 = (bf16[2048,1024]{1,0:T(8,128)(2,1)S(1)}, f32[8,128]{1,0:T(8,128)S(1)}) custom-call(bf16[128,1024]{1,0:T(8,128)(2,1)} %get-tuple-element.158.refs_0_, bf16[128,1024]{1,0:T(8,128)(2,1)} %collective-permute-done.29.refs_0_.refs_1_, bf16[128,1024]{1,0:T(8,128)(2,1)} %collective-permute-done.31.refs_0_.refs_2_, ...), custom_call_target="tpu_custom_call" | custom-call | flops 2000000 | bytes 2000000 | tf_op jit(solution)/shard_map/pallas_call | solution.py:86
  177.1 1.9 copy-done.9
  182.6 3.9 %collective-permute-start.43 = (f32[8,1024]{1,0:T(8,128)S(1)}, f32[8,1024]{1,0:T(8,128)S(1)}, u32[]{:S(2)}, u32[]{:S(2)}) collective-permute-start(f32[8,1024]{1,0:T(8,128)S(1)} %shard_map.282.refs_4_.refs_0_), channel_id=1, source_target_pairs={{2,0},{3,1},{4,2},{5,3},{6,4},{7,5},{10,8},{11,9},{12,10},{13,11},... | collective-permute-start | bytes 98312 | tf_op jit(solution)/shard_map/ppermute | solution.py:37
  186.6 2.5 collective-permute-done.43.refs_1_.refs_3_
  190.4 6.3 %collective-permute-done.46.refs_4_ = f32[8,1024]{1,0:T(8,128)S(1)} collective-permute-done((f32[8,1024]{1,0:T(8,128)S(1)}, f32[8,1024]{1,0:T(8,128)S(1)}, u32[]{:S(2)}, u32[]{:S(2)}) %collective-permute-start.46) | collective-permute-done | bytes 32800 | tf_op jit(solution)/shard_map/ppermute | solution.py:37
  205.3 3.3 %shard_map.289 = (f32[128,1024]{1,0:T(8,128)S(1)}, f32[128,1024]{1,0:T(8,128)S(1)}, f32[8,1024]{1,0:T(8,128)S(1)}, f32[8,1024]{1,0:T(8,128)S(1)}) custom-call(bf16[2,128,1024]{2,1,0:T(8,128)(2,1)S(1)} %shard_map.288.refs_0_.refs_2_, bf16[3,128,1024]{2,1,0:T(8,128)(2,1)S(1)} %get-tuple-element.193.refs_2_.refs_1_, bf16[2,1024,1024]{2,1,0:T(8,128)(2,1)S(1)} %copy-done.12, ...), custom_call_target="tpu_custom_call" | custom-call | flops 2000000 | bytes 2000000 | tf_op jit(solution)/shard_map/pallas_call | solution.py:86
  208.6 3.1 %collective-permute-start.47 = (f32[8,1024]{1,0:T(8,128)S(1)}, f32[8,1024]{1,0:T(8,128)S(1)}, u32[]{:S(2)}, u32[]{:S(2)}) collective-permute-start(f32[8,1024]{1,0:T(8,128)S(1)} %get-tuple-element.209), channel_id=1, source_target_pairs={{1,0},{2,1},{3,2},{4,3},{5,4},{6,5},{7,6},{9,8},{10,9},{11,10},{12... | collective-permute-start | bytes 98312 | tf_op jit(solution)/shard_map/ppermute | solution.py:37
  211.7 2.2 collective-permute-done.47.refs_2_
  213.9 3.9 %shard_map.290 = (f32[128,1024]{1,0:T(8,128)}, f32[16,1024]{1,0:T(8,128)S(1)}) custom-call(f32[128,1024]{1,0:T(8,128)S(1)} %get-tuple-element.207.refs_0_, f32[128,1024]{1,0:T(8,128)S(1)} %get-tuple-element.208.refs_1_, f32[8,1024]{1,0:T(8,128)S(1)} %collective-permute-done.47.refs_2_, f32[128,1024]{1,0:T(8,128)S(1)} %copy-done.25, ...), custom_call_target="tpu_custom_call" | custom-call | flops 2000000 | bytes 2000000 | tf_op jit(solution)/shard_map/pallas_call | solution.py:86
  223.9 18.9 %collective-permute-done.56.refs_2_ = bf16[192,1024]{1,0:T(8,128)(2,1)S(1)} collective-permute-done((bf16[192,1024]{1,0:T(8,128)(2,1)S(1)}, bf16[192,1024]{1,0:T(8,128)(2,1)S(1)}, u32[]{:S(2)}, u32[]{:S(2)}) %collective-permute-start.56) | collective-permute-done | bytes 393248 | tf_op jit(solution)/shard_map/ppermute | solution.py:37
  243.5 4.2 %collective-permute-start.60 = (bf16[96,1024]{1,0:T(8,128)(2,1)}, bf16[96,1024]{1,0:T(8,128)(2,1)S(1)}, u32[]{:S(2)}, u32[]{:S(2)}) collective-permute-start(bf16[96,1024]{1,0:T(8,128)(2,1)} %get-tuple-element.237), channel_id=1, source_target_pairs={{0,2},{1,3},{2,0},{3,1},{4,6},{5,7},{6,4},{7,5},{8,10},{9,11},{10,... | collective-permute-start | bytes 589832 | tf_op jit(solution)/shard_map/ppermute | solution.py:37
  250.2 2.7 collective-permute-start.57
  256.1 3.4 %all-to-all-start = ((bf16[4,32,1024]{2,1,0:T(8,128)(2,1)}), bf16[4,32,1024]{2,1,0:T(8,128)(2,1)S(1)}, u32[]{:S(2)}, u32[]{:S(2)}) async-start(bf16[4,32,1024]{2,1,0:T(8,128)(2,1)} %shard_map.298), calls=%async_computation.1 | async-start | bytes 524288 | tf_op jit(solution)/shard_map/all_to_all | solution.py:1239
  260.3 6.7 %collective-permute-done.58.refs_2_ = bf16[96,1024]{1,0:T(8,128)(2,1)S(1)} collective-permute-done((bf16[96,1024]{1,0:T(8,128)(2,1)}, bf16[96,1024]{1,0:T(8,128)(2,1)S(1)}, u32[]{:S(2)}, u32[]{:S(2)}) %collective-permute-start.58) | collective-permute-done | bytes 196640 | tf_op jit(solution)/shard_map/ppermute | solution.py:37
  267.0 4.6 %collective-permute-done.59.refs_3_ = bf16[96,1024]{1,0:T(8,128)(2,1)S(1)} collective-permute-done((bf16[96,1024]{1,0:T(8,128)(2,1)}, bf16[96,1024]{1,0:T(8,128)(2,1)S(1)}, u32[]{:S(2)}, u32[]{:S(2)}) %collective-permute-start.59) | collective-permute-done | bytes 196640 | tf_op jit(solution)/shard_map/ppermute | solution.py:37
  (269 shorter events, 92.1 us)
Async XLA Ops:
  7.2 104.4 %all-gather.2.cloned.1.call-start = ((), (), s32[]{:S(2)}) async-start(), calls=%async_computation.2 | async-start | bytes 4718592 | tf_op jit(solution)/shard_map/all_gather | solution.py:695
  9.6 20.4 %collective-permute-start.1 = (bf16[80,1024]{1,0:T(8,128)(2,1)}, bf16[80,1024]{1,0:T(8,128)(2,1)S(1)}, u32[]{:S(2)}, u32[]{:S(2)}) collective-permute-start(bf16[80,1024]{1,0:T(8,128)(2,1)} %get-tuple-element.140.refs_1_), channel_id=1, source_target_pairs={{0,2},{1,3},{2,0},{3,1},{4,6},{5,7},{6,4},{7,5},{8,10},{9,11},{10,... | collective-permute-start | bytes 491528 | tf_op jit(solution)/shard_map/ppermute | solution.py:37
  9.7 20.4 %collective-permute-start.2 = (bf16[80,1024]{1,0:T(8,128)(2,1)}, bf16[80,1024]{1,0:T(8,128)(2,1)S(1)}, u32[]{:S(2)}, u32[]{:S(2)}) collective-permute-start(bf16[80,1024]{1,0:T(8,128)(2,1)} %get-tuple-element.140.refs_1_), channel_id=1, source_target_pairs={{0,4},{1,5},{2,6},{3,7},{4,0},{5,1},{6,2},{7,3},{8,12},{9,13},{10,... | collective-permute-start | bytes 491528 | tf_op jit(solution)/shard_map/ppermute | solution.py:37
  12.7 17.3 %collective-permute-start.3 = (bf16[80,1024]{1,0:T(8,128)(2,1)}, bf16[80,1024]{1,0:T(8,128)(2,1)S(1)}, u32[]{:S(2)}, u32[]{:S(2)}) collective-permute-start(bf16[80,1024]{1,0:T(8,128)(2,1)} %get-tuple-element.140.refs_1_), channel_id=1, source_target_pairs={{0,6},{1,7},{2,4},{3,5},{4,2},{5,3},{6,0},{7,1},{8,14},{9,15},{10,... | collective-permute-start | bytes 491528 | tf_op jit(solution)/shard_map/ppermute | solution.py:37
  13.2 10.0 %collective-permute-start = (f32[16,1024]{1,0:T(8,128)}, f32[16,1024]{1,0:T(8,128)S(1)}, u32[]{:S(2)}, u32[]{:S(2)}) collective-permute-start(f32[16,1024]{1,0:T(8,128)} %get-tuple-element.132), channel_id=1, source_target_pairs={{0,1},{1,2},{2,3},{3,4},{4,5},{5,6},{6,7},{8,9},{9,10},{10,11},{11... | collective-permute-start | bytes 196616 | tf_op jit(solution)/shard_map/ppermute | solution.py:37
  15.1 9.6 %collective-permute-start.4 = (bf16[32,1024]{1,0:T(8,128)(2,1)}, bf16[32,1024]{1,0:T(8,128)(2,1)S(1)}, u32[]{:S(2)}, u32[]{:S(2)}) collective-permute-start(bf16[32,1024]{1,0:T(8,128)(2,1)} %get-tuple-element.141), channel_id=1, source_target_pairs={{0,8},{1,9},{2,10},{3,11},{4,12},{5,13},{6,14},{7,15},{8,0},{9,1},... | collective-permute-start | bytes 196616 | tf_op jit(solution)/shard_map/ppermute | solution.py:37
  23.1 6.8 %collective-permute-start.5 = (bf16[32,1024]{1,0:T(8,128)(2,1)}, bf16[32,1024]{1,0:T(8,128)(2,1)S(1)}, u32[]{:S(2)}, u32[]{:S(2)}) collective-permute-start(bf16[32,1024]{1,0:T(8,128)(2,1)} %get-tuple-element.142), channel_id=1, source_target_pairs={{0,16},{1,17},{2,18},{3,19},{4,20},{5,21},{6,22},{7,23},{8,24},{9,... | collective-permute-start | bytes 196616 | tf_op jit(solution)/shard_map/ppermute | solution.py:37
  32.0 26.3 %collective-permute-start.7 = (bf16[272,1024]{1,0:T(8,128)(2,1)S(1)}, bf16[272,1024]{1,0:T(8,128)(2,1)S(1)}, u32[]{:S(2)}, u32[]{:S(2)}) collective-permute-start(bf16[272,1024]{1,0:T(8,128)(2,1)S(1)} %get-tuple-element.144.refs_4_), channel_id=1, source_target_pairs={{0,8},{1,9},{2,10},{3,11},{4,12},{5,13},{6,14},{7,15},{8,0},{9,1},... | collective-permute-start | bytes 1671176 | tf_op jit(solution)/shard_map/ppermute | solution.py:37
  33.5 24.8 %collective-permute-start.8 = (bf16[272,1024]{1,0:T(8,128)(2,1)S(1)}, bf16[272,1024]{1,0:T(8,128)(2,1)S(1)}, u32[]{:S(2)}, u32[]{:S(2)}) collective-permute-start(bf16[272,1024]{1,0:T(8,128)(2,1)S(1)} %get-tuple-element.144.refs_4_), channel_id=1, source_target_pairs={{0,16},{1,17},{2,18},{3,19},{4,20},{5,21},{6,22},{7,23},{8,24},{9,... | collective-permute-start | bytes 1671176 | tf_op jit(solution)/shard_map/ppermute | solution.py:37
  34.0 24.3 %collective-permute-start.9 = (bf16[272,1024]{1,0:T(8,128)(2,1)S(1)}, bf16[272,1024]{1,0:T(8,128)(2,1)S(1)}, u32[]{:S(2)}, u32[]{:S(2)}) collective-permute-start(bf16[272,1024]{1,0:T(8,128)(2,1)S(1)} %get-tuple-element.144.refs_4_), channel_id=1, source_target_pairs={{0,24},{1,25},{2,26},{3,27},{4,28},{5,29},{6,30},{7,31},{8,16},{9,... | collective-permute-start | bytes 1671176 | tf_op jit(solution)/shard_map/ppermute | solution.py:37
  35.5 8.4 %collective-permute-start.17 = (bf16[96,1024]{1,0:T(8,128)(2,1)S(1)}, bf16[96,1024]{1,0:T(8,128)(2,1)S(1)}, u32[]{:S(2)}, u32[]{:S(2)}) collective-permute-start(bf16[96,1024]{1,0:T(8,128)(2,1)S(1)} %get-tuple-element.152.refs_5_), channel_id=1, source_target_pairs={{0,2},{1,3},{2,0},{3,1},{4,6},{5,7},{6,4},{7,5},{8,10},{9,11},{10,... | collective-permute-start | bytes 589832 | tf_op jit(solution)/shard_map/ppermute | solution.py:37
  35.5 19.4 %collective-permute-start.18 = (bf16[96,1024]{1,0:T(8,128)(2,1)S(1)}, bf16[96,1024]{1,0:T(8,128)(2,1)S(1)}, u32[]{:S(2)}, u32[]{:S(2)}) collective-permute-start(bf16[96,1024]{1,0:T(8,128)(2,1)S(1)} %get-tuple-element.152.refs_5_), channel_id=1, source_target_pairs={{0,4},{1,5},{2,6},{3,7},{4,0},{5,1},{6,2},{7,3},{8,12},{9,13},{10,... | collective-permute-start | bytes 589832 | tf_op jit(solution)/shard_map/ppermute | solution.py:37
  44.0 14.3 %collective-permute-start.19 = (bf16[96,1024]{1,0:T(8,128)(2,1)S(1)}, bf16[96,1024]{1,0:T(8,128)(2,1)S(1)}, u32[]{:S(2)}, u32[]{:S(2)}) collective-permute-start(bf16[96,1024]{1,0:T(8,128)(2,1)S(1)} %get-tuple-element.152.refs_5_), channel_id=1, source_target_pairs={{0,6},{1,7},{2,4},{3,5},{4,2},{5,3},{6,0},{7,1},{8,14},{9,15},{10,... | collective-permute-start | bytes 589832 | tf_op jit(solution)/shard_map/ppermute | solution.py:37
  61.6 192.8 %reduce-scatter.2.cloned.1.call-start = ((), (), s32[]{:S(2)}) async-start(), calls=%async_computation.3 | async-start | bytes 4718592 | tf_op jit(solution)/shard_map/reduce_scatter | solution.py:1102
  64.7 23.5 %collective-permute-start.20 = (bf16[4,64,1024]{2,1,0:T(8,128)(2,1)}, bf16[4,64,1024]{2,1,0:T(8,128)(2,1)S(1)}, u32[]{:S(2)}, u32[]{:S(2)}) collective-permute-start(bf16[4,64,1024]{2,1,0:T(8,128)(2,1)} %copy-done.50), channel_id=1, source_target_pairs={{0,8},{1,9},{2,10},{3,11},{4,12},{5,13},{6,14},{7,15},{8,0},{9,1},... | collective-permute-start | bytes 1572872 | tf_op jit(solution)/shard_map/ppermute | solution.py:37
  66.0 25.6 %collective-permute-start.21 = (bf16[4,64,1024]{2,1,0:T(8,128)(2,1)}, bf16[4,64,1024]{2,1,0:T(8,128)(2,1)S(1)}, u32[]{:S(2)}, u32[]{:S(2)}) collective-permute-start(bf16[4,64,1024]{2,1,0:T(8,128)(2,1)} %copy-done.50), channel_id=1, source_target_pairs={{0,16},{1,17},{2,18},{3,19},{4,20},{5,21},{6,22},{7,23},{8,24},{9,... | collective-permute-start | bytes 1572872 | tf_op jit(solution)/shard_map/ppermute | solution.py:37
  67.3 24.3 %collective-permute-start.22 = (bf16[4,64,1024]{2,1,0:T(8,128)(2,1)}, bf16[4,64,1024]{2,1,0:T(8,128)(2,1)S(1)}, u32[]{:S(2)}, u32[]{:S(2)}) collective-permute-start(bf16[4,64,1024]{2,1,0:T(8,128)(2,1)} %copy-done.50), channel_id=1, source_target_pairs={{0,24},{1,25},{2,26},{3,27},{4,28},{5,29},{6,30},{7,31},{8,16},{9,... | collective-permute-start | bytes 1572872 | tf_op jit(solution)/shard_map/ppermute | solution.py:37
  91.9 15.5 %collective-permute-start.25 = (bf16[4,32,1024]{2,1,0:T(8,128)(2,1)S(1)}, bf16[4,32,1024]{2,1,0:T(8,128)(2,1)S(1)}, u32[]{:S(2)}, u32[]{:S(2)}) collective-permute-start(bf16[4,32,1024]{2,1,0:T(8,128)(2,1)S(1)} %shard_map.269.refs_0_), channel_id=1, source_target_pairs={{0,8},{1,9},{2,10},{3,11},{4,12},{5,13},{6,14},{7,15},{8,0},{9,1},... | collective-permute-start | bytes 786440 | tf_op jit(solution)/shard_map/ppermute | solution.py:37
  92.5 14.9 %collective-permute-start.26 = (bf16[4,32,1024]{2,1,0:T(8,128)(2,1)S(1)}, bf16[4,32,1024]{2,1,0:T(8,128)(2,1)S(1)}, u32[]{:S(2)}, u32[]{:S(2)}) collective-permute-start(bf16[4,32,1024]{2,1,0:T(8,128)(2,1)S(1)} %shard_map.269.refs_0_), channel_id=1, source_target_pairs={{0,16},{1,17},{2,18},{3,19},{4,20},{5,21},{6,22},{7,23},{8,24},{9,... | collective-permute-start | bytes 786440 | tf_op jit(solution)/shard_map/ppermute | solution.py:37
  93.9 13.5 %collective-permute-start.27 = (bf16[4,32,1024]{2,1,0:T(8,128)(2,1)S(1)}, bf16[4,32,1024]{2,1,0:T(8,128)(2,1)S(1)}, u32[]{:S(2)}, u32[]{:S(2)}) collective-permute-start(bf16[4,32,1024]{2,1,0:T(8,128)(2,1)S(1)} %shard_map.269.refs_0_), channel_id=1, source_target_pairs={{0,24},{1,25},{2,26},{3,27},{4,28},{5,29},{6,30},{7,31},{8,16},{9,... | collective-permute-start | bytes 786440 | tf_op jit(solution)/shard_map/ppermute | solution.py:37
  107.5 20.9 %collective-permute-start.28 = (bf16[16,32,1024]{2,1,0:T(8,128)(2,1)S(1)}, bf16[16,32,1024]{2,1,0:T(8,128)(2,1)}, u32[]{:S(2)}, u32[]{:S(2)}) collective-permute-start(bf16[16,32,1024]{2,1,0:T(8,128)(2,1)S(1)} %shard_map.270.refs_4_), channel_id=1, source_target_pairs={{0,1},{1,0},{2,3},{3,2},{4,5},{5,4},{6,7},{7,6},{8,9},{9,8},{10,11... | collective-permute-start | bytes 3145736 | tf_op jit(solution)/shard_map/ppermute | solution.py:37
  108.1 9.5 %collective-permute-start.29 = (bf16[128,1024]{1,0:T(8,128)(2,1)}, bf16[128,1024]{1,0:T(8,128)(2,1)}, u32[]{:S(2)}, u32[]{:S(2)}) collective-permute-start(bf16[128,1024]{1,0:T(8,128)(2,1)} %get-tuple-element.158.refs_0_), channel_id=1, source_target_pairs={{0,8},{1,9},{2,10},{3,11},{4,12},{5,13},{6,14},{7,15},{8,0},{9,1},... | collective-permute-start | bytes 786440 | tf_op jit(solution)/shard_map/ppermute | solution.py:37
  108.7 13.2 %collective-permute-start.31 = (bf16[128,1024]{1,0:T(8,128)(2,1)}, bf16[128,1024]{1,0:T(8,128)(2,1)}, u32[]{:S(2)}, u32[]{:S(2)}) collective-permute-start(bf16[128,1024]{1,0:T(8,128)(2,1)} %get-tuple-element.158.refs_0_), channel_id=1, source_target_pairs={{0,16},{1,17},{2,18},{3,19},{4,20},{5,21},{6,22},{7,23},{8,24},{9,... | collective-permute-start | bytes 786440 | tf_op jit(solution)/shard_map/ppermute | solution.py:37
  110.1 14.9 %collective-permute-start.33 = (bf16[128,1024]{1,0:T(8,128)(2,1)}, bf16[128,1024]{1,0:T(8,128)(2,1)}, u32[]{:S(2)}, u32[]{:S(2)}) collective-permute-start(bf16[128,1024]{1,0:T(8,128)(2,1)} %get-tuple-element.158.refs_0_), channel_id=1, source_target_pairs={{0,24},{1,25},{2,26},{3,27},{4,28},{5,29},{6,30},{7,31},{8,16},{9,... | collective-permute-start | bytes 786440 | tf_op jit(solution)/shard_map/ppermute | solution.py:37
  119.3 13.2 %collective-permute-start.30 = (bf16[128,1024]{1,0:T(8,128)(2,1)S(1)}, bf16[128,1024]{1,0:T(8,128)(2,1)S(1)}, u32[]{:S(2)}, u32[]{:S(2)}) collective-permute-start(bf16[128,1024]{1,0:T(8,128)(2,1)S(1)} %get-tuple-element.169), channel_id=1, source_target_pairs={{0,8},{1,9},{2,10},{3,11},{4,12},{5,13},{6,14},{7,15},{8,0},{9,1},... | collective-permute-start | bytes 786440 | tf_op jit(solution)/shard_map/ppermute | solution.py:37
  123.7 11.8 %collective-permute-start.32 = (bf16[128,1024]{1,0:T(8,128)(2,1)S(1)}, bf16[128,1024]{1,0:T(8,128)(2,1)S(1)}, u32[]{:S(2)}, u32[]{:S(2)}) collective-permute-start(bf16[128,1024]{1,0:T(8,128)(2,1)S(1)} %get-tuple-element.170), channel_id=1, source_target_pairs={{0,16},{1,17},{2,18},{3,19},{4,20},{5,21},{6,22},{7,23},{8,24},{9,... | collective-permute-start | bytes 786440 | tf_op jit(solution)/shard_map/ppermute | solution.py:37
  126.7 8.8 %collective-permute-start.34 = (bf16[128,1024]{1,0:T(8,128)(2,1)S(1)}, bf16[128,1024]{1,0:T(8,128)(2,1)S(1)}, u32[]{:S(2)}, u32[]{:S(2)}) collective-permute-start(bf16[128,1024]{1,0:T(8,128)(2,1)S(1)} %get-tuple-element.171), channel_id=1, source_target_pairs={{0,24},{1,25},{2,26},{3,27},{4,28},{5,29},{6,30},{7,31},{8,16},{9,... | collective-permute-start | bytes 786440 | tf_op jit(solution)/shard_map/ppermute | solution.py:37
  136.4 6.7 %collective-permute-start.35 = (bf16[128,1024]{1,0:T(8,128)(2,1)S(1)}, bf16[128,1024]{1,0:T(8,128)(2,1)S(1)}, u32[]{:S(2)}, u32[]{:S(2)}) collective-permute-start(bf16[128,1024]{1,0:T(8,128)(2,1)S(1)} %get-tuple-element.173.refs_0_.refs_12_), channel_id=1, source_target_pairs={{0,8},{1,9},{2,10},{3,11},{4,12},{5,13},{6,14},{7,15},{8,0},{9,1},... | collective-permute-start | bytes 786440 | tf_op jit(solution)/shard_map/ppermute | solution.py:37
  138.8 8.8 %collective-permute-start.37 = (bf16[128,1024]{1,0:T(8,128)(2,1)S(1)}, bf16[128,1024]{1,0:T(8,128)(2,1)S(1)}, u32[]{:S(2)}, u32[]{:S(2)}) collective-permute-start(bf16[128,1024]{1,0:T(8,128)(2,1)S(1)} %get-tuple-element.173.refs_0_.refs_12_), channel_id=1, source_target_pairs={{0,16},{1,17},{2,18},{3,19},{4,20},{5,21},{6,22},{7,23},{8,24},{9,... | collective-permute-start | bytes 786440 | tf_op jit(solution)/shard_map/ppermute | solution.py:37
  138.8 10.4 %collective-permute-start.39 = (bf16[128,1024]{1,0:T(8,128)(2,1)S(1)}, bf16[128,1024]{1,0:T(8,128)(2,1)S(1)}, u32[]{:S(2)}, u32[]{:S(2)}) collective-permute-start(bf16[128,1024]{1,0:T(8,128)(2,1)S(1)} %get-tuple-element.173.refs_0_.refs_12_), channel_id=1, source_target_pairs={{0,24},{1,25},{2,26},{3,27},{4,28},{5,29},{6,30},{7,31},{8,16},{9,... | collective-permute-start | bytes 786440 | tf_op jit(solution)/shard_map/ppermute | solution.py:37
  140.2 30.5 %collective-permute-start.44 = (bf16[5,128,1024]{2,1,0:T(8,128)(2,1)S(1)}, bf16[5,128,1024]{2,1,0:T(8,128)(2,1)S(1)}, u32[]{:S(2)}, u32[]{:S(2)}) collective-permute-start(bf16[5,128,1024]{2,1,0:T(8,128)(2,1)S(1)} %get-tuple-element.192.refs_0_), channel_id=1, source_target_pairs={{0,1},{1,0},{2,3},{3,2},{4,5},{5,4},{6,7},{7,6},{8,9},{9,8},{10,11... | collective-permute-start | bytes 3932168 | tf_op jit(solution)/shard_map/ppermute | solution.py:37
  144.6 10.9 %collective-permute-start.36 = (bf16[128,1024]{1,0:T(8,128)(2,1)S(1)}, bf16[128,1024]{1,0:T(8,128)(2,1)S(1)}, u32[]{:S(2)}, u32[]{:S(2)}) collective-permute-start(bf16[128,1024]{1,0:T(8,128)(2,1)S(1)} %get-tuple-element.181), channel_id=1, source_target_pairs={{0,8},{1,9},{2,10},{3,11},{4,12},{5,13},{6,14},{7,15},{8,0},{9,1},... | collective-permute-start | bytes 786440 | tf_op jit(solution)/shard_map/ppermute | solution.py:37
  149.1 11.1 %collective-permute-start.38 = (bf16[128,1024]{1,0:T(8,128)(2,1)S(1)}, bf16[128,1024]{1,0:T(8,128)(2,1)S(1)}, u32[]{:S(2)}, u32[]{:S(2)}) collective-permute-start(bf16[128,1024]{1,0:T(8,128)(2,1)S(1)} %get-tuple-element.183), channel_id=1, source_target_pairs={{0,16},{1,17},{2,18},{3,19},{4,20},{5,21},{6,22},{7,23},{8,24},{9,... | collective-permute-start | bytes 786440 | tf_op jit(solution)/shard_map/ppermute | solution.py:37
  150.7 9.5 %collective-permute-start.40 = (bf16[128,1024]{1,0:T(8,128)(2,1)S(1)}, bf16[128,1024]{1,0:T(8,128)(2,1)S(1)}, u32[]{:S(2)}, u32[]{:S(2)}) collective-permute-start(bf16[128,1024]{1,0:T(8,128)(2,1)S(1)} %get-tuple-element.185), channel_id=1, source_target_pairs={{0,24},{1,25},{2,26},{3,27},{4,28},{5,29},{6,30},{7,31},{8,16},{9,... | collective-permute-start | bytes 786440 | tf_op jit(solution)/shard_map/ppermute | solution.py:37
  179.1 40.0 %collective-permute-start.50 = (bf16[384,1024]{1,0:T(8,128)(2,1)}, bf16[384,1024]{1,0:T(8,128)(2,1)S(1)}, u32[]{:S(2)}, u32[]{:S(2)}) collective-permute-start(bf16[384,1024]{1,0:T(8,128)(2,1)} %copy-done.69), channel_id=1, source_target_pairs={{0,8},{1,9},{2,10},{3,11},{4,12},{5,13},{6,14},{7,15},{8,0},{9,1},... | collective-permute-start | bytes 2359304 | tf_op jit(solution)/shard_map/ppermute | solution.py:37
  180.1 39.0 %collective-permute-start.51 = (bf16[384,1024]{1,0:T(8,128)(2,1)}, bf16[384,1024]{1,0:T(8,128)(2,1)S(1)}, u32[]{:S(2)}, u32[]{:S(2)}) collective-permute-start(bf16[384,1024]{1,0:T(8,128)(2,1)} %copy-done.68), channel_id=1, source_target_pairs={{0,16},{1,17},{2,18},{3,19},{4,20},{5,21},{6,22},{7,23},{8,24},{9,... | collective-permute-start | bytes 2359304 | tf_op jit(solution)/shard_map/ppermute | solution.py:37
  181.3 37.8 %collective-permute-start.52 = (bf16[384,1024]{1,0:T(8,128)(2,1)}, bf16[384,1024]{1,0:T(8,128)(2,1)S(1)}, u32[]{:S(2)}, u32[]{:S(2)}) collective-permute-start(bf16[384,1024]{1,0:T(8,128)(2,1)} %copy-done.67), channel_id=1, source_target_pairs={{0,24},{1,25},{2,26},{3,27},{4,28},{5,29},{6,30},{7,31},{8,16},{9,... | collective-permute-start | bytes 2359304 | tf_op jit(solution)/shard_map/ppermute | solution.py:37
  189.1 7.6 %collective-permute-start.46 = (f32[8,1024]{1,0:T(8,128)S(1)}, f32[8,1024]{1,0:T(8,128)S(1)}, u32[]{:S(2)}, u32[]{:S(2)}) collective-permute-start(f32[8,1024]{1,0:T(8,128)S(1)} %shard_map.284), channel_id=1, source_target_pairs={{4,0},{5,1},{6,2},{7,3},{12,8},{13,9},{14,10},{15,11},{20,16},{21,... | collective-permute-start | bytes 98312 | tf_op jit(solution)/shard_map/ppermute | solution.py:37
  202.0 17.5 %collective-permute-start.48 = (bf16[2,128,1024]{2,1,0:T(8,128)(2,1)S(1)}, bf16[2,128,1024]{2,1,0:T(8,128)(2,1)S(1)}, u32[]{:S(2)}, u32[]{:S(2)}) collective-permute-start(bf16[2,128,1024]{2,1,0:T(8,128)(2,1)S(1)} %shard_map.288.refs_0_.refs_2_), channel_id=1, source_target_pairs={{0,1},{1,0},{2,3},{3,2},{4,5},{5,4},{6,7},{7,6},{8,9},{9,8},{10,11... | collective-permute-start | bytes 1572872 | tf_op jit(solution)/shard_map/ppermute | solution.py:37
  220.3 27.5 %collective-permute-start.53 = (bf16[288,1024]{1,0:T(8,128)(2,1)S(1)}, bf16[288,1024]{1,0:T(8,128)(2,1)S(1)}, u32[]{:S(2)}, u32[]{:S(2)}) collective-permute-start(bf16[288,1024]{1,0:T(8,128)(2,1)S(1)} %get-tuple-element.222), channel_id=1, source_target_pairs={{0,8},{1,9},{2,10},{3,11},{4,12},{5,13},{6,14},{7,15},{8,0},{9,1},... | collective-permute-start | bytes 1769480 | tf_op jit(solution)/shard_map/ppermute | solution.py:37
  221.4 26.7 %collective-permute-start.54 = (bf16[288,1024]{1,0:T(8,128)(2,1)S(1)}, bf16[288,1024]{1,0:T(8,128)(2,1)S(1)}, u32[]{:S(2)}, u32[]{:S(2)}) collective-permute-start(bf16[288,1024]{1,0:T(8,128)(2,1)S(1)} %get-tuple-element.223), channel_id=1, source_target_pairs={{0,16},{1,17},{2,18},{3,19},{4,20},{5,21},{6,22},{7,23},{8,24},{9,... | collective-permute-start | bytes 1769480 | tf_op jit(solution)/shard_map/ppermute | solution.py:37
  222.6 26.8 %collective-permute-start.55 = (bf16[288,1024]{1,0:T(8,128)(2,1)S(1)}, bf16[288,1024]{1,0:T(8,128)(2,1)S(1)}, u32[]{:S(2)}, u32[]{:S(2)}) collective-permute-start(bf16[288,1024]{1,0:T(8,128)(2,1)S(1)} %get-tuple-element.224), channel_id=1, source_target_pairs={{0,24},{1,25},{2,26},{3,27},{4,28},{5,29},{6,30},{7,31},{8,16},{9,... | collective-permute-start | bytes 1769480 | tf_op jit(solution)/shard_map/ppermute | solution.py:37
  223.9 18.9 %collective-permute-start.56 = (bf16[192,1024]{1,0:T(8,128)(2,1)S(1)}, bf16[192,1024]{1,0:T(8,128)(2,1)S(1)}, u32[]{:S(2)}, u32[]{:S(2)}) collective-permute-start(bf16[192,1024]{1,0:T(8,128)(2,1)S(1)} %shard_map.293), channel_id=1, source_target_pairs={{0,4},{1,5},{2,6},{3,7},{4,0},{5,1},{6,2},{7,3},{8,12},{9,13},{10,... | collective-permute-start | bytes 1179656 | tf_op jit(solution)/shard_map/ppermute | solution.py:37
  243.5 16.0 %collective-permute-start.60 = (bf16[96,1024]{1,0:T(8,128)(2,1)}, bf16[96,1024]{1,0:T(8,128)(2,1)S(1)}, u32[]{:S(2)}, u32[]{:S(2)}) collective-permute-start(bf16[96,1024]{1,0:T(8,128)(2,1)} %get-tuple-element.237), channel_id=1, source_target_pairs={{0,2},{1,3},{2,0},{3,1},{4,6},{5,7},{6,4},{7,5},{8,10},{9,11},{10,... | collective-permute-start | bytes 589832 | tf_op jit(solution)/shard_map/ppermute | solution.py:37
  250.2 10.1 %collective-permute-start.57 = (bf16[96,1024]{1,0:T(8,128)(2,1)}, bf16[96,1024]{1,0:T(8,128)(2,1)S(1)}, u32[]{:S(2)}, u32[]{:S(2)}) collective-permute-start(bf16[96,1024]{1,0:T(8,128)(2,1)} %get-tuple-element.231), channel_id=1, source_target_pairs={{0,2},{1,3},{2,0},{3,1},{4,6},{5,7},{6,4},{7,5},{8,10},{9,11},{10,... | collective-permute-start | bytes 589832 | tf_op jit(solution)/shard_map/ppermute | solution.py:37
  252.9 14.1 %collective-permute-start.58 = (bf16[96,1024]{1,0:T(8,128)(2,1)}, bf16[96,1024]{1,0:T(8,128)(2,1)S(1)}, u32[]{:S(2)}, u32[]{:S(2)}) collective-permute-start(bf16[96,1024]{1,0:T(8,128)(2,1)} %get-tuple-element.232), channel_id=1, source_target_pairs={{0,4},{1,5},{2,6},{3,7},{4,0},{5,1},{6,2},{7,3},{8,12},{9,13},{10,... | collective-permute-start | bytes 589832 | tf_op jit(solution)/shard_map/ppermute | solution.py:37
  252.9 18.7 %collective-permute-start.59 = (bf16[96,1024]{1,0:T(8,128)(2,1)}, bf16[96,1024]{1,0:T(8,128)(2,1)S(1)}, u32[]{:S(2)}, u32[]{:S(2)}) collective-permute-start(bf16[96,1024]{1,0:T(8,128)(2,1)} %get-tuple-element.233), channel_id=1, source_target_pairs={{0,6},{1,7},{2,4},{3,5},{4,2},{5,3},{6,0},{7,1},{8,14},{9,15},{10,... | collective-permute-start | bytes 589832 | tf_op jit(solution)/shard_map/ppermute | solution.py:37
  256.1 16.2 %all-to-all-start = ((bf16[4,32,1024]{2,1,0:T(8,128)(2,1)}), bf16[4,32,1024]{2,1,0:T(8,128)(2,1)S(1)}, u32[]{:S(2)}, u32[]{:S(2)}) async-start(bf16[4,32,1024]{2,1,0:T(8,128)(2,1)} %shard_map.298), calls=%async_computation.1 | async-start | bytes 524288 | tf_op jit(solution)/shard_map/all_to_all | solution.py:1239
  (86 other events, 630.2 us)
Sparse Core Ops, SparseCore 0:
  61.7 46.7 all-gather.1
  179.2 47.0 reduce-scatter.1

commit v6 on v5

--- a/solution.py
+++ b/solution.py
@@ -435,36 +435,74 @@
     )[0]
 
 
-def split_parts(x):
-    high = x.astype(LOW)
-    return [high, (x - high.astype(FULL)).astype(LOW)]
+def columns_at(x, start, count, plain):
+    width = x.shape[1]
+    if plain:
+        return jnp.roll(x, -start, 1)[:, :count]
+    return pltpu.roll(x, (width - start) & (width - 1), 1)[:, :count]
+
+
+def pack_vectors(x, width):
+    count = width // x.shape[1]
+    high = x.astype(LOW).astype(FULL)
+    rows = [
+        jnp.concatenate([part[i + j : i + j + 1] for j in range(count)], axis=1)
+        for part in (high, x - high)
+        for i in range(0, 16, count)
+    ]
+    return stack_rows(rows, 16).astype(LOW)
+
+
+def unpack_vectors(x, columns):
+    x = x.astype(FULL)
+    count = x.shape[1] // columns
+    height = 16 // count
+    x = x[:height] + x[height : 2 * height]
+    return stack_rows(
+        [
+            x[i // count : i // count + 1, i % count * columns : (i % count + 1) * columns]
+            for i in range(16)
+        ],
+        16,
+    )
 
 
 def add_batch(own, got, count, plain, after=(), vectors=None):
-    depth = lax.axis_size("seq") // 2
-    height, width = own.shape
-    extra = 32 if vectors is not None else 0
-    height -= extra
+    batch, cols = sizes()
+    depth = cols // 2
+    width = own.shape[1]
+    extra = 16 if vectors is not None else 0
+    height = own.shape[0] - extra
     part = height // (count * depth)
+    columns = width // batch
+    few = min(LANES, columns)
+    each = columns // cols
     inputs = [own, *got] + ([vectors] if extra else [])
 
     def body(own, *got):
         got, sums = (got[:-1], got[-1]) if extra else (got, None)
-        got = [x.astype(FULL) for x in got]
-        total = sum((x[:height] for x in got), own[:height].astype(FULL))
+        total = sum((x[:height].astype(FULL) for x in got), own[:height].astype(FULL))
         blocks = [
             [total[(i * depth + k) * part : (i * depth + k + 1) * part] for i in range(count)]
             for k in range(depth)
         ]
         first, rest = blocks[0], [[x.astype(LOW) for x in block] for block in blocks[1:]]
+        results = [jnp.concatenate(first, axis=0)]
         if extra:
-            sums = sum((x[height : height + 16] + x[height + 16 :] for x in got), sums)
-            first, rest = first + [sums], [block + split_parts(sums) for block in rest]
-        return [jnp.concatenate(x, axis=0) for x in [first, *rest]]
+            b, z, core = places()
+            sums = columns_at(sums, b * columns, columns, plain)
+            sums = sum((unpack_vectors(x[height:], columns) for x in got), sums)
+            cuts = [
+                columns_at(sums, ((z ^ k) * 2 + core) * each, few, plain) for k in range(depth)
+            ]
+            rest = [block + [pack_vectors(x, width)] for block, x in zip(rest, cuts[1:], strict=True)]
+            results.append(cuts[0])
+        return results + [jnp.concatenate(x, axis=0) for x in rest]
 
     return fuse(
         body,
-        [((count * part + extra // 2, width), FULL)]
+        [((count * part, width), FULL)]
+        + [((16, few), FULL)] * (extra > 0)
         + [((count * part + extra, width), LOW)] * (depth - 1),
         *inputs,
         after=after,
@@ -473,22 +511,27 @@
     )
 
 
-def add_depth(pieces, count, part, outs, last, plain, after=()):
-    width = pieces[0].shape[1]
+def add_depth(own, pieces, count, part, plain, vectors=None, outs=(), last=None):
     height = count * part
-    got = [to_depth(pieces[k], k) for k in range(1, len(pieces))]
+    got = [to_depth(piece, k + 1) for k, piece in enumerate(pieces)]
 
     def body(own, *got):
-        got = [x.astype(FULL) for x in got]
-        total = sum((x[:height] for x in got), own[:height])
+        sums = None
+        if last is not None:
+            sums, got = got[0], got[1:]
+        total = sum((x[:height].astype(FULL) for x in got), own)
         results = [total[i * part : (i + 1) * part] for i in range(count)]
         if last is not None:
-            sums = sum((x[height : height + 16] + x[height + 16 :] for x in got), own[height:])
-            results += last(sums)
+            results += last(sum((unpack_vectors(x[height:], sums.shape[1]) for x in got), sums))
         return results
 
     return fuse(
-        body, [((part, width), FULL)] * count + outs, pieces[0], *got, after=after, plain=plain
+        body,
+        [((part, own.shape[1]), FULL)] * count + list(outs),
+        own,
+        *([vectors] if last is not None else []),
+        *got,
+        plain=plain,
     )
 
 
@@ -958,10 +1001,10 @@
             jnp.concatenate([grad, grad_got], axis=0),
         ).astype(LOW)
 
-    def cut(terms, *more):
+    def cut(terms):
         part = half // rows
         return [
-            jnp.concatenate([term[k * part : (k + 1) * part] for term in terms] + list(more), axis=0)
+            jnp.concatenate([term[k * part : (k + 1) * part] for term in terms], axis=0)
             for k in range(rows)
         ]
 
@@ -1194,12 +1237,19 @@
         *early_pieces, early_half = halve_depth(early_pieces, plain)
 
     def late_terms(sides, sides_got, grads, grads_got, sums):
+        b = places()[0]
         terms = [paired(sides[i], sides_got[i], grads[i], grads_got[i]) for i in range(2)]
-        return cut(terms, *split_parts(sums))
+        columns = width // rows
+        return [
+            jnp.concatenate(
+                [x, pack_vectors(columns_at(sums, (b ^ k) * columns, columns, plain), width)], axis=0
+            )
+            for k, x in enumerate(cut(terms))
+        ]
 
     late = fuse(
         late_terms,
-        [((2 * half // rows + 32, width), LOW)] * rows,
+        [((2 * half // rows + 16, width), LOW)] * rows,
         sides,
         sides_got,
         grad_late,
@@ -1209,24 +1259,24 @@
         plain=plain,
     )
     late_got = [to_batch(late[k], k) for k in range(1, rows)]
-    def own_columns(total):
-        b, z, core = places()
-        device = b * cols + z * 2 + core
-        if plain:
-            total = lax.dynamic_slice(total, (0, device * own), (16, own))
-        else:
-            total = pltpu.roll(total, (width - device * own) & (width - 1), 1)[:, :own]
-        return [total[0:2], total[2:4], total[4:9], total[9:10], total[10:11]]
-
-    *late_pieces, late_token = add_batch(late[0], late_got, 2, plain, (early_half,), vectors=sums)
-    output_grad, recept_grad, gate_grad = add_depth(early_pieces, 3, own, [], None, plain)
+    def own_columns(x):
+        return [x[0:2, :own], x[2:4, :own], x[4:9, :own], x[9:10, :own], x[10:11, :own]]
+
+    late_own, late_sums, *late_pieces, late_token = add_batch(
+        late[0], late_got, 2, plain, (early_half,), vectors=sums
+    )
+    output_grad, recept_grad, gate_grad = add_depth(
+        early_pieces[0], early_pieces[1:], 3, own, plain
+    )
     key_grad, value_grad, gains_grad, offsets_grad, mixes_grad, decay_grad, first_grad = add_depth(
+        late_own,
         late_pieces,
         2,
         own,
+        plain,
+        late_sums,
         [((2, own), FULL), ((2, own), FULL), ((5, own), FULL), ((1, own), FULL), ((1, own), FULL)],
         own_columns,
-        plain,
     )
 
     (crossed,) = fuse(

time: 281 us -> 282 us (level)
  no operation moved by 1% of the time
where the time goes in v6:
time: 282 us; the launch traced here: 281 us
  waiting for transfers between devices  97.4 us (35%)
  starting transfers between devices  88.3 us (31%)
  Pallas kernels  48.9 us (17%)
  local copies, waits for them, and re-layouts  31.1 us (11%)
  between operations  15 us (5%)
    ppermute x61, waiting for transfers between devices, send(): return lax.ppermute(block, BOTH, pairs)  97.4 us
    ppermute x61, starting transfers between devices, send(): return lax.ppermute(block, BOTH, pairs)  84.9 us
    pallas_call x44, Pallas kernels, fuse(): pl.pallas_call(kernel, out_shape=tuple((jax.ShapeDtypeStruct(shape, dtype...  47.6 us
    unnamed x140, local copies, waits for them, and re-layouts  31.1 us
  transfers between devices with their start and end apart: 64, of which 28 were waited for; matrix products, arithmetic and copies ran while one was open for 0% of the time, Pallas kernels for 14%

profile of v6, /device:TPU:8, one launch (start us, length us, event | category | flops | bytes accessed | tf_op | source)
XLA Modules:
  0.0 280.9 jit_solution(3110084571602064253)
XLA Ops:
  7.2 2.3 shard_map.254
  9.7 3.0 %collective-permute-start.2 = (bf16[80,1024]{1,0:T(8,128)(2,1)}, bf16[80,1024]{1,0:T(8,128)(2,1)S(1)}, u32[]{:S(2)}, u32[]{:S(2)}) collective-permute-start(bf16[80,1024]{1,0:T(8,128)(2,1)} %get-tuple-element.141.refs_1_), channel_id=1, source_target_pairs={{0,4},{1,5},{2,6},{3,7},{4,0},{5,1},{6,2},{7,3},{8,12},{9,13},{10,... | collective-permute-start | bytes 491528 | tf_op jit(solution)/shard_map/ppermute | solution.py:37
  13.2 1.9 collective-permute-start
  16.6 6.5 %collective-permute-done.refs_1_ = f32[16,1024]{1,0:T(8,128)S(1)} collective-permute-done((f32[16,1024]{1,0:T(8,128)}, f32[16,1024]{1,0:T(8,128)S(1)}, u32[]{:S(2)}, u32[]{:S(2)}) %collective-permute-start) | collective-permute-done | bytes 65568 | tf_op jit(solution)/shard_map/ppermute | solution.py:37
  35.5 8.4 %collective-permute-start.18 = (bf16[96,1024]{1,0:T(8,128)(2,1)S(1)}, bf16[96,1024]{1,0:T(8,128)(2,1)S(1)}, u32[]{:S(2)}, u32[]{:S(2)}) collective-permute-start(bf16[96,1024]{1,0:T(8,128)(2,1)S(1)} %get-tuple-element.153.refs_5_), channel_id=1, source_target_pairs={{0,4},{1,5},{2,6},{3,7},{4,0},{5,1},{6,2},{7,3},{8,12},{9,13},{10,... | collective-permute-start | bytes 589832 | tf_op jit(solution)/shard_map/ppermute | solution.py:37
  44.0 5.5 %collective-permute-start.19 = (bf16[96,1024]{1,0:T(8,128)(2,1)S(1)}, bf16[96,1024]{1,0:T(8,128)(2,1)S(1)}, u32[]{:S(2)}, u32[]{:S(2)}) collective-permute-start(bf16[96,1024]{1,0:T(8,128)(2,1)S(1)} %get-tuple-element.153.refs_5_), channel_id=1, source_target_pairs={{0,6},{1,7},{2,4},{3,5},{4,2},{5,3},{6,0},{7,1},{8,14},{9,15},{10,... | collective-permute-start | bytes 589832 | tf_op jit(solution)/shard_map/ppermute | solution.py:37
  49.4 5.5 %collective-permute-done.18.refs_7_ = bf16[96,1024]{1,0:T(8,128)(2,1)S(1)} collective-permute-done((bf16[96,1024]{1,0:T(8,128)(2,1)S(1)}, bf16[96,1024]{1,0:T(8,128)(2,1)S(1)}, u32[]{:S(2)}, u32[]{:S(2)}) %collective-permute-start.18) | collective-permute-done | bytes 196640 | tf_op jit(solution)/shard_map/ppermute | solution.py:37
  54.9 3.4 %collective-permute-done.19.refs_8_ = bf16[96,1024]{1,0:T(8,128)(2,1)S(1)} collective-permute-done((bf16[96,1024]{1,0:T(8,128)(2,1)S(1)}, bf16[96,1024]{1,0:T(8,128)(2,1)S(1)}, u32[]{:S(2)}, u32[]{:S(2)}) %collective-permute-start.19) | collective-permute-done | bytes 196640 | tf_op jit(solution)/shard_map/ppermute | solution.py:37
  61.6 2.5 collective-permute-start.10
  74.4 2.0 copy-done.11
  77.7 1.9 collective-permute-start.15
  79.7 4.6 %collective-permute-done.15.refs_1_.refs_3_ = f32[8,1024]{1,0:T(8,128)S(1)} collective-permute-done((f32[8,1024]{1,0:T(8,128)S(1)}, f32[8,1024]{1,0:T(8,128)S(1)}, u32[]{:S(2)}, u32[]{:S(2)}) %collective-permute-start.15) | collective-permute-done | bytes 32800 | tf_op jit(solution)/shard_map/ppermute | solution.py:37
  85.6 2.5 collective-permute-done.16.refs_4_
  88.2 3.4 %collective-permute-done.21.refs_2_ = bf16[4,64,1024]{2,1,0:T(8,128)(2,1)S(1)} collective-permute-done((bf16[4,64,1024]{2,1,0:T(8,128)(2,1)}, bf16[4,64,1024]{2,1,0:T(8,128)(2,1)S(1)}, u32[]{:S(2)}, u32[]{:S(2)}) %collective-permute-start.21) | collective-permute-done | bytes 524320 | tf_op jit(solution)/shard_map/ppermute | solution.py:37
  99.8 2.1 collective-permute-start.24
  101.9 3.8 %collective-permute-done.24.refs_1_ = f32[8,1024]{1,0:T(8,128)S(1)} collective-permute-done((f32[8,1024]{1,0:T(8,128)S(1)}, f32[8,1024]{1,0:T(8,128)S(1)}, u32[]{:S(2)}, u32[]{:S(2)}) %collective-permute-start.24) | collective-permute-done | bytes 32800 | tf_op jit(solution)/shard_map/ppermute | solution.py:37
  111.7 2.2 copy-done.10
  114.1 3.5 %collective-permute-done.29.refs_0_.refs_1_ = bf16[128,1024]{1,0:T(8,128)(2,1)} collective-permute-done((bf16[128,1024]{1,0:T(8,128)(2,1)}, bf16[128,1024]{1,0:T(8,128)(2,1)}, u32[]{:S(2)}, u32[]{:S(2)}) %collective-permute-start.29) | collective-permute-done | bytes 262176 | tf_op jit(solution)/shard_map/ppermute | solution.py:37
  120.1 1.9 collective-permute-done.31.refs_0_.refs_2_
  126.7 1.8 collective-permute-start.34
  128.5 2.1 shard_map.271
  130.7 2.0 shard_map.268
  132.7 2.9 %collective-permute-done.32.refs_5_ = bf16[128,1024]{1,0:T(8,128)(2,1)S(1)} collective-permute-done((bf16[128,1024]{1,0:T(8,128)(2,1)S(1)}, bf16[128,1024]{1,0:T(8,128)(2,1)S(1)}, u32[]{:S(2)}, u32[]{:S(2)}) %collective-permute-start.32) | collective-permute-done | bytes 262176 | tf_op jit(solution)/shard_map/ppermute | solution.py:37
  136.5 2.4 collective-permute-start.35
  140.3 2.9 %collective-permute-done.35.refs_0_.refs_13_ = bf16[128,1024]{1,0:T(8,128)(2,1)S(1)} collective-permute-done((bf16[128,1024]{1,0:T(8,128)(2,1)S(1)}, bf16[128,1024]{1,0:T(8,128)(2,1)S(1)}, u32[]{:S(2)}, u32[]{:S(2)}) %collective-permute-start.35) | collective-permute-done | bytes 262176 | tf_op jit(solution)/shard_map/ppermute | solution.py:37
  144.7 2.1 collective-permute-start.36
  151.9 3.5 %shard_map.276 = (bf16[128,1024]{1,0:T(8,128)(2,1)S(1)}, f32[128,1024]{1,0:T(8,128)S(1)}, f32[128,1024]{1,0:T(8,128)S(1)}) custom-call(bf16[128,1024]{1,0:T(8,128)(2,1)S(1)} %get-tuple-element.174.refs_0_.refs_12_, bf16[128,1024]{1,0:T(8,128)(2,1)S(1)} %get-tuple-element.175.refs_1_.refs_8_, bf16[1024,1024]{1,0:T(8,128)(2,1)S(1)} %get-tuple-element.161.refs_1_.refs_2_, ...), custom_call_target="tpu_custom_call" | custom-call | flops 2000000 | bytes 2000000 | tf_op jit(solution)/shard_map/pallas_call | solution.py:86
  155.5 4.8 %collective-permute-done.38.refs_6_ = bf16[128,1024]{1,0:T(8,128)(2,1)S(1)} collective-permute-done((bf16[128,1024]{1,0:T(8,128)(2,1)S(1)}, bf16[128,1024]{1,0:T(8,128)(2,1)S(1)}, u32[]{:S(2)}, u32[]{:S(2)}) %collective-permute-start.38) | collective-permute-done | bytes 262176 | tf_op jit(solution)/shard_map/ppermute | solution.py:37
  161.0 2.1 collective-permute-start.41
  164.5 2.6 shard_map.281
  167.1 1.7 collective-permute-start.45
  168.9 1.9 collective-permute-done.42.refs_1_
  172.8 4.3 %shard_map.285 = (bf16[2048,1024]{1,0:T(8,128)(2,1)S(1)}, f32[8,128]{1,0:T(8,128)S(1)}) custom-call(bf16[128,1024]{1,0:T(8,128)(2,1)} %get-tuple-element.159.refs_0_, bf16[128,1024]{1,0:T(8,128)(2,1)} %collective-permute-done.29.refs_0_.refs_1_, bf16[128,1024]{1,0:T(8,128)(2,1)} %collective-permute-done.31.refs_0_.refs_2_, ...), custom_call_target="tpu_custom_call" | custom-call | flops 2000000 | bytes 2000000 | tf_op jit(solution)/shard_map/pallas_call | solution.py:86
  177.2 2.1 copy-done.9
  182.8 4.0 %collective-permute-start.43 = (f32[8,1024]{1,0:T(8,128)S(1)}, f32[8,1024]{1,0:T(8,128)S(1)}, u32[]{:S(2)}, u32[]{:S(2)}) collective-permute-start(f32[8,1024]{1,0:T(8,128)S(1)} %shard_map.282.refs_4_.refs_0_), channel_id=1, source_target_pairs={{2,0},{3,1},{4,2},{5,3},{6,4},{7,5},{10,8},{11,9},{12,10},{13,11},... | collective-permute-start | bytes 98312 | tf_op jit(solution)/shard_map/ppermute | solution.py:37
  186.9 2.4 collective-permute-done.43.refs_1_.refs_3_
  190.6 6.3 %collective-permute-done.46.refs_4_ = f32[8,1024]{1,0:T(8,128)S(1)} collective-permute-done((f32[8,1024]{1,0:T(8,128)S(1)}, f32[8,1024]{1,0:T(8,128)S(1)}, u32[]{:S(2)}, u32[]{:S(2)}) %collective-permute-start.46) | collective-permute-done | bytes 32800 | tf_op jit(solution)/shard_map/ppermute | solution.py:37
  205.5 3.3 %shard_map.289 = (f32[128,1024]{1,0:T(8,128)S(1)}, f32[128,1024]{1,0:T(8,128)S(1)}, f32[8,1024]{1,0:T(8,128)S(1)}, f32[8,1024]{1,0:T(8,128)S(1)}) custom-call(bf16[2,128,1024]{2,1,0:T(8,128)(2,1)S(1)} %shard_map.288.refs_0_.refs_2_, bf16[3,128,1024]{2,1,0:T(8,128)(2,1)S(1)} %get-tuple-element.194.refs_2_.refs_1_, bf16[2,1024,1024]{2,1,0:T(8,128)(2,1)S(1)} %copy-done.12, ...), custom_call_target="tpu_custom_call" | custom-call | flops 2000000 | bytes 2000000 | tf_op jit(solution)/shard_map/pallas_call | solution.py:86
  208.8 3.2 %collective-permute-start.47 = (f32[8,1024]{1,0:T(8,128)S(1)}, f32[8,1024]{1,0:T(8,128)S(1)}, u32[]{:S(2)}, u32[]{:S(2)}) collective-permute-start(f32[8,1024]{1,0:T(8,128)S(1)} %get-tuple-element.210), channel_id=1, source_target_pairs={{1,0},{2,1},{3,2},{4,3},{5,4},{6,5},{7,6},{9,8},{10,9},{11,10},{12... | collective-permute-start | bytes 98312 | tf_op jit(solution)/shard_map/ppermute | solution.py:37
  212.0 2.1 collective-permute-done.47.refs_2_
  214.1 3.9 %shard_map.290 = (f32[128,1024]{1,0:T(8,128)}, f32[16,1024]{1,0:T(8,128)S(1)}) custom-call(f32[128,1024]{1,0:T(8,128)S(1)} %get-tuple-element.208.refs_0_, f32[128,1024]{1,0:T(8,128)S(1)} %get-tuple-element.209.refs_1_, f32[8,1024]{1,0:T(8,128)S(1)} %collective-permute-done.47.refs_2_, f32[128,1024]{1,0:T(8,128)S(1)} %copy-done.25, ...), custom_call_target="tpu_custom_call" | custom-call | flops 2000000 | bytes 2000000 | tf_op jit(solution)/shard_map/pallas_call | solution.py:86
  224.2 18.7 %collective-permute-done.56.refs_2_ = bf16[192,1024]{1,0:T(8,128)(2,1)S(1)} collective-permute-done((bf16[192,1024]{1,0:T(8,128)(2,1)S(1)}, bf16[192,1024]{1,0:T(8,128)(2,1)S(1)}, u32[]{:S(2)}, u32[]{:S(2)}) %collective-permute-start.56) | collective-permute-done | bytes 393248 | tf_op jit(solution)/shard_map/ppermute | solution.py:37
  243.0 4.3 %collective-permute-start.60 = (bf16[96,1024]{1,0:T(8,128)(2,1)S(1)}, bf16[96,1024]{1,0:T(8,128)(2,1)S(1)}, u32[]{:S(2)}, u32[]{:S(2)}) collective-permute-start(bf16[96,1024]{1,0:T(8,128)(2,1)S(1)} %get-tuple-element.239), channel_id=1, source_target_pairs={{0,2},{1,3},{2,0},{3,1},{4,6},{5,7},{6,4},{7,5},{8,10},{9,11},{10,... | collective-permute-start | bytes 589832 | tf_op jit(solution)/shard_map/ppermute | solution.py:37
  250.5 3.4 %all-to-all-start = ((bf16[4,32,1024]{2,1,0:T(8,128)(2,1)}), bf16[4,32,1024]{2,1,0:T(8,128)(2,1)S(1)}, u32[]{:S(2)}, u32[]{:S(2)}) async-start(bf16[4,32,1024]{2,1,0:T(8,128)(2,1)} %shard_map.298), calls=%async_computation.1 | async-start | bytes 524288 | tf_op jit(solution)/shard_map/all_to_all | solution.py:1289
  253.9 2.7 collective-permute-start.57
  258.9 2.7 collective-permute-done.57.refs_2_
  261.6 6.6 %collective-permute-done.58.refs_3_ = bf16[80,1024]{1,0:T(8,128)(2,1)S(1)} collective-permute-done((bf16[80,1024]{1,0:T(8,128)(2,1)S(1)}, bf16[80,1024]{1,0:T(8,128)(2,1)S(1)}, u32[]{:S(2)}, u32[]{:S(2)}) %collective-permute-start.58) | collective-permute-done | bytes 163872 | tf_op jit(solution)/shard_map/ppermute | solution.py:37
  268.2 4.1 %collective-permute-done.59.refs_4_ = bf16[80,1024]{1,0:T(8,128)(2,1)S(1)} collective-permute-done((bf16[80,1024]{1,0:T(8,128)(2,1)S(1)}, bf16[80,1024]{1,0:T(8,128)(2,1)S(1)}, u32[]{:S(2)}, u32[]{:S(2)}) %collective-permute-start.59) | collective-permute-done | bytes 163872 | tf_op jit(solution)/shard_map/ppermute | solution.py:37
  (269 shorter events, 91.9 us)
Async XLA Ops:
  7.2 104.5 %all-gather.2.cloned.1.call-start = ((), (), s32[]{:S(2)}) async-start(), calls=%async_computation.2 | async-start | bytes 4718592 | tf_op jit(solution)/shard_map/all_gather | solution.py:738
  9.6 20.4 %collective-permute-start.1 = (bf16[80,1024]{1,0:T(8,128)(2,1)}, bf16[80,1024]{1,0:T(8,128)(2,1)S(1)}, u32[]{:S(2)}, u32[]{:S(2)}) collective-permute-start(bf16[80,1024]{1,0:T(8,128)(2,1)} %get-tuple-element.141.refs_1_), channel_id=1, source_target_pairs={{0,2},{1,3},{2,0},{3,1},{4,6},{5,7},{6,4},{7,5},{8,10},{9,11},{10,... | collective-permute-start | bytes 491528 | tf_op jit(solution)/shard_map/ppermute | solution.py:37
  9.7 20.4 %collective-permute-start.2 = (bf16[80,1024]{1,0:T(8,128)(2,1)}, bf16[80,1024]{1,0:T(8,128)(2,1)S(1)}, u32[]{:S(2)}, u32[]{:S(2)}) collective-permute-start(bf16[80,1024]{1,0:T(8,128)(2,1)} %get-tuple-element.141.refs_1_), channel_id=1, source_target_pairs={{0,4},{1,5},{2,6},{3,7},{4,0},{5,1},{6,2},{7,3},{8,12},{9,13},{10,... | collective-permute-start | bytes 491528 | tf_op jit(solution)/shard_map/ppermute | solution.py:37
  12.7 17.3 %collective-permute-start.3 = (bf16[80,1024]{1,0:T(8,128)(2,1)}, bf16[80,1024]{1,0:T(8,128)(2,1)S(1)}, u32[]{:S(2)}, u32[]{:S(2)}) collective-permute-start(bf16[80,1024]{1,0:T(8,128)(2,1)} %get-tuple-element.141.refs_1_), channel_id=1, source_target_pairs={{0,6},{1,7},{2,4},{3,5},{4,2},{5,3},{6,0},{7,1},{8,14},{9,15},{10,... | collective-permute-start | bytes 491528 | tf_op jit(solution)/shard_map/ppermute | solution.py:37
  13.2 10.0 %collective-permute-start = (f32[16,1024]{1,0:T(8,128)}, f32[16,1024]{1,0:T(8,128)S(1)}, u32[]{:S(2)}, u32[]{:S(2)}) collective-permute-start(f32[16,1024]{1,0:T(8,128)} %get-tuple-element.133), channel_id=1, source_target_pairs={{0,1},{1,2},{2,3},{3,4},{4,5},{5,6},{6,7},{8,9},{9,10},{10,11},{11... | collective-permute-start | bytes 196616 | tf_op jit(solution)/shard_map/ppermute | solution.py:37
  15.1 9.6 %collective-permute-start.4 = (bf16[32,1024]{1,0:T(8,128)(2,1)}, bf16[32,1024]{1,0:T(8,128)(2,1)S(1)}, u32[]{:S(2)}, u32[]{:S(2)}) collective-permute-start(bf16[32,1024]{1,0:T(8,128)(2,1)} %get-tuple-element.142), channel_id=1, source_target_pairs={{0,8},{1,9},{2,10},{3,11},{4,12},{5,13},{6,14},{7,15},{8,0},{9,1},... | collective-permute-start | bytes 196616 | tf_op jit(solution)/shard_map/ppermute | solution.py:37
  23.1 6.8 %collective-permute-start.5 = (bf16[32,1024]{1,0:T(8,128)(2,1)}, bf16[32,1024]{1,0:T(8,128)(2,1)S(1)}, u32[]{:S(2)}, u32[]{:S(2)}) collective-permute-start(bf16[32,1024]{1,0:T(8,128)(2,1)} %get-tuple-element.143), channel_id=1, source_target_pairs={{0,16},{1,17},{2,18},{3,19},{4,20},{5,21},{6,22},{7,23},{8,24},{9,... | collective-permute-start | bytes 196616 | tf_op jit(solution)/shard_map/ppermute | solution.py:37
  32.0 26.3 %collective-permute-start.7 = (bf16[272,1024]{1,0:T(8,128)(2,1)S(1)}, bf16[272,1024]{1,0:T(8,128)(2,1)S(1)}, u32[]{:S(2)}, u32[]{:S(2)}) collective-permute-start(bf16[272,1024]{1,0:T(8,128)(2,1)S(1)} %get-tuple-element.145.refs_4_), channel_id=1, source_target_pairs={{0,8},{1,9},{2,10},{3,11},{4,12},{5,13},{6,14},{7,15},{8,0},{9,1},... | collective-permute-start | bytes 1671176 | tf_op jit(solution)/shard_map/ppermute | solution.py:37
  33.5 24.8 %collective-permute-start.8 = (bf16[272,1024]{1,0:T(8,128)(2,1)S(1)}, bf16[272,1024]{1,0:T(8,128)(2,1)S(1)}, u32[]{:S(2)}, u32[]{:S(2)}) collective-permute-start(bf16[272,1024]{1,0:T(8,128)(2,1)S(1)} %get-tuple-element.145.refs_4_), channel_id=1, source_target_pairs={{0,16},{1,17},{2,18},{3,19},{4,20},{5,21},{6,22},{7,23},{8,24},{9,... | collective-permute-start | bytes 1671176 | tf_op jit(solution)/shard_map/ppermute | solution.py:37
  34.0 24.3 %collective-permute-start.9 = (bf16[272,1024]{1,0:T(8,128)(2,1)S(1)}, bf16[272,1024]{1,0:T(8,128)(2,1)S(1)}, u32[]{:S(2)}, u32[]{:S(2)}) collective-permute-start(bf16[272,1024]{1,0:T(8,128)(2,1)S(1)} %get-tuple-element.145.refs_4_), channel_id=1, source_target_pairs={{0,24},{1,25},{2,26},{3,27},{4,28},{5,29},{6,30},{7,31},{8,16},{9,... | collective-permute-start | bytes 1671176 | tf_op jit(solution)/shard_map/ppermute | solution.py:37
  35.5 8.4 %collective-permute-start.17 = (bf16[96,1024]{1,0:T(8,128)(2,1)S(1)}, bf16[96,1024]{1,0:T(8,128)(2,1)S(1)}, u32[]{:S(2)}, u32[]{:S(2)}) collective-permute-start(bf16[96,1024]{1,0:T(8,128)(2,1)S(1)} %get-tuple-element.153.refs_5_), channel_id=1, source_target_pairs={{0,2},{1,3},{2,0},{3,1},{4,6},{5,7},{6,4},{7,5},{8,10},{9,11},{10,... | collective-permute-start | bytes 589832 | tf_op jit(solution)/shard_map/ppermute | solution.py:37
  35.5 19.4 %collective-permute-start.18 = (bf16[96,1024]{1,0:T(8,128)(2,1)S(1)}, bf16[96,1024]{1,0:T(8,128)(2,1)S(1)}, u32[]{:S(2)}, u32[]{:S(2)}) collective-permute-start(bf16[96,1024]{1,0:T(8,128)(2,1)S(1)} %get-tuple-element.153.refs_5_), channel_id=1, source_target_pairs={{0,4},{1,5},{2,6},{3,7},{4,0},{5,1},{6,2},{7,3},{8,12},{9,13},{10,... | collective-permute-start | bytes 589832 | tf_op jit(solution)/shard_map/ppermute | solution.py:37
  44.0 14.3 %collective-permute-start.19 = (bf16[96,1024]{1,0:T(8,128)(2,1)S(1)}, bf16[96,1024]{1,0:T(8,128)(2,1)S(1)}, u32[]{:S(2)}, u32[]{:S(2)}) collective-permute-start(bf16[96,1024]{1,0:T(8,128)(2,1)S(1)} %get-tuple-element.153.refs_5_), channel_id=1, source_target_pairs={{0,6},{1,7},{2,4},{3,5},{4,2},{5,3},{6,0},{7,1},{8,14},{9,15},{10,... | collective-permute-start | bytes 589832 | tf_op jit(solution)/shard_map/ppermute | solution.py:37
  61.6 187.1 %reduce-scatter.2.cloned.1.call-start = ((), (), s32[]{:S(2)}) async-start(), calls=%async_computation.3 | async-start | bytes 4718592 | tf_op jit(solution)/shard_map/reduce_scatter | solution.py:1145
  64.7 23.5 %collective-permute-start.20 = (bf16[4,64,1024]{2,1,0:T(8,128)(2,1)}, bf16[4,64,1024]{2,1,0:T(8,128)(2,1)S(1)}, u32[]{:S(2)}, u32[]{:S(2)}) collective-permute-start(bf16[4,64,1024]{2,1,0:T(8,128)(2,1)} %copy-done.50), channel_id=1, source_target_pairs={{0,8},{1,9},{2,10},{3,11},{4,12},{5,13},{6,14},{7,15},{8,0},{9,1},... | collective-permute-start | bytes 1572872 | tf_op jit(solution)/shard_map/ppermute | solution.py:37
  65.9 25.6 %collective-permute-start.21 = (bf16[4,64,1024]{2,1,0:T(8,128)(2,1)}, bf16[4,64,1024]{2,1,0:T(8,128)(2,1)S(1)}, u32[]{:S(2)}, u32[]{:S(2)}) collective-permute-start(bf16[4,64,1024]{2,1,0:T(8,128)(2,1)} %copy-done.50), channel_id=1, source_target_pairs={{0,16},{1,17},{2,18},{3,19},{4,20},{5,21},{6,22},{7,23},{8,24},{9,... | collective-permute-start | bytes 1572872 | tf_op jit(solution)/shard_map/ppermute | solution.py:37
  67.3 24.3 %collective-permute-start.22 = (bf16[4,64,1024]{2,1,0:T(8,128)(2,1)}, bf16[4,64,1024]{2,1,0:T(8,128)(2,1)S(1)}, u32[]{:S(2)}, u32[]{:S(2)}) collective-permute-start(bf16[4,64,1024]{2,1,0:T(8,128)(2,1)} %copy-done.50), channel_id=1, source_target_pairs={{0,24},{1,25},{2,26},{3,27},{4,28},{5,29},{6,30},{7,31},{8,16},{9,... | collective-permute-start | bytes 1572872 | tf_op jit(solution)/shard_map/ppermute | solution.py:37
  91.9 15.6 %collective-permute-start.25 = (bf16[4,32,1024]{2,1,0:T(8,128)(2,1)S(1)}, bf16[4,32,1024]{2,1,0:T(8,128)(2,1)S(1)}, u32[]{:S(2)}, u32[]{:S(2)}) collective-permute-start(bf16[4,32,1024]{2,1,0:T(8,128)(2,1)S(1)} %shard_map.269.refs_0_), channel_id=1, source_target_pairs={{0,8},{1,9},{2,10},{3,11},{4,12},{5,13},{6,14},{7,15},{8,0},{9,1},... | collective-permute-start | bytes 786440 | tf_op jit(solution)/shard_map/ppermute | solution.py:37
  92.5 14.9 %collective-permute-start.26 = (bf16[4,32,1024]{2,1,0:T(8,128)(2,1)S(1)}, bf16[4,32,1024]{2,1,0:T(8,128)(2,1)S(1)}, u32[]{:S(2)}, u32[]{:S(2)}) collective-permute-start(bf16[4,32,1024]{2,1,0:T(8,128)(2,1)S(1)} %shard_map.269.refs_0_), channel_id=1, source_target_pairs={{0,16},{1,17},{2,18},{3,19},{4,20},{5,21},{6,22},{7,23},{8,24},{9,... | collective-permute-start | bytes 786440 | tf_op jit(solution)/shard_map/ppermute | solution.py:37
  93.9 13.6 %collective-permute-start.27 = (bf16[4,32,1024]{2,1,0:T(8,128)(2,1)S(1)}, bf16[4,32,1024]{2,1,0:T(8,128)(2,1)S(1)}, u32[]{:S(2)}, u32[]{:S(2)}) collective-permute-start(bf16[4,32,1024]{2,1,0:T(8,128)(2,1)S(1)} %shard_map.269.refs_0_), channel_id=1, source_target_pairs={{0,24},{1,25},{2,26},{3,27},{4,28},{5,29},{6,30},{7,31},{8,16},{9,... | collective-permute-start | bytes 786440 | tf_op jit(solution)/shard_map/ppermute | solution.py:37
  107.6 20.9 %collective-permute-start.28 = (bf16[16,32,1024]{2,1,0:T(8,128)(2,1)S(1)}, bf16[16,32,1024]{2,1,0:T(8,128)(2,1)}, u32[]{:S(2)}, u32[]{:S(2)}) collective-permute-start(bf16[16,32,1024]{2,1,0:T(8,128)(2,1)S(1)} %shard_map.270.refs_4_), channel_id=1, source_target_pairs={{0,1},{1,0},{2,3},{3,2},{4,5},{5,4},{6,7},{7,6},{8,9},{9,8},{10,11... | collective-permute-start | bytes 3145736 | tf_op jit(solution)/shard_map/ppermute | solution.py:37
  108.2 9.5 %collective-permute-start.29 = (bf16[128,1024]{1,0:T(8,128)(2,1)}, bf16[128,1024]{1,0:T(8,128)(2,1)}, u32[]{:S(2)}, u32[]{:S(2)}) collective-permute-start(bf16[128,1024]{1,0:T(8,128)(2,1)} %get-tuple-element.159.refs_0_), channel_id=1, source_target_pairs={{0,8},{1,9},{2,10},{3,11},{4,12},{5,13},{6,14},{7,15},{8,0},{9,1},... | collective-permute-start | bytes 786440 | tf_op jit(solution)/shard_map/ppermute | solution.py:37
  108.8 13.2 %collective-permute-start.31 = (bf16[128,1024]{1,0:T(8,128)(2,1)}, bf16[128,1024]{1,0:T(8,128)(2,1)}, u32[]{:S(2)}, u32[]{:S(2)}) collective-permute-start(bf16[128,1024]{1,0:T(8,128)(2,1)} %get-tuple-element.159.refs_0_), channel_id=1, source_target_pairs={{0,16},{1,17},{2,18},{3,19},{4,20},{5,21},{6,22},{7,23},{8,24},{9,... | collective-permute-start | bytes 786440 | tf_op jit(solution)/shard_map/ppermute | solution.py:37
  110.1 14.9 %collective-permute-start.33 = (bf16[128,1024]{1,0:T(8,128)(2,1)}, bf16[128,1024]{1,0:T(8,128)(2,1)}, u32[]{:S(2)}, u32[]{:S(2)}) collective-permute-start(bf16[128,1024]{1,0:T(8,128)(2,1)} %get-tuple-element.159.refs_0_), channel_id=1, source_target_pairs={{0,24},{1,25},{2,26},{3,27},{4,28},{5,29},{6,30},{7,31},{8,16},{9,... | collective-permute-start | bytes 786440 | tf_op jit(solution)/shard_map/ppermute | solution.py:37
  119.4 13.3 %collective-permute-start.30 = (bf16[128,1024]{1,0:T(8,128)(2,1)S(1)}, bf16[128,1024]{1,0:T(8,128)(2,1)S(1)}, u32[]{:S(2)}, u32[]{:S(2)}) collective-permute-start(bf16[128,1024]{1,0:T(8,128)(2,1)S(1)} %get-tuple-element.170), channel_id=1, source_target_pairs={{0,8},{1,9},{2,10},{3,11},{4,12},{5,13},{6,14},{7,15},{8,0},{9,1},... | collective-permute-start | bytes 786440 | tf_op jit(solution)/shard_map/ppermute | solution.py:37
  123.8 11.8 %collective-permute-start.32 = (bf16[128,1024]{1,0:T(8,128)(2,1)S(1)}, bf16[128,1024]{1,0:T(8,128)(2,1)S(1)}, u32[]{:S(2)}, u32[]{:S(2)}) collective-permute-start(bf16[128,1024]{1,0:T(8,128)(2,1)S(1)} %get-tuple-element.171), channel_id=1, source_target_pairs={{0,16},{1,17},{2,18},{3,19},{4,20},{5,21},{6,22},{7,23},{8,24},{9,... | collective-permute-start | bytes 786440 | tf_op jit(solution)/shard_map/ppermute | solution.py:37
  126.7 8.9 %collective-permute-start.34 = (bf16[128,1024]{1,0:T(8,128)(2,1)S(1)}, bf16[128,1024]{1,0:T(8,128)(2,1)S(1)}, u32[]{:S(2)}, u32[]{:S(2)}) collective-permute-start(bf16[128,1024]{1,0:T(8,128)(2,1)S(1)} %get-tuple-element.172), channel_id=1, source_target_pairs={{0,24},{1,25},{2,26},{3,27},{4,28},{5,29},{6,30},{7,31},{8,16},{9,... | collective-permute-start | bytes 786440 | tf_op jit(solution)/shard_map/ppermute | solution.py:37
  136.5 6.7 %collective-permute-start.35 = (bf16[128,1024]{1,0:T(8,128)(2,1)S(1)}, bf16[128,1024]{1,0:T(8,128)(2,1)S(1)}, u32[]{:S(2)}, u32[]{:S(2)}) collective-permute-start(bf16[128,1024]{1,0:T(8,128)(2,1)S(1)} %get-tuple-element.174.refs_0_.refs_12_), channel_id=1, source_target_pairs={{0,8},{1,9},{2,10},{3,11},{4,12},{5,13},{6,14},{7,15},{8,0},{9,1},... | collective-permute-start | bytes 786440 | tf_op jit(solution)/shard_map/ppermute | solution.py:37
  138.9 8.9 %collective-permute-start.37 = (bf16[128,1024]{1,0:T(8,128)(2,1)S(1)}, bf16[128,1024]{1,0:T(8,128)(2,1)S(1)}, u32[]{:S(2)}, u32[]{:S(2)}) collective-permute-start(bf16[128,1024]{1,0:T(8,128)(2,1)S(1)} %get-tuple-element.174.refs_0_.refs_12_), channel_id=1, source_target_pairs={{0,16},{1,17},{2,18},{3,19},{4,20},{5,21},{6,22},{7,23},{8,24},{9,... | collective-permute-start | bytes 786440 | tf_op jit(solution)/shard_map/ppermute | solution.py:37
  138.9 10.5 %collective-permute-start.39 = (bf16[128,1024]{1,0:T(8,128)(2,1)S(1)}, bf16[128,1024]{1,0:T(8,128)(2,1)S(1)}, u32[]{:S(2)}, u32[]{:S(2)}) collective-permute-start(bf16[128,1024]{1,0:T(8,128)(2,1)S(1)} %get-tuple-element.174.refs_0_.refs_12_), channel_id=1, source_target_pairs={{0,24},{1,25},{2,26},{3,27},{4,28},{5,29},{6,30},{7,31},{8,16},{9,... | collective-permute-start | bytes 786440 | tf_op jit(solution)/shard_map/ppermute | solution.py:37
  140.3 30.5 %collective-permute-start.44 = (bf16[5,128,1024]{2,1,0:T(8,128)(2,1)S(1)}, bf16[5,128,1024]{2,1,0:T(8,128)(2,1)S(1)}, u32[]{:S(2)}, u32[]{:S(2)}) collective-permute-start(bf16[5,128,1024]{2,1,0:T(8,128)(2,1)S(1)} %get-tuple-element.193.refs_0_), channel_id=1, source_target_pairs={{0,1},{1,0},{2,3},{3,2},{4,5},{5,4},{6,7},{7,6},{8,9},{9,8},{10,11... | collective-permute-start | bytes 3932168 | tf_op jit(solution)/shard_map/ppermute | solution.py:37
  144.7 10.8 %collective-permute-start.36 = (bf16[128,1024]{1,0:T(8,128)(2,1)S(1)}, bf16[128,1024]{1,0:T(8,128)(2,1)S(1)}, u32[]{:S(2)}, u32[]{:S(2)}) collective-permute-start(bf16[128,1024]{1,0:T(8,128)(2,1)S(1)} %get-tuple-element.182), channel_id=1, source_target_pairs={{0,8},{1,9},{2,10},{3,11},{4,12},{5,13},{6,14},{7,15},{8,0},{9,1},... | collective-permute-start | bytes 786440 | tf_op jit(solution)/shard_map/ppermute | solution.py:37
  149.3 11.1 %collective-permute-start.38 = (bf16[128,1024]{1,0:T(8,128)(2,1)S(1)}, bf16[128,1024]{1,0:T(8,128)(2,1)S(1)}, u32[]{:S(2)}, u32[]{:S(2)}) collective-permute-start(bf16[128,1024]{1,0:T(8,128)(2,1)S(1)} %get-tuple-element.184), channel_id=1, source_target_pairs={{0,16},{1,17},{2,18},{3,19},{4,20},{5,21},{6,22},{7,23},{8,24},{9,... | collective-permute-start | bytes 786440 | tf_op jit(solution)/shard_map/ppermute | solution.py:37
  150.9 9.4 %collective-permute-start.40 = (bf16[128,1024]{1,0:T(8,128)(2,1)S(1)}, bf16[128,1024]{1,0:T(8,128)(2,1)S(1)}, u32[]{:S(2)}, u32[]{:S(2)}) collective-permute-start(bf16[128,1024]{1,0:T(8,128)(2,1)S(1)} %get-tuple-element.186), channel_id=1, source_target_pairs={{0,24},{1,25},{2,26},{3,27},{4,28},{5,29},{6,30},{7,31},{8,16},{9,... | collective-permute-start | bytes 786440 | tf_op jit(solution)/shard_map/ppermute | solution.py:37
  179.3 40.1 %collective-permute-start.50 = (bf16[384,1024]{1,0:T(8,128)(2,1)}, bf16[384,1024]{1,0:T(8,128)(2,1)S(1)}, u32[]{:S(2)}, u32[]{:S(2)}) collective-permute-start(bf16[384,1024]{1,0:T(8,128)(2,1)} %copy-done.69), channel_id=1, source_target_pairs={{0,8},{1,9},{2,10},{3,11},{4,12},{5,13},{6,14},{7,15},{8,0},{9,1},... | collective-permute-start | bytes 2359304 | tf_op jit(solution)/shard_map/ppermute | solution.py:37
  180.3 39.0 %collective-permute-start.51 = (bf16[384,1024]{1,0:T(8,128)(2,1)}, bf16[384,1024]{1,0:T(8,128)(2,1)S(1)}, u32[]{:S(2)}, u32[]{:S(2)}) collective-permute-start(bf16[384,1024]{1,0:T(8,128)(2,1)} %copy-done.68), channel_id=1, source_target_pairs={{0,16},{1,17},{2,18},{3,19},{4,20},{5,21},{6,22},{7,23},{8,24},{9,... | collective-permute-start | bytes 2359304 | tf_op jit(solution)/shard_map/ppermute | solution.py:37
  181.6 37.8 %collective-permute-start.52 = (bf16[384,1024]{1,0:T(8,128)(2,1)}, bf16[384,1024]{1,0:T(8,128)(2,1)S(1)}, u32[]{:S(2)}, u32[]{:S(2)}) collective-permute-start(bf16[384,1024]{1,0:T(8,128)(2,1)} %copy-done.67), channel_id=1, source_target_pairs={{0,24},{1,25},{2,26},{3,27},{4,28},{5,29},{6,30},{7,31},{8,16},{9,... | collective-permute-start | bytes 2359304 | tf_op jit(solution)/shard_map/ppermute | solution.py:37
  189.3 7.6 %collective-permute-start.46 = (f32[8,1024]{1,0:T(8,128)S(1)}, f32[8,1024]{1,0:T(8,128)S(1)}, u32[]{:S(2)}, u32[]{:S(2)}) collective-permute-start(f32[8,1024]{1,0:T(8,128)S(1)} %shard_map.284), channel_id=1, source_target_pairs={{4,0},{5,1},{6,2},{7,3},{12,8},{13,9},{14,10},{15,11},{20,16},{21,... | collective-permute-start | bytes 98312 | tf_op jit(solution)/shard_map/ppermute | solution.py:37
  202.2 17.6 %collective-permute-start.48 = (bf16[2,128,1024]{2,1,0:T(8,128)(2,1)S(1)}, bf16[2,128,1024]{2,1,0:T(8,128)(2,1)S(1)}, u32[]{:S(2)}, u32[]{:S(2)}) collective-permute-start(bf16[2,128,1024]{2,1,0:T(8,128)(2,1)S(1)} %shard_map.288.refs_0_.refs_2_), channel_id=1, source_target_pairs={{0,1},{1,0},{2,3},{3,2},{4,5},{5,4},{6,7},{7,6},{8,9},{9,8},{10,11... | collective-permute-start | bytes 1572872 | tf_op jit(solution)/shard_map/ppermute | solution.py:37
  220.6 26.7 %collective-permute-start.53 = (bf16[272,1024]{1,0:T(8,128)(2,1)S(1)}, bf16[272,1024]{1,0:T(8,128)(2,1)S(1)}, u32[]{:S(2)}, u32[]{:S(2)}) collective-permute-start(bf16[272,1024]{1,0:T(8,128)(2,1)S(1)} %get-tuple-element.223), channel_id=1, source_target_pairs={{0,8},{1,9},{2,10},{3,11},{4,12},{5,13},{6,14},{7,15},{8,0},{9,1},... | collective-permute-start | bytes 1671176 | tf_op jit(solution)/shard_map/ppermute | solution.py:37
  221.5 25.8 %collective-permute-start.54 = (bf16[272,1024]{1,0:T(8,128)(2,1)S(1)}, bf16[272,1024]{1,0:T(8,128)(2,1)S(1)}, u32[]{:S(2)}, u32[]{:S(2)}) collective-permute-start(bf16[272,1024]{1,0:T(8,128)(2,1)S(1)} %get-tuple-element.224), channel_id=1, source_target_pairs={{0,16},{1,17},{2,18},{3,19},{4,20},{5,21},{6,22},{7,23},{8,24},{9,... | collective-permute-start | bytes 1671176 | tf_op jit(solution)/shard_map/ppermute | solution.py:37
  222.7 25.5 %collective-permute-start.55 = (bf16[272,1024]{1,0:T(8,128)(2,1)S(1)}, bf16[272,1024]{1,0:T(8,128)(2,1)S(1)}, u32[]{:S(2)}, u32[]{:S(2)}) collective-permute-start(bf16[272,1024]{1,0:T(8,128)(2,1)S(1)} %get-tuple-element.225), channel_id=1, source_target_pairs={{0,24},{1,25},{2,26},{3,27},{4,28},{5,29},{6,30},{7,31},{8,16},{9,... | collective-permute-start | bytes 1671176 | tf_op jit(solution)/shard_map/ppermute | solution.py:37
  224.1 18.8 %collective-permute-start.56 = (bf16[192,1024]{1,0:T(8,128)(2,1)S(1)}, bf16[192,1024]{1,0:T(8,128)(2,1)S(1)}, u32[]{:S(2)}, u32[]{:S(2)}) collective-permute-start(bf16[192,1024]{1,0:T(8,128)(2,1)S(1)} %shard_map.293), channel_id=1, source_target_pairs={{0,4},{1,5},{2,6},{3,7},{4,0},{5,1},{6,2},{7,3},{8,12},{9,13},{10,... | collective-permute-start | bytes 1179656 | tf_op jit(solution)/shard_map/ppermute | solution.py:37
  243.0 15.1 %collective-permute-start.60 = (bf16[96,1024]{1,0:T(8,128)(2,1)S(1)}, bf16[96,1024]{1,0:T(8,128)(2,1)S(1)}, u32[]{:S(2)}, u32[]{:S(2)}) collective-permute-start(bf16[96,1024]{1,0:T(8,128)(2,1)S(1)} %get-tuple-element.239), channel_id=1, source_target_pairs={{0,2},{1,3},{2,0},{3,1},{4,6},{5,7},{6,4},{7,5},{8,10},{9,11},{10,... | collective-permute-start | bytes 589832 | tf_op jit(solution)/shard_map/ppermute | solution.py:37
  250.5 22.6 %all-to-all-start = ((bf16[4,32,1024]{2,1,0:T(8,128)(2,1)}), bf16[4,32,1024]{2,1,0:T(8,128)(2,1)S(1)}, u32[]{:S(2)}, u32[]{:S(2)}) async-start(bf16[4,32,1024]{2,1,0:T(8,128)(2,1)} %shard_map.298), calls=%async_computation.1 | async-start | bytes 524288 | tf_op jit(solution)/shard_map/all_to_all | solution.py:1289
  253.9 7.7 %collective-permute-start.57 = (bf16[80,1024]{1,0:T(8,128)(2,1)S(1)}, bf16[80,1024]{1,0:T(8,128)(2,1)S(1)}, u32[]{:S(2)}, u32[]{:S(2)}) collective-permute-start(bf16[80,1024]{1,0:T(8,128)(2,1)S(1)} %get-tuple-element.233), channel_id=1, source_target_pairs={{0,2},{1,3},{2,0},{3,1},{4,6},{5,7},{6,4},{7,5},{8,10},{9,11},{10,... | collective-permute-start | bytes 491528 | tf_op jit(solution)/shard_map/ppermute | solution.py:37
  256.5 11.7 %collective-permute-start.58 = (bf16[80,1024]{1,0:T(8,128)(2,1)S(1)}, bf16[80,1024]{1,0:T(8,128)(2,1)S(1)}, u32[]{:S(2)}, u32[]{:S(2)}) collective-permute-start(bf16[80,1024]{1,0:T(8,128)(2,1)S(1)} %get-tuple-element.234), channel_id=1, source_target_pairs={{0,4},{1,5},{2,6},{3,7},{4,0},{5,1},{6,2},{7,3},{8,12},{9,13},{10,... | collective-permute-start | bytes 491528 | tf_op jit(solution)/shard_map/ppermute | solution.py:37
  256.5 15.7 %collective-permute-start.59 = (bf16[80,1024]{1,0:T(8,128)(2,1)S(1)}, bf16[80,1024]{1,0:T(8,128)(2,1)S(1)}, u32[]{:S(2)}, u32[]{:S(2)}) collective-permute-start(bf16[80,1024]{1,0:T(8,128)(2,1)S(1)} %get-tuple-element.235), channel_id=1, source_target_pairs={{0,6},{1,7},{2,4},{3,5},{4,2},{5,3},{6,0},{7,1},{8,14},{9,15},{10,... | collective-permute-start | bytes 491528 | tf_op jit(solution)/shard_map/ppermute | solution.py:37
  (86 other events, 637.7 us)
Sparse Core Ops, SparseCore 0:
  61.7 46.7 all-gather.1
  179.4 46.9 reduce-scatter.1
